TPU v7x, 512 devices: a whole 4x8x8 slice. The times are simulated.
512 devices in a mesh: dp: 8 (over x, core), tensor: 64 (over z, y).
Axes of the slice: x: 4, y: 8, z: 8, core: 2. Of those that a mesh axis runs over, the one named last changes fastest.
Arguments:
- tokens: bfloat16 [4096, 4096], P('dp', 'tensor'), may hold values from -8 to 8
- gain: float32 [4096], replicated, may hold values from 0.1 to 1.9
- cotangent: bfloat16 [4096, 4096], P('dp', 'tensor'), may hold values from -30 to 30, as said below
- gate_weight: bfloat16 [4096, 14336], P('dp', 'tensor'), may hold values from -0.09375 to 0.09375
- up_weight: bfloat16 [4096, 14336], P('dp', 'tensor'), may hold values from -0.09375 to 0.09375
- down_weight: bfloat16 [14336, 4096], P('tensor', 'dp'), may hold values from -0.046875 to 0.046875
Outputs:
- grad_down: float32 [14336, 4096], P('tensor', 'dp')
- grad_gain: float32 [4096], P('tensor')
Inputs may be any that keep to these rules, and one draw needn't show every extreme that they name: Each sequence's cotangent has its own overall scale.
All inputs are finite; a program needn't handle non-finite values.
Results may differ from a plain program's by a relative error of at most 0.015.
Values may be sent and summed in bfloat16 or wider, within the bound.
No kernel may reach another device: no remote copies, remote signals or barrier semaphores. Data moves between devices by JAX's collectives and lax.ppermute only.
A program may use at most 64 MiB of HBM per device.

v0:
```python
import math

import jax
import jax.numpy as jnp
from jax import lax
from jax.sharding import PartitionSpec as P

MODEL_FEATURES = 4096
FF = 14336
SEQUENCE_LENGTH = 64


def body(tokens, gain, cotangent, gate_weight, up_weight, down_weight):
    whole_x, whole_dy = (
        lax.all_gather(tokens, "tensor", axis=1, tiled=True),
        lax.all_gather(cotangent, "tensor", axis=1, tiled=True),
    )
    seq_count = whole_x.shape[0] // SEQUENCE_LENGTH
    width = whole_x.shape[1]
    dp_count = lax.axis_size("dp")
    total_seqs = seq_count * dp_count
    input_float = whole_x.astype(jnp.float32)
    inverse_norm = lax.rsqrt(jnp.mean(input_float * input_float, axis=1, keepdims=True) + 1e-05)
    normed_input = (input_float * inverse_norm * gain).astype(jnp.bfloat16)
    gate_full, up_full = (
        lax.all_gather(gate_weight, "dp", axis=0, tiled=True),
        lax.all_gather(up_weight, "dp", axis=0, tiled=True),
    )
    gate = jnp.dot(normed_input, gate_full, preferred_element_type=jnp.float32)
    up = jnp.dot(normed_input, up_full, preferred_element_type=jnp.float32)
    contract = (((1,), (1,)), ((), ()))
    block = whole_dy
    back = lax.dot_general(
        block,
        lax.all_gather(down_weight, "dp", axis=1, tiled=True),
        contract,
        preferred_element_type=jnp.float32,
    )
    sigma = jax.nn.sigmoid(gate)
    swish = gate * sigma
    hidden = (swish * up).astype(jnp.bfloat16)
    d_gate = (back * up * sigma * (1.0 + gate * (1.0 - sigma))).astype(jnp.bfloat16)
    d_up = (back * swish).astype(jnp.bfloat16)
    normed_cotangent = lax.dot_general(
        d_gate, gate_full, contract, preferred_element_type=jnp.float32
    ) + lax.dot_general(d_up, up_full, contract, preferred_element_type=jnp.float32)
    gain_factor = jnp.sum(
        (input_float * inverse_norm * normed_cotangent).reshape(seq_count, SEQUENCE_LENGTH, width),
        axis=1,
    )
    hidden3 = hidden.reshape(seq_count, SEQUENCE_LENGTH, hidden.shape[1])
    cotangent3 = whole_dy.reshape(seq_count, SEQUENCE_LENGTH, width)
    down_part = jnp.einsum("sif,sjf->sij", hidden3, hidden3, preferred_element_type=jnp.float32)
    down_total, gain_whole = lax.psum((down_part, gain_factor), "tensor")
    gain_sq = jnp.sum(gain_whole * gain_whole, axis=1)
    share = width // lax.axis_size("tensor")
    gain_mine = lax.dynamic_slice_in_dim(gain_whole, lax.axis_index("tensor") * share, share, 1)
    dy_gram = jnp.einsum("sid,sjd->sij", cotangent3, cotangent3, preferred_element_type=jnp.float32)
    down_sq = jnp.sum(down_total * dy_gram, axis=(1, 2))
    down_bound = 0.6 * math.sqrt(SEQUENCE_LENGTH * FF * MODEL_FEATURES)
    gain_bound = 0.5 * math.sqrt(SEQUENCE_LENGTH * MODEL_FEATURES)
    down_scale = jnp.minimum(1.0, down_bound / (jnp.sqrt(down_sq) + 1e-06)) / total_seqs
    gain_scale = jnp.minimum(1.0, gain_bound / (jnp.sqrt(gain_sq) + 1e-06)) / total_seqs
    gain_local = jnp.sum(gain_scale[:, None] * gain_mine, axis=0)
    grad_gain = lax.psum(gain_local, "dp")
    weighted = (
        jnp.repeat(down_scale, SEQUENCE_LENGTH)[:, None] * whole_dy.astype(jnp.float32)
    ).astype(jnp.bfloat16)
    block = weighted
    grad_rows = lax.psum_scatter(
        lax.dot_general(
            block, hidden, (((0,), (0,)), ((), ())), preferred_element_type=jnp.float32
        ).astype(jnp.bfloat16),
        "dp",
        scatter_dimension=0,
        tiled=True,
    ).astype(jnp.float32)
    return (grad_rows.T, grad_gain)


def solution(mesh):
    in_specs = (
        P("dp", "tensor"),
        P(),
        P("dp", "tensor"),
        P("dp", "tensor"),
        P("dp", "tensor"),
        P("tensor", "dp"),
    )
    out_specs = (P("tensor", "dp"), P("tensor"))
    return jax.shard_map(body, mesh=mesh, in_specs=in_specs, out_specs=out_specs, check_vma=False)
```

profile of v0, /device:TPU:1, one launch (start us, length us, event | category | flops | bytes accessed | tf_op | source)
XLA Modules:
  0.0 501.2 jit_solution(3417777419510796181)
XLA Ops:
  7.2 0.7 all-gather.6.cloned.1.call-update
  7.9 0.7 all-gather.8.cloned.1.call-update
  8.7 0.7 all-gather.10.cloned.1.call-update
  10.6 89.2 %all-gather.6.cloned.1.call-done = bf16[512,4096]{0,1:T(8,128)(2,1)} async-done(((bf16[512,64]{0,1:T(8,128)(2,1)}), bf16[512,4096]{0,1:T(8,128)(2,1)}) %all-gather.6.cloned.1.call-update) | async-done | bytes 4194320 | tf_op jit(solution)/shard_map/all_gather | solution.py:15
  99.8 6.4 %copy.18 = bf16[512,4096]{1,0:T(8,128)(2,1)} copy(bf16[512,4096]{0,1:T(8,128)(2,1)} %all-gather.6.cloned.1.call-done) | data formatting | bytes 8388608 | tf_op jit(solution)/shard_map/all_gather | solution.py:15
  106.2 3.1 fusion.3
  109.3 23.9 %all-gather.8.cloned.1.call-done = bf16[4096,224]{0,1:T(8,128)(2,1)} async-done(((bf16[512,224]{0,1:T(8,128)(2,1)}), bf16[4096,224]{0,1:T(8,128)(2,1)}) %all-gather.8.cloned.1.call-update) | async-done | bytes 1835024 | tf_op jit(solution)/shard_map/all_gather | solution.py:26
  133.2 4.4 fusion.7
  137.6 28.2 %all-gather.10.cloned.1.call-done = bf16[4096,224]{0,1:T(8,128)(2,1)} async-done(((bf16[512,224]{0,1:T(8,128)(2,1)}), bf16[4096,224]{0,1:T(8,128)(2,1)}) %all-gather.10.cloned.1.call-update) | async-done | bytes 1835024 | tf_op jit(solution)/shard_map/all_gather | solution.py:27
  165.8 4.4 multiply_convert_fusion.4
  170.4 0.9 fusion.16
  171.3 27.0 %all-gather.14.cloned.1.call-done = bf16[224,4096]{1,0:T(8,128)(2,1)} async-done(((bf16[224,512]{1,0:T(8,128)(2,1)}), bf16[224,4096]{1,0:T(8,128)(2,1)}) %all-gather.14.cloned.1.call-update) | async-done | bytes 1835024 | tf_op jit(solution)/shard_map/all_gather | solution.py:35
  198.3 85.9 %all-gather.12.cloned.1.call-done = bf16[512,4096]{0,1:T(8,128)(2,1)} async-done(((bf16[512,64]{0,1:T(8,128)(2,1)}), bf16[512,4096]{0,1:T(8,128)(2,1)}) %all-gather.12.cloned.1.call-update) | async-done | bytes 4194320 | tf_op jit(solution)/shard_map/all_gather | solution.py:16
  284.2 3.8 fusion.17
  288.1 1.4 fusion.11
  289.5 0.7 copy-done
  290.8 3.0 bitcast_reduce_fusion
  293.9 6.4 %copy.20 = bf16[512,4096]{1,0:T(8,128)(2,1)} copy(bf16[512,4096]{0,1:T(8,128)(2,1)} %all-gather.12.cloned.1.call-done) | data formatting | bytes 8388608 | tf_op jit(solution)/shard_map/all_gather | solution.py:16
  300.3 145.0 %all-reduce.3.cloned.1.call-done = (f32[8,64,64]{2,1,0:T(8,128)}, f32[8,4096]{1,0:T(8,128)}) async-done(((f32[8,64,64]{2,1,0:T(8,128)}, f32[8,4096]{1,0:T(8,128)}), (f32[8,64,64]{2,1,0:T(8,128)}, f32[8,4096]{1,0:T(8,128)})) %all-reduce.3.cloned.1.call-update) | async-done | bytes 262160 | tf_op jit(solution)/shard_map/psum | solution.py:54
  445.3 4.8 fusion.9
  450.3 4.9 convolution_convert_fusion
  455.5 17.1 %psum.23 = f32[64]{0:T(128)} all-reduce(f32[64]{0:T(128)S(1)} %multiply_reduce_fusion.1), channel_id=1, replica_groups=mesh['dp'=8,'tensor'=64] {'dp'}, use_global_device_ids=true, to_apply=%region_8.0 | all-reduce | flops 64 | bytes 512 | tf_op jit(solution)/shard_map/psum | solution.py:65
  472.6 20.0 %reduce-scatter.2.cloned.1.call-done = bf16[512,224]{0,1:T(8,128)(2,1)} async-done(((bf16[4096,224]{0,1:T(8,128)(2,1)}), bf16[512,224]{0,1:T(8,128)(2,1)}) %reduce-scatter.2.cloned.1.call-update) | async-done | bytes 229392 | tf_op jit(solution)/shard_map/reduce_scatter | solution.py:70
  492.6 1.8 convert_bitcast_fusion
  (28 shorter events, 2.5 us)
Async XLA Ops:
  7.2 92.7 %all-gather.6.cloned.1.call-start = ((), (), s32[]{:S(2)}) async-start(), calls=%async_computation.1 | async-start | bytes 4259840 | tf_op jit(solution)/shard_map/all_gather | solution.py:15
  7.9 125.3 %all-gather.8.cloned.1.call-start = ((), (), s32[]{:S(2)}) async-start(), calls=%async_computation.2 | async-start | bytes 2064384 | tf_op jit(solution)/shard_map/all_gather | solution.py:26
  8.6 157.2 %all-gather.10.cloned.1.call-start = ((), (), s32[]{:S(2)}) async-start(), calls=%async_computation.3 | async-start | bytes 2064384 | tf_op jit(solution)/shard_map/all_gather | solution.py:27
  9.4 188.9 %all-gather.14.cloned.1.call-start = ((), (), s32[]{:S(2)}) async-start(), calls=%async_computation.6 | async-start | bytes 2064384 | tf_op jit(solution)/shard_map/all_gather | solution.py:35
  10.0 274.2 %all-gather.12.cloned.1.call-start = ((), (), s32[]{:S(2)}) async-start(), calls=%async_computation.4 | async-start | bytes 4259840 | tf_op jit(solution)/shard_map/all_gather | solution.py:16
  10.5 434.8 %all-reduce.3.cloned.1.call-start = ((), (), s32[]{:S(2)}) async-start(), calls=%async_computation.7 | async-start | bytes 786432 | tf_op jit(solution)/shard_map/psum | solution.py:54
  106.2 27.0 %copy-start.4 = (f32[4096]{0:T(1024)S(1)}, f32[4096]{0:T(1024)}, u32[]{:S(2)}) copy-start(f32[4096]{0:T(1024)} %param.7) | copy-start | bytes 49156
  170.2 117.8 %copy-start.1 = (bf16[4096,224]{0,1:T(8,128)(2,1)S(1)}, bf16[4096,224]{0,1:T(8,128)(2,1)}, u32[]{:S(2)}) copy-start(bf16[4096,224]{0,1:T(8,128)(2,1)} %all-gather.8.cloned.1.call-done) | copy-start | bytes 5505028
  288.1 2.2 copy-start
  288.1 2.8 copy-start.2
  293.9 198.8 %reduce-scatter.2.cloned.1.call-start = ((), (), s32[]{:S(2)}) async-start(), calls=%async_computation.5 | async-start | bytes 2064384 | tf_op jit(solution)/shard_map/reduce_scatter | solution.py:70
  450.3 5.0 copy-start.3
Sparse Core Ops, SparseCore 0:
  11.1 88.7 all-gather.5
  101.9 31.2 all-gather.7
  135.4 30.4 all-gather.9
  167.8 30.4 all-gather.13
  201.2 82.9 all-gather.11
  294.0 151.2 all-reduce.2
  455.4 37.1 reduce-scatter.1
where the time goes:
time: 503 us; the launch traced here: 501 us
  waiting for transfers between devices  422 us (84%)
  matrix products  27.7 us (6%)
  blocking collectives  17.1 us (3%)
  local copies, waits for them, and re-layouts  14.4 us (3%)
  between operations  14.2 us (3%)
  other arithmetic  5.12 us (1%)
    psum x1, waiting for transfers between devices, body(): down_total, gain_whole = lax.psum((down_part, gain_factor), 'tensor')  145 us
    all_gather x1, waiting for transfers between devices, body(): lax.all_gather(tokens, 'tensor', axis=1, tiled=True)  89.2 us
    all_gather x1, waiting for transfers between devices, body(): lax.all_gather(cotangent, 'tensor', axis=1, tiled=True)  85.9 us
    all_gather x1, waiting for transfers between devices, body(): lax.all_gather(up_weight, 'dp', axis=0, tiled=True)  28.2 us
    all_gather x1, waiting for transfers between devices, body(): lax.all_gather(down_weight, 'dp', axis=1, tiled=True)  27 us
    all_gather x1, waiting for transfers between devices, body(): lax.all_gather(gate_weight, 'dp', axis=0, tiled=True)  23.9 us
    reduce_scatter x1, waiting for transfers between devices, body(): lax.psum_scatter(lax.dot_general(block, hidden, (((0,), (0,)), ((), ())),...  20 us
    psum x1, blocking collectives, body(): grad_gain = lax.psum(gain_local, 'dp')  17.1 us
  transfers between devices with their start and end apart: 7, of which 7 were waited for; matrix products, arithmetic and copies ran while one was open for 5% of the time, Pallas kernels for 0%

commit v1 on v0

v1 whole, which is shorter than its diff:
```python
import math

import jax
import jax.numpy as jnp
from jax import lax
from jax.experimental import pallas as pl
from jax.experimental.pallas import tpu as pltpu
from jax.sharding import PartitionSpec as P

MODEL_FEATURES = 4096
FF = 14336
SEQUENCE_LENGTH = 64
NY = 8
NZ = 8
NX = 4


def shift_y(k):
    return [(z * NY + y, z * NY + (y + k) % NY) for z in range(NZ) for y in range(NY)]


def shift_z(k):
    return [(z * NY + y, (z + k) % NZ * NY + y) for z in range(NZ) for y in range(NY)]


def shift_x(k):
    return [(x * 2 + c, (x + k) % NX * 2 + c) for x in range(NX) for c in range(2)]


SWAP = [(x * 2 + c, x * 2 + 1 - c) for x in range(NX) for c in range(2)]


def ring8(block, axis, shift):
    up, down = [block], [block]
    for _ in range(3):
        up.append(lax.ppermute(up[-1], axis, shift(1)))
        down.append(lax.ppermute(down[-1], axis, shift(-1)))
    half = block.shape[0] // 2
    far = jnp.concatenate(
        [
            lax.ppermute(up[3][:half], axis, shift(1)),
            lax.ppermute(down[3][half:], axis, shift(-1)),
        ],
        axis=0,
    )
    return [block, up[1], up[2], up[3], far, down[3], down[2], down[1]]


def place_kernel(outer_is_y, *refs):
    pieces, out, sem = refs[:8], refs[8], refs[9]
    t = lax.axis_index("tensor")
    z, y = t // NY, lax.rem(t, NY)
    for j in range(8):
        for i in range(8):
            if outer_is_y:
                dst = out.at[lax.rem(z - i + 8, 8), lax.rem(y - j + 8, 8)]
            else:
                dst = out.at[lax.rem(z - j + 8, 8), lax.rem(y - i + 8, 8)]
            pltpu.make_async_copy(pieces[j].at[i], dst, sem).start()
    pltpu.make_async_copy(out, out, sem).wait()


def place(pieces, outer_is_y):
    rows, cols = pieces[0].shape[1:]

    def run(*refs):
        place_kernel(outer_is_y, *refs)

    return pl.pallas_call(
        run,
        out_shape=jax.ShapeDtypeStruct((8, 8, rows, cols), pieces[0].dtype),
        in_specs=[pl.BlockSpec(memory_space=pl.ANY)] * 8,
        out_specs=pl.BlockSpec(memory_space=pl.ANY),
        scratch_shapes=[pltpu.SemaphoreType.DMA],
        cost_estimate=pl.CostEstimate(flops=0, bytes_accessed=128 * rows * cols * 2, transcendentals=0),
    )(*pieces)


def gather_features(block, tokens_first):
    rows, cols = block.shape
    first, second = (shift_y, shift_z) if tokens_first else (shift_z, shift_y)
    inner = jnp.stack(ring8(block, "tensor", first))
    pieces = ring8(inner, "tensor", second)
    return place(pieces, not tokens_first).reshape(64 * rows, cols)


def place_columns_kernel(mine, other, out, sem):
    d = lax.axis_index("dp")
    x, c = d // 2, lax.rem(d, 2)
    width = mine.shape[2]
    for j in range(NX):
        src_x = lax.rem(x - j + NX, NX)
        for ref, core in ((mine, c), (other, 1 - c)):
            start = pl.multiple_of((src_x * 2 + core) * width, width)
            pltpu.make_async_copy(ref.at[j], out.at[:, pl.ds(start, width)], sem).start()
    pltpu.make_async_copy(out, out, sem).wait()


def gather_columns(block):
    rows, width = block.shape
    right = lax.ppermute(block, "dp", shift_x(1))
    left = lax.ppermute(block, "dp", shift_x(-1))
    half = rows // 2
    far = jnp.concatenate(
        [
            lax.ppermute(right[:half], "dp", shift_x(1)),
            lax.ppermute(left[half:], "dp", shift_x(-1)),
        ],
        axis=0,
    )
    mine = jnp.stack([block, right, far, left])
    other = lax.ppermute(mine, "dp", SWAP)
    return pl.pallas_call(
        place_columns_kernel,
        out_shape=jax.ShapeDtypeStruct((rows, 8 * width), block.dtype),
        in_specs=[pl.BlockSpec(memory_space=pl.ANY)] * 2,
        out_specs=pl.BlockSpec(memory_space=pl.ANY),
        scratch_shapes=[pltpu.SemaphoreType.DMA],
        cost_estimate=pl.CostEstimate(flops=0, bytes_accessed=32 * rows * width, transcendentals=0),
    )(mine, other)


def body(tokens, gain, cotangent, gate_weight, up_weight, down_weight):
    whole_x = gather_features(tokens.T, True).T
    whole_dy = gather_features(cotangent.T, False).T
    seq_count = whole_x.shape[0] // SEQUENCE_LENGTH
    width = whole_x.shape[1]
    dp_count = lax.axis_size("dp")
    total_seqs = seq_count * dp_count
    input_float = whole_x.astype(jnp.float32)
    inverse_norm = lax.rsqrt(jnp.mean(input_float * input_float, axis=1, keepdims=True) + 1e-05)
    normed_input = (input_float * inverse_norm * gain).astype(jnp.bfloat16)
    gate_full, up_full = (
        lax.all_gather(gate_weight, "dp", axis=0, tiled=True),
        lax.all_gather(up_weight, "dp", axis=0, tiled=True),
    )
    down_full = gather_columns(down_weight)
    gate = jnp.dot(normed_input, gate_full, preferred_element_type=jnp.float32)
    up = jnp.dot(normed_input, up_full, preferred_element_type=jnp.float32)
    contract = (((1,), (1,)), ((), ()))
    back = lax.dot_general(whole_dy, down_full, contract, preferred_element_type=jnp.float32)
    sigma = jax.nn.sigmoid(gate)
    swish = gate * sigma
    hidden = (swish * up).astype(jnp.bfloat16)
    hidden3 = hidden.reshape(seq_count, SEQUENCE_LENGTH, hidden.shape[1])
    cotangent3 = whole_dy.reshape(seq_count, SEQUENCE_LENGTH, width)
    down_part = jnp.einsum("sif,sjf->sij", hidden3, hidden3, preferred_element_type=jnp.float32)
    dy_gram = jnp.einsum("sid,sjd->sij", cotangent3, cotangent3, preferred_element_type=jnp.float32)
    down_sq = lax.psum(jnp.sum(down_part * dy_gram, axis=(1, 2)), "tensor")
    d_gate = (back * up * sigma * (1.0 + gate * (1.0 - sigma))).astype(jnp.bfloat16)
    d_up = (back * swish).astype(jnp.bfloat16)
    normed_cotangent = lax.dot_general(
        d_gate, gate_full, contract, preferred_element_type=jnp.float32
    ) + lax.dot_general(d_up, up_full, contract, preferred_element_type=jnp.float32)
    gain_factor = jnp.sum(
        (input_float * inverse_norm * normed_cotangent).reshape(seq_count, SEQUENCE_LENGTH, width),
        axis=1,
    )
    gain_mine = lax.psum_scatter(gain_factor, "tensor", scatter_dimension=1, tiled=True)
    gain_mine, down_sq = lax.optimization_barrier((gain_mine, down_sq))
    gain_sq = lax.psum(jnp.sum(gain_mine * gain_mine, axis=1), "tensor")
    down_bound = 0.6 * math.sqrt(SEQUENCE_LENGTH * FF * MODEL_FEATURES)
    gain_bound = 0.5 * math.sqrt(SEQUENCE_LENGTH * MODEL_FEATURES)
    down_scale = jnp.minimum(1.0, down_bound / (jnp.sqrt(down_sq) + 1e-06)) / total_seqs
    gain_scale = jnp.minimum(1.0, gain_bound / (jnp.sqrt(gain_sq) + 1e-06)) / total_seqs
    gain_local = jnp.sum(gain_scale[:, None] * gain_mine, axis=0)
    grad_gain = lax.psum(gain_local, "dp")
    weighted = (
        jnp.repeat(down_scale, SEQUENCE_LENGTH)[:, None] * whole_dy.astype(jnp.float32)
    ).astype(jnp.bfloat16)
    terms = jnp.einsum(
        "tu,tdf->duf", hidden, weighted.reshape(-1, dp_count, width // dp_count),
        preferred_element_type=jnp.float32,
    ).astype(jnp.bfloat16)
    shared = lax.all_to_all(terms, "dp", split_axis=0, concat_axis=0, tiled=True)
    return (jnp.sum(shared.astype(jnp.float32), axis=0), grad_gain)


def solution(mesh):
    in_specs = (
        P("dp", "tensor"),
        P(),
        P("dp", "tensor"),
        P("dp", "tensor"),
        P("dp", "tensor"),
        P("tensor", "dp"),
    )
    out_specs = (P("tensor", "dp"), P("tensor"))
    return jax.shard_map(body, mesh=mesh, in_specs=in_specs, out_specs=out_specs, check_vma=False)
```

time: 503 us -> 949 us (1.89)
  Pallas kernels: 0 us -> 313 us
  waiting for transfers between devices: 422 us -> 125 us
  blocking collectives: 17.1 us -> 269 us
  starting transfers between devices: 0.27 us -> 141 us
  other arithmetic: 5.12 us -> 25 us
  local copies, waits for them, and re-layouts: 14.4 us -> 28.4 us
    pallas_call x0 -> x3, Pallas kernels: none -> 313 us  [the longest x2 256 us: place(): pl.pallas_call(run, out_shape=jax.ShapeDtypeStruct((8, 8, rows, cols), pi...]
    psum x0 -> x2, blocking collectives: none -> 229 us  [the longest x1 116 us: body(): down_sq = lax.psum(jnp.sum(down_part * dy_gram, axis=(1, 2)), 'tensor')]
    all_gather x3 -> x0, waiting for transfers between devices: 202 us -> none  [the longest x1 89.2 us: body(): lax.all_gather(tokens, 'tensor', axis=1, tiled=True)]
    psum x1 -> x0, waiting for transfers between devices: 145 us -> none  [body(): down_total, gain_whole = lax.psum((down_part, gain_factor), 'tensor')]
    ppermute x0 -> x37, starting transfers between devices: none -> 131 us  [the longest x12 50 us: ring8(): down.append(lax.ppermute(down[-1], axis, shift(-1)))]
    unnamed x7 -> x4, waiting for transfers between devices: 3.15 us -> 117 us
    all_gather x1, waiting for transfers between devices: 28.2 us -> 0.02 us  [body(): lax.all_gather(up_weight, 'dp', axis=0, tiled=True)]
    all_gather x1, waiting for transfers between devices: 23.9 us -> 0.01 us  [body(): lax.all_gather(gate_weight, 'dp', axis=0, tiled=True)]
  transfers between devices with their start and end apart: 7 -> 41, of which waited for: 7 -> 3; matrix products, arithmetic and copies ran while one was open for 5% -> 5% of each run, Pallas kernels for 0% -> 33%
where the time goes in v1:
time: 949 us; the launch traced here: 947 us
  Pallas kernels  313 us (33%)
  blocking collectives  269 us (28%)
  starting transfers between devices  141 us (15%)
  waiting for transfers between devices  125 us (13%)
  matrix products  30.6 us (3%)
  local copies, waits for them, and re-layouts  28.4 us (3%)
  other arithmetic  25 us (3%)
  between operations  14.8 us (2%)
    pallas_call x2, Pallas kernels, place(): pl.pallas_call(run, out_shape=jax.ShapeDtypeStruct((8, 8, rows, cols), pi...  256 us
    unnamed x4, waiting for transfers between devices  117 us
    psum x1, blocking collectives, body(): down_sq = lax.psum(jnp.sum(down_part * dy_gram, axis=(1, 2)), 'tensor')  116 us
    psum x1, blocking collectives, body(): gain_sq = lax.psum(jnp.sum(gain_mine * gain_mine, axis=1), 'tensor')  113 us
    pallas_call x1, Pallas kernels, gather_columns(): pl.pallas_call(place_columns_kernel, out_shape=jax.ShapeDtypeStruct((rows...  56.7 us
    ppermute x12, starting transfers between devices, ring8(): down.append(lax.ppermute(down[-1], axis, shift(-1)))  50 us
    psum x1, blocking collectives, body(): grad_gain = lax.psum(gain_local, 'dp')  40.3 us
    ppermute x12, starting transfers between devices, ring8(): up.append(lax.ppermute(up[-1], axis, shift(1)))  30.6 us
  transfers between devices with their start and end apart: 41, of which 3 were waited for; matrix products, arithmetic and copies ran while one was open for 5% of the time, Pallas kernels for 33%

profile of v1, /device:TPU:1, one launch (start us, length us, event | category | flops | bytes accessed | tf_op | source)
XLA Modules:
  0.0 946.8 jit_solution(8750194553673745768)
XLA Ops:
  19.1 8.6 collective-permute-start.20
  44.3 4.6 collective-permute-start.21
  97.8 4.8 collective-permute-done.33
  109.0 10.7 %collective-permute-start.36 = (bf16[4,224,512]{2,1,0:T(8,128)(2,1)S(1)}, bf16[4,224,512]{2,1,0:T(8,128)(2,1)}, u32[]{:S(2)}, u32[]{:S(2)}) collective-permute-start(bf16[4,224,512]{2,1,0:T(8,128)(2,1)S(1)} %pad_maximum_fusion.mine), channel_id=1, source_target_pairs={{0,64},{64,0},{128,192},{192,128},{256,320},{320,256},{384,448},{4... | collective-permute-start | bytes 2752520 | tf_op jit(solution)/shard_map/ppermute | solution.py:112
  126.1 4.9 collective-permute-start.30
  136.2 5.3 collective-permute-start.15
  144.3 56.7 %shard_map.79 = bf16[224,4096]{1,0:T(8,128)(2,1)} custom-call(bf16[4,224,512]{2,1,0:T(8,128)(2,1)} %copy-done.1, bf16[4,224,512]{2,1,0:T(8,128)(2,1)} %collective-permute-done.36.other), custom_call_target="tpu_custom_call" | custom-call | bytes 3670016 | tf_op jit(solution)/shard_map/pallas_call | solution.py:113
  201.1 4.9 collective-permute-start.31
  210.0 128.2 %shard_map.77 = bf16[8,8,64,512]{3,2,1,0:T(8,128)(2,1)} custom-call(bf16[8,64,512]{2,1,0:T(8,128)(2,1)} %copy-done.10, bf16[8,64,512]{2,1,0:T(8,128)(2,1)} %copy-done.12, bf16[8,64,512]{2,1,0:T(8,128)(2,1)} %copy-done.16, bf16[8,64,512]{2,1,0:T(8,128)(2,1)} %copy-done.8, bf16[8,64,512]{2,1,0:T(8,128)(2,1)} %pad_maximum_fusion.1.refs_4_, ...), custom_call_target="tpu_custom_call" | custom-call | bytes 8388608 | tf_op jit(solution)/shard_map/pallas_call | solution.py:69
  338.2 6.7 bitcast_convert_fusion
  346.7 128.2 %shard_map.78 = bf16[8,8,64,512]{3,2,1,0:T(8,128)(2,1)} custom-call(bf16[8,64,512]{2,1,0:T(8,128)(2,1)} %copy-done.9, bf16[8,64,512]{2,1,0:T(8,128)(2,1)} %copy-done.14, bf16[8,64,512]{2,1,0:T(8,128)(2,1)} %collective-permute-done.25.refs_2_, bf16[8,64,512]{2,1,0:T(8,128)(2,1)} %copy-done.6, bf16[8,64,512]{2,1,0:T(8,128)(2,1)} %pad_maximum_fusion.2.refs_4_, ...), custom_call_target="tpu_custom_call" | custom-call | bytes 8388608 | tf_op jit(solution)/shard_map/pallas_call | solution.py:69
  474.8 6.4 copy.24
  481.2 9.1 copy.22
  504.9 5.1 multiply_convert_fusion.1
  513.0 5.2 bitcast_reduce_fusion
  520.2 4.8 fusion.1
  525.0 116.1 %psum.21 = f32[8]{0:T(128)S(1)} all-reduce(f32[8]{0:T(128)S(1)} %fusion.1), channel_id=1, replica_groups=mesh['dp'=8,'tensor'=64] {'tensor'}, use_global_device_ids=true, to_apply=%region_4.0 | all-reduce | flops 8 | bytes 64 | tf_op jit(solution)/shard_map/psum | solution.py:149
  641.1 117.0 %reduce-scatter.4.cloned.1.call-done = f32[64,8]{1,0:T(8,128)} async-done(((f32[4096,8]{1,0:T(8,128)}), f32[64,8]{1,0:T(8,128)}) %reduce-scatter.4.cloned.1.call-update) | async-done | bytes 2064
  759.1 5.7 multiply_convert_fusion
  764.8 6.5 copy.25
  771.3 4.9 convert_bitcast_fusion
  776.1 9.6 %all-to-all-start = ((bf16[8,224,512]{2,1,0:T(8,128)(2,1)}), bf16[8,224,512]{2,1,0:T(8,128)(2,1)S(1)}, u32[]{:S(2)}, u32[]{:S(2)}) async-start(bf16[8,224,512]{2,1,0:T(8,128)(2,1)} %convert_bitcast_fusion), calls=%async_computation | async-start | bytes 3670016 | tf_op jit(solution)/shard_map/all_to_all | solution.py:175
  785.9 113.0 %psum.22 = f32[8]{0:T(128)S(1)} all-reduce(f32[8]{0:T(128)S(1)} %multiply_reduce_fusion.2), channel_id=1, replica_groups=mesh['dp'=8,'tensor'=64] {'tensor'}, use_global_device_ids=true, to_apply=%region_7.0 | all-reduce | flops 8 | bytes 64 | tf_op jit(solution)/shard_map/psum | solution.py:161
  898.9 40.3 %psum.23 = f32[64]{0:T(128)} all-reduce(f32[64]{0:T(128)S(1)} %multiply_reduce_fusion.1), channel_id=1, replica_groups=mesh['dp'=8,'tensor'=64] {'dp'}, use_global_device_ids=true, to_apply=%region_9.0 | all-reduce | flops 64 | bytes 512 | tf_op jit(solution)/shard_map/psum | solution.py:167
  (159 shorter events, 125.0 us)
Async XLA Ops:
  7.2 493.5 %all-gather.5.cloned.1.call-start = ((), (), s32[]{:S(2)}) async-start(), calls=%async_computation.3 | async-start | bytes 2064384 | tf_op jit(solution)/shard_map/all_gather | solution.py:134
  7.2 26.6 %collective-permute-start = (bf16[64,512]{1,0:T(8,128)(2,1)}, bf16[64,512]{1,0:T(8,128)(2,1)S(1)}, u32[]{:S(2)}, u32[]{:S(2)}) collective-permute-start(bf16[64,512]{1,0:T(8,128)(2,1)} %bitcast.95), channel_id=1, source_target_pairs={{0,1},{1,2},{2,3},{3,4},{4,5},{5,6},{6,7},{7,0},{8,9},{9,10},{10,1... | collective-permute-start | bytes 196616 | tf_op jit(solution)/shard_map/ppermute | solution.py:36
  11.2 26.5 %collective-permute-start.4 = (bf16[64,512]{1,0:T(8,128)(2,1)}, bf16[64,512]{1,0:T(8,128)(2,1)S(1)}, u32[]{:S(2)}, u32[]{:S(2)}) collective-permute-start(bf16[64,512]{1,0:T(8,128)(2,1)} %bitcast.96), channel_id=1, source_target_pairs={{0,7},{1,0},{2,1},{3,2},{4,3},{5,4},{6,5},{7,6},{8,15},{9,8},{10,9... | collective-permute-start | bytes 196616 | tf_op jit(solution)/shard_map/ppermute | solution.py:37
  15.1 20.7 %collective-permute-start.16 = (bf16[64,512]{1,0:T(8,128)(2,1)}, bf16[64,512]{1,0:T(8,128)(2,1)S(1)}, u32[]{:S(2)}, u32[]{:S(2)}) collective-permute-start(bf16[64,512]{1,0:T(8,128)(2,1)} %bitcast.97), channel_id=1, source_target_pairs={{0,8},{1,9},{2,10},{3,11},{4,12},{5,13},{6,14},{7,15},{8,16},{9,17... | collective-permute-start | bytes 196616 | tf_op jit(solution)/shard_map/ppermute | solution.py:36
  19.1 20.6 %collective-permute-start.20 = (bf16[64,512]{1,0:T(8,128)(2,1)}, bf16[64,512]{1,0:T(8,128)(2,1)S(1)}, u32[]{:S(2)}, u32[]{:S(2)}) collective-permute-start(bf16[64,512]{1,0:T(8,128)(2,1)} %bitcast.98), channel_id=1, source_target_pairs={{0,56},{1,57},{2,58},{3,59},{4,60},{5,61},{6,62},{7,63},{8,0},{9,1... | collective-permute-start | bytes 196616 | tf_op jit(solution)/shard_map/ppermute | solution.py:37
  27.7 477.2 %all-gather.3.cloned.1.call-start = ((), (), s32[]{:S(2)}) async-start(), calls=%async_computation.2 | async-start | bytes 2064384 | tf_op jit(solution)/shard_map/all_gather | solution.py:135
  27.8 54.7 %collective-permute-start.34 = (bf16[224,512]{1,0:T(8,128)(2,1)}, bf16[224,512]{1,0:T(8,128)(2,1)S(1)}, u32[]{:S(2)}, u32[]{:S(2)}) collective-permute-start(bf16[224,512]{1,0:T(8,128)(2,1)} %param.11), channel_id=1, source_target_pairs={{0,384},{64,448},{128,0},{192,64},{256,128},{320,192},{384,256},{4... | collective-permute-start | bytes 688136 | tf_op jit(solution)/shard_map/ppermute | solution.py:102
  33.8 52.0 %collective-permute-start.32 = (bf16[224,512]{1,0:T(8,128)(2,1)}, bf16[224,512]{1,0:T(8,128)(2,1)S(1)}, u32[]{:S(2)}, u32[]{:S(2)}) collective-permute-start(bf16[224,512]{1,0:T(8,128)(2,1)} %param.11), channel_id=1, source_target_pairs={{0,128},{64,192},{128,256},{192,320},{256,384},{320,448},{384,0},{... | collective-permute-start | bytes 688136 | tf_op jit(solution)/shard_map/ppermute | solution.py:101
  80.5 22.1 %collective-permute-start.28 = (bf16[8,64,512]{2,1,0:T(8,128)(2,1)S(1)}, bf16[8,64,512]{2,1,0:T(8,128)(2,1)S(1)}, u32[]{:S(2)}, u32[]{:S(2)}) collective-permute-start(bf16[8,64,512]{2,1,0:T(8,128)(2,1)S(1)} %bitcast_dynamic-update-slice_fusion.2.refs_0_), channel_id=1, source_target_pairs={{0,7},{1,0},{2,1},{3,2},{4,3},{5,4},{6,5},{7,6},{8,15},{9,8},{10,9... | collective-permute-start | bytes 1572872 | tf_op jit(solution)/shard_map/ppermute | solution.py:37
  82.5 23.3 %collective-permute-start.24 = (bf16[8,64,512]{2,1,0:T(8,128)(2,1)S(1)}, bf16[8,64,512]{2,1,0:T(8,128)(2,1)S(1)}, u32[]{:S(2)}, u32[]{:S(2)}) collective-permute-start(bf16[8,64,512]{2,1,0:T(8,128)(2,1)S(1)} %bitcast_dynamic-update-slice_fusion.2.refs_0_), channel_id=1, source_target_pairs={{0,1},{1,2},{2,3},{3,4},{4,5},{5,6},{6,7},{7,0},{8,9},{9,10},{10,1... | collective-permute-start | bytes 1572872 | tf_op jit(solution)/shard_map/ppermute | solution.py:36
  90.5 29.3 %collective-permute-start.13 = (bf16[8,64,512]{2,1,0:T(8,128)(2,1)S(1)}, bf16[8,64,512]{2,1,0:T(8,128)(2,1)S(1)}, u32[]{:S(2)}, u32[]{:S(2)}) collective-permute-start(bf16[8,64,512]{2,1,0:T(8,128)(2,1)S(1)} %collective-permute-done.12.refs_7_), channel_id=1, source_target_pairs={{0,56},{1,57},{2,58},{3,59},{4,60},{5,61},{6,62},{7,63},{8,0},{9,1... | collective-permute-start | bytes 1572872 | tf_op jit(solution)/shard_map/ppermute | solution.py:37
  93.6 30.4 %collective-permute-start.9 = (bf16[8,64,512]{2,1,0:T(8,128)(2,1)S(1)}, bf16[8,64,512]{2,1,0:T(8,128)(2,1)S(1)}, u32[]{:S(2)}, u32[]{:S(2)}) collective-permute-start(bf16[8,64,512]{2,1,0:T(8,128)(2,1)S(1)} %collective-permute-done.8.refs_1_), channel_id=1, source_target_pairs={{0,8},{1,9},{2,10},{3,11},{4,12},{5,13},{6,14},{7,15},{8,16},{9,17... | collective-permute-start | bytes 1572872 | tf_op jit(solution)/shard_map/ppermute | solution.py:36
  102.6 23.4 %collective-permute-start.29 = (bf16[8,64,512]{2,1,0:T(8,128)(2,1)S(1)}, bf16[8,64,512]{2,1,0:T(8,128)(2,1)}, u32[]{:S(2)}, u32[]{:S(2)}) collective-permute-start(bf16[8,64,512]{2,1,0:T(8,128)(2,1)S(1)} %collective-permute-done.28.refs_7_), channel_id=1, source_target_pairs={{0,7},{1,0},{2,1},{3,2},{4,3},{5,4},{6,5},{7,6},{8,15},{9,8},{10,9... | collective-permute-start | bytes 1572872 | tf_op jit(solution)/shard_map/ppermute | solution.py:37
  105.8 25.1 %collective-permute-start.25 = (bf16[8,64,512]{2,1,0:T(8,128)(2,1)S(1)}, bf16[8,64,512]{2,1,0:T(8,128)(2,1)}, u32[]{:S(2)}, u32[]{:S(2)}) collective-permute-start(bf16[8,64,512]{2,1,0:T(8,128)(2,1)S(1)} %collective-permute-done.24.refs_1_), channel_id=1, source_target_pairs={{0,1},{1,2},{2,3},{3,4},{4,5},{5,6},{6,7},{7,0},{8,9},{9,10},{10,1... | collective-permute-start | bytes 1572872 | tf_op jit(solution)/shard_map/ppermute | solution.py:36
  109.0 35.3 %collective-permute-start.36 = (bf16[4,224,512]{2,1,0:T(8,128)(2,1)S(1)}, bf16[4,224,512]{2,1,0:T(8,128)(2,1)}, u32[]{:S(2)}, u32[]{:S(2)}) collective-permute-start(bf16[4,224,512]{2,1,0:T(8,128)(2,1)S(1)} %pad_maximum_fusion.mine), channel_id=1, source_target_pairs={{0,64},{64,0},{128,192},{192,128},{256,320},{320,256},{384,448},{4... | collective-permute-start | bytes 2752520 | tf_op jit(solution)/shard_map/ppermute | solution.py:112
  124.1 17.4 %collective-permute-start.10 = (bf16[8,64,512]{2,1,0:T(8,128)(2,1)S(1)}, bf16[8,64,512]{2,1,0:T(8,128)(2,1)S(1)}, u32[]{:S(2)}, u32[]{:S(2)}) collective-permute-start(bf16[8,64,512]{2,1,0:T(8,128)(2,1)S(1)} %collective-permute-done.9.refs_2_), channel_id=1, source_target_pairs={{0,8},{1,9},{2,10},{3,11},{4,12},{5,13},{6,14},{7,15},{8,16},{9,17... | collective-permute-start | bytes 1572872 | tf_op jit(solution)/shard_map/ppermute | solution.py:36
  126.1 75.0 %collective-permute-start.30 = (bf16[8,64,512]{2,1,0:T(8,128)(2,1)}, bf16[8,64,512]{2,1,0:T(8,128)(2,1)S(1)}, u32[]{:S(2)}, u32[]{:S(2)}) collective-permute-start(bf16[8,64,512]{2,1,0:T(8,128)(2,1)} %collective-permute-done.29.refs_6_), channel_id=1, source_target_pairs={{0,7},{1,0},{2,1},{3,2},{4,3},{5,4},{6,5},{7,6},{8,15},{9,8},{10,9... | collective-permute-start | bytes 1572872 | tf_op jit(solution)/shard_map/ppermute | solution.py:37
  130.9 75.0 %collective-permute-start.26 = (bf16[8,64,512]{2,1,0:T(8,128)(2,1)}, bf16[8,64,512]{2,1,0:T(8,128)(2,1)S(1)}, u32[]{:S(2)}, u32[]{:S(2)}) collective-permute-start(bf16[8,64,512]{2,1,0:T(8,128)(2,1)} %collective-permute-done.25.refs_2_), channel_id=1, source_target_pairs={{0,1},{1,2},{2,3},{3,4},{4,5},{5,6},{6,7},{7,0},{8,9},{9,10},{10,1... | collective-permute-start | bytes 1572872 | tf_op jit(solution)/shard_map/ppermute | solution.py:36
  136.2 72.0 %collective-permute-start.15 = (bf16[4,64,512]{2,1,0:T(8,128)(2,1)}, bf16[4,64,512]{2,1,0:T(8,128)(2,1)}, u32[]{:S(2)}, u32[]{:S(2)}) collective-permute-start(bf16[4,64,512]{2,1,0:T(8,128)(2,1)} %slice.43), channel_id=1, source_target_pairs={{0,56},{1,57},{2,58},{3,59},{4,60},{5,61},{6,62},{7,63},{8,0},{9,1... | collective-permute-start | bytes 786440 | tf_op jit(solution)/shard_map/ppermute | solution.py:42
  142.3 65.8 %collective-permute-start.11 = (bf16[4,64,512]{2,1,0:T(8,128)(2,1)}, bf16[4,64,512]{2,1,0:T(8,128)(2,1)}, u32[]{:S(2)}, u32[]{:S(2)}) collective-permute-start(bf16[4,64,512]{2,1,0:T(8,128)(2,1)} %slice.42), channel_id=1, source_target_pairs={{0,8},{1,9},{2,10},{3,11},{4,12},{5,13},{6,14},{7,15},{8,16},{9,17... | collective-permute-start | bytes 786440 | tf_op jit(solution)/shard_map/ppermute | solution.py:41
  144.3 613.9 %reduce-scatter.4.cloned.1.call-start = ((), (), s32[]{:S(2)}) async-start(), calls=%async_computation.4 | async-start | bytes 2129920
  201.1 143.8 %collective-permute-start.31 = (bf16[4,64,512]{2,1,0:T(8,128)(2,1)S(1)}, bf16[4,64,512]{2,1,0:T(8,128)(2,1)S(1)}, u32[]{:S(2)}, u32[]{:S(2)}) collective-permute-start(bf16[4,64,512]{2,1,0:T(8,128)(2,1)S(1)} %slice.49), channel_id=1, source_target_pairs={{0,7},{1,0},{2,1},{3,2},{4,3},{5,4},{6,5},{7,6},{8,15},{9,8},{10,9... | collective-permute-start | bytes 786440 | tf_op jit(solution)/shard_map/ppermute | solution.py:42
  206.0 138.9 %collective-permute-start.27 = (bf16[4,64,512]{2,1,0:T(8,128)(2,1)S(1)}, bf16[4,64,512]{2,1,0:T(8,128)(2,1)}, u32[]{:S(2)}, u32[]{:S(2)}) collective-permute-start(bf16[4,64,512]{2,1,0:T(8,128)(2,1)S(1)} %slice.48), channel_id=1, source_target_pairs={{0,1},{1,2},{2,3},{3,4},{4,5},{5,6},{6,7},{7,0},{8,9},{9,10},{10,1... | collective-permute-start | bytes 786440 | tf_op jit(solution)/shard_map/ppermute | solution.py:41
  776.1 163.2 %all-to-all-start = ((bf16[8,224,512]{2,1,0:T(8,128)(2,1)}), bf16[8,224,512]{2,1,0:T(8,128)(2,1)S(1)}, u32[]{:S(2)}, u32[]{:S(2)}) async-start(bf16[8,224,512]{2,1,0:T(8,128)(2,1)} %convert_bitcast_fusion), calls=%async_computation | async-start | bytes 3670016 | tf_op jit(solution)/shard_map/all_to_all | solution.py:175
  (35 other events, 999.6 us)
Sparse Core Ops, SparseCore 0:
  27.8 29.7 all-gather.4
  144.4 28.2 all-gather.2
  520.3 237.7 reduce-scatter.3

commit v2 on v0

v2 whole, which is shorter than its diff:
```python
import math

import jax
import jax.numpy as jnp
from jax import lax
from jax.experimental import pallas as pl
from jax.experimental.pallas import tpu as pltpu
from jax.sharding import Mesh
from jax.sharding import PartitionSpec as P

FEATURES = 4096
FF = 14336
SEQ = 64
SEQS = 64
NX, NC, NZ, NY = 4, 2, 8, 8
LOCAL = 8
TOK = LOCAL * SEQ
UNITS = FF // (NZ * NY)
SHARE = FEATURES // (NX * NC)
COLS = FEATURES // (NZ * NY)
F32 = jnp.float32
BF16 = jnp.bfloat16

SMEM = pl.BlockSpec(memory_space=pltpu.SMEM)
VMEM = pl.BlockSpec(memory_space=pltpu.VMEM)


def params(mib):
    return pltpu.CompilerParams(vmem_limit_bytes=mib * 1024 * 1024)


def cost(macs, nbytes):
    return pl.CostEstimate(flops=2 * macs, bytes_accessed=nbytes, transcendentals=0)


def each_share(idx, body):
    core = idx[1]

    def step(i, carry):
        body(i, 0, 2 * i + core)
        body(i, 1, 2 * i + 1 - core)
        return carry

    lax.fori_loop(0, NX, step, 0)


def hidden_kernel(idx, *refs):
    pieces, (mine, other, gain, xs, gate, up, hidden, inverse, acc) = refs[:NZ], refs[NZ:]
    z = idx[0]
    total = jnp.zeros((8, TOK), F32)
    for j in range(NZ):
        slot = lax.rem(z - j + NZ, NZ)
        for i in range(NY):
            block = pieces[j][i]
            xs[slot, pl.ds(i * COLS, COLS), :] = block
            wide = block.astype(F32)
            total += jnp.sum((wide * wide).reshape(COLS // 8, 8, TOK), axis=0)
    mean = jnp.sum(total, axis=0, keepdims=True) * (1.0 / FEATURES)
    inverse[...] = lax.rsqrt(mean + 1e-05)
    acc[...] = jnp.zeros_like(acc)

    def share(i, which, d):
        ref = other if which else mine
        scaled = ref[i].reshape(2 * UNITS, SHARE).astype(F32) * gain[pl.ds(d, 1), :]
        acc[...] += jnp.dot(scaled.astype(BF16), xs[d], preferred_element_type=F32)

    each_share(idx, share)

    def rows(i, carry):
        r = pl.multiple_of(i * 32, 32)
        inv = inverse[...]
        g = acc[pl.ds(r, 32), :] * inv
        u = acc[pl.ds(pl.multiple_of(UNITS + r, 32), 32), :] * inv
        gate[pl.ds(r, 32), :] = g
        up[pl.ds(r, 32), :] = u
        hidden[pl.ds(r, 32), :] = (g * jax.nn.sigmoid(g) * u).astype(BF16)
        return carry

    lax.fori_loop(0, UNITS // 32, rows, 0)


def hidden_call(idx, pieces, mine, other, gain):
    return pl.pallas_call(
        hidden_kernel,
        out_shape=(
            jax.ShapeDtypeStruct((NZ, SHARE, TOK), BF16),
            jax.ShapeDtypeStruct((UNITS, TOK), F32),
            jax.ShapeDtypeStruct((UNITS, TOK), F32),
            jax.ShapeDtypeStruct((UNITS, TOK), BF16),
            jax.ShapeDtypeStruct((1, TOK), F32),
        ),
        in_specs=[SMEM] + [VMEM] * (NZ + 3),
        out_specs=(VMEM,) * 5,
        scratch_shapes=[pltpu.VMEM((2 * UNITS, TOK), F32)],
        compiler_params=params(40),
        cost_estimate=cost(2 * UNITS * TOK * FEATURES, 14 << 20),
        name="hidden",
    )(idx, *pieces, mine, other, gain)


TN = (((0,), (0,)), ((), ()))
NT = (((1,), (1,)), ((), ()))


def gram_kernel(dy, hidden, out):
    half = TOK // 2
    for h in range(2):
        lanes = slice(h * half, (h + 1) * half)
        mine = hidden[:, lanes]
        own = lax.dot_general(mine, mine, TN, preferred_element_type=F32)

        def step(z, acc):
            block = dy[:, z, :, lanes].reshape(SHARE, half)
            return acc + lax.dot_general(block, block, TN, preferred_element_type=F32)

        pairs = own * lax.fori_loop(0, NZ, step, jnp.zeros((half, half), F32))
        for s in range(half // SEQ):
            part = pairs[s * SEQ : (s + 1) * SEQ, s * SEQ : (s + 1) * SEQ]
            value = jnp.sum(jnp.sum(part, axis=0, keepdims=True), axis=1, keepdims=True)
            i = h * (half // SEQ) + s
            out[:, i : i + 1, :] = jnp.broadcast_to(value.reshape(1, 1, 1), (NY, 1, 128))


def gram_call(dy, hidden):
    return pl.pallas_call(
        gram_kernel,
        out_shape=jax.ShapeDtypeStruct((NY, LOCAL, 128), F32),
        in_specs=[VMEM] * 2,
        out_specs=VMEM,
        compiler_params=params(24),
        cost_estimate=cost(TOK * TOK * (FEATURES + UNITS), 5 << 20),
        name="gram",
    )(dy, hidden)


def back_kernel(idx, dy, mine, other, gate, up, grads, acc):
    acc[...] = jnp.zeros_like(acc)

    def share(i, which, d):
        ref = other if which else mine
        block = dy[:, d, :, :].reshape(SHARE, TOK)
        acc[...] += jnp.dot(ref[i], block, preferred_element_type=F32)

    each_share(idx, share)

    def rows(i, carry):
        r = pl.multiple_of(i * 32, 32)
        b, g, u = acc[pl.ds(r, 32), :], gate[pl.ds(r, 32), :], up[pl.ds(r, 32), :]
        sigma = jax.nn.sigmoid(g)
        grads[pl.ds(r, 32), :] = (b * u * sigma * (1.0 + g * (1.0 - sigma))).astype(BF16)
        grads[pl.ds(pl.multiple_of(UNITS + r, 32), 32), :] = (b * g * sigma).astype(BF16)
        return carry

    lax.fori_loop(0, UNITS // 32, rows, 0)


def back_call(idx, dy, mine, other, gate, up):
    return pl.pallas_call(
        back_kernel,
        out_shape=jax.ShapeDtypeStruct((2 * UNITS, TOK), BF16),
        in_specs=[SMEM] + [VMEM] * 5,
        out_specs=VMEM,
        scratch_shapes=[pltpu.VMEM((UNITS, TOK), F32)],
        compiler_params=params(28),
        cost_estimate=cost(UNITS * TOK * FEATURES, 7 << 20),
        name="back",
    )(idx, dy, mine, other, gate, up)


def gain_kernel(idx, grads, inverse, xs, mine, other, out):
    token = lax.broadcasted_iota(jnp.int32, (TOK, 128), 0)
    column = lax.broadcasted_iota(jnp.int32, (TOK, 128), 1)
    select = jnp.where(token // SEQ == column, 1.0, 0.0).astype(BF16)
    core = idx[1]
    wide = SHARE // 2

    def term(weight, d, h):
        f = slice(h * wide, (h + 1) * wide)
        normed = lax.dot_general(weight[:, f], grads[...], TN, preferred_element_type=F32)
        product = xs[d, f, :].astype(F32) * inverse[...] * normed
        high = product.astype(BF16)
        low = (product - high.astype(F32)).astype(BF16)
        total = jnp.dot(high, select, preferred_element_type=F32)
        total += jnp.dot(low, select, preferred_element_type=F32)
        return total.T[:LOCAL]

    def step(i, carry):
        for h in range(2):
            a = term(mine[i].reshape(2 * UNITS, SHARE), 2 * i + core, h)
            b = term(other[i].reshape(2 * UNITS, SHARE), 2 * i + 1 - core, h)
            even, odd = jnp.where(core == 0, a, b), jnp.where(core == 0, b, a)
            for y in range(wide // COLS):
                lanes = slice(y * COLS, (y + 1) * COLS)
                rows = pl.ds(pl.multiple_of(i * LOCAL, LOCAL), LOCAL)
                out[h * (wide // COLS) + y, rows, :] = jnp.concatenate([even[:, lanes], odd[:, lanes]], axis=1)
        return carry

    lax.fori_loop(0, NX, step, 0)


def gain_call(idx, grads, inverse, xs, mine, other):
    return pl.pallas_call(
        gain_kernel,
        out_shape=jax.ShapeDtypeStruct((NY, NX * LOCAL, 128), F32),
        in_specs=[SMEM] + [VMEM] * 5,
        out_specs=VMEM,
        compiler_params=params(40),
        cost_estimate=cost(3 * UNITS * TOK * FEATURES, 9 << 20),
        name="gain_term",
    )(idx, grads, inverse, xs, mine, other)


def add_kernel(part, out):
    out[...] = jnp.broadcast_to(jnp.sum(part[...], axis=0, keepdims=True), out.shape)


def add_and_repeat(part):
    return pl.pallas_call(add_kernel, out_shape=jax.ShapeDtypeStruct(part.shape, F32), name="add_parts")(part)


def gain_sq_kernel(part, total, square):
    whole = jnp.sum(part[...], axis=0)
    total[...] = whole
    rows = jnp.sum((whole * whole).reshape(NX, LOCAL, 128), axis=0)
    value = jnp.sum(rows, axis=1, keepdims=True)
    square[...] = jnp.broadcast_to(value[None], square.shape)


def gain_scale_kernel(idx, part, total, out):
    square = jnp.sum(part[...], axis=0)
    bound = 0.5 * math.sqrt(SEQ * FEATURES)
    scale = jnp.minimum(1.0, bound / (jnp.sqrt(square) + 1e-06)) / SEQS
    rows = total[pl.ds(pl.multiple_of(idx[0] // 2 * LOCAL, LOCAL), LOCAL), :]
    value = jnp.sum(scale * rows, axis=0, keepdims=True)
    out[...] = jnp.broadcast_to(value[None], out.shape)


def grad_kernel(down_sq, hidden, dy, out):
    bound = 0.6 * math.sqrt(SEQ * FF * FEATURES)
    total = jnp.sum(down_sq[...], axis=0)
    scale = jnp.minimum(1.0, bound / (jnp.sqrt(total) + 1e-06)) / SEQS
    first = lax.broadcasted_iota(jnp.int32, (1, 128), 1) < SEQ
    row = jnp.concatenate(
        [jnp.where(first, scale[2 * k : 2 * k + 1], scale[2 * k + 1 : 2 * k + 2]) for k in range(LOCAL // 2)],
        axis=1,
    )
    scaled = (hidden[...].astype(F32) * row).astype(BF16)

    def step(d, carry):
        block = dy[:, d, :, :].reshape(SHARE, TOK)
        out[d] = lax.dot_general(scaled, block, NT, preferred_element_type=F32).astype(BF16)
        return carry

    lax.fori_loop(0, NX * NC, step, 0)


def grad_call(down_sq, hidden, dy):
    return pl.pallas_call(
        grad_kernel,
        out_shape=jax.ShapeDtypeStruct((NX * NC, UNITS, SHARE), BF16),
        in_specs=[VMEM] * 3,
        out_specs=VMEM,
        compiler_params=params(24),
        cost_estimate=cost(UNITS * TOK * FEATURES, 6 << 20),
        name="grad_down",
    )(down_sq, hidden, dy)


def spread(block, axis, count):
    return lax.all_to_all(
        jnp.broadcast_to(block[None], (count,) + block.shape), axis, split_axis=0, concat_axis=0, tiled=True
    )


def exchange(blocks, axis):
    return lax.all_to_all(blocks, axis, split_axis=0, concat_axis=0, tiled=True)


def ring(block, axis, size):
    shift = lambda k: [(i, (i + k) % size) for i in range(size)]
    up, down = [block], [block]
    for step in range(size // 2):
        up.append(lax.ppermute(up[-1], axis, shift(1)))
        if step < size // 2 - 1:
            down.append(lax.ppermute(down[-1], axis, shift(-1)))
    return up + down[:0:-1]


def body(tokens, gain, cotangent, gate_weight, up_weight, down_weight):
    idx = jnp.stack([lax.axis_index("z"), lax.axis_index("core")]).astype(jnp.int32)
    x_part = spread(tokens.T, "y", NY)
    both = jnp.stack([gate_weight.T, up_weight.T])
    mine = spread(both, "x", NX)
    dy_part = spread(cotangent.T, "z", NZ)
    dmine = spread(down_weight, "x", NX)
    swap = [(0, 1), (1, 0)]
    pieces = ring(x_part, "z", NZ)
    dy = lax.all_gather(dy_part, "y", axis=0)
    other = lax.ppermute(mine, "core", swap)
    dother = lax.ppermute(dmine, "core", swap)

    xs, gate, up, hidden, inverse = hidden_call(idx, pieces, mine, other, gain.reshape(NX * NC, SHARE))
    gram = gram_call(dy, hidden)
    part = exchange(gram, "y")
    dy_back, gram = lax.optimization_barrier((dy, gram))
    grads = back_call(idx, dy_back, dmine, dother, gate, up)
    part, grads = lax.optimization_barrier((part, grads))
    down_sq = exchange(add_and_repeat(part), "z")
    gain_part = gain_call(idx, grads, inverse, xs, mine, other)
    down_sq, gain_part = lax.optimization_barrier((down_sq, gain_part))
    terms = grad_call(down_sq, hidden, dy)
    grad = exchange(terms, ("x", "core"))
    gain_part, terms = lax.optimization_barrier((gain_part, terms))

    gain_part = exchange(add_and_repeat(exchange(gain_part, "y")), "z")
    gain_y, sq_part = pl.pallas_call(
        gain_sq_kernel,
        out_shape=(
            jax.ShapeDtypeStruct((NX * LOCAL, 128), F32),
            jax.ShapeDtypeStruct((NY, LOCAL, 128), F32),
        ),
        name="gain_sq",
    )(gain_part)
    gain_local = pl.pallas_call(
        gain_scale_kernel,
        out_shape=jax.ShapeDtypeStruct((NX * NC, 8, 128), F32),
        in_specs=[SMEM, VMEM, VMEM],
        name="gain_scale",
    )(idx, exchange(sq_part, "y"), gain_y)
    gain_all = jnp.sum(exchange(gain_local, ("x", "core"))[:, 0], axis=0)
    grad_gain = jnp.where(idx[0] % 2 == 0, gain_all[:COLS], gain_all[COLS:])
    grad_down = jnp.sum(grad.astype(F32), axis=0)
    return (grad_down, grad_gain)


def solution(mesh):
    split = Mesh(mesh.devices.reshape(NX, NC, NZ, NY), ("x", "core", "z", "y"))
    dp, tensor = ("x", "core"), ("z", "y")
    in_specs = (P(dp, tensor), P(), P(dp, tensor), P(dp, tensor), P(dp, tensor), P(tensor, dp))
    out_specs = (P(tensor, dp), P(tensor))
    return jax.shard_map(body, mesh=split, in_specs=in_specs, out_specs=out_specs, check_vma=False)
```

time: 503 us -> 291 us (0.58)
  waiting for transfers between devices: 422 us -> 78 us
  blocking collectives: 17.1 us -> 82.1 us
  starting transfers between devices: 0.27 us -> 59.6 us
  Pallas kernels: 0 us -> 33.3 us
  matrix products: 27.7 us -> 0 us
  local copies, waits for them, and re-layouts: 14.4 us -> 19.9 us
    all_gather x5 -> x1, waiting for transfers between devices: 254 us -> 0.01 us  [body(): dy = lax.all_gather(dy_part, 'y', axis=0)]
    psum x1 -> x0, waiting for transfers between devices: 145 us -> none  [body(): down_total, gain_whole = lax.psum((down_part, gain_factor), 'tensor')]
    all_to_all x0 -> x5, blocking collectives: none -> 82.1 us  [the longest x4 55.3 us: exchange(): return lax.all_to_all(blocks, axis, split_axis=0, concat_axis=0, tiled=True)]
    all_to_all x0 -> x6, waiting for transfers between devices: none -> 52.9 us  [the longest x3 30 us: spread(): lax.all_to_all(jnp.broadcast_to(block[None], (count,) + block.shape), axi...]
    ppermute x0 -> x9, starting transfers between devices: none -> 34.2 us  [the longest x1 11.2 us: body(): other = lax.ppermute(mine, 'core', swap)]
    pallas_call x0 -> x9, Pallas kernels: none -> 33.3 us  [the longest x1 8.63 us: gain_call(): pl.pallas_call(gain_kernel, out_shape=jax.ShapeDtypeStruct((NY, NX * LOCA...]
    dot_general x8 -> x0, matrix products: 27.7 us -> none  [the longest x1 4.95 us: body(): lax.dot_general(block, hidden, (((0,), (0,)), ((), ())), preferred_elemen...]
    all_to_all x0 -> x6, starting transfers between devices: none -> 25.4 us  [the longest x3 14.5 us: spread(): lax.all_to_all(jnp.broadcast_to(block[None], (count,) + block.shape), axi...]
  transfers between devices with their start and end apart: 7 -> 16, of which waited for: 7 -> 10; matrix products, arithmetic and copies ran while one was open for 5% -> 1% of each run, Pallas kernels for 0% -> 8%
where the time goes in v2:
time: 291 us; the launch traced here: 289 us
  blocking collectives  82.1 us (28%)
  waiting for transfers between devices  78 us (27%)
  starting transfers between devices  59.6 us (20%)
  Pallas kernels  33.3 us (11%)
  local copies, waits for them, and re-layouts  19.9 us (7%)
  between operations  14.3 us (5%)
    all_to_all x4, blocking collectives, exchange(): return lax.all_to_all(blocks, axis, split_axis=0, concat_axis=0, tiled=True)  55.3 us
    all_to_all x3, waiting for transfers between devices, spread(): lax.all_to_all(jnp.broadcast_to(block[None], (count,) + block.shape), axi...  30 us
    all_to_all x1, blocking collectives, spread(): lax.all_to_all(jnp.broadcast_to(block[None], (count,) + block.shape), axi...  26.8 us
    all_to_all x3, waiting for transfers between devices, exchange(): return lax.all_to_all(blocks, axis, split_axis=0, concat_axis=0, tiled=True)  22.9 us
    ppermute x3, waiting for transfers between devices, ring(): down.append(lax.ppermute(down[-1], axis, shift(-1)))  16.5 us
    unnamed x36, local copies, waits for them, and re-layouts  15.7 us
    all_to_all x3, starting transfers between devices, spread(): lax.all_to_all(jnp.broadcast_to(block[None], (count,) + block.shape), axi...  14.5 us
    ppermute x1, starting transfers between devices, body(): other = lax.ppermute(mine, 'core', swap)  11.2 us
  transfers between devices with their start and end apart: 16, of which 10 were waited for; matrix products, arithmetic and copies ran while one was open for 1% of the time, Pallas kernels for 8%

profile of v2, /device:TPU:1, one launch (start us, length us, event | category | flops | bytes accessed | tf_op | source)
XLA Modules:
  0.0 289.0 jit_solution(8549910640763148535)
XLA Ops:
  8.2 26.8 %all_to_all.55 = bf16[8,64,512]{2,1,0:T(8,128)(2,1)} all-to-all(bf16[8,64,512]{2,1,0:T(8,128)(2,1)S(1)} %broadcast_in_dim.8), channel_id=1, replica_groups=mesh['x'=4,'core'=2,'z'=8,'y'=8] {'z'}, dimensions={0} | all-to-all | bytes 1048576 | tf_op jit(solution)/shard_map/all_to_all | solution.py:270
  35.8 6.8 %all-to-all-start.1 = ((bf16[8,64,512]{2,1,0:T(8,128)(2,1)}), bf16[8,64,512]{2,1,0:T(8,128)(2,1)S(1)}, u32[]{:S(2)}, u32[]{:S(2)}) async-start(bf16[8,64,512]{2,1,0:T(8,128)(2,1)} %broadcast_in_dim.9), calls=%async_computation.1 | async-start | bytes 1048576 | tf_op jit(solution)/shard_map/all_to_all | solution.py:270
  42.7 16.1 %all-to-all-done.1.refs_0_ = bf16[8,64,512]{2,1,0:T(8,128)(2,1)S(1)} async-done(((bf16[8,64,512]{2,1,0:T(8,128)(2,1)}), bf16[8,64,512]{2,1,0:T(8,128)(2,1)S(1)}, u32[]{:S(2)}, u32[]{:S(2)}) %all-to-all-start.1) | async-done | bytes 524320 | tf_op jit(solution)/shard_map/all_to_all | solution.py:270
  60.2 4.2 %all-to-all-start.2 = ((bf16[4,2,224,512]{3,2,1,0:T(8,128)(2,1)}), bf16[4,2,224,512]{3,2,1,0:T(8,128)(2,1)S(1)}, u32[]{:S(2)}, u32[]{:S(2)}) async-start(bf16[4,2,224,512]{3,2,1,0:T(8,128)(2,1)} %broadcast_in_dim.10), calls=%async_computation.2 | async-start | bytes 3670016 | tf_op jit(solution)/shard_map/all_to_all | solution.py:270
  66.4 13.1 %all-to-all-done.2.refs_8_.mine = bf16[4,2,224,512]{3,2,1,0:T(8,128)(2,1)S(1)} async-done(((bf16[4,2,224,512]{3,2,1,0:T(8,128)(2,1)}), bf16[4,2,224,512]{3,2,1,0:T(8,128)(2,1)S(1)}, u32[]{:S(2)}, u32[]{:S(2)}) %all-to-all-start.2) | async-done | bytes 1835040 | tf_op jit(solution)/shard_map/all_to_all | solution.py:270
  79.5 11.2 %collective-permute-start.7 = (bf16[4,2,224,512]{3,2,1,0:T(8,128)(2,1)S(1)}, bf16[4,2,224,512]{3,2,1,0:T(8,128)(2,1)}, u32[]{:S(2)}, u32[]{:S(2)}) collective-permute-start(bf16[4,2,224,512]{3,2,1,0:T(8,128)(2,1)S(1)} %all-to-all-done.2.refs_8_.mine), channel_id=1, source_target_pairs={{0,64},{64,0},{1,65},{65,1},{2,66},{66,2},{3,67},{67,3},{4,68},{68... | collective-permute-start | bytes 5505032 | tf_op jit(solution)/shard_map/ppermute | solution.py:299
  92.7 3.4 %collective-permute-start.1 = (bf16[8,64,512]{2,1,0:T(8,128)(2,1)}, bf16[8,64,512]{2,1,0:T(8,128)(2,1)}, u32[]{:S(2)}, u32[]{:S(2)}) collective-permute-start(bf16[8,64,512]{2,1,0:T(8,128)(2,1)} %collective-permute-done.refs_1_), channel_id=1, source_target_pairs={{0,8},{8,16},{16,24},{24,32},{32,40},{40,48},{48,56},{56,0},{1,9},... | collective-permute-start | bytes 1572872 | tf_op jit(solution)/shard_map/ppermute | solution.py:283
  97.1 3.5 %all-to-all-start.4 = ((bf16[4,224,512]{2,1,0:T(8,128)(2,1)}), bf16[4,224,512]{2,1,0:T(8,128)(2,1)S(1)}, u32[]{:S(2)}, u32[]{:S(2)}) async-start(bf16[4,224,512]{2,1,0:T(8,128)(2,1)} %broadcast_in_dim.11), calls=%async_computation.4 | async-start | bytes 1835008 | tf_op jit(solution)/shard_map/all_to_all | solution.py:270
  100.6 5.7 %collective-permute-done.4.refs_7_ = bf16[8,64,512]{2,1,0:T(8,128)(2,1)} collective-permute-done((bf16[8,64,512]{2,1,0:T(8,128)(2,1)S(1)}, bf16[8,64,512]{2,1,0:T(8,128)(2,1)}, u32[]{:S(2)}, u32[]{:S(2)}) %collective-permute-start.4) | collective-permute-done | bytes 524320 | tf_op jit(solution)/shard_map/ppermute | solution.py:285
  106.3 3.6 %collective-permute-start.5 = (bf16[8,64,512]{2,1,0:T(8,128)(2,1)}, bf16[8,64,512]{2,1,0:T(8,128)(2,1)}, u32[]{:S(2)}, u32[]{:S(2)}) collective-permute-start(bf16[8,64,512]{2,1,0:T(8,128)(2,1)} %collective-permute-done.4.refs_7_), channel_id=1, source_target_pairs={{0,56},{8,0},{16,8},{24,16},{32,24},{40,32},{48,40},{56,48},{1,57}... | collective-permute-start | bytes 1572872 | tf_op jit(solution)/shard_map/ppermute | solution.py:285
  117.1 4.0 %collective-permute-done.5.refs_6_ = bf16[8,64,512]{2,1,0:T(8,128)(2,1)} collective-permute-done((bf16[8,64,512]{2,1,0:T(8,128)(2,1)}, bf16[8,64,512]{2,1,0:T(8,128)(2,1)}, u32[]{:S(2)}, u32[]{:S(2)}) %collective-permute-start.5) | collective-permute-done | bytes 524320 | tf_op jit(solution)/shard_map/ppermute | solution.py:285
  121.2 4.8 %collective-permute-start.6 = (bf16[8,64,512]{2,1,0:T(8,128)(2,1)}, bf16[8,64,512]{2,1,0:T(8,128)(2,1)}, u32[]{:S(2)}, u32[]{:S(2)}) collective-permute-start(bf16[8,64,512]{2,1,0:T(8,128)(2,1)} %collective-permute-done.5.refs_6_), channel_id=1, source_target_pairs={{0,56},{8,0},{16,8},{24,16},{32,24},{40,32},{48,40},{56,48},{1,57}... | collective-permute-start | bytes 1572872 | tf_op jit(solution)/shard_map/ppermute | solution.py:285
  129.1 6.7 %collective-permute-done.6.refs_5_ = bf16[8,64,512]{2,1,0:T(8,128)(2,1)} collective-permute-done((bf16[8,64,512]{2,1,0:T(8,128)(2,1)}, bf16[8,64,512]{2,1,0:T(8,128)(2,1)}, u32[]{:S(2)}, u32[]{:S(2)}) %collective-permute-start.6) | collective-permute-done | bytes 524320 | tf_op jit(solution)/shard_map/ppermute | solution.py:285
  135.8 6.4 %collective-permute-done.3.refs_4_ = bf16[8,64,512]{2,1,0:T(8,128)(2,1)} collective-permute-done((bf16[8,64,512]{2,1,0:T(8,128)(2,1)}, bf16[8,64,512]{2,1,0:T(8,128)(2,1)}, u32[]{:S(2)}, u32[]{:S(2)}) %collective-permute-start.3) | collective-permute-done | bytes 524320 | tf_op jit(solution)/shard_map/ppermute | solution.py:283
  142.2 6.0 %hidden.1 = (bf16[8,512,512]{2,1,0:T(8,128)(2,1)S(1)}, f32[224,512]{1,0:T(8,128)S(1)}, f32[224,512]{1,0:T(8,128)S(1)}, bf16[224,512]{1,0:T(8,128)(2,1)S(1)}, f32[1,512]{1,0:T(1,128)S(1)}) custom-call(s32[2]{0:T(128)S(1)} %pad_add_fusion.idx, bf16[8,64,512]{2,1,0:T(8,128)(2,1)S(1)} %all-to-all-done.1.refs_0_, ...), custom_call_target="tpu_custom_call" | custom-call | flops 1879048192 | bytes 14680064 | tf_op jit(solution)/shard_map/hidden/pallas_call | solution.py:83
  154.0 5.6 %gram.1 = f32[8,8,128]{2,1,0:T(8,128)} custom-call(bf16[8,8,64,512]{3,2,1,0:T(8,128)(2,1)S(1)} %bitcast.11, bf16[224,512]{1,0:T(8,128)(2,1)S(1)} %get-tuple-element.15.hidden), custom_call_target="tpu_custom_call" | custom-call | flops 2264924160 | bytes 5242880 | tf_op jit(solution)/shard_map/gram/pallas_call | solution.py:125
  178.6 8.6 %gain_term.1 = f32[8,32,128]{2,1,0:T(8,128)S(1)} custom-call(s32[2]{0:T(128)S(1)} %pad_add_fusion.idx, bf16[448,512]{1,0:T(8,128)(2,1)S(1)} %copy-done.8, f32[1,512]{1,0:T(1,128)S(1)} %get-tuple-element.21.inverse, bf16[8,512,512]{2,1,0:T(8,128)(2,1)S(1)} %copy-done.11, bf16[4,2,224,512]{3,2,1,0:T(8,128)(2,1)S(1)} %all-to-all-done.2.refs_8_.mine, ...), custom_call_target="tpu_custom_call" | custom-call | flops 2818572288 | bytes 9437184 | tf_op jit(solution)/shard_map/gain_term/pallas_call | solution.py:202
  189.4 4.0 %grad_down.1 = bf16[8,224,512]{2,1,0:T(8,128)(2,1)} custom-call(f32[8,8,128]{2,1,0:T(8,128)S(1)} %all-to-all-done.5.down_sq, bf16[224,512]{1,0:T(8,128)(2,1)S(1)} %get-tuple-element.15.hidden, bf16[8,8,64,512]{3,2,1,0:T(8,128)(2,1)S(1)} %bitcast.13), custom_call_target="tpu_custom_call" | custom-call | flops 939524096 | bytes 6291456 | tf_op jit(solution)/shard_map/grad_down/pallas_call | solution.py:258
  193.4 14.3 %all_to_all.56.part = f32[8,32,128]{2,1,0:T(8,128)} all-to-all(f32[8,32,128]{2,1,0:T(8,128)S(1)} %gain_term.1), channel_id=1, replica_groups=mesh['x'=4,'core'=2,'z'=8,'y'=8] {'y'}, dimensions={0} | all-to-all | bytes 262144 | tf_op jit(solution)/shard_map/all_to_all | solution.py:276
  209.3 14.6 %all_to_all.57.part = f32[8,32,128]{2,1,0:T(8,128)} all-to-all(f32[8,32,128]{2,1,0:T(8,128)} %add_parts.3), channel_id=1, replica_groups=mesh['x'=4,'core'=2,'z'=8,'y'=8] {'z'}, dimensions={0} | all-to-all | bytes 262144 | tf_op jit(solution)/shard_map/all_to_all | solution.py:276
  225.5 10.8 %all_to_all.58.part = f32[8,8,128]{2,1,0:T(8,128)} all-to-all(f32[8,8,128]{2,1,0:T(8,128)} %get-tuple-element.26), channel_id=1, replica_groups=mesh['x'=4,'core'=2,'z'=8,'y'=8] {'y'}, dimensions={0} | all-to-all | bytes 65536 | tf_op jit(solution)/shard_map/all_to_all | solution.py:276
  237.8 15.6 %all_to_all.59 = f32[8,8,128]{2,1,0:T(8,128)S(1)} all-to-all(f32[8,8,128]{2,1,0:T(8,128)} %gain_scale.1), channel_id=1, replica_groups=mesh['x'=4,'core'=2,'z'=8,'y'=8] {'x','core'}, dimensions={0} | all-to-all | bytes 65536 | tf_op jit(solution)/shard_map/all_to_all | solution.py:276
  253.3 4.2 %all-to-all-start.6 = ((bf16[8,224,512]{2,1,0:T(8,128)(2,1)}), bf16[8,224,512]{2,1,0:T(8,128)(2,1)S(1)}, u32[]{:S(2)}, u32[]{:S(2)}) async-start(bf16[8,224,512]{2,1,0:T(8,128)(2,1)} %grad_down.1), calls=%async_computation.6 | async-start | bytes 3670016 | tf_op jit(solution)/shard_map/all_to_all | solution.py:276
  258.2 22.9 %all-to-all-done.6 = bf16[8,224,512]{2,1,0:T(8,128)(2,1)S(1)} async-done(((bf16[8,224,512]{2,1,0:T(8,128)(2,1)}), bf16[8,224,512]{2,1,0:T(8,128)(2,1)S(1)}, u32[]{:S(2)}, u32[]{:S(2)}) %all-to-all-start.6) | async-done | bytes 1835040 | tf_op jit(solution)/shard_map/all_to_all | solution.py:276
  (69 shorter events, 51.5 us)
Async XLA Ops:
  7.2 27.8 %copy-start.16 = (bf16[512,64]{0,1:T(8,128)(2,1)S(1)}, bf16[512,64]{0,1:T(8,128)(2,1)}, u32[]{:S(2)}) copy-start(bf16[512,64]{0,1:T(8,128)(2,1)} %param.6) | copy-start | bytes 196612
  7.2 144.6 %all-gather.3.cloned.1.call-start = ((), (), s32[]{:S(2)}) async-start(), calls=%async_computation.11 | async-start | bytes 4718592 | tf_op jit(solution)/shard_map/all_gather | solution.py:298
  7.2 35.4 %copy-start.12 = (bf16[512,224]{0,1:T(8,128)(2,1)S(1)}, bf16[512,224]{0,1:T(8,128)(2,1)}, u32[]{:S(2)}) copy-start(bf16[512,224]{0,1:T(8,128)(2,1)} %param.10) | copy-start | bytes 688132
  7.2 35.4 %copy-start.13 = (bf16[512,224]{0,1:T(8,128)(2,1)S(1)}, bf16[512,224]{0,1:T(8,128)(2,1)}, u32[]{:S(2)}) copy-start(bf16[512,224]{0,1:T(8,128)(2,1)} %param.9) | copy-start | bytes 688132
  35.8 23.0 %all-to-all-start.1 = ((bf16[8,64,512]{2,1,0:T(8,128)(2,1)}), bf16[8,64,512]{2,1,0:T(8,128)(2,1)S(1)}, u32[]{:S(2)}, u32[]{:S(2)}) async-start(bf16[8,64,512]{2,1,0:T(8,128)(2,1)} %broadcast_in_dim.9), calls=%async_computation.1 | async-start | bytes 1048576 | tf_op jit(solution)/shard_map/all_to_all | solution.py:270
  60.2 35.9 %copy-start.14 = (bf16[224,512]{1,0:T(8,128)(2,1)S(1)}, bf16[224,512]{1,0:T(8,128)(2,1)}, u32[]{:S(2)}) copy-start(bf16[224,512]{1,0:T(8,128)(2,1)} %param.11) | copy-start | bytes 688132
  60.2 19.3 %all-to-all-start.2 = ((bf16[4,2,224,512]{3,2,1,0:T(8,128)(2,1)}), bf16[4,2,224,512]{3,2,1,0:T(8,128)(2,1)S(1)}, u32[]{:S(2)}, u32[]{:S(2)}) async-start(bf16[4,2,224,512]{3,2,1,0:T(8,128)(2,1)} %broadcast_in_dim.10), calls=%async_computation.2 | async-start | bytes 3670016 | tf_op jit(solution)/shard_map/all_to_all | solution.py:270
  64.4 64.6 %copy-start.17 = (f32[4096]{0:T(1024)S(1)}, f32[4096]{0:T(1024)}, u32[]{:S(2)}) copy-start(f32[4096]{0:T(1024)} %param.7) | copy-start | bytes 49156
  64.4 28.3 %collective-permute-start = (bf16[8,64,512]{2,1,0:T(8,128)(2,1)S(1)}, bf16[8,64,512]{2,1,0:T(8,128)(2,1)}, u32[]{:S(2)}, u32[]{:S(2)}) collective-permute-start(bf16[8,64,512]{2,1,0:T(8,128)(2,1)S(1)} %all-to-all-done.1.refs_0_), channel_id=1, source_target_pairs={{0,8},{8,16},{16,24},{24,32},{32,40},{40,48},{48,56},{56,0},{1,9},... | collective-permute-start | bytes 1572872 | tf_op jit(solution)/shard_map/ppermute | solution.py:283
  79.5 62.7 %collective-permute-start.7 = (bf16[4,2,224,512]{3,2,1,0:T(8,128)(2,1)S(1)}, bf16[4,2,224,512]{3,2,1,0:T(8,128)(2,1)}, u32[]{:S(2)}, u32[]{:S(2)}) collective-permute-start(bf16[4,2,224,512]{3,2,1,0:T(8,128)(2,1)S(1)} %all-to-all-done.2.refs_8_.mine), channel_id=1, source_target_pairs={{0,64},{64,0},{1,65},{65,1},{2,66},{66,2},{3,67},{67,3},{4,68},{68... | collective-permute-start | bytes 5505032 | tf_op jit(solution)/shard_map/ppermute | solution.py:299
  90.8 15.5 %collective-permute-start.4 = (bf16[8,64,512]{2,1,0:T(8,128)(2,1)S(1)}, bf16[8,64,512]{2,1,0:T(8,128)(2,1)}, u32[]{:S(2)}, u32[]{:S(2)}) collective-permute-start(bf16[8,64,512]{2,1,0:T(8,128)(2,1)S(1)} %all-to-all-done.1.refs_0_), channel_id=1, source_target_pairs={{0,56},{8,0},{16,8},{24,16},{32,24},{40,32},{48,40},{56,48},{1,57}... | collective-permute-start | bytes 1572872 | tf_op jit(solution)/shard_map/ppermute | solution.py:285
  92.7 18.3 %collective-permute-start.1 = (bf16[8,64,512]{2,1,0:T(8,128)(2,1)}, bf16[8,64,512]{2,1,0:T(8,128)(2,1)}, u32[]{:S(2)}, u32[]{:S(2)}) collective-permute-start(bf16[8,64,512]{2,1,0:T(8,128)(2,1)} %collective-permute-done.refs_1_), channel_id=1, source_target_pairs={{0,8},{8,16},{16,24},{24,32},{32,40},{40,48},{48,56},{56,0},{1,9},... | collective-permute-start | bytes 1572872 | tf_op jit(solution)/shard_map/ppermute | solution.py:283
  97.1 16.7 %all-to-all-start.4 = ((bf16[4,224,512]{2,1,0:T(8,128)(2,1)}), bf16[4,224,512]{2,1,0:T(8,128)(2,1)S(1)}, u32[]{:S(2)}, u32[]{:S(2)}) async-start(bf16[4,224,512]{2,1,0:T(8,128)(2,1)} %broadcast_in_dim.11), calls=%async_computation.4 | async-start | bytes 1835008 | tf_op jit(solution)/shard_map/all_to_all | solution.py:270
  106.3 14.9 %collective-permute-start.5 = (bf16[8,64,512]{2,1,0:T(8,128)(2,1)}, bf16[8,64,512]{2,1,0:T(8,128)(2,1)}, u32[]{:S(2)}, u32[]{:S(2)}) collective-permute-start(bf16[8,64,512]{2,1,0:T(8,128)(2,1)} %collective-permute-done.4.refs_7_), channel_id=1, source_target_pairs={{0,56},{8,0},{16,8},{24,16},{32,24},{40,32},{48,40},{56,48},{1,57}... | collective-permute-start | bytes 1572872 | tf_op jit(solution)/shard_map/ppermute | solution.py:285
  111.0 16.1 %collective-permute-start.2 = (bf16[8,64,512]{2,1,0:T(8,128)(2,1)}, bf16[8,64,512]{2,1,0:T(8,128)(2,1)}, u32[]{:S(2)}, u32[]{:S(2)}) collective-permute-start(bf16[8,64,512]{2,1,0:T(8,128)(2,1)} %collective-permute-done.1.refs_2_), channel_id=1, source_target_pairs={{0,8},{8,16},{16,24},{24,32},{32,40},{40,48},{48,56},{56,0},{1,9},... | collective-permute-start | bytes 1572872 | tf_op jit(solution)/shard_map/ppermute | solution.py:283
  113.8 49.2 %collective-permute-start.8 = (bf16[4,224,512]{2,1,0:T(8,128)(2,1)S(1)}, bf16[4,224,512]{2,1,0:T(8,128)(2,1)}, u32[]{:S(2)}, u32[]{:S(2)}) collective-permute-start(bf16[4,224,512]{2,1,0:T(8,128)(2,1)S(1)} %all-to-all-done.4.mine), channel_id=1, source_target_pairs={{0,64},{64,0},{1,65},{65,1},{2,66},{66,2},{3,67},{67,3},{4,68},{68... | collective-permute-start | bytes 2752520 | tf_op jit(solution)/shard_map/ppermute | solution.py:300
  121.2 14.7 %collective-permute-start.6 = (bf16[8,64,512]{2,1,0:T(8,128)(2,1)}, bf16[8,64,512]{2,1,0:T(8,128)(2,1)}, u32[]{:S(2)}, u32[]{:S(2)}) collective-permute-start(bf16[8,64,512]{2,1,0:T(8,128)(2,1)} %collective-permute-done.5.refs_6_), channel_id=1, source_target_pairs={{0,56},{8,0},{16,8},{24,16},{32,24},{40,32},{48,40},{56,48},{1,57}... | collective-permute-start | bytes 1572872 | tf_op jit(solution)/shard_map/ppermute | solution.py:285
  127.1 15.1 %collective-permute-start.3 = (bf16[8,64,512]{2,1,0:T(8,128)(2,1)}, bf16[8,64,512]{2,1,0:T(8,128)(2,1)}, u32[]{:S(2)}, u32[]{:S(2)}) collective-permute-start(bf16[8,64,512]{2,1,0:T(8,128)(2,1)} %collective-permute-done.2.refs_3_), channel_id=1, source_target_pairs={{0,8},{8,16},{16,24},{24,32},{32,40},{40,48},{48,56},{56,0},{1,9},... | collective-permute-start | bytes 1572872 | tf_op jit(solution)/shard_map/ppermute | solution.py:283
  129.1 46.2 %copy-start.9 = (s32[2]{0:T(128)}, s32[2]{0:T(128)S(1)}, u32[]{:S(2)}) copy-start(s32[2]{0:T(128)S(1)} %pad_add_fusion.idx) | copy-start | bytes 28
  154.0 9.0 %copy-start.4 = (f32[224,512]{1,0:T(8,128)S(1)}, f32[224,512]{1,0:T(8,128)}, u32[]{:S(2)}) copy-start(f32[224,512]{1,0:T(8,128)} %copy-done.3) | copy-start | bytes 1376260
  159.6 10.4 %all-to-all-start.3 = ((f32[8,8,128]{2,1,0:T(8,128)}), f32[8,8,128]{2,1,0:T(8,128)S(1)}, u32[]{:S(2)}, u32[]{:S(2)}) async-start(f32[8,8,128]{2,1,0:T(8,128)} %gram.1), calls=%async_computation.3 | async-start | bytes 65536 | tf_op jit(solution)/shard_map/all_to_all | solution.py:276
  172.0 15.2 %all-to-all-start.5 = ((f32[8,8,128]{2,1,0:T(8,128)}), f32[8,8,128]{2,1,0:T(8,128)S(1)}, u32[]{:S(2)}, u32[]{:S(2)}) async-start(f32[8,8,128]{2,1,0:T(8,128)} %add_parts.2), calls=%async_computation.5 | async-start | bytes 65536 | tf_op jit(solution)/shard_map/all_to_all | solution.py:276
  187.2 2.2 copy-start.2
  253.3 27.8 %all-to-all-start.6 = ((bf16[8,224,512]{2,1,0:T(8,128)(2,1)}), bf16[8,224,512]{2,1,0:T(8,128)(2,1)S(1)}, u32[]{:S(2)}, u32[]{:S(2)}) async-start(bf16[8,224,512]{2,1,0:T(8,128)(2,1)} %grad_down.1), calls=%async_computation.6 | async-start | bytes 3670016 | tf_op jit(solution)/shard_map/all_to_all | solution.py:276
  (10 other events, 13.5 us)
Sparse Core Ops, SparseCore 0:
  35.1 62.7 all-gather.2

commit v3 on v2

--- a/solution.py
+++ b/solution.py
@@ -44,8 +44,44 @@
     lax.fori_loop(0, NX, step, 0)
 
 
+TN = (((0,), (0,)), ((), ()))
+NT = (((1,), (1,)), ((), ()))
+HALF = TOK // 2
+
+
+def cotangent_kernel(idx, *refs):
+    pieces, (dy, gram) = refs[:NY], refs[NY:]
+    y = idx[2]
+    for j in range(NY):
+        slot = lax.rem(y - j + NY, NY)
+        for i in range(NZ):
+            dy[i, pl.ds(pl.multiple_of(slot * COLS, COLS), COLS), :] = pieces[j][i]
+    for h in range(2):
+
+        def step(z, acc):
+            block = dy[z, :, h * HALF : (h + 1) * HALF]
+            return acc + lax.dot_general(block, block, TN, preferred_element_type=F32)
+
+        gram[h] = lax.fori_loop(0, NZ, step, jnp.zeros((HALF, HALF), F32))
+
+
+def cotangent_call(idx, pieces):
+    return pl.pallas_call(
+        cotangent_kernel,
+        out_shape=(
+            jax.ShapeDtypeStruct((NZ, SHARE, TOK), BF16),
+            jax.ShapeDtypeStruct((2, HALF, HALF), F32),
+        ),
+        in_specs=[SMEM] + [VMEM] * NY,
+        out_specs=(VMEM,) * 2,
+        compiler_params=params(16),
+        cost_estimate=cost(TOK * HALF * FEATURES, 9 << 20),
+        name="cotangent_gram",
+    )(idx, *pieces)
+
+
 def hidden_kernel(idx, *refs):
-    pieces, (mine, other, gain, xs, gate, up, hidden, inverse, acc) = refs[:NZ], refs[NZ:]
+    pieces, (wg, wu, gain, dy_gram, xs, gate, up, hidden, inverse, down_sq, acc) = refs[:NZ], refs[NZ:]
     z = idx[0]
     total = jnp.zeros((8, TOK), F32)
     for j in range(NZ):
@@ -59,27 +95,37 @@
     inverse[...] = lax.rsqrt(mean + 1e-05)
     acc[...] = jnp.zeros_like(acc)
 
-    def share(i, which, d):
-        ref = other if which else mine
-        scaled = ref[i].reshape(2 * UNITS, SHARE).astype(F32) * gain[pl.ds(d, 1), :]
-        acc[...] += jnp.dot(scaled.astype(BF16), xs[d], preferred_element_type=F32)
-
-    each_share(idx, share)
+    def share(d, carry):
+        row = gain[pl.ds(d, 1), :]
+        for k, ref in enumerate((wg, wu)):
+            scaled = (ref[d].astype(F32) * row).astype(BF16)
+            acc[k] += jnp.dot(scaled, xs[d], preferred_element_type=F32)
+        return carry
+
+    lax.fori_loop(0, NX * NC, share, 0)
 
     def rows(i, carry):
-        r = pl.multiple_of(i * 32, 32)
+        r = pl.ds(pl.multiple_of(i * 32, 32), 32)
         inv = inverse[...]
-        g = acc[pl.ds(r, 32), :] * inv
-        u = acc[pl.ds(pl.multiple_of(UNITS + r, 32), 32), :] * inv
-        gate[pl.ds(r, 32), :] = g
-        up[pl.ds(r, 32), :] = u
-        hidden[pl.ds(r, 32), :] = (g * jax.nn.sigmoid(g) * u).astype(BF16)
+        g = acc[0, r, :] * inv
+        u = acc[1, r, :] * inv
+        gate[r, :] = g
+        up[r, :] = u
+        hidden[r, :] = (g * jax.nn.sigmoid(g) * u).astype(BF16)
         return carry
 
     lax.fori_loop(0, UNITS // 32, rows, 0)
-
-
-def hidden_call(idx, pieces, mine, other, gain):
+    for h in range(2):
+        own = hidden[:, h * HALF : (h + 1) * HALF]
+        pairs = lax.dot_general(own, own, TN, preferred_element_type=F32) * dy_gram[h]
+        for s in range(HALF // SEQ):
+            part = pairs[s * SEQ : (s + 1) * SEQ, s * SEQ : (s + 1) * SEQ]
+            value = jnp.sum(jnp.sum(part, axis=0, keepdims=True), axis=1, keepdims=True)
+            i = h * (HALF // SEQ) + s
+            down_sq[:, i : i + 1, :] = jnp.broadcast_to(value.reshape(1, 1, 1), (NY, 1, 128))
+
+
+def hidden_call(idx, pieces, wg, wu, gain, dy_gram):
     return pl.pallas_call(
         hidden_kernel,
         out_shape=(
@@ -88,49 +134,15 @@
             jax.ShapeDtypeStruct((UNITS, TOK), F32),
             jax.ShapeDtypeStruct((UNITS, TOK), BF16),
             jax.ShapeDtypeStruct((1, TOK), F32),
+            jax.ShapeDtypeStruct((NY, LOCAL, 128), F32),
         ),
-        in_specs=[SMEM] + [VMEM] * (NZ + 3),
-        out_specs=(VMEM,) * 5,
-        scratch_shapes=[pltpu.VMEM((2 * UNITS, TOK), F32)],
-        compiler_params=params(40),
+        in_specs=[SMEM] + [VMEM] * (NZ + 4),
+        out_specs=(VMEM,) * 6,
+        scratch_shapes=[pltpu.VMEM((2, UNITS, TOK), F32)],
+        compiler_params=params(24),
         cost_estimate=cost(2 * UNITS * TOK * FEATURES, 14 << 20),
         name="hidden",
-    )(idx, *pieces, mine, other, gain)
-
-
-TN = (((0,), (0,)), ((), ()))
-NT = (((1,), (1,)), ((), ()))
-
-
-def gram_kernel(dy, hidden, out):
-    half = TOK // 2
-    for h in range(2):
-        lanes = slice(h * half, (h + 1) * half)
-        mine = hidden[:, lanes]
-        own = lax.dot_general(mine, mine, TN, preferred_element_type=F32)
-
-        def step(z, acc):
-            block = dy[:, z, :, lanes].reshape(SHARE, half)
-            return acc + lax.dot_general(block, block, TN, preferred_element_type=F32)
-
-        pairs = own * lax.fori_loop(0, NZ, step, jnp.zeros((half, half), F32))
-        for s in range(half // SEQ):
-            part = pairs[s * SEQ : (s + 1) * SEQ, s * SEQ : (s + 1) * SEQ]
-            value = jnp.sum(jnp.sum(part, axis=0, keepdims=True), axis=1, keepdims=True)
-            i = h * (half // SEQ) + s
-            out[:, i : i + 1, :] = jnp.broadcast_to(value.reshape(1, 1, 1), (NY, 1, 128))
-
-
-def gram_call(dy, hidden):
-    return pl.pallas_call(
-        gram_kernel,
-        out_shape=jax.ShapeDtypeStruct((NY, LOCAL, 128), F32),
-        in_specs=[VMEM] * 2,
-        out_specs=VMEM,
-        compiler_params=params(24),
-        cost_estimate=cost(TOK * TOK * (FEATURES + UNITS), 5 << 20),
-        name="gram",
-    )(dy, hidden)
+    )(idx, *pieces, wg, wu, gain, dy_gram)
 
 
 def back_kernel(idx, dy, mine, other, gate, up, grads, acc):
@@ -138,8 +150,7 @@
 
     def share(i, which, d):
         ref = other if which else mine
-        block = dy[:, d, :, :].reshape(SHARE, TOK)
-        acc[...] += jnp.dot(ref[i], block, preferred_element_type=F32)
+        acc[...] += jnp.dot(ref[i], dy[d], preferred_element_type=F32)
 
     each_share(idx, share)
 
@@ -161,22 +172,22 @@
         in_specs=[SMEM] + [VMEM] * 5,
         out_specs=VMEM,
         scratch_shapes=[pltpu.VMEM((UNITS, TOK), F32)],
-        compiler_params=params(28),
+        compiler_params=params(16),
         cost_estimate=cost(UNITS * TOK * FEATURES, 7 << 20),
         name="back",
     )(idx, dy, mine, other, gate, up)
 
 
-def gain_kernel(idx, grads, inverse, xs, mine, other, out):
+def gain_kernel(grads, inverse, xs, wg, wu, out):
     token = lax.broadcasted_iota(jnp.int32, (TOK, 128), 0)
     column = lax.broadcasted_iota(jnp.int32, (TOK, 128), 1)
     select = jnp.where(token // SEQ == column, 1.0, 0.0).astype(BF16)
-    core = idx[1]
     wide = SHARE // 2
 
-    def term(weight, d, h):
+    def term(d, h):
         f = slice(h * wide, (h + 1) * wide)
-        normed = lax.dot_general(weight[:, f], grads[...], TN, preferred_element_type=F32)
+        normed = lax.dot_general(wg[d, :, f], grads[:UNITS], TN, preferred_element_type=F32)
+        normed += lax.dot_general(wu[d, :, f], grads[UNITS:], TN, preferred_element_type=F32)
         product = xs[d, f, :].astype(F32) * inverse[...] * normed
         high = product.astype(BF16)
         low = (product - high.astype(F32)).astype(BF16)
@@ -186,9 +197,7 @@
 
     def step(i, carry):
         for h in range(2):
-            a = term(mine[i].reshape(2 * UNITS, SHARE), 2 * i + core, h)
-            b = term(other[i].reshape(2 * UNITS, SHARE), 2 * i + 1 - core, h)
-            even, odd = jnp.where(core == 0, a, b), jnp.where(core == 0, b, a)
+            even, odd = term(2 * i, h), term(2 * i + 1, h)
             for y in range(wide // COLS):
                 lanes = slice(y * COLS, (y + 1) * COLS)
                 rows = pl.ds(pl.multiple_of(i * LOCAL, LOCAL), LOCAL)
@@ -198,16 +207,16 @@
     lax.fori_loop(0, NX, step, 0)
 
 
-def gain_call(idx, grads, inverse, xs, mine, other):
+def gain_call(grads, inverse, xs, wg, wu):
     return pl.pallas_call(
         gain_kernel,
         out_shape=jax.ShapeDtypeStruct((NY, NX * LOCAL, 128), F32),
-        in_specs=[SMEM] + [VMEM] * 5,
+        in_specs=[VMEM] * 5,
         out_specs=VMEM,
-        compiler_params=params(40),
+        compiler_params=params(20),
         cost_estimate=cost(3 * UNITS * TOK * FEATURES, 9 << 20),
         name="gain_term",
-    )(idx, grads, inverse, xs, mine, other)
+    )(grads, inverse, xs, wg, wu)
 
 
 def add_kernel(part, out):
@@ -247,8 +256,7 @@
     scaled = (hidden[...].astype(F32) * row).astype(BF16)
 
     def step(d, carry):
-        block = dy[:, d, :, :].reshape(SHARE, TOK)
-        out[d] = lax.dot_general(scaled, block, NT, preferred_element_type=F32).astype(BF16)
+        out[d] = lax.dot_general(scaled, dy[d], NT, preferred_element_type=F32).astype(BF16)
         return carry
 
     lax.fori_loop(0, NX * NC, step, 0)
@@ -260,7 +268,7 @@
         out_shape=jax.ShapeDtypeStruct((NX * NC, UNITS, SHARE), BF16),
         in_specs=[VMEM] * 3,
         out_specs=VMEM,
-        compiler_params=params(24),
+        compiler_params=params(14),
         cost_estimate=cost(UNITS * TOK * FEATURES, 6 << 20),
         name="grad_down",
     )(down_sq, hidden, dy)
@@ -287,30 +295,30 @@
 
 
 def body(tokens, gain, cotangent, gate_weight, up_weight, down_weight):
-    idx = jnp.stack([lax.axis_index("z"), lax.axis_index("core")]).astype(jnp.int32)
-    x_part = spread(tokens.T, "y", NY)
-    both = jnp.stack([gate_weight.T, up_weight.T])
-    mine = spread(both, "x", NX)
+    idx = jnp.stack([lax.axis_index("z"), lax.axis_index("core"), lax.axis_index("y")]).astype(jnp.int32)
+    dp = ("x", "core")
+    x_part = lax.all_gather(tokens.T, "y", axis=0)
+    wg = lax.all_gather(gate_weight.T, dp, axis=0)
+    wu = lax.all_gather(up_weight.T, dp, axis=0)
     dy_part = spread(cotangent.T, "z", NZ)
     dmine = spread(down_weight, "x", NX)
-    swap = [(0, 1), (1, 0)]
+    dy_pieces = ring(dy_part, "y", NY)
     pieces = ring(x_part, "z", NZ)
-    dy = lax.all_gather(dy_part, "y", axis=0)
-    other = lax.ppermute(mine, "core", swap)
-    dother = lax.ppermute(dmine, "core", swap)
-
-    xs, gate, up, hidden, inverse = hidden_call(idx, pieces, mine, other, gain.reshape(NX * NC, SHARE))
-    gram = gram_call(dy, hidden)
-    part = exchange(gram, "y")
-    dy_back, gram = lax.optimization_barrier((dy, gram))
+    dother = lax.ppermute(dmine, "core", [(0, 1), (1, 0)])
+
+    dy, dy_gram = cotangent_call(idx, dy_pieces)
+    xs, gate, up, hidden, inverse, sq_part = hidden_call(
+        idx, pieces, wg, wu, gain.reshape(NX * NC, SHARE), dy_gram
+    )
+    part = exchange(sq_part, "y")
+    dy_back, sq_part = lax.optimization_barrier((dy, sq_part))
     grads = back_call(idx, dy_back, dmine, dother, gate, up)
     part, grads = lax.optimization_barrier((part, grads))
     down_sq = exchange(add_and_repeat(part), "z")
-    gain_part = gain_call(idx, grads, inverse, xs, mine, other)
+    gain_part = gain_call(grads, inverse, xs, wg, wu)
     down_sq, gain_part = lax.optimization_barrier((down_sq, gain_part))
     terms = grad_call(down_sq, hidden, dy)
-    grad = exchange(terms, ("x", "core"))
-    gain_part, terms = lax.optimization_barrier((gain_part, terms))
+    grad_down = lax.psum_scatter(terms, dp, scatter_dimension=0).astype(F32)
 
     gain_part = exchange(add_and_repeat(exchange(gain_part, "y")), "z")
     gain_y, sq_part = pl.pallas_call(
@@ -329,7 +337,6 @@
     )(idx, exchange(sq_part, "y"), gain_y)
     gain_all = jnp.sum(exchange(gain_local, ("x", "core"))[:, 0], axis=0)
     grad_gain = jnp.where(idx[0] % 2 == 0, gain_all[:COLS], gain_all[COLS:])
-    grad_down = jnp.sum(grad.astype(F32), axis=0)
     return (grad_down, grad_gain)
 
 

time: 291 us -> 268 us (0.921)
  waiting for transfers between devices: 78 us -> 31.2 us
  starting transfers between devices: 59.6 us -> 87 us
  blocking collectives: 82.1 us -> 70.5 us
  local copies, waits for them, and re-layouts: 19.9 us -> 27.8 us
    all_gather x0 -> x1, blocking collectives: none -> 30.5 us  [body(): x_part = lax.all_gather(tokens.T, 'y', axis=0)]
    all_to_all x1 -> x0, blocking collectives: 26.8 us -> none  [spread(): lax.all_to_all(jnp.broadcast_to(block[None], (count,) + block.shape), axi...]
    all_to_all x3, waiting for transfers between devices: 22.9 us -> 4.72 us  [exchange(): return lax.all_to_all(blocks, axis, split_axis=0, concat_axis=0, tiled=True)]
    all_to_all x4 -> x3, blocking collectives: 55.3 us -> 40 us  [exchange(): return lax.all_to_all(blocks, axis, split_axis=0, concat_axis=0, tiled=True)]
    ppermute x3 -> x6, starting transfers between devices: 10.4 us -> 24.4 us  [ring(): down.append(lax.ppermute(down[-1], axis, shift(-1)))]
    ppermute x3 -> x6, waiting for transfers between devices: 16.5 us -> 2.79 us  [ring(): down.append(lax.ppermute(down[-1], axis, shift(-1)))]
    all_to_all x3 -> x2, waiting for transfers between devices: 30 us -> 17.2 us  [spread(): lax.all_to_all(jnp.broadcast_to(block[None], (count,) + block.shape), axi...]
    unnamed x36 -> x52, local copies, waits for them, and re-layouts: 15.7 us -> 25.1 us
  transfers between devices with their start and end apart: 16 -> 23, of which waited for: 10 -> 4; matrix products, arithmetic and copies ran while one was open for 1% -> 1% of each run, Pallas kernels for 8% -> 10%
where the time goes in v3:
time: 268 us; the launch traced here: 266 us
  starting transfers between devices  87 us (32%)
  blocking collectives  70.5 us (26%)
  Pallas kernels  33 us (12%)
  waiting for transfers between devices  31.2 us (12%)
  local copies, waits for them, and re-layouts  27.8 us (10%)
  between operations  14.2 us (5%)
    all_to_all x3, blocking collectives, exchange(): return lax.all_to_all(blocks, axis, split_axis=0, concat_axis=0, tiled=True)  40 us
    all_gather x1, blocking collectives, body(): x_part = lax.all_gather(tokens.T, 'y', axis=0)  30.5 us
    unnamed x52, local copies, waits for them, and re-layouts  25.1 us
    ppermute x6, starting transfers between devices, ring(): down.append(lax.ppermute(down[-1], axis, shift(-1)))  24.4 us
    all_to_all x3, starting transfers between devices, exchange(): return lax.all_to_all(blocks, axis, split_axis=0, concat_axis=0, tiled=True)  19.8 us
    ppermute x8, starting transfers between devices, ring(): up.append(lax.ppermute(up[-1], axis, shift(1)))  17.8 us
    all_to_all x2, waiting for transfers between devices, spread(): lax.all_to_all(jnp.broadcast_to(block[None], (count,) + block.shape), axi...  17.2 us
    all_to_all x2, starting transfers between devices, spread(): lax.all_to_all(jnp.broadcast_to(block[None], (count,) + block.shape), axi...  14.4 us
  transfers between devices with their start and end apart: 23, of which 4 were waited for; matrix products, arithmetic and copies ran while one was open for 1% of the time, Pallas kernels for 10%

profile of v3, /device:TPU:1, one launch (start us, length us, event | category | flops | bytes accessed | tf_op | source)
XLA Modules:
  0.0 266.1 jit_solution(12139337786584096600)
XLA Ops:
  9.6 10.9 %all-to-all-start = ((bf16[8,64,512]{2,1,0:T(8,128)(2,1)}), bf16[8,64,512]{2,1,0:T(8,128)(2,1)S(1)}, u32[]{:S(2)}, u32[]{:S(2)}) async-start(bf16[8,64,512]{2,1,0:T(8,128)(2,1)} %broadcast_in_dim.4), calls=%async_computation | async-start | bytes 1048576 | tf_op jit(solution)/shard_map/all_to_all | solution.py:278
  21.2 17.2 %all-to-all-done.refs_0_ = bf16[8,64,512]{2,1,0:T(8,128)(2,1)S(1)} async-done(((bf16[8,64,512]{2,1,0:T(8,128)(2,1)}), bf16[8,64,512]{2,1,0:T(8,128)(2,1)S(1)}, u32[]{:S(2)}, u32[]{:S(2)}) %all-to-all-start) | async-done | bytes 524320 | tf_op jit(solution)/shard_map/all_to_all | solution.py:278
  38.4 3.2 %collective-permute-start.7 = (bf16[8,64,512]{2,1,0:T(8,128)(2,1)S(1)}, bf16[8,64,512]{2,1,0:T(8,128)(2,1)S(1)}, u32[]{:S(2)}, u32[]{:S(2)}) collective-permute-start(bf16[8,64,512]{2,1,0:T(8,128)(2,1)S(1)} %all-to-all-done.refs_0_), channel_id=1, source_target_pairs={{0,1},{1,2},{2,3},{3,4},{4,5},{5,6},{6,7},{7,0},{8,9},{9,10},{10,1... | collective-permute-start | bytes 1572872 | tf_op jit(solution)/shard_map/ppermute | solution.py:291
  41.6 30.5 %all-gather = bf16[512,512]{1,0:T(8,128)(2,1)S(1)} all-gather(bf16[64,512]{1,0:T(8,128)(2,1)S(1)} %bitcast.23), channel_id=2, replica_groups=mesh['x'=4,'core'=2,'z'=8,'y'=8] {'y'}, dimensions={0}, use_global_device_ids=true | all-gather | bytes 589824 | tf_op jit(solution)/shard_map/all_gather | solution.py:300
  76.3 3.1 %collective-permute-start.8 = (bf16[8,64,512]{2,1,0:T(8,128)(2,1)S(1)}, bf16[8,64,512]{2,1,0:T(8,128)(2,1)}, u32[]{:S(2)}, u32[]{:S(2)}) collective-permute-start(bf16[8,64,512]{2,1,0:T(8,128)(2,1)S(1)} %collective-permute-done.7.refs_1_), channel_id=1, source_target_pairs={{0,1},{1,2},{2,3},{3,4},{4,5},{5,6},{6,7},{7,0},{8,9},{9,10},{10,1... | collective-permute-start | bytes 1572872 | tf_op jit(solution)/shard_map/ppermute | solution.py:291
  79.4 4.6 %collective-permute-start.4 = (bf16[8,64,512]{2,1,0:T(8,128)(2,1)S(1)}, bf16[8,64,512]{2,1,0:T(8,128)(2,1)}, u32[]{:S(2)}, u32[]{:S(2)}) collective-permute-start(bf16[8,64,512]{2,1,0:T(8,128)(2,1)S(1)} %bitcast.14), channel_id=1, source_target_pairs={{0,56},{8,0},{16,8},{24,16},{32,24},{40,32},{48,40},{56,48},{1,57}... | collective-permute-start | bytes 1572872 | tf_op jit(solution)/shard_map/ppermute | solution.py:293
  87.0 3.5 %all-to-all-start.2 = ((bf16[4,224,512]{2,1,0:T(8,128)(2,1)}), bf16[4,224,512]{2,1,0:T(8,128)(2,1)S(1)}, u32[]{:S(2)}, u32[]{:S(2)}) async-start(bf16[4,224,512]{2,1,0:T(8,128)(2,1)} %broadcast_in_dim.5), calls=%async_computation.2 | async-start | bytes 1835008 | tf_op jit(solution)/shard_map/all_to_all | solution.py:278
  90.5 3.4 %collective-permute-start.12 = (bf16[8,64,512]{2,1,0:T(8,128)(2,1)}, bf16[8,64,512]{2,1,0:T(8,128)(2,1)}, u32[]{:S(2)}, u32[]{:S(2)}) collective-permute-start(bf16[8,64,512]{2,1,0:T(8,128)(2,1)} %collective-permute-done.11.refs_7_), channel_id=1, source_target_pairs={{0,7},{1,0},{2,1},{3,2},{4,3},{5,4},{6,5},{7,6},{8,15},{9,8},{10,9... | collective-permute-start | bytes 1572872 | tf_op jit(solution)/shard_map/ppermute | solution.py:293
  95.8 4.6 %collective-permute-start.5 = (bf16[8,64,512]{2,1,0:T(8,128)(2,1)}, bf16[8,64,512]{2,1,0:T(8,128)(2,1)}, u32[]{:S(2)}, u32[]{:S(2)}) collective-permute-start(bf16[8,64,512]{2,1,0:T(8,128)(2,1)} %collective-permute-done.4.refs_7_), channel_id=1, source_target_pairs={{0,56},{8,0},{16,8},{24,16},{32,24},{40,32},{48,40},{56,48},{1,57}... | collective-permute-start | bytes 1572872 | tf_op jit(solution)/shard_map/ppermute | solution.py:293
  102.4 10.5 %collective-permute-start.14 = (bf16[4,224,512]{2,1,0:T(8,128)(2,1)S(1)}, bf16[4,224,512]{2,1,0:T(8,128)(2,1)S(1)}, u32[]{:S(2)}, u32[]{:S(2)}) collective-permute-start(bf16[4,224,512]{2,1,0:T(8,128)(2,1)S(1)} %all-to-all-done.2.mine), channel_id=1, source_target_pairs={{0,64},{64,0},{1,65},{65,1},{2,66},{66,2},{3,67},{67,3},{4,68},{68... | collective-permute-start | bytes 2752520 | tf_op jit(solution)/shard_map/ppermute | solution.py:307
  112.9 4.9 %collective-permute-start.13 = (bf16[8,64,512]{2,1,0:T(8,128)(2,1)}, bf16[8,64,512]{2,1,0:T(8,128)(2,1)}, u32[]{:S(2)}, u32[]{:S(2)}) collective-permute-start(bf16[8,64,512]{2,1,0:T(8,128)(2,1)} %collective-permute-done.12.refs_6_), channel_id=1, source_target_pairs={{0,7},{1,0},{2,1},{3,2},{4,3},{5,4},{6,5},{7,6},{8,15},{9,8},{10,9... | collective-permute-start | bytes 1572872 | tf_op jit(solution)/shard_map/ppermute | solution.py:293
  119.7 4.9 %collective-permute-start.6 = (bf16[8,64,512]{2,1,0:T(8,128)(2,1)}, bf16[8,64,512]{2,1,0:T(8,128)(2,1)}, u32[]{:S(2)}, u32[]{:S(2)}) collective-permute-start(bf16[8,64,512]{2,1,0:T(8,128)(2,1)} %collective-permute-done.5.refs_6_), channel_id=1, source_target_pairs={{0,56},{8,0},{16,8},{24,16},{32,24},{40,32},{48,40},{56,48},{1,57}... | collective-permute-start | bytes 1572872 | tf_op jit(solution)/shard_map/ppermute | solution.py:293
  129.4 5.0 %collective-permute-done.10.refs_4_ = bf16[8,64,512]{2,1,0:T(8,128)(2,1)} collective-permute-done((bf16[8,64,512]{2,1,0:T(8,128)(2,1)}, bf16[8,64,512]{2,1,0:T(8,128)(2,1)}, u32[]{:S(2)}, u32[]{:S(2)}) %collective-permute-start.10) | collective-permute-done | bytes 524320 | tf_op jit(solution)/shard_map/ppermute | solution.py:291
  135.4 6.6 %cotangent_gram.1 = (bf16[8,512,512]{2,1,0:T(8,128)(2,1)S(1)}, f32[2,256,256]{2,1,0:T(8,128)S(1)}) custom-call(s32[3]{0:T(128)S(1)} %pad_add_fusion.idx, bf16[8,64,512]{2,1,0:T(8,128)(2,1)S(1)} %all-to-all-done.refs_0_, bf16[8,64,512]{2,1,0:T(8,128)(2,1)S(1)} %copy-done.10, bf16[8,64,512]{2,1,0:T(8,128)(2,1)} %collective-permute-done.8.refs_2_, ...), custom_call_target="tpu_custom_call" | custom-call | flops 1073741824 | bytes 9437184 | tf_op jit(solution)/shard_map/cotangent_gram/pallas_call | solution.py:69
  149.0 6.9 %hidden.1 = (bf16[8,512,512]{2,1,0:T(8,128)(2,1)S(1)}, f32[224,512]{1,0:T(8,128)S(1)}, f32[224,512]{1,0:T(8,128)S(1)}, bf16[224,512]{1,0:T(8,128)(2,1)S(1)}, f32[1,512]{1,0:T(1,128)S(1)}, /*index=5*/f32[8,8,128]{2,1,0:T(8,128)}) custom-call(s32[3]{0:T(128)S(1)} %pad_add_fusion.idx, bf16[8,64,512]{2,1,0:T(8,128)(2,1)S(1)} %bitcast.15, ...), custom_call_target="tpu_custom_call" | custom-call | flops 1879048192 | bytes 14680064 | tf_op jit(solution)/shard_map/hidden/pallas_call | solution.py:129
  160.1 4.7 %all-to-all-start.1 = ((f32[8,8,128]{2,1,0:T(8,128)}), f32[8,8,128]{2,1,0:T(8,128)S(1)}, u32[]{:S(2)}, u32[]{:S(2)}) async-start(f32[8,8,128]{2,1,0:T(8,128)} %get-tuple-element.18), calls=%async_computation.1 | async-start | bytes 65536 | tf_op jit(solution)/shard_map/all_to_all | solution.py:284
  175.7 4.2 %all-to-all-start.3 = ((f32[8,8,128]{2,1,0:T(8,128)}), f32[8,8,128]{2,1,0:T(8,128)S(1)}, u32[]{:S(2)}, u32[]{:S(2)}) async-start(f32[8,8,128]{2,1,0:T(8,128)} %add_parts.2), calls=%async_computation.3 | async-start | bytes 65536 | tf_op jit(solution)/shard_map/all_to_all | solution.py:284
  183.6 7.0 %gain_term.1 = f32[8,32,128]{2,1,0:T(8,128)S(1)} custom-call(bf16[448,512]{1,0:T(8,128)(2,1)S(1)} %back.1.grads, f32[1,512]{1,0:T(1,128)S(1)} %get-tuple-element.25.inverse, bf16[8,512,512]{2,1,0:T(8,128)(2,1)S(1)} %copy-done.21, bf16[8,224,512]{2,1,0:T(8,128)(2,1)S(1)} %bitcast.17, bf16[8,224,512]{2,1,0:T(8,128)(2,1)S(1)} %bitcast.19), custom_call_target="tpu_custom_call" | custom-call | flops 2818572288 | bytes 9437184 | tf_op jit(solution)/shard_map/gain_term/pallas_call | solution.py:211
  192.9 4.0 %grad_down.1 = bf16[8,224,512]{2,1,0:T(8,128)(2,1)} custom-call(f32[8,8,128]{2,1,0:T(8,128)S(1)} %all-to-all-done.3.down_sq, bf16[224,512]{1,0:T(8,128)(2,1)S(1)} %copy-done.18, bf16[8,512,512]{2,1,0:T(8,128)(2,1)S(1)} %copy-done.2), custom_call_target="tpu_custom_call" | custom-call | flops 939524096 | bytes 6291456 | tf_op jit(solution)/shard_map/grad_down/pallas_call | solution.py:266
  196.9 14.6 %all_to_all.40.part = f32[8,32,128]{2,1,0:T(8,128)} all-to-all(f32[8,32,128]{2,1,0:T(8,128)S(1)} %gain_term.1), channel_id=1, replica_groups=mesh['x'=4,'core'=2,'z'=8,'y'=8] {'y'}, dimensions={0} | all-to-all | bytes 262144 | tf_op jit(solution)/shard_map/all_to_all | solution.py:284
  213.1 14.6 %all_to_all.41.part = f32[8,32,128]{2,1,0:T(8,128)} all-to-all(f32[8,32,128]{2,1,0:T(8,128)} %add_parts.3), channel_id=1, replica_groups=mesh['x'=4,'core'=2,'z'=8,'y'=8] {'z'}, dimensions={0} | all-to-all | bytes 262144 | tf_op jit(solution)/shard_map/all_to_all | solution.py:284
  229.3 10.8 %all_to_all.42.part = f32[8,8,128]{2,1,0:T(8,128)} all-to-all(f32[8,8,128]{2,1,0:T(8,128)} %get-tuple-element.30), channel_id=1, replica_groups=mesh['x'=4,'core'=2,'z'=8,'y'=8] {'y'}, dimensions={0} | all-to-all | bytes 65536 | tf_op jit(solution)/shard_map/all_to_all | solution.py:284
  241.5 10.9 %all-to-all-start.7 = ((f32[8,8,128]{2,1,0:T(8,128)}), f32[8,8,128]{2,1,0:T(8,128)S(1)}, u32[]{:S(2)}, u32[]{:S(2)}) async-start(f32[8,8,128]{2,1,0:T(8,128)} %gain_scale.1), calls=%async_computation.8 | async-start | bytes 65536 | tf_op jit(solution)/shard_map/all_to_all | solution.py:284
  252.4 4.7 %all-to-all-done.7 = f32[8,8,128]{2,1,0:T(8,128)S(1)} async-done(((f32[8,8,128]{2,1,0:T(8,128)}), f32[8,8,128]{2,1,0:T(8,128)S(1)}, u32[]{:S(2)}, u32[]{:S(2)}) %all-to-all-start.7) | async-done | bytes 32800 | tf_op jit(solution)/shard_map/all_to_all | solution.py:284
  (97 shorter events, 56.7 us)
Async XLA Ops:
  7.2 137.7 %all-gather.6.cloned.1.call-start = ((), (), s32[]{:S(2)}) async-start(), calls=%async_computation.10 | async-start | bytes 2064384 | tf_op jit(solution)/shard_map/all_gather | solution.py:301
  9.6 28.8 %all-to-all-start = ((bf16[8,64,512]{2,1,0:T(8,128)(2,1)}), bf16[8,64,512]{2,1,0:T(8,128)(2,1)S(1)}, u32[]{:S(2)}, u32[]{:S(2)}) async-start(bf16[8,64,512]{2,1,0:T(8,128)(2,1)} %broadcast_in_dim.4), calls=%async_computation | async-start | bytes 1048576 | tf_op jit(solution)/shard_map/all_to_all | solution.py:278
  20.5 124.5 %all-gather.8.cloned.1.call-start = ((), (), s32[]{:S(2)}) async-start(), calls=%async_computation.11 | async-start | bytes 2064384 | tf_op jit(solution)/shard_map/all_gather | solution.py:302
  21.2 105.3 %copy-start.25 = (f32[4096]{0:T(1024)S(1)}, f32[4096]{0:T(1024)}, u32[]{:S(2)}) copy-start(f32[4096]{0:T(1024)} %param.7) | copy-start | bytes 49156
  38.4 37.8 %collective-permute-start.7 = (bf16[8,64,512]{2,1,0:T(8,128)(2,1)S(1)}, bf16[8,64,512]{2,1,0:T(8,128)(2,1)S(1)}, u32[]{:S(2)}, u32[]{:S(2)}) collective-permute-start(bf16[8,64,512]{2,1,0:T(8,128)(2,1)S(1)} %all-to-all-done.refs_0_), channel_id=1, source_target_pairs={{0,1},{1,2},{2,3},{3,4},{4,5},{5,6},{6,7},{7,0},{8,9},{9,10},{10,1... | collective-permute-start | bytes 1572872 | tf_op jit(solution)/shard_map/ppermute | solution.py:291
  72.2 11.8 %collective-permute-start = (bf16[8,64,512]{2,1,0:T(8,128)(2,1)S(1)}, bf16[8,64,512]{2,1,0:T(8,128)(2,1)S(1)}, u32[]{:S(2)}, u32[]{:S(2)}) collective-permute-start(bf16[8,64,512]{2,1,0:T(8,128)(2,1)S(1)} %bitcast.13), channel_id=1, source_target_pairs={{0,8},{8,16},{16,24},{24,32},{32,40},{40,48},{48,56},{56,0},{1,9},... | collective-permute-start | bytes 1572872 | tf_op jit(solution)/shard_map/ppermute | solution.py:291
  74.1 16.4 %collective-permute-start.11 = (bf16[8,64,512]{2,1,0:T(8,128)(2,1)S(1)}, bf16[8,64,512]{2,1,0:T(8,128)(2,1)}, u32[]{:S(2)}, u32[]{:S(2)}) collective-permute-start(bf16[8,64,512]{2,1,0:T(8,128)(2,1)S(1)} %all-to-all-done.refs_0_), channel_id=1, source_target_pairs={{0,7},{1,0},{2,1},{3,2},{4,3},{5,4},{6,5},{7,6},{8,15},{9,8},{10,9... | collective-permute-start | bytes 1572872 | tf_op jit(solution)/shard_map/ppermute | solution.py:293
  76.3 17.6 %collective-permute-start.8 = (bf16[8,64,512]{2,1,0:T(8,128)(2,1)S(1)}, bf16[8,64,512]{2,1,0:T(8,128)(2,1)}, u32[]{:S(2)}, u32[]{:S(2)}) collective-permute-start(bf16[8,64,512]{2,1,0:T(8,128)(2,1)S(1)} %collective-permute-done.7.refs_1_), channel_id=1, source_target_pairs={{0,1},{1,2},{2,3},{3,4},{4,5},{5,6},{6,7},{7,0},{8,9},{9,10},{10,1... | collective-permute-start | bytes 1572872 | tf_op jit(solution)/shard_map/ppermute | solution.py:291
  79.4 16.4 %collective-permute-start.4 = (bf16[8,64,512]{2,1,0:T(8,128)(2,1)S(1)}, bf16[8,64,512]{2,1,0:T(8,128)(2,1)}, u32[]{:S(2)}, u32[]{:S(2)}) collective-permute-start(bf16[8,64,512]{2,1,0:T(8,128)(2,1)S(1)} %bitcast.14), channel_id=1, source_target_pairs={{0,56},{8,0},{16,8},{24,16},{32,24},{40,32},{48,40},{56,48},{1,57}... | collective-permute-start | bytes 1572872 | tf_op jit(solution)/shard_map/ppermute | solution.py:293
  84.0 16.4 %collective-permute-start.1 = (bf16[8,64,512]{2,1,0:T(8,128)(2,1)S(1)}, bf16[8,64,512]{2,1,0:T(8,128)(2,1)}, u32[]{:S(2)}, u32[]{:S(2)}) collective-permute-start(bf16[8,64,512]{2,1,0:T(8,128)(2,1)S(1)} %collective-permute-done.refs_1_), channel_id=1, source_target_pairs={{0,8},{8,16},{16,24},{24,32},{32,40},{40,48},{48,56},{56,0},{1,9},... | collective-permute-start | bytes 1572872 | tf_op jit(solution)/shard_map/ppermute | solution.py:291
  87.0 15.4 %all-to-all-start.2 = ((bf16[4,224,512]{2,1,0:T(8,128)(2,1)}), bf16[4,224,512]{2,1,0:T(8,128)(2,1)S(1)}, u32[]{:S(2)}, u32[]{:S(2)}) async-start(bf16[4,224,512]{2,1,0:T(8,128)(2,1)} %broadcast_in_dim.5), calls=%async_computation.2 | async-start | bytes 1835008 | tf_op jit(solution)/shard_map/all_to_all | solution.py:278
  90.5 22.4 %collective-permute-start.12 = (bf16[8,64,512]{2,1,0:T(8,128)(2,1)}, bf16[8,64,512]{2,1,0:T(8,128)(2,1)}, u32[]{:S(2)}, u32[]{:S(2)}) collective-permute-start(bf16[8,64,512]{2,1,0:T(8,128)(2,1)} %collective-permute-done.11.refs_7_), channel_id=1, source_target_pairs={{0,7},{1,0},{2,1},{3,2},{4,3},{5,4},{6,5},{7,6},{8,15},{9,8},{10,9... | collective-permute-start | bytes 1572872 | tf_op jit(solution)/shard_map/ppermute | solution.py:293
  93.9 23.8 %collective-permute-start.9 = (bf16[8,64,512]{2,1,0:T(8,128)(2,1)}, bf16[8,64,512]{2,1,0:T(8,128)(2,1)}, u32[]{:S(2)}, u32[]{:S(2)}) collective-permute-start(bf16[8,64,512]{2,1,0:T(8,128)(2,1)} %collective-permute-done.8.refs_2_), channel_id=1, source_target_pairs={{0,1},{1,2},{2,3},{3,4},{4,5},{5,6},{6,7},{7,0},{8,9},{9,10},{10,1... | collective-permute-start | bytes 1572872 | tf_op jit(solution)/shard_map/ppermute | solution.py:291
  95.8 23.8 %collective-permute-start.5 = (bf16[8,64,512]{2,1,0:T(8,128)(2,1)}, bf16[8,64,512]{2,1,0:T(8,128)(2,1)}, u32[]{:S(2)}, u32[]{:S(2)}) collective-permute-start(bf16[8,64,512]{2,1,0:T(8,128)(2,1)} %collective-permute-done.4.refs_7_), channel_id=1, source_target_pairs={{0,56},{8,0},{16,8},{24,16},{32,24},{40,32},{48,40},{56,48},{1,57}... | collective-permute-start | bytes 1572872 | tf_op jit(solution)/shard_map/ppermute | solution.py:293
  100.4 24.1 %collective-permute-start.2 = (bf16[8,64,512]{2,1,0:T(8,128)(2,1)}, bf16[8,64,512]{2,1,0:T(8,128)(2,1)}, u32[]{:S(2)}, u32[]{:S(2)}) collective-permute-start(bf16[8,64,512]{2,1,0:T(8,128)(2,1)} %collective-permute-done.1.refs_2_), channel_id=1, source_target_pairs={{0,8},{8,16},{16,24},{24,32},{32,40},{40,48},{48,56},{56,0},{1,9},... | collective-permute-start | bytes 1572872 | tf_op jit(solution)/shard_map/ppermute | solution.py:291
  102.4 62.4 %collective-permute-start.14 = (bf16[4,224,512]{2,1,0:T(8,128)(2,1)S(1)}, bf16[4,224,512]{2,1,0:T(8,128)(2,1)S(1)}, u32[]{:S(2)}, u32[]{:S(2)}) collective-permute-start(bf16[4,224,512]{2,1,0:T(8,128)(2,1)S(1)} %all-to-all-done.2.mine), channel_id=1, source_target_pairs={{0,64},{64,0},{1,65},{65,1},{2,66},{66,2},{3,67},{67,3},{4,68},{68... | collective-permute-start | bytes 2752520 | tf_op jit(solution)/shard_map/ppermute | solution.py:307
  112.9 16.5 %collective-permute-start.13 = (bf16[8,64,512]{2,1,0:T(8,128)(2,1)}, bf16[8,64,512]{2,1,0:T(8,128)(2,1)}, u32[]{:S(2)}, u32[]{:S(2)}) collective-permute-start(bf16[8,64,512]{2,1,0:T(8,128)(2,1)} %collective-permute-done.12.refs_6_), channel_id=1, source_target_pairs={{0,7},{1,0},{2,1},{3,2},{4,3},{5,4},{6,5},{7,6},{8,15},{9,8},{10,9... | collective-permute-start | bytes 1572872 | tf_op jit(solution)/shard_map/ppermute | solution.py:293
  117.7 16.6 %collective-permute-start.10 = (bf16[8,64,512]{2,1,0:T(8,128)(2,1)}, bf16[8,64,512]{2,1,0:T(8,128)(2,1)}, u32[]{:S(2)}, u32[]{:S(2)}) collective-permute-start(bf16[8,64,512]{2,1,0:T(8,128)(2,1)} %collective-permute-done.9.refs_3_), channel_id=1, source_target_pairs={{0,1},{1,2},{2,3},{3,4},{4,5},{5,6},{6,7},{7,0},{8,9},{9,10},{10,1... | collective-permute-start | bytes 1572872 | tf_op jit(solution)/shard_map/ppermute | solution.py:291
  119.7 25.2 %collective-permute-start.6 = (bf16[8,64,512]{2,1,0:T(8,128)(2,1)}, bf16[8,64,512]{2,1,0:T(8,128)(2,1)}, u32[]{:S(2)}, u32[]{:S(2)}) collective-permute-start(bf16[8,64,512]{2,1,0:T(8,128)(2,1)} %collective-permute-done.5.refs_6_), channel_id=1, source_target_pairs={{0,56},{8,0},{16,8},{24,16},{32,24},{40,32},{48,40},{56,48},{1,57}... | collective-permute-start | bytes 1572872 | tf_op jit(solution)/shard_map/ppermute | solution.py:293
  124.5 20.4 %collective-permute-start.3 = (bf16[8,64,512]{2,1,0:T(8,128)(2,1)}, bf16[8,64,512]{2,1,0:T(8,128)(2,1)}, u32[]{:S(2)}, u32[]{:S(2)}) collective-permute-start(bf16[8,64,512]{2,1,0:T(8,128)(2,1)} %collective-permute-done.2.refs_3_), channel_id=1, source_target_pairs={{0,8},{8,16},{16,24},{24,32},{32,40},{40,48},{48,56},{56,0},{1,9},... | collective-permute-start | bytes 1572872 | tf_op jit(solution)/shard_map/ppermute | solution.py:291
  160.1 13.5 %all-to-all-start.1 = ((f32[8,8,128]{2,1,0:T(8,128)}), f32[8,8,128]{2,1,0:T(8,128)S(1)}, u32[]{:S(2)}, u32[]{:S(2)}) async-start(f32[8,8,128]{2,1,0:T(8,128)} %get-tuple-element.18), calls=%async_computation.1 | async-start | bytes 65536 | tf_op jit(solution)/shard_map/all_to_all | solution.py:284
  175.7 15.0 %all-to-all-start.3 = ((f32[8,8,128]{2,1,0:T(8,128)}), f32[8,8,128]{2,1,0:T(8,128)S(1)}, u32[]{:S(2)}, u32[]{:S(2)}) async-start(f32[8,8,128]{2,1,0:T(8,128)} %add_parts.2), calls=%async_computation.3 | async-start | bytes 65536 | tf_op jit(solution)/shard_map/all_to_all | solution.py:284
  179.9 77.9 %reduce-scatter.2.cloned.1.call-start = ((), (), s32[]{:S(2)}) async-start(), calls=%async_computation.9 | async-start | bytes 2064384 | tf_op jit(solution)/shard_map/reduce_scatter | solution.py:321
  241.5 15.7 %all-to-all-start.7 = ((f32[8,8,128]{2,1,0:T(8,128)}), f32[8,8,128]{2,1,0:T(8,128)S(1)}, u32[]{:S(2)}, u32[]{:S(2)}) async-start(f32[8,8,128]{2,1,0:T(8,128)} %gain_scale.1), calls=%async_computation.8 | async-start | bytes 65536 | tf_op jit(solution)/shard_map/all_to_all | solution.py:284
  (25 other events, 219.3 us)
Sparse Core Ops, SparseCore 0:
  10.1 36.1 all-gather.5
  48.5 30.4 all-gather.7
  197.0 39.9 reduce-scatter.1

commit v4 on v3

v4 whole, which is shorter than its diff:
```python
import math

import jax
import jax.numpy as jnp
from jax import lax
from jax.experimental import pallas as pl
from jax.experimental.pallas import tpu as pltpu
from jax.sharding import Mesh
from jax.sharding import PartitionSpec as P

FEATURES = 4096
FF = 14336
SEQ = 64
SEQS = 64
NX, NC, NZ, NY = 4, 2, 8, 8
LOCAL = 8
TOK = LOCAL * SEQ
UNITS = FF // (NZ * NY)
SHARE = FEATURES // (NX * NC)
COLS = FEATURES // (NZ * NY)
F32 = jnp.float32
BF16 = jnp.bfloat16

SMEM = pl.BlockSpec(memory_space=pltpu.SMEM)
VMEM = pl.BlockSpec(memory_space=pltpu.VMEM)


def params(mib):
    return pltpu.CompilerParams(vmem_limit_bytes=mib * 1024 * 1024)


def cost(macs, nbytes):
    return pl.CostEstimate(flops=2 * macs, bytes_accessed=nbytes, transcendentals=0)


TN = (((0,), (0,)), ((), ()))
NT = (((1,), (1,)), ((), ()))
HALF = TOK // 2
ANY = pl.BlockSpec(memory_space=pl.ANY)


def whole(shape):
    return pl.BlockSpec(shape, lambda i: (0,) * len(shape))


def lead(shape):
    return pl.BlockSpec(shape, lambda i: (i,) + (0,) * (len(shape) - 1))


def cotangent_kernel(idx, *refs):
    pieces, (dy, gram, held, sems, out_sem) = refs[:NY], refs[NY:]
    y = idx[2]
    for j in range(NY):
        slot = lax.rem(y - j + NY, NY)
        pltpu.make_async_copy(pieces[j], held.at[:, slot], sems.at[j]).start()
    for j in range(NY):
        slot = lax.rem(y - j + NY, NY)
        pltpu.make_async_copy(pieces[j], held.at[:, slot], sems.at[j]).wait()
    keep = pltpu.make_async_copy(held, dy, out_sem)
    keep.start()
    for h in range(2):

        def step(z, acc):
            block = held[z, :, :, h * HALF : (h + 1) * HALF].reshape(SHARE, HALF)
            return acc + lax.dot_general(block, block, TN, preferred_element_type=F32)

        gram[h] = lax.fori_loop(0, NZ, step, jnp.zeros((HALF, HALF), F32))
    keep.wait()


def cotangent_call(idx, pieces):
    return pl.pallas_call(
        cotangent_kernel,
        out_shape=(
            jax.ShapeDtypeStruct((NZ, NY, COLS, TOK), BF16),
            jax.ShapeDtypeStruct((2, HALF, HALF), F32),
        ),
        in_specs=[SMEM] + [ANY] * NY,
        out_specs=(ANY, VMEM),
        scratch_shapes=[
            pltpu.VMEM((NZ, NY, COLS, TOK), BF16),
            pltpu.SemaphoreType.DMA((NY,)),
            pltpu.SemaphoreType.DMA,
        ],
        compiler_params=params(24),
        cost_estimate=cost(TOK * HALF * FEATURES, 9 << 20),
        name="cotangent_gram",
    )(idx, *pieces)


def back_kernel(idx, dy, mine, other, back):
    core = idx[1]

    @pl.when(pl.program_id(0) == 0)
    def _():
        back[...] = jnp.zeros_like(back)

    back[...] += jnp.dot(mine[0], dy[core].reshape(SHARE, TOK), preferred_element_type=F32)
    back[...] += jnp.dot(other[0], dy[1 - core].reshape(SHARE, TOK), preferred_element_type=F32)


def back_call(idx, dy, mine, other):
    return pl.pallas_call(
        back_kernel,
        grid=(NX,),
        out_shape=jax.ShapeDtypeStruct((UNITS, TOK), F32),
        in_specs=[SMEM, lead((2, NY, COLS, TOK)), lead((1, UNITS, SHARE)), lead((1, UNITS, SHARE))],
        out_specs=whole((UNITS, TOK)),
        compiler_params=params(24),
        cost_estimate=cost(UNITS * TOK * FEATURES, 7 << 20),
        name="back",
    )(idx, dy, mine, other)


def hidden_kernel(idx, *refs):
    pieces, (wg, wu, gain, dy_gram, back, xs, hidden, inverse, down_sq, grads) = refs[:NZ], refs[NZ : NZ + 10]
    x, g_held, u_held, acc, sems, out_sems = refs[NZ + 10 :]
    z = idx[0]

    def copies(j, source):
        d = lax.rem(z - j + NZ, NZ)
        return (
            pltpu.make_async_copy(source, x.at[d], sems.at[0, j]),
            pltpu.make_async_copy(wg.at[d], g_held.at[d], sems.at[1, j]),
            pltpu.make_async_copy(wu.at[d], u_held.at[d], sems.at[2, j]),
        )

    for j in range(NZ):
        for copy in copies(j, pieces[j]):
            copy.start()
    acc[...] = jnp.zeros_like(acc)

    def keep(j):
        d = lax.rem(z - j + NZ, NZ)
        return pltpu.make_async_copy(x.at[d], xs.at[d], out_sems.at[j])

    def share(j, total):
        d = lax.rem(z - j + NZ, NZ)
        for copy in copies(j, pieces[0]):
            copy.wait()
        keep(j).start()
        row = gain[pl.ds(d, 1), :]
        block = x[d].reshape(SHARE, TOK)
        for k, ref in enumerate((g_held, u_held)):
            scaled = (ref[d].astype(F32) * row).astype(BF16)
            acc[k] += jnp.dot(scaled, block, preferred_element_type=F32)
        for i in range(NY):
            wide = x[d, i].astype(F32)
            total += jnp.sum((wide * wide).reshape(COLS // 8, 8, TOK), axis=0)
        return total

    total = lax.fori_loop(0, NZ, share, jnp.zeros((8, TOK), F32))
    mean = jnp.sum(total, axis=0, keepdims=True) * (1.0 / FEATURES)
    inverse[...] = lax.rsqrt(mean + 1e-05)

    def rows(i, carry):
        r = pl.ds(pl.multiple_of(i * 32, 32), 32)
        inv = inverse[...]
        g = acc[0, r, :] * inv
        u = acc[1, r, :] * inv
        b = back[r, :]
        sigma = jax.nn.sigmoid(g)
        swish = g * sigma
        hidden[r, :] = (swish * u).astype(BF16)
        grads[0, r, :] = (b * u * sigma * (1.0 + g * (1.0 - sigma))).astype(BF16)
        grads[1, r, :] = (b * swish).astype(BF16)
        return carry

    lax.fori_loop(0, UNITS // 32, rows, 0)
    for h in range(2):
        own = hidden[:, h * HALF : (h + 1) * HALF]
        pairs = lax.dot_general(own, own, TN, preferred_element_type=F32) * dy_gram[h]
        for s in range(HALF // SEQ):
            part = pairs[s * SEQ : (s + 1) * SEQ, s * SEQ : (s + 1) * SEQ]
            value = jnp.sum(jnp.sum(part, axis=0, keepdims=True), axis=1, keepdims=True)
            i = h * (HALF // SEQ) + s
            down_sq[:, i : i + 1, :] = jnp.broadcast_to(value.reshape(1, 1, 1), (NY, 1, 128))

    def drain(j, carry):
        keep(j).wait()
        return carry

    lax.fori_loop(0, NZ, drain, 0)


def hidden_call(idx, pieces, wg, wu, gain, dy_gram, back):
    return pl.pallas_call(
        hidden_kernel,
        out_shape=(
            jax.ShapeDtypeStruct((NZ, NY, COLS, TOK), BF16),
            jax.ShapeDtypeStruct((UNITS, TOK), BF16),
            jax.ShapeDtypeStruct((1, TOK), F32),
            jax.ShapeDtypeStruct((NY, LOCAL, 128), F32),
            jax.ShapeDtypeStruct((2, UNITS, TOK), BF16),
        ),
        in_specs=[SMEM] + [ANY] * (NZ + 2) + [VMEM] * 3,
        out_specs=(ANY,) + (VMEM,) * 4,
        scratch_shapes=[
            pltpu.VMEM((NZ, NY, COLS, TOK), BF16),
            pltpu.VMEM((NX * NC, UNITS, SHARE), BF16),
            pltpu.VMEM((NX * NC, UNITS, SHARE), BF16),
            pltpu.VMEM((2, UNITS, TOK), F32),
            pltpu.SemaphoreType.DMA((3, NZ)),
            pltpu.SemaphoreType.DMA((NZ,)),
        ],
        compiler_params=params(40),
        cost_estimate=cost(2 * UNITS * TOK * FEATURES, 14 << 20),
        name="hidden",
    )(idx, *pieces, wg, wu, gain, dy_gram, back)


def gain_kernel(grads, inverse, xs, wg, wu, out):
    token = lax.broadcasted_iota(jnp.int32, (TOK, 128), 0)
    column = lax.broadcasted_iota(jnp.int32, (TOK, 128), 1)
    select = jnp.where(token // SEQ == column, 1.0, 0.0).astype(BF16)
    parts, wide = 2, SHARE // 2
    for d in range(2):
        for h in range(parts):
            f = slice(h * wide, (h + 1) * wide)
            normed = lax.dot_general(wg[d, :, f], grads[0], TN, preferred_element_type=F32)
            normed += lax.dot_general(wu[d, :, f], grads[1], TN, preferred_element_type=F32)
            group = wide // COLS
            block = xs[d, h * group : (h + 1) * group].reshape(wide, TOK)
            product = block.astype(F32) * inverse[...] * normed
            high = product.astype(BF16)
            low = (product - high.astype(F32)).astype(BF16)
            total = jnp.dot(high, select, preferred_element_type=F32)
            total += jnp.dot(low, select, preferred_element_type=F32)
            flat = total.T[:LOCAL]
            for k in range(wide // 128):
                tile = h * (wide // 128) + k
                out[d, tile * LOCAL : (tile + 1) * LOCAL, :] = flat[:, k * 128 : (k + 1) * 128]


def gain_call(grads, inverse, xs, wg, wu):
    return pl.pallas_call(
        gain_kernel,
        grid=(NZ // 2,),
        out_shape=jax.ShapeDtypeStruct((NZ, SHARE // 128 * LOCAL, 128), F32),
        in_specs=[
            whole((2, UNITS, TOK)),
            whole((1, TOK)),
            lead((2, NY, COLS, TOK)),
            lead((2, UNITS, SHARE)),
            lead((2, UNITS, SHARE)),
        ],
        out_specs=lead((2, SHARE // 128 * LOCAL, 128)),
        compiler_params=params(32),
        cost_estimate=cost(3 * UNITS * TOK * FEATURES, 9 << 20),
        name="gain_term",
    )(grads, inverse, xs, wg, wu)


def join_kernel(part, gain_part, out):
    total = jnp.sum(part[...], axis=0, keepdims=True)
    out[:, :LOCAL, :] = jnp.broadcast_to(total, (NZ, LOCAL, 128))
    out[:, LOCAL:, :] = gain_part[...]


def join_call(part, gain_part):
    rows = LOCAL + gain_part.shape[1]
    return pl.pallas_call(join_kernel, out_shape=jax.ShapeDtypeStruct((NZ, rows, 128), F32), name="join_parts")(
        part, gain_part
    )


def add_kernel(part, out):
    total = jnp.sum(part[:, LOCAL:, :], axis=0, keepdims=True)
    out[...] = jnp.broadcast_to(total, out.shape)


def add_call(part):
    shape = (NY, part.shape[1] - LOCAL, 128)
    return pl.pallas_call(add_kernel, out_shape=jax.ShapeDtypeStruct(shape, F32), name="add_parts")(part)


def gain_sq_kernel(part, total, square):
    gain = jnp.sum(part[...], axis=0)
    total[...] = gain
    rows = jnp.sum((gain * gain).reshape(SHARE // 128, LOCAL, 128), axis=0)
    value = jnp.sum(rows, axis=1, keepdims=True)
    square[...] = jnp.broadcast_to(value[None], square.shape)


def gain_scale_kernel(idx, part, total, out):
    square = jnp.sum(part[...], axis=0)
    bound = 0.5 * math.sqrt(SEQ * FEATURES)
    scale = jnp.minimum(1.0, bound / (jnp.sqrt(square) + 1e-06)) / SEQS
    rows = total[pl.ds(pl.multiple_of(idx[2] // 2 * LOCAL, LOCAL), LOCAL), :]
    value = jnp.sum(scale * rows, axis=0, keepdims=True)
    out[...] = jnp.broadcast_to(value[None], out.shape)


def grad_kernel(part, hidden, dy, out, scaled):
    @pl.when(pl.program_id(0) == 0)
    def _():
        bound = 0.6 * math.sqrt(SEQ * FF * FEATURES)
        total = jnp.sum(part[:, :LOCAL, :], axis=0)
        scale = jnp.minimum(1.0, bound / (jnp.sqrt(total) + 1e-06)) / SEQS
        first = lax.broadcasted_iota(jnp.int32, (1, 128), 1) < SEQ
        row = jnp.concatenate(
            [jnp.where(first, scale[2 * k : 2 * k + 1], scale[2 * k + 1 : 2 * k + 2]) for k in range(LOCAL // 2)],
            axis=1,
        )
        scaled[...] = (hidden[...].astype(F32) * row).astype(BF16)

    for d in range(2):
        block = dy[d].reshape(SHARE, TOK)
        out[d] = lax.dot_general(scaled[...], block, NT, preferred_element_type=F32).astype(BF16)


def grad_call(part, hidden, dy):
    return pl.pallas_call(
        grad_kernel,
        grid=(NZ // 2,),
        out_shape=jax.ShapeDtypeStruct((NX * NC, UNITS, SHARE), BF16),
        in_specs=[whole(part.shape), whole((UNITS, TOK)), lead((2, NY, COLS, TOK))],
        out_specs=lead((2, UNITS, SHARE)),
        scratch_shapes=[pltpu.VMEM((UNITS, TOK), BF16)],
        compiler_params=params(24),
        cost_estimate=cost(UNITS * TOK * FEATURES, 6 << 20),
        name="grad_down",
    )(part, hidden, dy)


def spread(block, axis, count):
    return lax.all_to_all(
        jnp.broadcast_to(block[None], (count,) + block.shape), axis, split_axis=0, concat_axis=0, tiled=True
    )


def exchange(blocks, axis):
    return lax.all_to_all(blocks, axis, split_axis=0, concat_axis=0, tiled=True)


def ring(block, axis, size):
    shift = lambda k: [(i, (i + k) % size) for i in range(size)]
    up, down = [block], [block]
    for step in range(size // 2):
        up.append(lax.ppermute(up[-1], axis, shift(1)))
        if step < size // 2 - 1:
            down.append(lax.ppermute(down[-1], axis, shift(-1)))
    return up + down[:0:-1]


def body(tokens, gain, cotangent, gate_weight, up_weight, down_weight):
    idx = jnp.stack([lax.axis_index("z"), lax.axis_index("core"), lax.axis_index("y")]).astype(jnp.int32)
    dp = ("x", "core")
    wg = lax.all_gather(gate_weight.T, dp, axis=0)
    wu = lax.all_gather(up_weight.T, dp, axis=0)
    dy_part = spread(cotangent.T, "z", NZ)
    tokens, dy_part = lax.optimization_barrier((tokens, dy_part))
    x_part = spread(tokens.T, "y", NY)
    down_weight, x_part = lax.optimization_barrier((down_weight, x_part))
    dmine = spread(down_weight, "x", NX)
    dy_pieces = ring(dy_part, "y", NY)
    pieces = ring(x_part, "z", NZ)
    dother = lax.ppermute(dmine, "core", [(0, 1), (1, 0)])

    dy, dy_gram = cotangent_call(idx, dy_pieces)
    back = back_call(idx, dy, dmine, dother)
    xs, hidden, inverse, sq_part, grads = hidden_call(
        idx, pieces, wg, wu, gain.reshape(NX * NC, SHARE), dy_gram, back
    )
    part = exchange(sq_part, "y")
    grads, sq_part = lax.optimization_barrier((grads, sq_part))
    gain_part = gain_call(grads, inverse, xs, wg, wu)
    part = exchange(join_call(part, gain_part), "z")
    terms = grad_call(part, hidden, dy)
    part, terms = lax.optimization_barrier((part, terms))
    grad_down = lax.psum_scatter(terms, dp, scatter_dimension=0).astype(F32)

    gain_z, gain_sq = pl.pallas_call(
        gain_sq_kernel,
        out_shape=(
            jax.ShapeDtypeStruct((SHARE // 128 * LOCAL, 128), F32),
            jax.ShapeDtypeStruct((NZ, LOCAL, 128), F32),
        ),
        name="gain_sq",
    )(exchange(add_call(part), "y"))
    gain_local = pl.pallas_call(
        gain_scale_kernel,
        out_shape=jax.ShapeDtypeStruct((NX * NC, 8, 128), F32),
        in_specs=[SMEM, VMEM, VMEM],
        name="gain_scale",
    )(idx, exchange(gain_sq, "z"), gain_z)
    gain_all = jnp.sum(exchange(gain_local, dp)[:, 0], axis=0)
    grad_gain = jnp.where(idx[2] % 2 == 0, gain_all[:COLS], gain_all[COLS:])
    return (grad_down, grad_gain)


def solution(mesh):
    split = Mesh(mesh.devices.reshape(NX, NC, NZ, NY), ("x", "core", "z", "y"))
    dp, tensor = ("x", "core"), ("z", "y")
    in_specs = (P(dp, tensor), P(), P(dp, tensor), P(dp, tensor), P(dp, tensor), P(tensor, dp))
    out_specs = (P(tensor, dp), P(tensor))
    return jax.shard_map(body, mesh=split, in_specs=in_specs, out_specs=out_specs, check_vma=False)
```

time: 268 us -> 250 us (0.933)
  blocking collectives: 70.5 us -> 37.6 us
  waiting for transfers between devices: 31.2 us -> 51.2 us
  starting transfers between devices: 87 us -> 80.5 us
  Pallas kernels: 33 us -> 36.7 us
    all_gather x1 -> x0, blocking collectives: 30.5 us -> none  [body(): x_part = lax.all_gather(tokens.T, 'y', axis=0)]
    all_to_all x2 -> x3, waiting for transfers between devices: 17.2 us -> 31.5 us  [spread(): lax.all_to_all(jnp.broadcast_to(block[None], (count,) + block.shape), axi...]
    all_to_all x2 -> x3, starting transfers between devices: 14.4 us -> 21.8 us  [spread(): lax.all_to_all(jnp.broadcast_to(block[None], (count,) + block.shape), axi...]
    ppermute x1, starting transfers between devices: 10.5 us -> 4.99 us  [body(): dother = lax.ppermute(dmine, 'core', [(0, 1), (1, 0)])]
    all_to_all x3 -> x2, starting transfers between devices: 19.8 us -> 14.7 us  [exchange(): return lax.all_to_all(blocks, axis, split_axis=0, concat_axis=0, tiled=True)]
    ppermute x6, starting transfers between devices: 24.4 us -> 20.2 us  [ring(): down.append(lax.ppermute(down[-1], axis, shift(-1)))]
    ppermute x8, waiting for transfers between devices: 5.04 us -> 9.2 us  [ring(): up.append(lax.ppermute(up[-1], axis, shift(1)))]
    pallas_call x8, Pallas kernels: 31.6 us -> 35.3 us  [the longest x1 10.7 us: hidden_call(): pl.pallas_call(hidden_kernel, out_shape=(jax.ShapeDtypeStruct((NZ, NY, CO...]
  transfers between devices with their start and end apart: 23 -> 23, of which waited for: 4 -> 7; matrix products, arithmetic and copies ran while one was open for 1% -> 2% of each run, Pallas kernels for 10% -> 9%
where the time goes in v4:
time: 250 us; the launch traced here: 249 us
  starting transfers between devices  80.5 us (32%)
  waiting for transfers between devices  51.2 us (20%)
  blocking collectives  37.6 us (15%)
  Pallas kernels  36.7 us (15%)
  local copies, waits for them, and re-layouts  26.1 us (10%)
  between operations  14.1 us (6%)
    all_to_all x3, blocking collectives, exchange(): return lax.all_to_all(blocks, axis, split_axis=0, concat_axis=0, tiled=True)  37.6 us
    all_to_all x3, waiting for transfers between devices, spread(): lax.all_to_all(jnp.broadcast_to(block[None], (count,) + block.shape), axi...  31.5 us
    unnamed x50, local copies, waits for them, and re-layouts  22.5 us
    all_to_all x3, starting transfers between devices, spread(): lax.all_to_all(jnp.broadcast_to(block[None], (count,) + block.shape), axi...  21.8 us
    ppermute x6, starting transfers between devices, ring(): down.append(lax.ppermute(down[-1], axis, shift(-1)))  20.2 us
    ppermute x8, starting transfers between devices, ring(): up.append(lax.ppermute(up[-1], axis, shift(1)))  18.7 us
    all_to_all x2, starting transfers between devices, exchange(): return lax.all_to_all(blocks, axis, split_axis=0, concat_axis=0, tiled=True)  14.7 us
    pallas_call x1, Pallas kernels, hidden_call(): pl.pallas_call(hidden_kernel, out_shape=(jax.ShapeDtypeStruct((NZ, NY, CO...  10.7 us
  transfers between devices with their start and end apart: 23, of which 7 were waited for; matrix products, arithmetic and copies ran while one was open for 2% of the time, Pallas kernels for 9%

profile of v4, /device:TPU:1, one launch (start us, length us, event | category | flops | bytes accessed | tf_op | source)
XLA Modules:
  0.0 248.6 jit_solution(18144345838988843460)
XLA Ops:
  9.6 10.9 %all-to-all-start = ((bf16[8,64,512]{2,1,0:T(8,128)(2,1)}), bf16[8,64,512]{2,1,0:T(8,128)(2,1)S(1)}, u32[]{:S(2)}, u32[]{:S(2)}) async-start(bf16[8,64,512]{2,1,0:T(8,128)(2,1)} %broadcast_in_dim.6), calls=%async_computation | async-start | bytes 1048576 | tf_op jit(solution)/shard_map/all_to_all | solution.py:327
  21.2 17.2 %all-to-all-done.refs_0_ = bf16[8,64,512]{2,1,0:T(8,128)(2,1)S(1)} async-done(((bf16[8,64,512]{2,1,0:T(8,128)(2,1)}), bf16[8,64,512]{2,1,0:T(8,128)(2,1)S(1)}, u32[]{:S(2)}, u32[]{:S(2)}) %all-to-all-start) | async-done | bytes 524320 | tf_op jit(solution)/shard_map/all_to_all | solution.py:327
  39.3 7.0 %all-to-all-start.1 = ((bf16[8,64,512]{2,1,0:T(8,128)(2,1)}), bf16[8,64,512]{2,1,0:T(8,128)(2,1)S(1)}, u32[]{:S(2)}, u32[]{:S(2)}) async-start(bf16[8,64,512]{2,1,0:T(8,128)(2,1)} %broadcast_in_dim.7), calls=%async_computation.1 | async-start | bytes 1048576 | tf_op jit(solution)/shard_map/all_to_all | solution.py:327
  46.2 3.4 %collective-permute-start.7 = (bf16[8,64,512]{2,1,0:T(8,128)(2,1)S(1)}, bf16[8,64,512]{2,1,0:T(8,128)(2,1)}, u32[]{:S(2)}, u32[]{:S(2)}) collective-permute-start(bf16[8,64,512]{2,1,0:T(8,128)(2,1)S(1)} %all-to-all-done.refs_0_), channel_id=1, source_target_pairs={{0,1},{1,2},{2,3},{3,4},{4,5},{5,6},{6,7},{7,0},{8,9},{9,10},{10,1... | collective-permute-start | bytes 1572872 | tf_op jit(solution)/shard_map/ppermute | solution.py:340
  49.6 14.3 %all-to-all-done.1.refs_0_ = bf16[8,64,512]{2,1,0:T(8,128)(2,1)S(1)} async-done(((bf16[8,64,512]{2,1,0:T(8,128)(2,1)}), bf16[8,64,512]{2,1,0:T(8,128)(2,1)S(1)}, u32[]{:S(2)}, u32[]{:S(2)}) %all-to-all-start.1) | async-done | bytes 524320 | tf_op jit(solution)/shard_map/all_to_all | solution.py:327
  67.7 4.2 %collective-permute-done.7.refs_1_ = bf16[8,64,512]{2,1,0:T(8,128)(2,1)} collective-permute-done((bf16[8,64,512]{2,1,0:T(8,128)(2,1)S(1)}, bf16[8,64,512]{2,1,0:T(8,128)(2,1)}, u32[]{:S(2)}, u32[]{:S(2)}) %collective-permute-start.7) | collective-permute-done | bytes 524320 | tf_op jit(solution)/shard_map/ppermute | solution.py:340
  74.9 4.0 %all-to-all-start.2 = ((bf16[4,224,512]{2,1,0:T(8,128)(2,1)}), bf16[4,224,512]{2,1,0:T(8,128)(2,1)S(1)}, u32[]{:S(2)}, u32[]{:S(2)}) async-start(bf16[4,224,512]{2,1,0:T(8,128)(2,1)} %broadcast_in_dim.8), calls=%async_computation.2 | async-start | bytes 1835008 | tf_op jit(solution)/shard_map/all_to_all | solution.py:327
  80.8 3.4 %collective-permute-start.1 = (bf16[8,64,512]{2,1,0:T(8,128)(2,1)S(1)}, bf16[8,64,512]{2,1,0:T(8,128)(2,1)}, u32[]{:S(2)}, u32[]{:S(2)}) collective-permute-start(bf16[8,64,512]{2,1,0:T(8,128)(2,1)S(1)} %collective-permute-done.refs_1_), channel_id=1, source_target_pairs={{0,8},{8,16},{16,24},{24,32},{32,40},{40,48},{48,56},{56,0},{1,9},... | collective-permute-start | bytes 1572872 | tf_op jit(solution)/shard_map/ppermute | solution.py:340
  85.0 4.6 %collective-permute-start.12 = (bf16[8,64,512]{2,1,0:T(8,128)(2,1)}, bf16[8,64,512]{2,1,0:T(8,128)(2,1)}, u32[]{:S(2)}, u32[]{:S(2)}) collective-permute-start(bf16[8,64,512]{2,1,0:T(8,128)(2,1)} %collective-permute-done.11.refs_7_), channel_id=1, source_target_pairs={{0,7},{1,0},{2,1},{3,2},{4,3},{5,4},{6,5},{7,6},{8,15},{9,8},{10,9... | collective-permute-start | bytes 1572872 | tf_op jit(solution)/shard_map/ppermute | solution.py:342
  97.9 5.0 %collective-permute-start.14 = (bf16[4,224,512]{2,1,0:T(8,128)(2,1)S(1)}, bf16[4,224,512]{2,1,0:T(8,128)(2,1)S(1)}, u32[]{:S(2)}, u32[]{:S(2)}) collective-permute-start(bf16[4,224,512]{2,1,0:T(8,128)(2,1)S(1)} %all-to-all-done.2.mine), channel_id=1, source_target_pairs={{0,64},{64,0},{1,65},{65,1},{2,66},{66,2},{3,67},{67,3},{4,68},{68... | collective-permute-start | bytes 2752520 | tf_op jit(solution)/shard_map/ppermute | solution.py:358
  102.9 4.6 %collective-permute-start.13 = (bf16[8,64,512]{2,1,0:T(8,128)(2,1)}, bf16[8,64,512]{2,1,0:T(8,128)(2,1)}, u32[]{:S(2)}, u32[]{:S(2)}) collective-permute-start(bf16[8,64,512]{2,1,0:T(8,128)(2,1)} %collective-permute-done.12.refs_6_), channel_id=1, source_target_pairs={{0,7},{1,0},{2,1},{3,2},{4,3},{5,4},{6,5},{7,6},{8,15},{9,8},{10,9... | collective-permute-start | bytes 1572872 | tf_op jit(solution)/shard_map/ppermute | solution.py:342
  109.4 4.3 %collective-permute-start.6 = (bf16[8,64,512]{2,1,0:T(8,128)(2,1)}, bf16[8,64,512]{2,1,0:T(8,128)(2,1)}, u32[]{:S(2)}, u32[]{:S(2)}) collective-permute-start(bf16[8,64,512]{2,1,0:T(8,128)(2,1)} %collective-permute-done.5.refs_6_), channel_id=1, source_target_pairs={{0,56},{8,0},{16,8},{24,16},{32,24},{40,32},{48,40},{56,48},{1,57}... | collective-permute-start | bytes 1572872 | tf_op jit(solution)/shard_map/ppermute | solution.py:342
  115.8 3.3 %collective-permute-done.13.refs_5_ = bf16[8,64,512]{2,1,0:T(8,128)(2,1)} collective-permute-done((bf16[8,64,512]{2,1,0:T(8,128)(2,1)}, bf16[8,64,512]{2,1,0:T(8,128)(2,1)}, u32[]{:S(2)}, u32[]{:S(2)}) %collective-permute-start.13) | collective-permute-done | bytes 524320 | tf_op jit(solution)/shard_map/ppermute | solution.py:342
  119.1 5.0 %collective-permute-done.10.refs_4_ = bf16[8,64,512]{2,1,0:T(8,128)(2,1)} collective-permute-done((bf16[8,64,512]{2,1,0:T(8,128)(2,1)}, bf16[8,64,512]{2,1,0:T(8,128)(2,1)}, u32[]{:S(2)}, u32[]{:S(2)}) %collective-permute-start.10) | collective-permute-done | bytes 524320 | tf_op jit(solution)/shard_map/ppermute | solution.py:340
  124.1 7.5 %cotangent_gram.1 = (bf16[8,8,64,512]{3,2,1,0:T(8,128)(2,1)S(1)}, f32[2,256,256]{2,1,0:T(8,128)S(1)}) custom-call(s32[3]{0:T(128)S(1)} %pad_add_fusion.idx, bf16[8,64,512]{2,1,0:T(8,128)(2,1)S(1)} %all-to-all-done.refs_0_, bf16[8,64,512]{2,1,0:T(8,128)(2,1)} %collective-permute-done.7.refs_1_, bf16[8,64,512]{2,1,0:T(8,128)(2,1)} %collective-permute-done.8.refs_2_, ...), custom_call_target="tpu_custom_call" | custom-call | flops 1073741824 | bytes 9437184 | tf_op jit(solution)/shard_map/cotangent_gram/pallas_call | solution.py:72
  144.7 10.7 %hidden.1 = (bf16[8,8,64,512]{3,2,1,0:T(8,128)(2,1)S(1)}, bf16[224,512]{1,0:T(8,128)(2,1)S(1)}, f32[1,512]{1,0:T(1,128)S(1)}, f32[8,8,128]{2,1,0:T(8,128)}, bf16[2,224,512]{2,1,0:T(8,128)(2,1)S(1)}) custom-call(s32[3]{0:T(128)S(1)} %pad_add_fusion.idx, bf16[8,64,512]{2,1,0:T(8,128)(2,1)S(1)} %all-to-all-done.1.refs_0_, bf16[8,64,512]{2,1,0:T(8,128)(2,1)S(1)} %copy-done.10, ...), custom_call_target="tpu_custom_call" | custom-call | flops 1879048192 | bytes 14680064 | tf_op jit(solution)/shard_map/hidden/pallas_call | solution.py:187
  158.2 4.6 %all-to-all-start.3 = ((f32[8,8,128]{2,1,0:T(8,128)}), f32[8,8,128]{2,1,0:T(8,128)S(1)}, u32[]{:S(2)}, u32[]{:S(2)}) async-start(f32[8,8,128]{2,1,0:T(8,128)} %get-tuple-element.24), calls=%async_computation.3 | async-start | bytes 65536 | tf_op jit(solution)/shard_map/all_to_all | solution.py:333
  167.5 6.9 %gain_term.1.gain_part = f32[8,32,128]{2,1,0:T(8,128)S(1)} custom-call(bf16[2,224,512]{2,1,0:T(8,128)(2,1)S(1)} %copy-done.20, f32[1,512]{1,0:T(1,128)S(1)} %get-tuple-element.27.inverse, bf16[8,8,64,512]{3,2,1,0:T(8,128)(2,1)S(1)} %copy-done.18, bf16[8,224,512]{2,1,0:T(8,128)(2,1)S(1)} %bitcast.13, bf16[8,224,512]{2,1,0:T(8,128)(2,1)S(1)} %bitcast.15), custom_call_target="tpu_custom_call" | custom-call | flops 2818572288 | bytes 9437184 | tf_op jit(solution)/shard_map/gain_term/pallas_call | solution.py:236
  177.3 12.1 %all_to_all.40.part = f32[8,40,128]{2,1,0:T(8,128)S(1)} all-to-all(f32[8,40,128]{2,1,0:T(8,128)} %join_parts.1), channel_id=1, replica_groups=mesh['x'=4,'core'=2,'z'=8,'y'=8] {'z'}, dimensions={0} | all-to-all | bytes 327680 | tf_op jit(solution)/shard_map/all_to_all | solution.py:333
  191.7 3.1 %grad_down.1 = bf16[8,224,512]{2,1,0:T(8,128)(2,1)} custom-call(f32[8,40,128]{2,1,0:T(8,128)S(1)} %all_to_all.40.part, bf16[224,512]{1,0:T(8,128)(2,1)S(1)} %get-tuple-element.29.hidden, bf16[8,8,64,512]{3,2,1,0:T(8,128)(2,1)S(1)} %copy-done.1), custom_call_target="tpu_custom_call" | custom-call | flops 939524096 | bytes 6291456 | tf_op jit(solution)/shard_map/grad_down/pallas_call | solution.py:313
  196.4 14.7 %all_to_all.41.part = f32[8,32,128]{2,1,0:T(8,128)} all-to-all(f32[8,32,128]{2,1,0:T(8,128)} %add_parts.1), channel_id=1, replica_groups=mesh['x'=4,'core'=2,'z'=8,'y'=8] {'y'}, dimensions={0} | all-to-all | bytes 262144 | tf_op jit(solution)/shard_map/all_to_all | solution.py:333
  212.7 10.8 %all_to_all.42.part = f32[8,8,128]{2,1,0:T(8,128)} all-to-all(f32[8,8,128]{2,1,0:T(8,128)} %get-tuple-element.32), channel_id=1, replica_groups=mesh['x'=4,'core'=2,'z'=8,'y'=8] {'z'}, dimensions={0} | all-to-all | bytes 65536 | tf_op jit(solution)/shard_map/all_to_all | solution.py:333
  224.9 10.1 %all-to-all-start.7 = ((f32[8,8,128]{2,1,0:T(8,128)}), f32[8,8,128]{2,1,0:T(8,128)S(1)}, u32[]{:S(2)}, u32[]{:S(2)}) async-start(f32[8,8,128]{2,1,0:T(8,128)} %gain_scale.1), calls=%async_computation.8 | async-start | bytes 65536 | tf_op jit(solution)/shard_map/all_to_all | solution.py:333
  235.0 4.7 %all-to-all-done.7 = f32[8,8,128]{2,1,0:T(8,128)S(1)} async-done(((f32[8,8,128]{2,1,0:T(8,128)}), f32[8,8,128]{2,1,0:T(8,128)S(1)}, u32[]{:S(2)}, u32[]{:S(2)}) %all-to-all-start.7) | async-done | bytes 32800 | tf_op jit(solution)/shard_map/all_to_all | solution.py:333
  (95 shorter events, 58.4 us)
Async XLA Ops:
  7.2 130.4 %all-gather.5.cloned.1.call-start = ((), (), s32[]{:S(2)}) async-start(), calls=%async_computation.10 | async-start | bytes 2064384 | tf_op jit(solution)/shard_map/all_gather | solution.py:349
  9.6 28.8 %all-to-all-start = ((bf16[8,64,512]{2,1,0:T(8,128)(2,1)}), bf16[8,64,512]{2,1,0:T(8,128)(2,1)S(1)}, u32[]{:S(2)}, u32[]{:S(2)}) async-start(bf16[8,64,512]{2,1,0:T(8,128)(2,1)} %broadcast_in_dim.6), calls=%async_computation | async-start | bytes 1048576 | tf_op jit(solution)/shard_map/all_to_all | solution.py:327
  20.5 117.1 %all-gather.7.cloned.1.call-start = ((), (), s32[]{:S(2)}) async-start(), calls=%async_computation.11 | async-start | bytes 2064384 | tf_op jit(solution)/shard_map/all_gather | solution.py:350
  39.3 76.5 %copy-start.24 = (f32[4096]{0:T(1024)S(1)}, f32[4096]{0:T(1024)}, u32[]{:S(2)}) copy-start(f32[4096]{0:T(1024)} %param.7) | copy-start | bytes 49156
  39.3 24.6 %all-to-all-start.1 = ((bf16[8,64,512]{2,1,0:T(8,128)(2,1)}), bf16[8,64,512]{2,1,0:T(8,128)(2,1)S(1)}, u32[]{:S(2)}, u32[]{:S(2)}) async-start(bf16[8,64,512]{2,1,0:T(8,128)(2,1)} %broadcast_in_dim.7), calls=%async_computation.1 | async-start | bytes 1048576 | tf_op jit(solution)/shard_map/all_to_all | solution.py:327
  46.2 25.7 %collective-permute-start.7 = (bf16[8,64,512]{2,1,0:T(8,128)(2,1)S(1)}, bf16[8,64,512]{2,1,0:T(8,128)(2,1)}, u32[]{:S(2)}, u32[]{:S(2)}) collective-permute-start(bf16[8,64,512]{2,1,0:T(8,128)(2,1)S(1)} %all-to-all-done.refs_0_), channel_id=1, source_target_pairs={{0,1},{1,2},{2,3},{3,4},{4,5},{5,6},{6,7},{7,0},{8,9},{9,10},{10,1... | collective-permute-start | bytes 1572872 | tf_op jit(solution)/shard_map/ppermute | solution.py:340
  63.9 16.9 %collective-permute-start = (bf16[8,64,512]{2,1,0:T(8,128)(2,1)S(1)}, bf16[8,64,512]{2,1,0:T(8,128)(2,1)S(1)}, u32[]{:S(2)}, u32[]{:S(2)}) collective-permute-start(bf16[8,64,512]{2,1,0:T(8,128)(2,1)S(1)} %all-to-all-done.1.refs_0_), channel_id=1, source_target_pairs={{0,8},{8,16},{16,24},{24,32},{32,40},{40,48},{48,56},{56,0},{1,9},... | collective-permute-start | bytes 1572872 | tf_op jit(solution)/shard_map/ppermute | solution.py:340
  65.8 19.2 %collective-permute-start.11 = (bf16[8,64,512]{2,1,0:T(8,128)(2,1)S(1)}, bf16[8,64,512]{2,1,0:T(8,128)(2,1)}, u32[]{:S(2)}, u32[]{:S(2)}) collective-permute-start(bf16[8,64,512]{2,1,0:T(8,128)(2,1)S(1)} %all-to-all-done.refs_0_), channel_id=1, source_target_pairs={{0,7},{1,0},{2,1},{3,2},{4,3},{5,4},{6,5},{7,6},{8,15},{9,8},{10,9... | collective-permute-start | bytes 1572872 | tf_op jit(solution)/shard_map/ppermute | solution.py:342
  71.9 17.7 %collective-permute-start.8 = (bf16[8,64,512]{2,1,0:T(8,128)(2,1)}, bf16[8,64,512]{2,1,0:T(8,128)(2,1)}, u32[]{:S(2)}, u32[]{:S(2)}) collective-permute-start(bf16[8,64,512]{2,1,0:T(8,128)(2,1)} %collective-permute-done.7.refs_1_), channel_id=1, source_target_pairs={{0,1},{1,2},{2,3},{3,4},{4,5},{5,6},{6,7},{7,0},{8,9},{9,10},{10,1... | collective-permute-start | bytes 1572872 | tf_op jit(solution)/shard_map/ppermute | solution.py:340
  74.9 23.0 %all-to-all-start.2 = ((bf16[4,224,512]{2,1,0:T(8,128)(2,1)}), bf16[4,224,512]{2,1,0:T(8,128)(2,1)S(1)}, u32[]{:S(2)}, u32[]{:S(2)}) async-start(bf16[4,224,512]{2,1,0:T(8,128)(2,1)} %broadcast_in_dim.8), calls=%async_computation.2 | async-start | bytes 1835008 | tf_op jit(solution)/shard_map/all_to_all | solution.py:327
  78.9 13.7 %collective-permute-start.4 = (bf16[8,64,512]{2,1,0:T(8,128)(2,1)S(1)}, bf16[8,64,512]{2,1,0:T(8,128)(2,1)S(1)}, u32[]{:S(2)}, u32[]{:S(2)}) collective-permute-start(bf16[8,64,512]{2,1,0:T(8,128)(2,1)S(1)} %all-to-all-done.1.refs_0_), channel_id=1, source_target_pairs={{0,56},{8,0},{16,8},{24,16},{32,24},{40,32},{48,40},{56,48},{1,57}... | collective-permute-start | bytes 1572872 | tf_op jit(solution)/shard_map/ppermute | solution.py:342
  80.8 14.7 %collective-permute-start.1 = (bf16[8,64,512]{2,1,0:T(8,128)(2,1)S(1)}, bf16[8,64,512]{2,1,0:T(8,128)(2,1)}, u32[]{:S(2)}, u32[]{:S(2)}) collective-permute-start(bf16[8,64,512]{2,1,0:T(8,128)(2,1)S(1)} %collective-permute-done.refs_1_), channel_id=1, source_target_pairs={{0,8},{8,16},{16,24},{24,32},{32,40},{40,48},{48,56},{56,0},{1,9},... | collective-permute-start | bytes 1572872 | tf_op jit(solution)/shard_map/ppermute | solution.py:340
  85.0 17.9 %collective-permute-start.12 = (bf16[8,64,512]{2,1,0:T(8,128)(2,1)}, bf16[8,64,512]{2,1,0:T(8,128)(2,1)}, u32[]{:S(2)}, u32[]{:S(2)}) collective-permute-start(bf16[8,64,512]{2,1,0:T(8,128)(2,1)} %collective-permute-done.11.refs_7_), channel_id=1, source_target_pairs={{0,7},{1,0},{2,1},{3,2},{4,3},{5,4},{6,5},{7,6},{8,15},{9,8},{10,9... | collective-permute-start | bytes 1572872 | tf_op jit(solution)/shard_map/ppermute | solution.py:342
  89.6 17.9 %collective-permute-start.9 = (bf16[8,64,512]{2,1,0:T(8,128)(2,1)}, bf16[8,64,512]{2,1,0:T(8,128)(2,1)}, u32[]{:S(2)}, u32[]{:S(2)}) collective-permute-start(bf16[8,64,512]{2,1,0:T(8,128)(2,1)} %collective-permute-done.8.refs_2_), channel_id=1, source_target_pairs={{0,1},{1,2},{2,3},{3,4},{4,5},{5,6},{6,7},{7,0},{8,9},{9,10},{10,1... | collective-permute-start | bytes 1572872 | tf_op jit(solution)/shard_map/ppermute | solution.py:340
  92.6 16.8 %collective-permute-start.5 = (bf16[8,64,512]{2,1,0:T(8,128)(2,1)S(1)}, bf16[8,64,512]{2,1,0:T(8,128)(2,1)}, u32[]{:S(2)}, u32[]{:S(2)}) collective-permute-start(bf16[8,64,512]{2,1,0:T(8,128)(2,1)S(1)} %collective-permute-done.4.refs_7_), channel_id=1, source_target_pairs={{0,56},{8,0},{16,8},{24,16},{32,24},{40,32},{48,40},{56,48},{1,57}... | collective-permute-start | bytes 1572872 | tf_op jit(solution)/shard_map/ppermute | solution.py:342
  95.5 18.3 %collective-permute-start.2 = (bf16[8,64,512]{2,1,0:T(8,128)(2,1)}, bf16[8,64,512]{2,1,0:T(8,128)(2,1)}, u32[]{:S(2)}, u32[]{:S(2)}) collective-permute-start(bf16[8,64,512]{2,1,0:T(8,128)(2,1)} %collective-permute-done.1.refs_2_), channel_id=1, source_target_pairs={{0,8},{8,16},{16,24},{24,32},{32,40},{40,48},{48,56},{56,0},{1,9},... | collective-permute-start | bytes 1572872 | tf_op jit(solution)/shard_map/ppermute | solution.py:340
  97.9 34.6 %collective-permute-start.14 = (bf16[4,224,512]{2,1,0:T(8,128)(2,1)S(1)}, bf16[4,224,512]{2,1,0:T(8,128)(2,1)S(1)}, u32[]{:S(2)}, u32[]{:S(2)}) collective-permute-start(bf16[4,224,512]{2,1,0:T(8,128)(2,1)S(1)} %all-to-all-done.2.mine), channel_id=1, source_target_pairs={{0,64},{64,0},{1,65},{65,1},{2,66},{66,2},{3,67},{67,3},{4,68},{68... | collective-permute-start | bytes 2752520 | tf_op jit(solution)/shard_map/ppermute | solution.py:358
  102.9 16.2 %collective-permute-start.13 = (bf16[8,64,512]{2,1,0:T(8,128)(2,1)}, bf16[8,64,512]{2,1,0:T(8,128)(2,1)}, u32[]{:S(2)}, u32[]{:S(2)}) collective-permute-start(bf16[8,64,512]{2,1,0:T(8,128)(2,1)} %collective-permute-done.12.refs_6_), channel_id=1, source_target_pairs={{0,7},{1,0},{2,1},{3,2},{4,3},{5,4},{6,5},{7,6},{8,15},{9,8},{10,9... | collective-permute-start | bytes 1572872 | tf_op jit(solution)/shard_map/ppermute | solution.py:342
  107.5 16.6 %collective-permute-start.10 = (bf16[8,64,512]{2,1,0:T(8,128)(2,1)}, bf16[8,64,512]{2,1,0:T(8,128)(2,1)}, u32[]{:S(2)}, u32[]{:S(2)}) collective-permute-start(bf16[8,64,512]{2,1,0:T(8,128)(2,1)} %collective-permute-done.9.refs_3_), channel_id=1, source_target_pairs={{0,1},{1,2},{2,3},{3,4},{4,5},{5,6},{6,7},{7,0},{8,9},{9,10},{10,1... | collective-permute-start | bytes 1572872 | tf_op jit(solution)/shard_map/ppermute | solution.py:340
  109.4 28.1 %collective-permute-start.6 = (bf16[8,64,512]{2,1,0:T(8,128)(2,1)}, bf16[8,64,512]{2,1,0:T(8,128)(2,1)}, u32[]{:S(2)}, u32[]{:S(2)}) collective-permute-start(bf16[8,64,512]{2,1,0:T(8,128)(2,1)} %collective-permute-done.5.refs_6_), channel_id=1, source_target_pairs={{0,56},{8,0},{16,8},{24,16},{32,24},{40,32},{48,40},{56,48},{1,57}... | collective-permute-start | bytes 1572872 | tf_op jit(solution)/shard_map/ppermute | solution.py:342
  113.8 23.7 %collective-permute-start.3 = (bf16[8,64,512]{2,1,0:T(8,128)(2,1)}, bf16[8,64,512]{2,1,0:T(8,128)(2,1)}, u32[]{:S(2)}, u32[]{:S(2)}) collective-permute-start(bf16[8,64,512]{2,1,0:T(8,128)(2,1)} %collective-permute-done.2.refs_3_), channel_id=1, source_target_pairs={{0,8},{8,16},{16,24},{24,32},{32,40},{40,48},{48,56},{56,0},{1,9},... | collective-permute-start | bytes 1572872 | tf_op jit(solution)/shard_map/ppermute | solution.py:340
  158.2 16.9 %all-to-all-start.3 = ((f32[8,8,128]{2,1,0:T(8,128)}), f32[8,8,128]{2,1,0:T(8,128)S(1)}, u32[]{:S(2)}, u32[]{:S(2)}) async-start(f32[8,8,128]{2,1,0:T(8,128)} %get-tuple-element.24), calls=%async_computation.3 | async-start | bytes 65536 | tf_op jit(solution)/shard_map/all_to_all | solution.py:333
  162.8 77.5 %reduce-scatter.2.cloned.1.call-start = ((), (), s32[]{:S(2)}) async-start(), calls=%async_computation.9 | async-start | bytes 2064384 | tf_op jit(solution)/shard_map/reduce_scatter | solution.py:371
  224.9 14.8 %all-to-all-start.7 = ((f32[8,8,128]{2,1,0:T(8,128)}), f32[8,8,128]{2,1,0:T(8,128)S(1)}, u32[]{:S(2)}, u32[]{:S(2)}) async-start(f32[8,8,128]{2,1,0:T(8,128)} %gain_scale.1), calls=%async_computation.8 | async-start | bytes 65536 | tf_op jit(solution)/shard_map/all_to_all | solution.py:333
  (24 other events, 204.7 us)
Sparse Core Ops, SparseCore 0:
  10.1 36.1 all-gather.4
  48.4 30.4 all-gather.6
  194.9 35.2 reduce-scatter.1

commit v5 on v4

--- a/solution.py
+++ b/solution.py
@@ -82,7 +82,7 @@
             pltpu.SemaphoreType.DMA((NY,)),
             pltpu.SemaphoreType.DMA,
         ],
-        compiler_params=params(24),
+        compiler_params=params(60),
         cost_estimate=cost(TOK * HALF * FEATURES, 9 << 20),
         name="cotangent_gram",
     )(idx, *pieces)
@@ -106,122 +106,98 @@
         out_shape=jax.ShapeDtypeStruct((UNITS, TOK), F32),
         in_specs=[SMEM, lead((2, NY, COLS, TOK)), lead((1, UNITS, SHARE)), lead((1, UNITS, SHARE))],
         out_specs=whole((UNITS, TOK)),
-        compiler_params=params(24),
+        compiler_params=params(60),
         cost_estimate=cost(UNITS * TOK * FEATURES, 7 << 20),
         name="back",
     )(idx, dy, mine, other)
 
 
-def hidden_kernel(idx, *refs):
-    pieces, (wg, wu, gain, dy_gram, back, xs, hidden, inverse, down_sq, grads) = refs[:NZ], refs[NZ : NZ + 10]
-    x, g_held, u_held, acc, sems, out_sems = refs[NZ + 10 :]
-    z = idx[0]
-
-    def copies(j, source):
-        d = lax.rem(z - j + NZ, NZ)
-        return (
-            pltpu.make_async_copy(source, x.at[d], sems.at[0, j]),
-            pltpu.make_async_copy(wg.at[d], g_held.at[d], sems.at[1, j]),
-            pltpu.make_async_copy(wu.at[d], u_held.at[d], sems.at[2, j]),
-        )
-
-    for j in range(NZ):
-        for copy in copies(j, pieces[j]):
-            copy.start()
-    acc[...] = jnp.zeros_like(acc)
-
-    def keep(j):
-        d = lax.rem(z - j + NZ, NZ)
-        return pltpu.make_async_copy(x.at[d], xs.at[d], out_sems.at[j])
-
-    def share(j, total):
-        d = lax.rem(z - j + NZ, NZ)
-        for copy in copies(j, pieces[0]):
-            copy.wait()
-        keep(j).start()
-        row = gain[pl.ds(d, 1), :]
-        block = x[d].reshape(SHARE, TOK)
-        for k, ref in enumerate((g_held, u_held)):
-            scaled = (ref[d].astype(F32) * row).astype(BF16)
+def hidden_kernel(idx, xs, mine, other, gain, dy_gram, back, hidden, inverse, down_sq, grads, acc, squares):
+    step, core = pl.program_id(0), idx[1]
+
+    @pl.when(step == 0)
+    def _():
+        acc[...] = jnp.zeros_like(acc)
+        squares[...] = jnp.zeros_like(squares)
+
+    for ref, d in ((mine, core), (other, 1 - core)):
+        row = gain[pl.ds(2 * step + d, 1), :]
+        block = xs[d]
+        for k in range(2):
+            scaled = (ref[0, k].astype(F32) * row).astype(BF16)
             acc[k] += jnp.dot(scaled, block, preferred_element_type=F32)
         for i in range(NY):
-            wide = x[d, i].astype(F32)
-            total += jnp.sum((wide * wide).reshape(COLS // 8, 8, TOK), axis=0)
-        return total
-
-    total = lax.fori_loop(0, NZ, share, jnp.zeros((8, TOK), F32))
-    mean = jnp.sum(total, axis=0, keepdims=True) * (1.0 / FEATURES)
-    inverse[...] = lax.rsqrt(mean + 1e-05)
-
-    def rows(i, carry):
-        r = pl.ds(pl.multiple_of(i * 32, 32), 32)
-        inv = inverse[...]
-        g = acc[0, r, :] * inv
-        u = acc[1, r, :] * inv
-        b = back[r, :]
-        sigma = jax.nn.sigmoid(g)
-        swish = g * sigma
-        hidden[r, :] = (swish * u).astype(BF16)
-        grads[0, r, :] = (b * u * sigma * (1.0 + g * (1.0 - sigma))).astype(BF16)
-        grads[1, r, :] = (b * swish).astype(BF16)
-        return carry
-
-    lax.fori_loop(0, UNITS // 32, rows, 0)
-    for h in range(2):
-        own = hidden[:, h * HALF : (h + 1) * HALF]
-        pairs = lax.dot_general(own, own, TN, preferred_element_type=F32) * dy_gram[h]
-        for s in range(HALF // SEQ):
-            part = pairs[s * SEQ : (s + 1) * SEQ, s * SEQ : (s + 1) * SEQ]
-            value = jnp.sum(jnp.sum(part, axis=0, keepdims=True), axis=1, keepdims=True)
-            i = h * (HALF // SEQ) + s
-            down_sq[:, i : i + 1, :] = jnp.broadcast_to(value.reshape(1, 1, 1), (NY, 1, 128))
-
-    def drain(j, carry):
-        keep(j).wait()
-        return carry
-
-    lax.fori_loop(0, NZ, drain, 0)
-
-
-def hidden_call(idx, pieces, wg, wu, gain, dy_gram, back):
+            wide = xs[d, i * COLS : (i + 1) * COLS, :].astype(F32)
+            squares[...] += jnp.sum((wide * wide).reshape(COLS // 8, 8, TOK), axis=0)
+
+    @pl.when(step == NX - 1)
+    def _():
+        mean = jnp.sum(squares[...], axis=0, keepdims=True) * (1.0 / FEATURES)
+        inverse[...] = lax.rsqrt(mean + 1e-05)
+
+        def rows(i, carry):
+            r = pl.ds(pl.multiple_of(i * 32, 32), 32)
+            inv = inverse[...]
+            g = acc[0, r, :] * inv
+            u = acc[1, r, :] * inv
+            b = back[r, :]
+            sigma = jax.nn.sigmoid(g)
+            swish = g * sigma
+            hidden[r, :] = (swish * u).astype(BF16)
+            grads[0, r, :] = (b * u * sigma * (1.0 + g * (1.0 - sigma))).astype(BF16)
+            grads[1, r, :] = (b * swish).astype(BF16)
+            return carry
+
+        lax.fori_loop(0, UNITS // 32, rows, 0)
+        for h in range(2):
+            own = hidden[:, h * HALF : (h + 1) * HALF]
+            pairs = lax.dot_general(own, own, TN, preferred_element_type=F32) * dy_gram[h]
+            for s in range(HALF // SEQ):
+                part = pairs[s * SEQ : (s + 1) * SEQ, s * SEQ : (s + 1) * SEQ]
+                value = jnp.sum(jnp.sum(part, axis=0, keepdims=True), axis=1, keepdims=True)
+                i = h * (HALF // SEQ) + s
+                down_sq[:, i : i + 1, :] = jnp.broadcast_to(value.reshape(1, 1, 1), (NY, 1, 128))
+
+
+def hidden_call(idx, xs, mine, other, gain, dy_gram, back):
     return pl.pallas_call(
         hidden_kernel,
+        grid=(NX,),
         out_shape=(
-            jax.ShapeDtypeStruct((NZ, NY, COLS, TOK), BF16),
             jax.ShapeDtypeStruct((UNITS, TOK), BF16),
             jax.ShapeDtypeStruct((1, TOK), F32),
             jax.ShapeDtypeStruct((NY, LOCAL, 128), F32),
             jax.ShapeDtypeStruct((2, UNITS, TOK), BF16),
         ),
-        in_specs=[SMEM] + [ANY] * (NZ + 2) + [VMEM] * 3,
-        out_specs=(ANY,) + (VMEM,) * 4,
-        scratch_shapes=[
-            pltpu.VMEM((NZ, NY, COLS, TOK), BF16),
-            pltpu.VMEM((NX * NC, UNITS, SHARE), BF16),
-            pltpu.VMEM((NX * NC, UNITS, SHARE), BF16),
-            pltpu.VMEM((2, UNITS, TOK), F32),
-            pltpu.SemaphoreType.DMA((3, NZ)),
-            pltpu.SemaphoreType.DMA((NZ,)),
+        in_specs=[
+            SMEM,
+            lead((2, SHARE, TOK)),
+            lead((1, 2, UNITS, SHARE)),
+            lead((1, 2, UNITS, SHARE)),
+            whole((NX * NC, SHARE)),
+            whole((2, HALF, HALF)),
+            whole((UNITS, TOK)),
         ],
-        compiler_params=params(40),
+        out_specs=(whole((UNITS, TOK)), whole((1, TOK)), whole((NY, LOCAL, 128)), whole((2, UNITS, TOK))),
+        scratch_shapes=[pltpu.VMEM((2, UNITS, TOK), F32), pltpu.VMEM((8, TOK), F32)],
+        compiler_params=params(60),
         cost_estimate=cost(2 * UNITS * TOK * FEATURES, 14 << 20),
         name="hidden",
-    )(idx, *pieces, wg, wu, gain, dy_gram, back)
-
-
-def gain_kernel(grads, inverse, xs, wg, wu, out):
+    )(idx, xs, mine, other, gain, dy_gram, back)
+
+
+def gain_kernel(idx, grads, inverse, xs, mine, other, out):
     token = lax.broadcasted_iota(jnp.int32, (TOK, 128), 0)
     column = lax.broadcasted_iota(jnp.int32, (TOK, 128), 1)
     select = jnp.where(token // SEQ == column, 1.0, 0.0).astype(BF16)
+    core = idx[1]
     parts, wide = 2, SHARE // 2
-    for d in range(2):
+    for ref, d in ((mine, core), (other, 1 - core)):
         for h in range(parts):
             f = slice(h * wide, (h + 1) * wide)
-            normed = lax.dot_general(wg[d, :, f], grads[0], TN, preferred_element_type=F32)
-            normed += lax.dot_general(wu[d, :, f], grads[1], TN, preferred_element_type=F32)
-            group = wide // COLS
-            block = xs[d, h * group : (h + 1) * group].reshape(wide, TOK)
-            product = block.astype(F32) * inverse[...] * normed
+            normed = lax.dot_general(ref[0, 0, :, f], grads[0], TN, preferred_element_type=F32)
+            normed += lax.dot_general(ref[0, 1, :, f], grads[1], TN, preferred_element_type=F32)
+            product = xs[d, f, :].astype(F32) * inverse[...] * normed
             high = product.astype(BF16)
             low = (product - high.astype(F32)).astype(BF16)
             total = jnp.dot(high, select, preferred_element_type=F32)
@@ -232,23 +208,24 @@
                 out[d, tile * LOCAL : (tile + 1) * LOCAL, :] = flat[:, k * 128 : (k + 1) * 128]
 
 
-def gain_call(grads, inverse, xs, wg, wu):
+def gain_call(idx, grads, inverse, xs, mine, other):
     return pl.pallas_call(
         gain_kernel,
-        grid=(NZ // 2,),
+        grid=(NX,),
         out_shape=jax.ShapeDtypeStruct((NZ, SHARE // 128 * LOCAL, 128), F32),
         in_specs=[
+            SMEM,
             whole((2, UNITS, TOK)),
             whole((1, TOK)),
-            lead((2, NY, COLS, TOK)),
-            lead((2, UNITS, SHARE)),
-            lead((2, UNITS, SHARE)),
+            lead((2, SHARE, TOK)),
+            lead((1, 2, UNITS, SHARE)),
+            lead((1, 2, UNITS, SHARE)),
         ],
         out_specs=lead((2, SHARE // 128 * LOCAL, 128)),
-        compiler_params=params(32),
+        compiler_params=params(60),
         cost_estimate=cost(3 * UNITS * TOK * FEATURES, 9 << 20),
         name="gain_term",
-    )(grads, inverse, xs, wg, wu)
+    )(idx, grads, inverse, xs, mine, other)
 
 
 def join_kernel(part, gain_part, out):
@@ -317,7 +294,7 @@
         in_specs=[whole(part.shape), whole((UNITS, TOK)), lead((2, NY, COLS, TOK))],
         out_specs=lead((2, UNITS, SHARE)),
         scratch_shapes=[pltpu.VMEM((UNITS, TOK), BF16)],
-        compiler_params=params(24),
+        compiler_params=params(60),
         cost_estimate=cost(UNITS * TOK * FEATURES, 6 << 20),
         name="grad_down",
     )(part, hidden, dy)
@@ -346,25 +323,25 @@
 def body(tokens, gain, cotangent, gate_weight, up_weight, down_weight):
     idx = jnp.stack([lax.axis_index("z"), lax.axis_index("core"), lax.axis_index("y")]).astype(jnp.int32)
     dp = ("x", "core")
-    wg = lax.all_gather(gate_weight.T, dp, axis=0)
-    wu = lax.all_gather(up_weight.T, dp, axis=0)
+    xs = lax.all_gather(tokens.T, ("z", "y"), axis=0, tiled=True).reshape(NZ, SHARE, TOK)
     dy_part = spread(cotangent.T, "z", NZ)
-    tokens, dy_part = lax.optimization_barrier((tokens, dy_part))
-    x_part = spread(tokens.T, "y", NY)
-    down_weight, x_part = lax.optimization_barrier((down_weight, x_part))
+    gate_weight, up_weight, dy_part = lax.optimization_barrier((gate_weight, up_weight, dy_part))
+    mine = spread(jnp.stack([gate_weight.T, up_weight.T]), "x", NX)
+    down_weight, mine = lax.optimization_barrier((down_weight, mine))
     dmine = spread(down_weight, "x", NX)
     dy_pieces = ring(dy_part, "y", NY)
-    pieces = ring(x_part, "z", NZ)
-    dother = lax.ppermute(dmine, "core", [(0, 1), (1, 0)])
+    swap = [(0, 1), (1, 0)]
+    other = lax.ppermute(mine, "core", swap)
+    dother = lax.ppermute(dmine, "core", swap)
 
     dy, dy_gram = cotangent_call(idx, dy_pieces)
     back = back_call(idx, dy, dmine, dother)
-    xs, hidden, inverse, sq_part, grads = hidden_call(
-        idx, pieces, wg, wu, gain.reshape(NX * NC, SHARE), dy_gram, back
+    hidden, inverse, sq_part, grads = hidden_call(
+        idx, xs, mine, other, gain.reshape(NX * NC, SHARE), dy_gram, back
     )
     part = exchange(sq_part, "y")
     grads, sq_part = lax.optimization_barrier((grads, sq_part))
-    gain_part = gain_call(grads, inverse, xs, wg, wu)
+    gain_part = gain_call(idx, grads, inverse, xs, mine, other)
     part = exchange(join_call(part, gain_part), "z")
     terms = grad_call(part, hidden, dy)
     part, terms = lax.optimization_barrier((part, terms))

time: 250 us -> 245 us (0.980)
  blocking collectives: 37.6 us -> 64.4 us
  starting transfers between devices: 80.5 us -> 55.4 us
  local copies, waits for them, and re-layouts: 26.1 us -> 4.53 us
  waiting for transfers between devices: 51.2 us -> 61 us
  Pallas kernels: 36.7 us -> 41.1 us
    ppermute x6 -> x3, waiting for transfers between devices: 4.37 us -> 32.8 us  [ring(): down.append(lax.ppermute(down[-1], axis, shift(-1)))]
    all_to_all x0 -> x1, blocking collectives: none -> 26.7 us  [spread(): lax.all_to_all(jnp.broadcast_to(block[None], (count,) + block.shape), axi...]
    unnamed x50 -> x18, local copies, waits for them, and re-layouts: 22.5 us -> 0.63 us
    all_to_all x3 -> x2, starting transfers between devices: 21.8 us -> 7.67 us  [spread(): lax.all_to_all(jnp.broadcast_to(block[None], (count,) + block.shape), axi...]
    all_to_all x3 -> x2, waiting for transfers between devices: 31.5 us -> 17.5 us  [spread(): lax.all_to_all(jnp.broadcast_to(block[None], (count,) + block.shape), axi...]
    ppermute x8 -> x4, starting transfers between devices: 18.7 us -> 9.09 us  [ring(): up.append(lax.ppermute(up[-1], axis, shift(1)))]
    ppermute x1 -> x2, starting transfers between devices: 4.99 us -> 9.57 us  [the longest x1 5.58 us: body(): other = lax.ppermute(mine, 'core', swap)]
    ppermute x6 -> x3, starting transfers between devices: 20.2 us -> 15.7 us  [ring(): down.append(lax.ppermute(down[-1], axis, shift(-1)))]
  transfers between devices with their start and end apart: 23 -> 15, of which waited for: 7 -> 6; matrix products, arithmetic and copies ran while one was open for 2% -> 2% of each run, Pallas kernels for 9% -> 11%
where the time goes in v5:
time: 245 us; the launch traced here: 244 us
  blocking collectives  64.4 us (26%)
  waiting for transfers between devices  61 us (25%)
  starting transfers between devices  55.4 us (23%)
  Pallas kernels  41.1 us (17%)
  between operations  14.3 us (6%)
  local copies, waits for them, and re-layouts  4.53 us (2%)
  other arithmetic  3.01 us (1%)
    all_to_all x3, blocking collectives, exchange(): return lax.all_to_all(blocks, axis, split_axis=0, concat_axis=0, tiled=True)  37.8 us
    ppermute x3, waiting for transfers between devices, ring(): down.append(lax.ppermute(down[-1], axis, shift(-1)))  32.8 us
    all_to_all x1, blocking collectives, spread(): lax.all_to_all(jnp.broadcast_to(block[None], (count,) + block.shape), axi...  26.7 us
    all_to_all x2, waiting for transfers between devices, spread(): lax.all_to_all(jnp.broadcast_to(block[None], (count,) + block.shape), axi...  17.5 us
    ppermute x3, starting transfers between devices, ring(): down.append(lax.ppermute(down[-1], axis, shift(-1)))  15.7 us
    all_to_all x2, starting transfers between devices, exchange(): return lax.all_to_all(blocks, axis, split_axis=0, concat_axis=0, tiled=True)  13.2 us
    pallas_call x1, Pallas kernels, gain_call(): pl.pallas_call(gain_kernel, grid=(NX,), out_shape=jax.ShapeDtypeStruct((N...  9.22 us
    ppermute x4, starting transfers between devices, ring(): up.append(lax.ppermute(up[-1], axis, shift(1)))  9.09 us
  transfers between devices with their start and end apart: 15, of which 6 were waited for; matrix products, arithmetic and copies ran while one was open for 2% of the time, Pallas kernels for 11%

profile of v5, /device:TPU:1, one launch (start us, length us, event | category | flops | bytes accessed | tf_op | source)
XLA Modules:
  0.0 243.7 jit_solution(11395978636579672468)
XLA Ops:
  8.8 26.7 %all_to_all.40.refs_0_ = bf16[8,64,512]{2,1,0:T(8,128)(2,1)S(1)} all-to-all(bf16[8,64,512]{2,1,0:T(8,128)(2,1)S(1)} %broadcast_in_dim.6), channel_id=1, replica_groups=mesh['x'=4,'core'=2,'z'=8,'y'=8] {'z'}, dimensions={0} | all-to-all | bytes 1048576 | tf_op jit(solution)/shard_map/all_to_all | solution.py:304
  36.9 4.1 %all-to-all-start.1 = ((bf16[4,2,224,512]{3,2,1,0:T(8,128)(2,1)}), bf16[4,2,224,512]{3,2,1,0:T(8,128)(2,1)S(1)}, u32[]{:S(2)}, u32[]{:S(2)}) async-start(bf16[4,2,224,512]{3,2,1,0:T(8,128)(2,1)} %broadcast_in_dim.7), calls=%async_computation.1 | async-start | bytes 3670016 | tf_op jit(solution)/shard_map/all_to_all | solution.py:304
  44.4 17.5 %all-to-all-done.1.mine = bf16[4,2,224,512]{3,2,1,0:T(8,128)(2,1)S(1)} async-done(((bf16[4,2,224,512]{3,2,1,0:T(8,128)(2,1)}), bf16[4,2,224,512]{3,2,1,0:T(8,128)(2,1)S(1)}, u32[]{:S(2)}, u32[]{:S(2)}) %all-to-all-start.1) | async-done | bytes 1835040 | tf_op jit(solution)/shard_map/all_to_all | solution.py:304
  61.9 5.6 %collective-permute-start = (bf16[4,2,224,512]{3,2,1,0:T(8,128)(2,1)S(1)}, bf16[4,2,224,512]{3,2,1,0:T(8,128)(2,1)}, u32[]{:S(2)}, u32[]{:S(2)}) collective-permute-start(bf16[4,2,224,512]{3,2,1,0:T(8,128)(2,1)S(1)} %all-to-all-done.1.mine), channel_id=1, source_target_pairs={{0,64},{64,0},{1,65},{65,1},{2,66},{66,2},{3,67},{67,3},{4,68},{68... | collective-permute-start | bytes 5505032 | tf_op jit(solution)/shard_map/ppermute | solution.py:334
  67.5 5.1 %collective-permute-start.5 = (bf16[8,64,512]{2,1,0:T(8,128)(2,1)S(1)}, bf16[8,64,512]{2,1,0:T(8,128)(2,1)}, u32[]{:S(2)}, u32[]{:S(2)}) collective-permute-start(bf16[8,64,512]{2,1,0:T(8,128)(2,1)S(1)} %all_to_all.40.refs_0_), channel_id=1, source_target_pairs={{0,7},{1,0},{2,1},{3,2},{4,3},{5,4},{6,5},{7,6},{8,15},{9,8},{10,9... | collective-permute-start | bytes 1572872 | tf_op jit(solution)/shard_map/ppermute | solution.py:319
  75.5 3.5 %all-to-all-start.2 = ((bf16[4,224,512]{2,1,0:T(8,128)(2,1)}), bf16[4,224,512]{2,1,0:T(8,128)(2,1)S(1)}, u32[]{:S(2)}, u32[]{:S(2)}) async-start(bf16[4,224,512]{2,1,0:T(8,128)(2,1)} %broadcast_in_dim.8), calls=%async_computation.2 | async-start | bytes 1835008 | tf_op jit(solution)/shard_map/all_to_all | solution.py:304
  79.1 13.8 %collective-permute-done.5.refs_7_ = bf16[8,64,512]{2,1,0:T(8,128)(2,1)} collective-permute-done((bf16[8,64,512]{2,1,0:T(8,128)(2,1)S(1)}, bf16[8,64,512]{2,1,0:T(8,128)(2,1)}, u32[]{:S(2)}, u32[]{:S(2)}) %collective-permute-start.5) | collective-permute-done | bytes 524320 | tf_op jit(solution)/shard_map/ppermute | solution.py:319
  92.9 5.4 %collective-permute-start.6 = (bf16[8,64,512]{2,1,0:T(8,128)(2,1)}, bf16[8,64,512]{2,1,0:T(8,128)(2,1)S(1)}, u32[]{:S(2)}, u32[]{:S(2)}) collective-permute-start(bf16[8,64,512]{2,1,0:T(8,128)(2,1)} %collective-permute-done.5.refs_7_), channel_id=1, source_target_pairs={{0,7},{1,0},{2,1},{3,2},{4,3},{5,4},{6,5},{7,6},{8,15},{9,8},{10,9... | collective-permute-start | bytes 1572872 | tf_op jit(solution)/shard_map/ppermute | solution.py:319
  100.3 4.0 %collective-permute-start.8 = (bf16[4,224,512]{2,1,0:T(8,128)(2,1)S(1)}, bf16[4,224,512]{2,1,0:T(8,128)(2,1)}, u32[]{:S(2)}, u32[]{:S(2)}) collective-permute-start(bf16[4,224,512]{2,1,0:T(8,128)(2,1)S(1)} %all-to-all-done.2.mine), channel_id=1, source_target_pairs={{0,64},{64,0},{1,65},{65,1},{2,66},{66,2},{3,67},{67,3},{4,68},{68... | collective-permute-start | bytes 2752520 | tf_op jit(solution)/shard_map/ppermute | solution.py:335
  104.3 11.7 %collective-permute-done.6.refs_6_ = bf16[8,64,512]{2,1,0:T(8,128)(2,1)S(1)} collective-permute-done((bf16[8,64,512]{2,1,0:T(8,128)(2,1)}, bf16[8,64,512]{2,1,0:T(8,128)(2,1)S(1)}, u32[]{:S(2)}, u32[]{:S(2)}) %collective-permute-start.6) | collective-permute-done | bytes 524320 | tf_op jit(solution)/shard_map/ppermute | solution.py:319
  115.9 5.2 %collective-permute-start.7 = (bf16[8,64,512]{2,1,0:T(8,128)(2,1)S(1)}, bf16[8,64,512]{2,1,0:T(8,128)(2,1)}, u32[]{:S(2)}, u32[]{:S(2)}) collective-permute-start(bf16[8,64,512]{2,1,0:T(8,128)(2,1)S(1)} %collective-permute-done.6.refs_6_), channel_id=1, source_target_pairs={{0,7},{1,0},{2,1},{3,2},{4,3},{5,4},{6,5},{7,6},{8,15},{9,8},{10,9... | collective-permute-start | bytes 1572872 | tf_op jit(solution)/shard_map/ppermute | solution.py:319
  124.3 7.3 %collective-permute-done.7.refs_5_ = bf16[8,64,512]{2,1,0:T(8,128)(2,1)} collective-permute-done((bf16[8,64,512]{2,1,0:T(8,128)(2,1)S(1)}, bf16[8,64,512]{2,1,0:T(8,128)(2,1)}, u32[]{:S(2)}, u32[]{:S(2)}) %collective-permute-start.7) | collective-permute-done | bytes 524320 | tf_op jit(solution)/shard_map/ppermute | solution.py:319
  131.6 5.3 %collective-permute-done.4.refs_4_ = bf16[8,64,512]{2,1,0:T(8,128)(2,1)} collective-permute-done((bf16[8,64,512]{2,1,0:T(8,128)(2,1)}, bf16[8,64,512]{2,1,0:T(8,128)(2,1)}, u32[]{:S(2)}, u32[]{:S(2)}) %collective-permute-start.4) | collective-permute-done | bytes 524320 | tf_op jit(solution)/shard_map/ppermute | solution.py:317
  136.9 8.2 %cotangent_gram.1 = (bf16[8,8,64,512]{3,2,1,0:T(8,128)(2,1)}, f32[2,256,256]{2,1,0:T(8,128)}) custom-call(s32[3]{0:T(128)} %pad_add_fusion.idx, bf16[8,64,512]{2,1,0:T(8,128)(2,1)} %copy-done.2, bf16[8,64,512]{2,1,0:T(8,128)(2,1)} %collective-permute-done.1.refs_1_, bf16[8,64,512]{2,1,0:T(8,128)(2,1)} %collective-permute-done.2.refs_2_, ...), custom_call_target="tpu_custom_call" | custom-call | flops 1073741824 | bytes 9437184 | tf_op jit(solution)/shard_map/cotangent_gram/pallas_call | solution.py:72
  145.2 4.9 %back.1 = f32[224,512]{1,0:T(8,128)} custom-call(s32[3]{0:T(128)} %pad_add_fusion.idx, bf16[8,8,64,512]{3,2,1,0:T(8,128)(2,1)} %get-tuple-element.23.dy, bf16[4,224,512]{2,1,0:T(8,128)(2,1)} %copy-done.1, bf16[4,224,512]{2,1,0:T(8,128)(2,1)} %collective-permute-done.8.other), custom_call_target="tpu_custom_call" | custom-call | flops 939524096 | bytes 7340032 | tf_op jit(solution)/shard_map/back/pallas_call | solution.py:103
  150.2 7.3 %hidden.1 = (bf16[224,512]{1,0:T(8,128)(2,1)}, f32[1,512]{1,0:T(1,128)}, f32[8,8,128]{2,1,0:T(8,128)}, bf16[2,224,512]{2,1,0:T(8,128)(2,1)}) custom-call(s32[3]{0:T(128)} %pad_add_fusion.idx, bf16[8,512,512]{2,1,0:T(8,128)(2,1)} %bitcast.15, bf16[4,2,224,512]{3,2,1,0:T(8,128)(2,1)} %copy-done, bf16[4,2,224,512]{3,2,1,0:T(8,128)(2,1)} %collective-permute-done.other, ...), custom_call_target="tpu_custom_call" | custom-call | flops 1879048192 | bytes 14680064 | tf_op jit(solution)/shard_map/hidden/pallas_call | solution.py:163
  157.4 3.6 %all-to-all-start.3 = ((f32[8,8,128]{2,1,0:T(8,128)}), f32[8,8,128]{2,1,0:T(8,128)S(1)}, u32[]{:S(2)}, u32[]{:S(2)}) async-start(f32[8,8,128]{2,1,0:T(8,128)} %get-tuple-element.25), calls=%async_computation.3 | async-start | bytes 65536 | tf_op jit(solution)/shard_map/all_to_all | solution.py:310
  161.1 9.2 %gain_term.1.gain_part = f32[8,32,128]{2,1,0:T(8,128)} custom-call(s32[3]{0:T(128)} %pad_add_fusion.idx, bf16[2,224,512]{2,1,0:T(8,128)(2,1)} %get-tuple-element.27.grads, f32[1,512]{1,0:T(1,128)} %get-tuple-element.28.inverse, bf16[8,512,512]{2,1,0:T(8,128)(2,1)} %bitcast.16, bf16[4,2,224,512]{3,2,1,0:T(8,128)(2,1)} %copy-done, ...), custom_call_target="tpu_custom_call" | custom-call | flops 2818572288 | bytes 9437184 | tf_op jit(solution)/shard_map/gain_term/pallas_call | solution.py:212
  172.5 12.4 %all_to_all.41.part = f32[8,40,128]{2,1,0:T(8,128)} all-to-all(f32[8,40,128]{2,1,0:T(8,128)} %join_parts.1), channel_id=1, replica_groups=mesh['x'=4,'core'=2,'z'=8,'y'=8] {'z'}, dimensions={0} | all-to-all | bytes 327680 | tf_op jit(solution)/shard_map/all_to_all | solution.py:310
  184.9 5.2 %grad_down.1 = bf16[8,224,512]{2,1,0:T(8,128)(2,1)} custom-call(f32[8,40,128]{2,1,0:T(8,128)} %all_to_all.41.part, bf16[224,512]{1,0:T(8,128)(2,1)} %get-tuple-element.29.hidden, bf16[8,8,64,512]{3,2,1,0:T(8,128)(2,1)} %get-tuple-element.23.dy), custom_call_target="tpu_custom_call" | custom-call | flops 939524096 | bytes 6291456 | tf_op jit(solution)/shard_map/grad_down/pallas_call | solution.py:290
  191.7 14.6 %all_to_all.42.part = f32[8,32,128]{2,1,0:T(8,128)} all-to-all(f32[8,32,128]{2,1,0:T(8,128)} %add_parts.1), channel_id=1, replica_groups=mesh['x'=4,'core'=2,'z'=8,'y'=8] {'y'}, dimensions={0} | all-to-all | bytes 262144 | tf_op jit(solution)/shard_map/all_to_all | solution.py:310
  207.9 10.8 %all_to_all.43.part = f32[8,8,128]{2,1,0:T(8,128)} all-to-all(f32[8,8,128]{2,1,0:T(8,128)} %get-tuple-element.32), channel_id=1, replica_groups=mesh['x'=4,'core'=2,'z'=8,'y'=8] {'z'}, dimensions={0} | all-to-all | bytes 65536 | tf_op jit(solution)/shard_map/all_to_all | solution.py:310
  220.1 9.6 %all-to-all-start.7 = ((f32[8,8,128]{2,1,0:T(8,128)}), f32[8,8,128]{2,1,0:T(8,128)S(1)}, u32[]{:S(2)}, u32[]{:S(2)}) async-start(f32[8,8,128]{2,1,0:T(8,128)} %gain_scale.1), calls=%async_computation.8 | async-start | bytes 65536 | tf_op jit(solution)/shard_map/all_to_all | solution.py:310
  229.8 4.7 %all-to-all-done.7 = f32[8,8,128]{2,1,0:T(8,128)S(1)} async-done(((f32[8,8,128]{2,1,0:T(8,128)}), f32[8,8,128]{2,1,0:T(8,128)S(1)}, u32[]{:S(2)}, u32[]{:S(2)}) %all-to-all-start.7) | async-done | bytes 32800 | tf_op jit(solution)/shard_map/all_to_all | solution.py:310
  (48 shorter events, 23.6 us)
Async XLA Ops:
  7.2 28.3 %copy-start.4 = (bf16[512,224]{0,1:T(8,128)(2,1)S(1)}, bf16[512,224]{0,1:T(8,128)(2,1)}, u32[]{:S(2)}) copy-start(bf16[512,224]{0,1:T(8,128)(2,1)} %param.10) | copy-start | bytes 688132
  7.2 28.3 %copy-start.5 = (bf16[512,224]{0,1:T(8,128)(2,1)S(1)}, bf16[512,224]{0,1:T(8,128)(2,1)}, u32[]{:S(2)}) copy-start(bf16[512,224]{0,1:T(8,128)(2,1)} %param.9) | copy-start | bytes 688132
  7.2 143.0 %all-gather.2.cloned.1.call-start = ((), (), s32[]{:S(2)}) async-start(), calls=%async_computation.9 | async-start | bytes 4259840 | tf_op jit(solution)/shard_map/all_gather | solution.py:326
  35.5 32.0 %copy-start.2 = (bf16[8,64,512]{2,1,0:T(8,128)(2,1)}, bf16[8,64,512]{2,1,0:T(8,128)(2,1)S(1)}, u32[]{:S(2)}) copy-start(bf16[8,64,512]{2,1,0:T(8,128)(2,1)S(1)} %all_to_all.40.refs_0_) | copy-start | bytes 1572868
  36.9 37.6 %copy-start.6 = (bf16[224,512]{1,0:T(8,128)(2,1)S(1)}, bf16[224,512]{1,0:T(8,128)(2,1)}, u32[]{:S(2)}) copy-start(bf16[224,512]{1,0:T(8,128)(2,1)} %param.11) | copy-start | bytes 688132
  36.9 24.9 %all-to-all-start.1 = ((bf16[4,2,224,512]{3,2,1,0:T(8,128)(2,1)}), bf16[4,2,224,512]{3,2,1,0:T(8,128)(2,1)S(1)}, u32[]{:S(2)}, u32[]{:S(2)}) async-start(bf16[4,2,224,512]{3,2,1,0:T(8,128)(2,1)} %broadcast_in_dim.7), calls=%async_computation.1 | async-start | bytes 3670016 | tf_op jit(solution)/shard_map/all_to_all | solution.py:304
  41.1 82.0 %copy-start.8 = (f32[4096]{0:T(1024)S(1)}, f32[4096]{0:T(1024)}, u32[]{:S(2)}) copy-start(f32[4096]{0:T(1024)} %param.7) | copy-start | bytes 49156
  41.1 31.5 %collective-permute-start.1 = (bf16[8,64,512]{2,1,0:T(8,128)(2,1)S(1)}, bf16[8,64,512]{2,1,0:T(8,128)(2,1)}, u32[]{:S(2)}, u32[]{:S(2)}) collective-permute-start(bf16[8,64,512]{2,1,0:T(8,128)(2,1)S(1)} %all_to_all.40.refs_0_), channel_id=1, source_target_pairs={{0,1},{1,2},{2,3},{3,4},{4,5},{5,6},{6,7},{7,0},{8,9},{9,10},{10,1... | collective-permute-start | bytes 1572872 | tf_op jit(solution)/shard_map/ppermute | solution.py:317
  61.9 83.3 %copy-start = (bf16[4,2,224,512]{3,2,1,0:T(8,128)(2,1)}, bf16[4,2,224,512]{3,2,1,0:T(8,128)(2,1)S(1)}, u32[]{:S(2)}) copy-start(bf16[4,2,224,512]{3,2,1,0:T(8,128)(2,1)S(1)} %all-to-all-done.1.mine) | copy-start | bytes 5505028
  61.9 88.3 %collective-permute-start = (bf16[4,2,224,512]{3,2,1,0:T(8,128)(2,1)S(1)}, bf16[4,2,224,512]{3,2,1,0:T(8,128)(2,1)}, u32[]{:S(2)}, u32[]{:S(2)}) collective-permute-start(bf16[4,2,224,512]{3,2,1,0:T(8,128)(2,1)S(1)} %all-to-all-done.1.mine), channel_id=1, source_target_pairs={{0,64},{64,0},{1,65},{65,1},{2,66},{66,2},{3,67},{67,3},{4,68},{68... | collective-permute-start | bytes 5505032 | tf_op jit(solution)/shard_map/ppermute | solution.py:334
  67.5 25.4 %collective-permute-start.5 = (bf16[8,64,512]{2,1,0:T(8,128)(2,1)S(1)}, bf16[8,64,512]{2,1,0:T(8,128)(2,1)}, u32[]{:S(2)}, u32[]{:S(2)}) collective-permute-start(bf16[8,64,512]{2,1,0:T(8,128)(2,1)S(1)} %all_to_all.40.refs_0_), channel_id=1, source_target_pairs={{0,7},{1,0},{2,1},{3,2},{4,3},{5,4},{6,5},{7,6},{8,15},{9,8},{10,9... | collective-permute-start | bytes 1572872 | tf_op jit(solution)/shard_map/ppermute | solution.py:319
  72.6 25.7 %collective-permute-start.2 = (bf16[8,64,512]{2,1,0:T(8,128)(2,1)}, bf16[8,64,512]{2,1,0:T(8,128)(2,1)}, u32[]{:S(2)}, u32[]{:S(2)}) collective-permute-start(bf16[8,64,512]{2,1,0:T(8,128)(2,1)} %collective-permute-done.1.refs_1_), channel_id=1, source_target_pairs={{0,1},{1,2},{2,3},{3,4},{4,5},{5,6},{6,7},{7,0},{8,9},{9,10},{10,1... | collective-permute-start | bytes 1572872 | tf_op jit(solution)/shard_map/ppermute | solution.py:317
  75.5 24.7 %all-to-all-start.2 = ((bf16[4,224,512]{2,1,0:T(8,128)(2,1)}), bf16[4,224,512]{2,1,0:T(8,128)(2,1)S(1)}, u32[]{:S(2)}, u32[]{:S(2)}) async-start(bf16[4,224,512]{2,1,0:T(8,128)(2,1)} %broadcast_in_dim.8), calls=%async_computation.2 | async-start | bytes 1835008 | tf_op jit(solution)/shard_map/all_to_all | solution.py:304
  92.9 23.0 %collective-permute-start.6 = (bf16[8,64,512]{2,1,0:T(8,128)(2,1)}, bf16[8,64,512]{2,1,0:T(8,128)(2,1)S(1)}, u32[]{:S(2)}, u32[]{:S(2)}) collective-permute-start(bf16[8,64,512]{2,1,0:T(8,128)(2,1)} %collective-permute-done.5.refs_7_), channel_id=1, source_target_pairs={{0,7},{1,0},{2,1},{3,2},{4,3},{5,4},{6,5},{7,6},{8,15},{9,8},{10,9... | collective-permute-start | bytes 1572872 | tf_op jit(solution)/shard_map/ppermute | solution.py:319
  98.3 22.8 %collective-permute-start.3 = (bf16[8,64,512]{2,1,0:T(8,128)(2,1)}, bf16[8,64,512]{2,1,0:T(8,128)(2,1)}, u32[]{:S(2)}, u32[]{:S(2)}) collective-permute-start(bf16[8,64,512]{2,1,0:T(8,128)(2,1)} %collective-permute-done.2.refs_2_), channel_id=1, source_target_pairs={{0,1},{1,2},{2,3},{3,4},{4,5},{5,6},{6,7},{7,0},{8,9},{9,10},{10,1... | collective-permute-start | bytes 1572872 | tf_op jit(solution)/shard_map/ppermute | solution.py:317
  100.2 45.0 %copy-start.1 = (bf16[4,224,512]{2,1,0:T(8,128)(2,1)}, bf16[4,224,512]{2,1,0:T(8,128)(2,1)S(1)}, u32[]{:S(2)}) copy-start(bf16[4,224,512]{2,1,0:T(8,128)(2,1)S(1)} %all-to-all-done.2.mine) | copy-start | bytes 2752516
  100.3 45.0 %collective-permute-start.8 = (bf16[4,224,512]{2,1,0:T(8,128)(2,1)S(1)}, bf16[4,224,512]{2,1,0:T(8,128)(2,1)}, u32[]{:S(2)}, u32[]{:S(2)}) collective-permute-start(bf16[4,224,512]{2,1,0:T(8,128)(2,1)S(1)} %all-to-all-done.2.mine), channel_id=1, source_target_pairs={{0,64},{64,0},{1,65},{65,1},{2,66},{66,2},{3,67},{67,3},{4,68},{68... | collective-permute-start | bytes 2752520 | tf_op jit(solution)/shard_map/ppermute | solution.py:335
  115.9 21.0 %copy-start.3 = (bf16[8,64,512]{2,1,0:T(8,128)(2,1)}, bf16[8,64,512]{2,1,0:T(8,128)(2,1)S(1)}, u32[]{:S(2)}) copy-start(bf16[8,64,512]{2,1,0:T(8,128)(2,1)S(1)} %collective-permute-done.6.refs_6_) | copy-start | bytes 1572868
  115.9 15.7 %collective-permute-start.7 = (bf16[8,64,512]{2,1,0:T(8,128)(2,1)S(1)}, bf16[8,64,512]{2,1,0:T(8,128)(2,1)}, u32[]{:S(2)}, u32[]{:S(2)}) collective-permute-start(bf16[8,64,512]{2,1,0:T(8,128)(2,1)S(1)} %collective-permute-done.6.refs_6_), channel_id=1, source_target_pairs={{0,7},{1,0},{2,1},{3,2},{4,3},{5,4},{6,5},{7,6},{8,15},{9,8},{10,9... | collective-permute-start | bytes 1572872 | tf_op jit(solution)/shard_map/ppermute | solution.py:319
  121.1 15.8 %collective-permute-start.4 = (bf16[8,64,512]{2,1,0:T(8,128)(2,1)}, bf16[8,64,512]{2,1,0:T(8,128)(2,1)}, u32[]{:S(2)}, u32[]{:S(2)}) collective-permute-start(bf16[8,64,512]{2,1,0:T(8,128)(2,1)} %collective-permute-done.3.refs_3_), channel_id=1, source_target_pairs={{0,1},{1,2},{2,3},{3,4},{4,5},{5,6},{6,7},{7,0},{8,9},{9,10},{10,1... | collective-permute-start | bytes 1572872 | tf_op jit(solution)/shard_map/ppermute | solution.py:317
  157.4 12.9 %all-to-all-start.3 = ((f32[8,8,128]{2,1,0:T(8,128)}), f32[8,8,128]{2,1,0:T(8,128)S(1)}, u32[]{:S(2)}, u32[]{:S(2)}) async-start(f32[8,8,128]{2,1,0:T(8,128)} %get-tuple-element.25), calls=%async_computation.3 | async-start | bytes 65536 | tf_op jit(solution)/shard_map/all_to_all | solution.py:310
  161.0 74.1 %reduce-scatter.2.cloned.1.call-start = ((), (), s32[]{:S(2)}) async-start(), calls=%async_computation.10 | async-start | bytes 2064384 | tf_op jit(solution)/shard_map/reduce_scatter | solution.py:348
  170.3 0.6 copy-start.7
  220.1 14.4 %all-to-all-start.7 = ((f32[8,8,128]{2,1,0:T(8,128)}), f32[8,8,128]{2,1,0:T(8,128)S(1)}, u32[]{:S(2)}, u32[]{:S(2)}) async-start(f32[8,8,128]{2,1,0:T(8,128)} %gain_scale.1), calls=%async_computation.8 | async-start | bytes 65536 | tf_op jit(solution)/shard_map/all_to_all | solution.py:310
Sparse Core Ops, SparseCore 0:
  11.1 99.8 all-gather.1
  190.2 34.0 reduce-scatter.1

commit v6 on v5

--- a/solution.py
+++ b/solution.py
@@ -47,6 +47,18 @@
     return pl.BlockSpec(shape, lambda i: (i,) + (0,) * (len(shape) - 1))
 
 
+def rotated(shape):
+    return pl.BlockSpec(shape, lambda i, idx: (lax.rem(idx[3] - i + NX, NX),) + (0,) * (len(shape) - 1))
+
+
+def fixed(shape):
+    return pl.BlockSpec(shape, lambda i, idx: (0,) * len(shape))
+
+
+def weights(first, count):
+    return pl.BlockSpec((1, count, UNITS, SHARE), lambda i, idx: (i, first // count, 0, 0))
+
+
 def cotangent_kernel(idx, *refs):
     pieces, (dy, gram, held, sems, out_sem) = refs[:NY], refs[NY:]
     y = idx[2]
@@ -95,17 +107,20 @@
     def _():
         back[...] = jnp.zeros_like(back)
 
-    back[...] += jnp.dot(mine[0], dy[core].reshape(SHARE, TOK), preferred_element_type=F32)
-    back[...] += jnp.dot(other[0], dy[1 - core].reshape(SHARE, TOK), preferred_element_type=F32)
+    back[...] += jnp.dot(mine[0, 0], dy[core].reshape(SHARE, TOK), preferred_element_type=F32)
+    back[...] += jnp.dot(other[0, 0], dy[1 - core].reshape(SHARE, TOK), preferred_element_type=F32)
 
 
 def back_call(idx, dy, mine, other):
     return pl.pallas_call(
         back_kernel,
-        grid=(NX,),
         out_shape=jax.ShapeDtypeStruct((UNITS, TOK), F32),
-        in_specs=[SMEM, lead((2, NY, COLS, TOK)), lead((1, UNITS, SHARE)), lead((1, UNITS, SHARE))],
-        out_specs=whole((UNITS, TOK)),
+        grid_spec=pltpu.PrefetchScalarGridSpec(
+            num_scalar_prefetch=1,
+            grid=(NX,),
+            in_specs=[rotated((2, NY, COLS, TOK)), weights(2, 1), weights(2, 1)],
+            out_specs=fixed((UNITS, TOK)),
+        ),
         compiler_params=params(60),
         cost_estimate=cost(UNITS * TOK * FEATURES, 7 << 20),
         name="back",
@@ -114,6 +129,7 @@
 
 def hidden_kernel(idx, xs, mine, other, gain, dy_gram, back, hidden, inverse, down_sq, grads, acc, squares):
     step, core = pl.program_id(0), idx[1]
+    chip = lax.rem(idx[3] - step + NX, NX)
 
     @pl.when(step == 0)
     def _():
@@ -121,7 +137,7 @@
         squares[...] = jnp.zeros_like(squares)
 
     for ref, d in ((mine, core), (other, 1 - core)):
-        row = gain[pl.ds(2 * step + d, 1), :]
+        row = gain[pl.ds(2 * chip + d, 1), :]
         block = xs[d]
         for k in range(2):
             scaled = (ref[0, k].astype(F32) * row).astype(BF16)
@@ -162,24 +178,26 @@
 def hidden_call(idx, xs, mine, other, gain, dy_gram, back):
     return pl.pallas_call(
         hidden_kernel,
-        grid=(NX,),
         out_shape=(
             jax.ShapeDtypeStruct((UNITS, TOK), BF16),
             jax.ShapeDtypeStruct((1, TOK), F32),
             jax.ShapeDtypeStruct((NY, LOCAL, 128), F32),
             jax.ShapeDtypeStruct((2, UNITS, TOK), BF16),
         ),
-        in_specs=[
-            SMEM,
-            lead((2, SHARE, TOK)),
-            lead((1, 2, UNITS, SHARE)),
-            lead((1, 2, UNITS, SHARE)),
-            whole((NX * NC, SHARE)),
-            whole((2, HALF, HALF)),
-            whole((UNITS, TOK)),
-        ],
-        out_specs=(whole((UNITS, TOK)), whole((1, TOK)), whole((NY, LOCAL, 128)), whole((2, UNITS, TOK))),
-        scratch_shapes=[pltpu.VMEM((2, UNITS, TOK), F32), pltpu.VMEM((8, TOK), F32)],
+        grid_spec=pltpu.PrefetchScalarGridSpec(
+            num_scalar_prefetch=1,
+            grid=(NX,),
+            in_specs=[
+                rotated((2, SHARE, TOK)),
+                weights(0, 2),
+                weights(0, 2),
+                fixed((NX * NC, SHARE)),
+                fixed((2, HALF, HALF)),
+                fixed((UNITS, TOK)),
+            ],
+            out_specs=(fixed((UNITS, TOK)), fixed((1, TOK)), fixed((NY, LOCAL, 128)), fixed((2, UNITS, TOK))),
+            scratch_shapes=[pltpu.VMEM((2, UNITS, TOK), F32), pltpu.VMEM((8, TOK), F32)],
+        ),
         compiler_params=params(60),
         cost_estimate=cost(2 * UNITS * TOK * FEATURES, 14 << 20),
         name="hidden",
@@ -211,17 +229,19 @@
 def gain_call(idx, grads, inverse, xs, mine, other):
     return pl.pallas_call(
         gain_kernel,
-        grid=(NX,),
         out_shape=jax.ShapeDtypeStruct((NZ, SHARE // 128 * LOCAL, 128), F32),
-        in_specs=[
-            SMEM,
-            whole((2, UNITS, TOK)),
-            whole((1, TOK)),
-            lead((2, SHARE, TOK)),
-            lead((1, 2, UNITS, SHARE)),
-            lead((1, 2, UNITS, SHARE)),
-        ],
-        out_specs=lead((2, SHARE // 128 * LOCAL, 128)),
+        grid_spec=pltpu.PrefetchScalarGridSpec(
+            num_scalar_prefetch=1,
+            grid=(NX,),
+            in_specs=[
+                fixed((2, UNITS, TOK)),
+                fixed((1, TOK)),
+                rotated((2, SHARE, TOK)),
+                weights(0, 2),
+                weights(0, 2),
+            ],
+            out_specs=rotated((2, SHARE // 128 * LOCAL, 128)),
+        ),
         compiler_params=params(60),
         cost_estimate=cost(3 * UNITS * TOK * FEATURES, 9 << 20),
         name="gain_term",
@@ -321,21 +341,22 @@
 
 
 def body(tokens, gain, cotangent, gate_weight, up_weight, down_weight):
-    idx = jnp.stack([lax.axis_index("z"), lax.axis_index("core"), lax.axis_index("y")]).astype(jnp.int32)
+    idx = jnp.stack([lax.axis_index(name) for name in ("z", "core", "y", "x")]).astype(jnp.int32)
     dp = ("x", "core")
     xs = lax.all_gather(tokens.T, ("z", "y"), axis=0, tiled=True).reshape(NZ, SHARE, TOK)
     dy_part = spread(cotangent.T, "z", NZ)
-    gate_weight, up_weight, dy_part = lax.optimization_barrier((gate_weight, up_weight, dy_part))
-    mine = spread(jnp.stack([gate_weight.T, up_weight.T]), "x", NX)
-    down_weight, mine = lax.optimization_barrier((down_weight, mine))
-    dmine = spread(down_weight, "x", NX)
+    block = jnp.stack([gate_weight.T, up_weight.T, down_weight])
+    block, dy_part = lax.optimization_barrier((block, dy_part))
+    turn = lambda k: [(i, (i + k) % NX) for i in range(NX)]
+    right = lax.ppermute(block, "x", turn(1))
+    left = lax.ppermute(block, "x", turn(-1))
+    far = lax.ppermute(right, "x", turn(1))
+    mine = jnp.stack([block, right, far, left])
+    other = lax.ppermute(mine, "core", [(0, 1), (1, 0)])
     dy_pieces = ring(dy_part, "y", NY)
-    swap = [(0, 1), (1, 0)]
-    other = lax.ppermute(mine, "core", swap)
-    dother = lax.ppermute(dmine, "core", swap)
 
     dy, dy_gram = cotangent_call(idx, dy_pieces)
-    back = back_call(idx, dy, dmine, dother)
+    back = back_call(idx, dy, mine, other)
     hidden, inverse, sq_part, grads = hidden_call(
         idx, xs, mine, other, gain.reshape(NX * NC, SHARE), dy_gram, back
     )
@@ -343,8 +364,9 @@
     grads, sq_part = lax.optimization_barrier((grads, sq_part))
     gain_part = gain_call(idx, grads, inverse, xs, mine, other)
     part = exchange(join_call(part, gain_part), "z")
+    added = add_call(part)
+    part, added = lax.optimization_barrier((part, added))
     terms = grad_call(part, hidden, dy)
-    part, terms = lax.optimization_barrier((part, terms))
     grad_down = lax.psum_scatter(terms, dp, scatter_dimension=0).astype(F32)
 
     gain_z, gain_sq = pl.pallas_call(
@@ -354,7 +376,7 @@
             jax.ShapeDtypeStruct((NZ, LOCAL, 128), F32),
         ),
         name="gain_sq",
-    )(exchange(add_call(part), "y"))
+    )(exchange(added, "y"))
     gain_local = pl.pallas_call(
         gain_scale_kernel,
         out_shape=jax.ShapeDtypeStruct((NX * NC, 8, 128), F32),

time: 245 us -> 268 us (1.094)
  waiting for transfers between devices: 61 us -> 101 us
  blocking collectives: 64.4 us -> 37.6 us
  starting transfers between devices: 55.4 us -> 63.5 us
    ppermute x4, waiting for transfers between devices: 5.34 us -> 49.2 us  [ring(): up.append(lax.ppermute(up[-1], axis, shift(1)))]
    ppermute x3, waiting for transfers between devices: 32.8 us -> 0.01 us  [ring(): down.append(lax.ppermute(down[-1], axis, shift(-1)))]
    ppermute x2 -> x4, waiting for transfers between devices: 0.01 us -> 29.8 us  [the longest x1 16.7 us: body(): far = lax.ppermute(right, 'x', turn(1))]
    all_to_all x1 -> x0, blocking collectives: 26.7 us -> none  [spread(): lax.all_to_all(jnp.broadcast_to(block[None], (count,) + block.shape), axi...]
    all_to_all x2, starting transfers between devices: 13.2 us -> 18.1 us  [exchange(): return lax.all_to_all(blocks, axis, split_axis=0, concat_axis=0, tiled=True)]
    all_to_all x2 -> x1, starting transfers between devices: 7.67 us -> 10.9 us  [spread(): lax.all_to_all(jnp.broadcast_to(block[None], (count,) + block.shape), axi...]
    ppermute x2 -> x4, starting transfers between devices: 9.57 us -> 12.6 us  [the longest x1 4.09 us: body(): other = lax.ppermute(mine, 'core', [(0, 1), (1, 0)])]
    ppermute x3, starting transfers between devices: 15.7 us -> 12.9 us  [ring(): down.append(lax.ppermute(down[-1], axis, shift(-1)))]
  transfers between devices with their start and end apart: 15 -> 16, of which waited for: 6 -> 8; matrix products, arithmetic and copies ran while one was open for 2% -> 2% of each run, Pallas kernels for 11% -> 10%
where the time goes in v6:
time: 268 us; the launch traced here: 267 us
  waiting for transfers between devices  101 us (38%)
  starting transfers between devices  63.5 us (24%)
  Pallas kernels  43 us (16%)
  blocking collectives  37.6 us (14%)
  between operations  14.3 us (5%)
  other arithmetic  4.57 us (2%)
  local copies, waits for them, and re-layouts  2.93 us (1%)
    ppermute x4, waiting for transfers between devices, ring(): up.append(lax.ppermute(up[-1], axis, shift(1)))  49.2 us
    all_to_all x3, blocking collectives, exchange(): return lax.all_to_all(blocks, axis, split_axis=0, concat_axis=0, tiled=True)  37.6 us
    all_to_all x2, starting transfers between devices, exchange(): return lax.all_to_all(blocks, axis, split_axis=0, concat_axis=0, tiled=True)  18.1 us
    ppermute x1, waiting for transfers between devices, body(): far = lax.ppermute(right, 'x', turn(1))  16.7 us
    all_to_all x1, waiting for transfers between devices, spread(): lax.all_to_all(jnp.broadcast_to(block[None], (count,) + block.shape), axi...  16.7 us
    ppermute x1, waiting for transfers between devices, body(): right = lax.ppermute(block, 'x', turn(1))  13.1 us
    ppermute x3, starting transfers between devices, ring(): down.append(lax.ppermute(down[-1], axis, shift(-1)))  12.9 us
    all_to_all x1, starting transfers between devices, spread(): lax.all_to_all(jnp.broadcast_to(block[None], (count,) + block.shape), axi...  10.9 us
  transfers between devices with their start and end apart: 16, of which 8 were waited for; matrix products, arithmetic and copies ran while one was open for 2% of the time, Pallas kernels for 10%

profile of v6, /device:TPU:1, one launch (start us, length us, event | category | flops | bytes accessed | tf_op | source)
XLA Modules:
  0.0 267.1 jit_solution(12667678731800682905)
XLA Ops:
  9.6 10.9 %all-to-all-start = ((bf16[8,64,512]{2,1,0:T(8,128)(2,1)}), bf16[8,64,512]{2,1,0:T(8,128)(2,1)S(1)}, u32[]{:S(2)}, u32[]{:S(2)}) async-start(bf16[8,64,512]{2,1,0:T(8,128)(2,1)} %broadcast_in_dim.2), calls=%async_computation | async-start | bytes 1048576 | tf_op jit(solution)/shard_map/all_to_all | solution.py:324
  21.7 16.7 %all-to-all-done.refs_0_ = bf16[8,64,512]{2,1,0:T(8,128)(2,1)S(1)} async-done(((bf16[8,64,512]{2,1,0:T(8,128)(2,1)}), bf16[8,64,512]{2,1,0:T(8,128)(2,1)S(1)}, u32[]{:S(2)}, u32[]{:S(2)}) %all-to-all-start) | async-done | bytes 524320 | tf_op jit(solution)/shard_map/all_to_all | solution.py:324
  41.5 3.4 %collective-permute-start.2 = (bf16[3,224,512]{2,1,0:T(8,128)(2,1)S(1)}, bf16[3,224,512]{2,1,0:T(8,128)(2,1)S(1)}, u32[]{:S(2)}, u32[]{:S(2)}) collective-permute-start(bf16[3,224,512]{2,1,0:T(8,128)(2,1)S(1)} %pad_maximum_fusion.1), channel_id=1, source_target_pairs={{0,384},{128,0},{256,128},{384,256},{1,385},{129,1},{257,129},{385... | collective-permute-start | bytes 2064392 | tf_op jit(solution)/shard_map/ppermute | solution.py:352
  44.9 13.1 %collective-permute-done = bf16[3,224,512]{2,1,0:T(8,128)(2,1)S(1)} collective-permute-done((bf16[3,224,512]{2,1,0:T(8,128)(2,1)S(1)}, bf16[3,224,512]{2,1,0:T(8,128)(2,1)S(1)}, u32[]{:S(2)}, u32[]{:S(2)}) %collective-permute-start) | collective-permute-done | bytes 688160 | tf_op jit(solution)/shard_map/ppermute | solution.py:351
  60.0 16.7 %collective-permute-done.1 = bf16[3,224,512]{2,1,0:T(8,128)(2,1)S(1)} collective-permute-done((bf16[3,224,512]{2,1,0:T(8,128)(2,1)S(1)}, bf16[3,224,512]{2,1,0:T(8,128)(2,1)S(1)}, u32[]{:S(2)}, u32[]{:S(2)}) %collective-permute-start.1) | collective-permute-done | bytes 688160 | tf_op jit(solution)/shard_map/ppermute | solution.py:353
  77.2 4.1 %collective-permute-start.3 = (bf16[4,3,224,512]{3,2,1,0:T(8,128)(2,1)S(1)}, bf16[4,3,224,512]{3,2,1,0:T(8,128)(2,1)}, u32[]{:S(2)}, u32[]{:S(2)}) collective-permute-start(bf16[4,3,224,512]{3,2,1,0:T(8,128)(2,1)S(1)} %pad_maximum_fusion.mine), channel_id=1, source_target_pairs={{0,64},{64,0},{1,65},{65,1},{2,66},{66,2},{3,67},{67,3},{4,68},{68... | collective-permute-start | bytes 8257544 | tf_op jit(solution)/shard_map/ppermute | solution.py:355
  84.5 3.9 %collective-permute-start.8 = (bf16[8,64,512]{2,1,0:T(8,128)(2,1)S(1)}, bf16[8,64,512]{2,1,0:T(8,128)(2,1)S(1)}, u32[]{:S(2)}, u32[]{:S(2)}) collective-permute-start(bf16[8,64,512]{2,1,0:T(8,128)(2,1)S(1)} %copy-done.2), channel_id=1, source_target_pairs={{0,7},{1,0},{2,1},{3,2},{4,3},{5,4},{6,5},{7,6},{8,15},{9,8},{10,9... | collective-permute-start | bytes 1572872 | tf_op jit(solution)/shard_map/ppermute | solution.py:339
  88.4 20.8 %collective-permute-done.4.refs_1_ = bf16[8,64,512]{2,1,0:T(8,128)(2,1)S(1)} collective-permute-done((bf16[8,64,512]{2,1,0:T(8,128)(2,1)S(1)}, bf16[8,64,512]{2,1,0:T(8,128)(2,1)S(1)}, u32[]{:S(2)}, u32[]{:S(2)}) %collective-permute-start.4) | collective-permute-done | bytes 524320 | tf_op jit(solution)/shard_map/ppermute | solution.py:337
  111.2 4.4 %collective-permute-start.9 = (bf16[8,64,512]{2,1,0:T(8,128)(2,1)S(1)}, bf16[8,64,512]{2,1,0:T(8,128)(2,1)}, u32[]{:S(2)}, u32[]{:S(2)}) collective-permute-start(bf16[8,64,512]{2,1,0:T(8,128)(2,1)S(1)} %collective-permute-done.8.refs_7_), channel_id=1, source_target_pairs={{0,7},{1,0},{2,1},{3,2},{4,3},{5,4},{6,5},{7,6},{8,15},{9,8},{10,9... | collective-permute-start | bytes 1572872 | tf_op jit(solution)/shard_map/ppermute | solution.py:339
  115.7 9.1 %collective-permute-done.5.refs_2_ = bf16[8,64,512]{2,1,0:T(8,128)(2,1)S(1)} collective-permute-done((bf16[8,64,512]{2,1,0:T(8,128)(2,1)S(1)}, bf16[8,64,512]{2,1,0:T(8,128)(2,1)S(1)}, u32[]{:S(2)}, u32[]{:S(2)}) %collective-permute-start.5) | collective-permute-done | bytes 524320 | tf_op jit(solution)/shard_map/ppermute | solution.py:337
  126.8 4.6 %collective-permute-start.10 = (bf16[8,64,512]{2,1,0:T(8,128)(2,1)}, bf16[8,64,512]{2,1,0:T(8,128)(2,1)}, u32[]{:S(2)}, u32[]{:S(2)}) collective-permute-start(bf16[8,64,512]{2,1,0:T(8,128)(2,1)} %collective-permute-done.9.refs_6_), channel_id=1, source_target_pairs={{0,7},{1,0},{2,1},{3,2},{4,3},{5,4},{6,5},{7,6},{8,15},{9,8},{10,9... | collective-permute-start | bytes 1572872 | tf_op jit(solution)/shard_map/ppermute | solution.py:339
  131.3 8.3 %collective-permute-done.6.refs_3_ = bf16[8,64,512]{2,1,0:T(8,128)(2,1)} collective-permute-done((bf16[8,64,512]{2,1,0:T(8,128)(2,1)S(1)}, bf16[8,64,512]{2,1,0:T(8,128)(2,1)}, u32[]{:S(2)}, u32[]{:S(2)}) %collective-permute-start.6) | collective-permute-done | bytes 524320 | tf_op jit(solution)/shard_map/ppermute | solution.py:337
  142.8 11.0 %collective-permute-done.7.refs_4_ = bf16[8,64,512]{2,1,0:T(8,128)(2,1)} collective-permute-done((bf16[8,64,512]{2,1,0:T(8,128)(2,1)}, bf16[8,64,512]{2,1,0:T(8,128)(2,1)}, u32[]{:S(2)}, u32[]{:S(2)}) %collective-permute-start.7) | collective-permute-done | bytes 524320 | tf_op jit(solution)/shard_map/ppermute | solution.py:337
  153.8 8.2 %cotangent_gram.1 = (bf16[8,8,64,512]{3,2,1,0:T(8,128)(2,1)}, f32[2,256,256]{2,1,0:T(8,128)}) custom-call(s32[4]{0:T(128)} %pad_add_fusion.idx, bf16[8,64,512]{2,1,0:T(8,128)(2,1)} %copy-done.1, bf16[8,64,512]{2,1,0:T(8,128)(2,1)} %copy-done.3, bf16[8,64,512]{2,1,0:T(8,128)(2,1)} %copy-done.5, bf16[8,64,512]{2,1,0:T(8,128)(2,1)} %collective-permute-done.6.refs_3_, ...), custom_call_target="tpu_custom_call" | custom-call | flops 1073741824 | bytes 9437184 | tf_op jit(solution)/shard_map/cotangent_gram/pallas_call | solution.py:84
  162.0 5.6 %back.1 = f32[224,512]{1,0:T(8,128)} custom-call(s32[4]{0:T(128)} %pad_add_fusion.idx, bf16[8,8,64,512]{3,2,1,0:T(8,128)(2,1)} %get-tuple-element.18.dy, bf16[4,3,224,512]{3,2,1,0:T(8,128)(2,1)} %copy-done, bf16[4,3,224,512]{3,2,1,0:T(8,128)(2,1)} %collective-permute-done.3.other), custom_call_target="tpu_custom_call" | custom-call | flops 939524096 | bytes 7340032 | tf_op jit(solution)/shard_map/back/pallas_call | solution.py:115
  167.6 7.9 %hidden.1 = (bf16[224,512]{1,0:T(8,128)(2,1)}, f32[1,512]{1,0:T(1,128)}, f32[8,8,128]{2,1,0:T(8,128)}, bf16[2,224,512]{2,1,0:T(8,128)(2,1)}) custom-call(s32[4]{0:T(128)} %pad_add_fusion.idx, bf16[8,512,512]{2,1,0:T(8,128)(2,1)} %bitcast.21, bf16[4,3,224,512]{3,2,1,0:T(8,128)(2,1)} %copy-done, bf16[4,3,224,512]{3,2,1,0:T(8,128)(2,1)} %collective-permute-done.3.other, ...), custom_call_target="tpu_custom_call" | custom-call | flops 1879048192 | bytes 14680064 | tf_op jit(solution)/shard_map/hidden/pallas_call | solution.py:179
  175.5 7.5 %all-to-all-start.1 = ((f32[8,8,128]{2,1,0:T(8,128)}), f32[8,8,128]{2,1,0:T(8,128)S(1)}, u32[]{:S(2)}, u32[]{:S(2)}) async-start(f32[8,8,128]{2,1,0:T(8,128)} %get-tuple-element.19), calls=%async_computation.1 | async-start | bytes 65536 | tf_op jit(solution)/shard_map/all_to_all | solution.py:330
  183.1 9.8 %gain_term.1.gain_part = f32[8,32,128]{2,1,0:T(8,128)} custom-call(s32[4]{0:T(128)} %pad_add_fusion.idx, bf16[2,224,512]{2,1,0:T(8,128)(2,1)} %get-tuple-element.21.grads, f32[1,512]{1,0:T(1,128)} %get-tuple-element.22.inverse, bf16[8,512,512]{2,1,0:T(8,128)(2,1)} %bitcast.22, bf16[4,3,224,512]{3,2,1,0:T(8,128)(2,1)} %copy-done, ...), custom_call_target="tpu_custom_call" | custom-call | flops 2818572288 | bytes 9437184 | tf_op jit(solution)/shard_map/gain_term/pallas_call | solution.py:230
  195.1 12.4 %all_to_all.30.part = f32[8,40,128]{2,1,0:T(8,128)} all-to-all(f32[8,40,128]{2,1,0:T(8,128)} %join_parts.1), channel_id=1, replica_groups=mesh['x'=4,'core'=2,'z'=8,'y'=8] {'z'}, dimensions={0} | all-to-all | bytes 327680 | tf_op jit(solution)/shard_map/all_to_all | solution.py:330
  209.1 5.2 %grad_down.1 = bf16[8,224,512]{2,1,0:T(8,128)(2,1)} custom-call(f32[8,40,128]{2,1,0:T(8,128)} %all_to_all.30.part, bf16[224,512]{1,0:T(8,128)(2,1)} %get-tuple-element.24.hidden, bf16[8,8,64,512]{3,2,1,0:T(8,128)(2,1)} %get-tuple-element.18.dy), custom_call_target="tpu_custom_call" | custom-call | flops 939524096 | bytes 6291456 | tf_op jit(solution)/shard_map/grad_down/pallas_call | solution.py:310
  214.4 14.4 %all_to_all.31.part = f32[8,32,128]{2,1,0:T(8,128)} all-to-all(f32[8,32,128]{2,1,0:T(8,128)S(1)} %copy-done.6), channel_id=1, replica_groups=mesh['x'=4,'core'=2,'z'=8,'y'=8] {'y'}, dimensions={0} | all-to-all | bytes 262144 | tf_op jit(solution)/shard_map/all_to_all | solution.py:330
  230.4 10.8 %all_to_all.32.part = f32[8,8,128]{2,1,0:T(8,128)} all-to-all(f32[8,8,128]{2,1,0:T(8,128)} %get-tuple-element.26), channel_id=1, replica_groups=mesh['x'=4,'core'=2,'z'=8,'y'=8] {'z'}, dimensions={0} | all-to-all | bytes 65536 | tf_op jit(solution)/shard_map/all_to_all | solution.py:330
  242.6 10.6 %all-to-all-start.5 = ((f32[8,8,128]{2,1,0:T(8,128)}), f32[8,8,128]{2,1,0:T(8,128)S(1)}, u32[]{:S(2)}, u32[]{:S(2)}) async-start(f32[8,8,128]{2,1,0:T(8,128)} %gain_scale.1), calls=%async_computation.6 | async-start | bytes 65536 | tf_op jit(solution)/shard_map/all_to_all | solution.py:330
  253.2 4.7 %all-to-all-done.5 = f32[8,8,128]{2,1,0:T(8,128)S(1)} async-done(((f32[8,8,128]{2,1,0:T(8,128)}), f32[8,8,128]{2,1,0:T(8,128)S(1)}, u32[]{:S(2)}, u32[]{:S(2)}) %all-to-all-start.5) | async-done | bytes 32800 | tf_op jit(solution)/shard_map/all_to_all | solution.py:330
  (48 shorter events, 28.7 us)
Async XLA Ops:
  7.2 160.5 %all-gather.2.cloned.1.call-start = ((), (), s32[]{:S(2)}) async-start(), calls=%async_computation.7 | async-start | bytes 4259840 | tf_op jit(solution)/shard_map/all_gather | solution.py:346
  9.6 28.8 %all-to-all-start = ((bf16[8,64,512]{2,1,0:T(8,128)(2,1)}), bf16[8,64,512]{2,1,0:T(8,128)(2,1)S(1)}, u32[]{:S(2)}, u32[]{:S(2)}) async-start(bf16[8,64,512]{2,1,0:T(8,128)(2,1)} %broadcast_in_dim.2), calls=%async_computation | async-start | bytes 1048576 | tf_op jit(solution)/shard_map/all_to_all | solution.py:324
  38.4 38.4 %copy-start.1 = (bf16[8,64,512]{2,1,0:T(8,128)(2,1)}, bf16[8,64,512]{2,1,0:T(8,128)(2,1)S(1)}, u32[]{:S(2)}) copy-start(bf16[8,64,512]{2,1,0:T(8,128)(2,1)S(1)} %all-to-all-done.refs_0_) | copy-start | bytes 1572868
  38.4 19.6 %collective-permute-start = (bf16[3,224,512]{2,1,0:T(8,128)(2,1)S(1)}, bf16[3,224,512]{2,1,0:T(8,128)(2,1)S(1)}, u32[]{:S(2)}, u32[]{:S(2)}) collective-permute-start(bf16[3,224,512]{2,1,0:T(8,128)(2,1)S(1)} %pad_maximum_fusion.1), channel_id=1, source_target_pairs={{0,128},{128,256},{256,384},{384,0},{1,129},{129,257},{257,385},{3... | collective-permute-start | bytes 2064392 | tf_op jit(solution)/shard_map/ppermute | solution.py:351
  41.5 18.5 %collective-permute-start.2 = (bf16[3,224,512]{2,1,0:T(8,128)(2,1)S(1)}, bf16[3,224,512]{2,1,0:T(8,128)(2,1)S(1)}, u32[]{:S(2)}, u32[]{:S(2)}) collective-permute-start(bf16[3,224,512]{2,1,0:T(8,128)(2,1)S(1)} %pad_maximum_fusion.1), channel_id=1, source_target_pairs={{0,384},{128,0},{256,128},{384,256},{1,385},{129,1},{257,129},{385... | collective-permute-start | bytes 2064392 | tf_op jit(solution)/shard_map/ppermute | solution.py:352
  58.0 18.8 %collective-permute-start.1 = (bf16[3,224,512]{2,1,0:T(8,128)(2,1)S(1)}, bf16[3,224,512]{2,1,0:T(8,128)(2,1)S(1)}, u32[]{:S(2)}, u32[]{:S(2)}) collective-permute-start(bf16[3,224,512]{2,1,0:T(8,128)(2,1)S(1)} %collective-permute-done), channel_id=1, source_target_pairs={{0,128},{128,256},{256,384},{384,0},{1,129},{129,257},{257,385},{3... | collective-permute-start | bytes 2064392 | tf_op jit(solution)/shard_map/ppermute | solution.py:353
  76.8 4.5 %copy-start.2 = (bf16[8,64,512]{2,1,0:T(8,128)(2,1)S(1)}, bf16[8,64,512]{2,1,0:T(8,128)(2,1)}, u32[]{:S(2)}) copy-start(bf16[8,64,512]{2,1,0:T(8,128)(2,1)} %copy-done.1) | copy-start | bytes 1572868
  76.8 64.8 %copy-start.8 = (f32[4096]{0:T(1024)S(1)}, f32[4096]{0:T(1024)}, u32[]{:S(2)}) copy-start(f32[4096]{0:T(1024)} %param.7) | copy-start | bytes 49156
  77.1 84.9 %copy-start = (bf16[4,3,224,512]{3,2,1,0:T(8,128)(2,1)}, bf16[4,3,224,512]{3,2,1,0:T(8,128)(2,1)S(1)}, u32[]{:S(2)}) copy-start(bf16[4,3,224,512]{3,2,1,0:T(8,128)(2,1)S(1)} %pad_maximum_fusion.mine) | copy-start | bytes 8257540
  77.2 84.9 %collective-permute-start.3 = (bf16[4,3,224,512]{3,2,1,0:T(8,128)(2,1)S(1)}, bf16[4,3,224,512]{3,2,1,0:T(8,128)(2,1)}, u32[]{:S(2)}, u32[]{:S(2)}) collective-permute-start(bf16[4,3,224,512]{3,2,1,0:T(8,128)(2,1)S(1)} %pad_maximum_fusion.mine), channel_id=1, source_target_pairs={{0,64},{64,0},{1,65},{65,1},{2,66},{66,2},{3,67},{67,3},{4,68},{68... | collective-permute-start | bytes 8257544 | tf_op jit(solution)/shard_map/ppermute | solution.py:355
  81.3 27.9 %collective-permute-start.4 = (bf16[8,64,512]{2,1,0:T(8,128)(2,1)S(1)}, bf16[8,64,512]{2,1,0:T(8,128)(2,1)S(1)}, u32[]{:S(2)}, u32[]{:S(2)}) collective-permute-start(bf16[8,64,512]{2,1,0:T(8,128)(2,1)S(1)} %copy-done.2), channel_id=1, source_target_pairs={{0,1},{1,2},{2,3},{3,4},{4,5},{5,6},{6,7},{7,0},{8,9},{9,10},{10,1... | collective-permute-start | bytes 1572872 | tf_op jit(solution)/shard_map/ppermute | solution.py:337
  84.5 26.7 %collective-permute-start.8 = (bf16[8,64,512]{2,1,0:T(8,128)(2,1)S(1)}, bf16[8,64,512]{2,1,0:T(8,128)(2,1)S(1)}, u32[]{:S(2)}, u32[]{:S(2)}) collective-permute-start(bf16[8,64,512]{2,1,0:T(8,128)(2,1)S(1)} %copy-done.2), channel_id=1, source_target_pairs={{0,7},{1,0},{2,1},{3,2},{4,3},{5,4},{6,5},{7,6},{8,15},{9,8},{10,9... | collective-permute-start | bytes 1572872 | tf_op jit(solution)/shard_map/ppermute | solution.py:339
  109.2 44.6 %copy-start.3 = (bf16[8,64,512]{2,1,0:T(8,128)(2,1)}, bf16[8,64,512]{2,1,0:T(8,128)(2,1)S(1)}, u32[]{:S(2)}) copy-start(bf16[8,64,512]{2,1,0:T(8,128)(2,1)S(1)} %collective-permute-done.4.refs_1_) | copy-start | bytes 1572868
  109.2 15.6 %collective-permute-start.5 = (bf16[8,64,512]{2,1,0:T(8,128)(2,1)S(1)}, bf16[8,64,512]{2,1,0:T(8,128)(2,1)S(1)}, u32[]{:S(2)}, u32[]{:S(2)}) collective-permute-start(bf16[8,64,512]{2,1,0:T(8,128)(2,1)S(1)} %collective-permute-done.4.refs_1_), channel_id=1, source_target_pairs={{0,1},{1,2},{2,3},{3,4},{4,5},{5,6},{6,7},{7,0},{8,9},{9,10},{10,1... | collective-permute-start | bytes 1572872 | tf_op jit(solution)/shard_map/ppermute | solution.py:337
  111.2 13.6 %copy-start.4 = (bf16[8,64,512]{2,1,0:T(8,128)(2,1)}, bf16[8,64,512]{2,1,0:T(8,128)(2,1)S(1)}, u32[]{:S(2)}) copy-start(bf16[8,64,512]{2,1,0:T(8,128)(2,1)S(1)} %collective-permute-done.8.refs_7_) | copy-start | bytes 1572868
  111.2 15.5 %collective-permute-start.9 = (bf16[8,64,512]{2,1,0:T(8,128)(2,1)S(1)}, bf16[8,64,512]{2,1,0:T(8,128)(2,1)}, u32[]{:S(2)}, u32[]{:S(2)}) collective-permute-start(bf16[8,64,512]{2,1,0:T(8,128)(2,1)S(1)} %collective-permute-done.8.refs_7_), channel_id=1, source_target_pairs={{0,7},{1,0},{2,1},{3,2},{4,3},{5,4},{6,5},{7,6},{8,15},{9,8},{10,9... | collective-permute-start | bytes 1572872 | tf_op jit(solution)/shard_map/ppermute | solution.py:339
  124.8 1.9 copy-start.5
  124.8 14.8 %collective-permute-start.6 = (bf16[8,64,512]{2,1,0:T(8,128)(2,1)S(1)}, bf16[8,64,512]{2,1,0:T(8,128)(2,1)}, u32[]{:S(2)}, u32[]{:S(2)}) collective-permute-start(bf16[8,64,512]{2,1,0:T(8,128)(2,1)S(1)} %collective-permute-done.5.refs_2_), channel_id=1, source_target_pairs={{0,1},{1,2},{2,3},{3,4},{4,5},{5,6},{6,7},{7,0},{8,9},{9,10},{10,1... | collective-permute-start | bytes 1572872 | tf_op jit(solution)/shard_map/ppermute | solution.py:337
  126.8 16.0 %collective-permute-start.10 = (bf16[8,64,512]{2,1,0:T(8,128)(2,1)}, bf16[8,64,512]{2,1,0:T(8,128)(2,1)}, u32[]{:S(2)}, u32[]{:S(2)}) collective-permute-start(bf16[8,64,512]{2,1,0:T(8,128)(2,1)} %collective-permute-done.9.refs_6_), channel_id=1, source_target_pairs={{0,7},{1,0},{2,1},{3,2},{4,3},{5,4},{6,5},{7,6},{8,15},{9,8},{10,9... | collective-permute-start | bytes 1572872 | tf_op jit(solution)/shard_map/ppermute | solution.py:339
  139.6 14.1 %collective-permute-start.7 = (bf16[8,64,512]{2,1,0:T(8,128)(2,1)}, bf16[8,64,512]{2,1,0:T(8,128)(2,1)}, u32[]{:S(2)}, u32[]{:S(2)}) collective-permute-start(bf16[8,64,512]{2,1,0:T(8,128)(2,1)} %collective-permute-done.6.refs_3_), channel_id=1, source_target_pairs={{0,1},{1,2},{2,3},{3,4},{4,5},{5,6},{6,7},{7,0},{8,9},{9,10},{10,1... | collective-permute-start | bytes 1572872 | tf_op jit(solution)/shard_map/ppermute | solution.py:337
  175.5 17.4 %all-to-all-start.1 = ((f32[8,8,128]{2,1,0:T(8,128)}), f32[8,8,128]{2,1,0:T(8,128)S(1)}, u32[]{:S(2)}, u32[]{:S(2)}) async-start(f32[8,8,128]{2,1,0:T(8,128)} %get-tuple-element.19), calls=%async_computation.1 | async-start | bytes 65536 | tf_op jit(solution)/shard_map/all_to_all | solution.py:330
  183.0 75.5 %reduce-scatter.2.cloned.1.call-start = ((), (), s32[]{:S(2)}) async-start(), calls=%async_computation.8 | async-start | bytes 2064384 | tf_op jit(solution)/shard_map/reduce_scatter | solution.py:370
  209.1 5.3 %copy-start.6 = (f32[8,32,128]{2,1,0:T(8,128)S(1)}, f32[8,32,128]{2,1,0:T(8,128)}, u32[]{:S(2)}) copy-start(f32[8,32,128]{2,1,0:T(8,128)} %add_parts.1) | copy-start | bytes 393220
  242.6 15.3 %all-to-all-start.5 = ((f32[8,8,128]{2,1,0:T(8,128)}), f32[8,8,128]{2,1,0:T(8,128)S(1)}, u32[]{:S(2)}, u32[]{:S(2)}) async-start(f32[8,8,128]{2,1,0:T(8,128)} %gain_scale.1), calls=%async_computation.6 | async-start | bytes 65536 | tf_op jit(solution)/shard_map/all_to_all | solution.py:330
  (1 other events, 0.6 us)
Sparse Core Ops, SparseCore 0:
  11.1 99.6 all-gather.1
  214.5 35.8 reduce-scatter.1

commit v7 on v6

--- a/solution.py
+++ b/solution.py
@@ -60,14 +60,22 @@
 
 
 def cotangent_kernel(idx, *refs):
-    pieces, (dy, gram, held, sems, out_sem) = refs[:NY], refs[NY:]
-    y = idx[2]
+    pieces, (mine, other, dy, gram, back, held, down, sems, down_sems, out_sem) = refs[:NY], refs[NY:]
+    core, y, x = idx[1], idx[2], idx[3]
+
+    def incoming(j):
+        return pltpu.make_async_copy(pieces[j], held.at[:, lax.rem(y - j + NY, NY)], sems.at[j])
+
+    def weight(which, ref, i):
+        return pltpu.make_async_copy(ref.at[i, 2], down.at[which, i], down_sems.at[which, i])
+
     for j in range(NY):
-        slot = lax.rem(y - j + NY, NY)
-        pltpu.make_async_copy(pieces[j], held.at[:, slot], sems.at[j]).start()
+        incoming(j).start()
+    for which, ref in enumerate((mine, other)):
+        for i in range(NX):
+            weight(which, ref, i).start()
     for j in range(NY):
-        slot = lax.rem(y - j + NY, NY)
-        pltpu.make_async_copy(pieces[j], held.at[:, slot], sems.at[j]).wait()
+        incoming(j).wait()
     keep = pltpu.make_async_copy(held, dy, out_sem)
     keep.start()
     for h in range(2):
@@ -77,54 +85,43 @@
             return acc + lax.dot_general(block, block, TN, preferred_element_type=F32)
 
         gram[h] = lax.fori_loop(0, NZ, step, jnp.zeros((HALF, HALF), F32))
+    for which, ref in enumerate((mine, other)):
+        for i in range(NX):
+            weight(which, ref, i).wait()
+    back[...] = jnp.zeros_like(back)
+
+    def share(i, carry):
+        chip = lax.rem(x - i + NX, NX)
+        for which, d in ((0, core), (1, 1 - core)):
+            block = held[2 * chip + d].reshape(SHARE, TOK)
+            back[...] += jnp.dot(down[which, i], block, preferred_element_type=F32)
+        return carry
+
+    lax.fori_loop(0, NX, share, 0)
     keep.wait()
 
 
-def cotangent_call(idx, pieces):
+def cotangent_call(idx, pieces, mine, other):
     return pl.pallas_call(
         cotangent_kernel,
         out_shape=(
             jax.ShapeDtypeStruct((NZ, NY, COLS, TOK), BF16),
             jax.ShapeDtypeStruct((2, HALF, HALF), F32),
-        ),
-        in_specs=[SMEM] + [ANY] * NY,
-        out_specs=(ANY, VMEM),
+            jax.ShapeDtypeStruct((UNITS, TOK), F32),
+        ),
+        in_specs=[SMEM] + [ANY] * (NY + 2),
+        out_specs=(ANY, VMEM, VMEM),
         scratch_shapes=[
             pltpu.VMEM((NZ, NY, COLS, TOK), BF16),
+            pltpu.VMEM((2, NX, UNITS, SHARE), BF16),
             pltpu.SemaphoreType.DMA((NY,)),
+            pltpu.SemaphoreType.DMA((2, NX)),
             pltpu.SemaphoreType.DMA,
         ],
         compiler_params=params(60),
-        cost_estimate=cost(TOK * HALF * FEATURES, 9 << 20),
-        name="cotangent_gram",
-    )(idx, *pieces)
-
-
-def back_kernel(idx, dy, mine, other, back):
-    core = idx[1]
-
-    @pl.when(pl.program_id(0) == 0)
-    def _():
-        back[...] = jnp.zeros_like(back)
-
-    back[...] += jnp.dot(mine[0, 0], dy[core].reshape(SHARE, TOK), preferred_element_type=F32)
-    back[...] += jnp.dot(other[0, 0], dy[1 - core].reshape(SHARE, TOK), preferred_element_type=F32)
-
-
-def back_call(idx, dy, mine, other):
-    return pl.pallas_call(
-        back_kernel,
-        out_shape=jax.ShapeDtypeStruct((UNITS, TOK), F32),
-        grid_spec=pltpu.PrefetchScalarGridSpec(
-            num_scalar_prefetch=1,
-            grid=(NX,),
-            in_specs=[rotated((2, NY, COLS, TOK)), weights(2, 1), weights(2, 1)],
-            out_specs=fixed((UNITS, TOK)),
-        ),
-        compiler_params=params(60),
-        cost_estimate=cost(UNITS * TOK * FEATURES, 7 << 20),
-        name="back",
-    )(idx, dy, mine, other)
+        cost_estimate=cost((UNITS + HALF) * TOK * FEATURES, 11 << 20),
+        name="cotangent",
+    )(idx, *pieces, mine, other)
 
 
 def hidden_kernel(idx, xs, mine, other, gain, dy_gram, back, hidden, inverse, down_sq, grads, acc, squares):
@@ -261,16 +258,6 @@
     )
 
 
-def add_kernel(part, out):
-    total = jnp.sum(part[:, LOCAL:, :], axis=0, keepdims=True)
-    out[...] = jnp.broadcast_to(total, out.shape)
-
-
-def add_call(part):
-    shape = (NY, part.shape[1] - LOCAL, 128)
-    return pl.pallas_call(add_kernel, out_shape=jax.ShapeDtypeStruct(shape, F32), name="add_parts")(part)
-
-
 def gain_sq_kernel(part, total, square):
     gain = jnp.sum(part[...], axis=0)
     total[...] = gain
@@ -288,7 +275,7 @@
     out[...] = jnp.broadcast_to(value[None], out.shape)
 
 
-def grad_kernel(part, hidden, dy, out, scaled):
+def grad_kernel(part, hidden, dy, out, added, scaled):
     @pl.when(pl.program_id(0) == 0)
     def _():
         bound = 0.6 * math.sqrt(SEQ * FF * FEATURES)
@@ -300,6 +287,8 @@
             axis=1,
         )
         scaled[...] = (hidden[...].astype(F32) * row).astype(BF16)
+        gain = jnp.sum(part[:, LOCAL:, :], axis=0, keepdims=True)
+        added[...] = jnp.broadcast_to(gain, added.shape)
 
     for d in range(2):
         block = dy[d].reshape(SHARE, TOK)
@@ -307,12 +296,16 @@
 
 
 def grad_call(part, hidden, dy):
+    gain_shape = (NY, part.shape[1] - LOCAL, 128)
     return pl.pallas_call(
         grad_kernel,
         grid=(NZ // 2,),
-        out_shape=jax.ShapeDtypeStruct((NX * NC, UNITS, SHARE), BF16),
+        out_shape=(
+            jax.ShapeDtypeStruct((NX * NC, UNITS, SHARE), BF16),
+            jax.ShapeDtypeStruct(gain_shape, F32),
+        ),
         in_specs=[whole(part.shape), whole((UNITS, TOK)), lead((2, NY, COLS, TOK))],
-        out_specs=lead((2, UNITS, SHARE)),
+        out_specs=(lead((2, UNITS, SHARE)), whole(gain_shape)),
         scratch_shapes=[pltpu.VMEM((UNITS, TOK), BF16)],
         compiler_params=params(60),
         cost_estimate=cost(UNITS * TOK * FEATURES, 6 << 20),
@@ -330,14 +323,9 @@
     return lax.all_to_all(blocks, axis, split_axis=0, concat_axis=0, tiled=True)
 
 
-def ring(block, axis, size):
-    shift = lambda k: [(i, (i + k) % size) for i in range(size)]
-    up, down = [block], [block]
-    for step in range(size // 2):
-        up.append(lax.ppermute(up[-1], axis, shift(1)))
-        if step < size // 2 - 1:
-            down.append(lax.ppermute(down[-1], axis, shift(-1)))
-    return up + down[:0:-1]
+def turn(block, axis, k):
+    size = lax.axis_size(axis)
+    return lax.ppermute(block, axis, [(i, (i + k) % size) for i in range(size)])
 
 
 def body(tokens, gain, cotangent, gate_weight, up_weight, down_weight):
@@ -347,16 +335,18 @@
     dy_part = spread(cotangent.T, "z", NZ)
     block = jnp.stack([gate_weight.T, up_weight.T, down_weight])
     block, dy_part = lax.optimization_barrier((block, dy_part))
-    turn = lambda k: [(i, (i + k) % NX) for i in range(NX)]
-    right = lax.ppermute(block, "x", turn(1))
-    left = lax.ppermute(block, "x", turn(-1))
-    far = lax.ppermute(right, "x", turn(1))
+    stage = lax.optimization_barrier(
+        (turn(dy_part, "y", 1), turn(dy_part, "y", -1), turn(block, "x", 1), turn(block, "x", -1))
+    )
+    up_1, down_1, right, left = stage
+    up_2, down_2, far = lax.optimization_barrier((turn(up_1, "y", 1), turn(down_1, "y", -1), turn(right, "x", 1)))
+    up_3, down_3 = lax.optimization_barrier((turn(up_2, "y", 1), turn(down_2, "y", -1)))
     mine = jnp.stack([block, right, far, left])
-    other = lax.ppermute(mine, "core", [(0, 1), (1, 0)])
-    dy_pieces = ring(dy_part, "y", NY)
-
-    dy, dy_gram = cotangent_call(idx, dy_pieces)
-    back = back_call(idx, dy, mine, other)
+    other = turn(mine, "core", 1)
+    up_4 = turn(up_3, "y", 1)
+    dy_pieces = [dy_part, up_1, up_2, up_3, up_4, down_3, down_2, down_1]
+
+    dy, dy_gram, back = cotangent_call(idx, dy_pieces, mine, other)
     hidden, inverse, sq_part, grads = hidden_call(
         idx, xs, mine, other, gain.reshape(NX * NC, SHARE), dy_gram, back
     )
@@ -364,9 +354,7 @@
     grads, sq_part = lax.optimization_barrier((grads, sq_part))
     gain_part = gain_call(idx, grads, inverse, xs, mine, other)
     part = exchange(join_call(part, gain_part), "z")
-    added = add_call(part)
-    part, added = lax.optimization_barrier((part, added))
-    terms = grad_call(part, hidden, dy)
+    terms, added = grad_call(part, hidden, dy)
     grad_down = lax.psum_scatter(terms, dp, scatter_dimension=0).astype(F32)
 
     gain_z, gain_sq = pl.pallas_call(

time: 268 us -> 242 us (0.903)
  waiting for transfers between devices: 101 us -> 78.1 us
  Pallas kernels: 43 us -> 38.2 us
    ppermute x11, waiting for transfers between devices: 79.1 us -> 56 us  [turn(): return lax.ppermute(block, axis, [(i, (i + k) % size) for i in range(size)])]
    pallas_call x3 -> x1, Pallas kernels: 12.4 us -> 5.21 us  [grad_call(): pl.pallas_call(grad_kernel, grid=(NZ // 2,), out_shape=(jax.ShapeDtypeStr...]
    ppermute x11, starting transfers between devices: 34.5 us -> 37.6 us  [turn(): return lax.ppermute(block, axis, [(i, (i + k) % size) for i in range(size)])]
    all_to_all x2, starting transfers between devices: 18.1 us -> 15.2 us  [exchange(): return lax.all_to_all(blocks, axis, split_axis=0, concat_axis=0, tiled=True)]
  transfers between devices with their start and end apart: 16 -> 16, of which waited for: 8 -> 9; matrix products, arithmetic and copies ran while one was open for 2% -> 2% of each run, Pallas kernels for 10% -> 10%
where the time goes in v7:
time: 242 us; the launch traced here: 241 us
  waiting for transfers between devices  78.1 us (32%)
  starting transfers between devices  63.7 us (26%)
  Pallas kernels  38.2 us (16%)
  blocking collectives  37.8 us (16%)
  between operations  14.2 us (6%)
  other arithmetic  4.58 us (2%)
  local copies, waits for them, and re-layouts  3.77 us (2%)
    ppermute x11, waiting for transfers between devices, turn(): return lax.ppermute(block, axis, [(i, (i + k) % size) for i in range(size)])  56 us
    all_to_all x3, blocking collectives, exchange(): return lax.all_to_all(blocks, axis, split_axis=0, concat_axis=0, tiled=True)  37.8 us
    ppermute x11, starting transfers between devices, turn(): return lax.ppermute(block, axis, [(i, (i + k) % size) for i in range(size)])  37.6 us
    all_to_all x1, waiting for transfers between devices, spread(): lax.all_to_all(jnp.broadcast_to(block[None], (count,) + block.shape), axi...  16.7 us
    all_to_all x2, starting transfers between devices, exchange(): return lax.all_to_all(blocks, axis, split_axis=0, concat_axis=0, tiled=True)  15.2 us
    all_to_all x1, starting transfers between devices, spread(): lax.all_to_all(jnp.broadcast_to(block[None], (count,) + block.shape), axi...  10.9 us
    pallas_call x1, Pallas kernels, cotangent_call(): pl.pallas_call(cotangent_kernel, out_shape=(jax.ShapeDtypeStruct((NZ, NY,...  10.7 us
    pallas_call x1, Pallas kernels, gain_call(): pl.pallas_call(gain_kernel, out_shape=jax.ShapeDtypeStruct((NZ, SHARE //...  9.83 us
  transfers between devices with their start and end apart: 16, of which 9 were waited for; matrix products, arithmetic and copies ran while one was open for 2% of the time, Pallas kernels for 10%

profile of v7, /device:TPU:1, one launch (start us, length us, event | category | flops | bytes accessed | tf_op | source)
XLA Modules:
  0.0 240.5 jit_solution(16411062335936622217)
XLA Ops:
  9.6 10.9 %all-to-all-start = ((bf16[8,64,512]{2,1,0:T(8,128)(2,1)}), bf16[8,64,512]{2,1,0:T(8,128)(2,1)S(1)}, u32[]{:S(2)}, u32[]{:S(2)}) async-start(bf16[8,64,512]{2,1,0:T(8,128)(2,1)} %broadcast_in_dim.2), calls=%async_computation | async-start | bytes 1048576 | tf_op jit(solution)/shard_map/all_to_all | solution.py:317
  21.7 16.7 %all-to-all-done.refs_0_ = bf16[8,64,512]{2,1,0:T(8,128)(2,1)S(1)} async-done(((bf16[8,64,512]{2,1,0:T(8,128)(2,1)}), bf16[8,64,512]{2,1,0:T(8,128)(2,1)S(1)}, u32[]{:S(2)}, u32[]{:S(2)}) %all-to-all-start) | async-done | bytes 524320 | tf_op jit(solution)/shard_map/all_to_all | solution.py:317
  41.5 3.4 %collective-permute-start.3 = (bf16[3,224,512]{2,1,0:T(8,128)(2,1)S(1)}, bf16[3,224,512]{2,1,0:T(8,128)(2,1)S(1)}, u32[]{:S(2)}, u32[]{:S(2)}) collective-permute-start(bf16[3,224,512]{2,1,0:T(8,128)(2,1)S(1)} %pad_maximum_fusion.1), channel_id=1, source_target_pairs={{0,384},{128,0},{256,128},{384,256},{1,385},{129,1},{257,129},{385... | collective-permute-start | bytes 2064392 | tf_op jit(solution)/shard_map/ppermute | solution.py:328
  44.9 3.2 %collective-permute-start = (bf16[8,64,512]{2,1,0:T(8,128)(2,1)S(1)}, bf16[8,64,512]{2,1,0:T(8,128)(2,1)S(1)}, u32[]{:S(2)}, u32[]{:S(2)}) collective-permute-start(bf16[8,64,512]{2,1,0:T(8,128)(2,1)S(1)} %all-to-all-done.refs_0_), channel_id=1, source_target_pairs={{0,1},{1,2},{2,3},{3,4},{4,5},{5,6},{6,7},{7,0},{8,9},{9,10},{10,1... | collective-permute-start | bytes 1572872 | tf_op jit(solution)/shard_map/ppermute | solution.py:328
  48.1 3.8 %collective-permute-start.1 = (bf16[8,64,512]{2,1,0:T(8,128)(2,1)S(1)}, bf16[8,64,512]{2,1,0:T(8,128)(2,1)S(1)}, u32[]{:S(2)}, u32[]{:S(2)}) collective-permute-start(bf16[8,64,512]{2,1,0:T(8,128)(2,1)S(1)} %all-to-all-done.refs_0_), channel_id=1, source_target_pairs={{0,7},{1,0},{2,1},{3,2},{4,3},{5,4},{6,5},{7,6},{8,15},{9,8},{10,9... | collective-permute-start | bytes 1572872 | tf_op jit(solution)/shard_map/ppermute | solution.py:328
  52.0 10.1 %collective-permute-done.refs_1_ = bf16[8,64,512]{2,1,0:T(8,128)(2,1)S(1)} collective-permute-done((bf16[8,64,512]{2,1,0:T(8,128)(2,1)S(1)}, bf16[8,64,512]{2,1,0:T(8,128)(2,1)S(1)}, u32[]{:S(2)}, u32[]{:S(2)}) %collective-permute-start) | collective-permute-done | bytes 524320 | tf_op jit(solution)/shard_map/ppermute | solution.py:328
  68.3 3.5 %collective-permute-start.5 = (bf16[8,64,512]{2,1,0:T(8,128)(2,1)S(1)}, bf16[8,64,512]{2,1,0:T(8,128)(2,1)S(1)}, u32[]{:S(2)}, u32[]{:S(2)}) collective-permute-start(bf16[8,64,512]{2,1,0:T(8,128)(2,1)S(1)} %collective-permute-done.1.refs_7_), channel_id=1, source_target_pairs={{0,7},{1,0},{2,1},{3,2},{4,3},{5,4},{6,5},{7,6},{8,15},{9,8},{10,9... | collective-permute-start | bytes 1572872 | tf_op jit(solution)/shard_map/ppermute | solution.py:328
  71.8 12.6 %collective-permute-done.4.refs_2_ = bf16[8,64,512]{2,1,0:T(8,128)(2,1)S(1)} collective-permute-done((bf16[8,64,512]{2,1,0:T(8,128)(2,1)S(1)}, bf16[8,64,512]{2,1,0:T(8,128)(2,1)S(1)}, u32[]{:S(2)}, u32[]{:S(2)}) %collective-permute-start.4) | collective-permute-done | bytes 524320 | tf_op jit(solution)/shard_map/ppermute | solution.py:328
  84.4 9.3 %collective-permute-done.5.refs_6_ = bf16[8,64,512]{2,1,0:T(8,128)(2,1)S(1)} collective-permute-done((bf16[8,64,512]{2,1,0:T(8,128)(2,1)S(1)}, bf16[8,64,512]{2,1,0:T(8,128)(2,1)S(1)}, u32[]{:S(2)}, u32[]{:S(2)}) %collective-permute-start.5) | collective-permute-done | bytes 524320 | tf_op jit(solution)/shard_map/ppermute | solution.py:328
  94.2 5.0 %collective-permute-start.7 = (bf16[4,3,224,512]{3,2,1,0:T(8,128)(2,1)S(1)}, bf16[4,3,224,512]{3,2,1,0:T(8,128)(2,1)}, u32[]{:S(2)}, u32[]{:S(2)}) collective-permute-start(bf16[4,3,224,512]{3,2,1,0:T(8,128)(2,1)S(1)} %pad_maximum_fusion.refs_8_.mine), channel_id=1, source_target_pairs={{0,64},{64,0},{1,65},{65,1},{2,66},{66,2},{3,67},{67,3},{4,68},{68... | collective-permute-start | bytes 8257544 | tf_op jit(solution)/shard_map/ppermute | solution.py:328
  99.2 3.7 %collective-permute-start.8 = (bf16[8,64,512]{2,1,0:T(8,128)(2,1)S(1)}, bf16[8,64,512]{2,1,0:T(8,128)(2,1)S(1)}, u32[]{:S(2)}, u32[]{:S(2)}) collective-permute-start(bf16[8,64,512]{2,1,0:T(8,128)(2,1)S(1)} %collective-permute-done.4.refs_2_), channel_id=1, source_target_pairs={{0,1},{1,2},{2,3},{3,4},{4,5},{5,6},{6,7},{7,0},{8,9},{9,10},{10,1... | collective-permute-start | bytes 1572872 | tf_op jit(solution)/shard_map/ppermute | solution.py:328
  105.7 11.5 %collective-permute-done.8.refs_3_ = bf16[8,64,512]{2,1,0:T(8,128)(2,1)S(1)} collective-permute-done((bf16[8,64,512]{2,1,0:T(8,128)(2,1)S(1)}, bf16[8,64,512]{2,1,0:T(8,128)(2,1)S(1)}, u32[]{:S(2)}, u32[]{:S(2)}) %collective-permute-start.8) | collective-permute-done | bytes 524320 | tf_op jit(solution)/shard_map/ppermute | solution.py:328
  119.1 3.5 %collective-permute-start.10 = (bf16[8,64,512]{2,1,0:T(8,128)(2,1)S(1)}, bf16[8,64,512]{2,1,0:T(8,128)(2,1)}, u32[]{:S(2)}, u32[]{:S(2)}) collective-permute-start(bf16[8,64,512]{2,1,0:T(8,128)(2,1)S(1)} %collective-permute-done.8.refs_3_), channel_id=1, source_target_pairs={{0,1},{1,2},{2,3},{3,4},{4,5},{5,6},{6,7},{7,0},{8,9},{9,10},{10,1... | collective-permute-start | bytes 1572872 | tf_op jit(solution)/shard_map/ppermute | solution.py:328
  123.9 10.7 %collective-permute-done.10.refs_4_ = bf16[8,64,512]{2,1,0:T(8,128)(2,1)} collective-permute-done((bf16[8,64,512]{2,1,0:T(8,128)(2,1)S(1)}, bf16[8,64,512]{2,1,0:T(8,128)(2,1)}, u32[]{:S(2)}, u32[]{:S(2)}) %collective-permute-start.10) | collective-permute-done | bytes 524320 | tf_op jit(solution)/shard_map/ppermute | solution.py:328
  134.6 10.7 %cotangent.1 = (bf16[8,8,64,512]{3,2,1,0:T(8,128)(2,1)}, f32[2,256,256]{2,1,0:T(8,128)}, f32[224,512]{1,0:T(8,128)}) custom-call(s32[4]{0:T(128)} %pad_add_fusion.idx, bf16[8,64,512]{2,1,0:T(8,128)(2,1)} %copy-done.1, bf16[8,64,512]{2,1,0:T(8,128)(2,1)} %copy-done.2, bf16[8,64,512]{2,1,0:T(8,128)(2,1)} %copy-done.4, bf16[8,64,512]{2,1,0:T(8,128)(2,1)} %copy-done.6, ...), custom_call_target="tpu_custom_call" | custom-call | flops 2013265920 | bytes 11534336 | tf_op jit(solution)/shard_map/cotangent/pallas_call | solution.py:105
  145.3 7.9 %hidden.1 = (bf16[224,512]{1,0:T(8,128)(2,1)}, f32[1,512]{1,0:T(1,128)}, f32[8,8,128]{2,1,0:T(8,128)}, bf16[2,224,512]{2,1,0:T(8,128)(2,1)}) custom-call(s32[4]{0:T(128)} %pad_add_fusion.idx, bf16[8,512,512]{2,1,0:T(8,128)(2,1)} %bitcast.21, bf16[4,3,224,512]{3,2,1,0:T(8,128)(2,1)} %copy-done, bf16[4,3,224,512]{3,2,1,0:T(8,128)(2,1)} %collective-permute-done.7.refs_9_.other, ...), custom_call_target="tpu_custom_call" | custom-call | flops 1879048192 | bytes 14680064 | tf_op jit(solution)/shard_map/hidden/pallas_call | solution.py:176
  153.2 5.4 %all-to-all-start.1 = ((f32[8,8,128]{2,1,0:T(8,128)}), f32[8,8,128]{2,1,0:T(8,128)S(1)}, u32[]{:S(2)}, u32[]{:S(2)}) async-start(f32[8,8,128]{2,1,0:T(8,128)} %get-tuple-element.38), calls=%async_computation.1 | async-start | bytes 65536 | tf_op jit(solution)/shard_map/all_to_all | solution.py:323
  158.7 9.8 %gain_term.1.gain_part = f32[8,32,128]{2,1,0:T(8,128)} custom-call(s32[4]{0:T(128)} %pad_add_fusion.idx, bf16[2,224,512]{2,1,0:T(8,128)(2,1)} %get-tuple-element.40.grads, f32[1,512]{1,0:T(1,128)} %get-tuple-element.41.inverse, bf16[8,512,512]{2,1,0:T(8,128)(2,1)} %bitcast.22, bf16[4,3,224,512]{3,2,1,0:T(8,128)(2,1)} %copy-done, ...), custom_call_target="tpu_custom_call" | custom-call | flops 2818572288 | bytes 9437184 | tf_op jit(solution)/shard_map/gain_term/pallas_call | solution.py:227
  170.7 12.4 %all_to_all.30.part = f32[8,40,128]{2,1,0:T(8,128)} all-to-all(f32[8,40,128]{2,1,0:T(8,128)} %join_parts.1), channel_id=1, replica_groups=mesh['x'=4,'core'=2,'z'=8,'y'=8] {'z'}, dimensions={0} | all-to-all | bytes 327680 | tf_op jit(solution)/shard_map/all_to_all | solution.py:323
  183.1 5.2 %grad_down.1 = (bf16[8,224,512]{2,1,0:T(8,128)(2,1)}, f32[8,32,128]{2,1,0:T(8,128)}) custom-call(f32[8,40,128]{2,1,0:T(8,128)} %all_to_all.30.part, bf16[224,512]{1,0:T(8,128)(2,1)} %get-tuple-element.42.hidden, bf16[8,8,64,512]{3,2,1,0:T(8,128)(2,1)} %get-tuple-element.43.dy), custom_call_target="tpu_custom_call" | custom-call | flops 939524096 | bytes 6291456 | tf_op jit(solution)/shard_map/grad_down/pallas_call | solution.py:300
  188.3 14.7 %all_to_all.31.part = f32[8,32,128]{2,1,0:T(8,128)} all-to-all(f32[8,32,128]{2,1,0:T(8,128)} %get-tuple-element.45), channel_id=1, replica_groups=mesh['x'=4,'core'=2,'z'=8,'y'=8] {'y'}, dimensions={0} | all-to-all | bytes 262144 | tf_op jit(solution)/shard_map/all_to_all | solution.py:323
  204.6 10.8 %all_to_all.32.part = f32[8,8,128]{2,1,0:T(8,128)} all-to-all(f32[8,8,128]{2,1,0:T(8,128)} %get-tuple-element.46), channel_id=1, replica_groups=mesh['x'=4,'core'=2,'z'=8,'y'=8] {'z'}, dimensions={0} | all-to-all | bytes 65536 | tf_op jit(solution)/shard_map/all_to_all | solution.py:323
  216.8 9.7 %all-to-all-start.5 = ((f32[8,8,128]{2,1,0:T(8,128)}), f32[8,8,128]{2,1,0:T(8,128)S(1)}, u32[]{:S(2)}, u32[]{:S(2)}) async-start(f32[8,8,128]{2,1,0:T(8,128)} %gain_scale.1), calls=%async_computation.6 | async-start | bytes 65536 | tf_op jit(solution)/shard_map/all_to_all | solution.py:323
  226.6 4.7 %all-to-all-done.5 = f32[8,8,128]{2,1,0:T(8,128)S(1)} async-done(((f32[8,8,128]{2,1,0:T(8,128)}), f32[8,8,128]{2,1,0:T(8,128)S(1)}, u32[]{:S(2)}, u32[]{:S(2)}) %all-to-all-start.5) | async-done | bytes 32800 | tf_op jit(solution)/shard_map/all_to_all | solution.py:323
  (48 shorter events, 27.1 us)
Async XLA Ops:
  7.2 138.2 %all-gather.2.cloned.1.call-start = ((), (), s32[]{:S(2)}) async-start(), calls=%async_computation.7 | async-start | bytes 4259840 | tf_op jit(solution)/shard_map/all_gather | solution.py:334
  9.6 28.8 %all-to-all-start = ((bf16[8,64,512]{2,1,0:T(8,128)(2,1)}), bf16[8,64,512]{2,1,0:T(8,128)(2,1)S(1)}, u32[]{:S(2)}, u32[]{:S(2)}) async-start(bf16[8,64,512]{2,1,0:T(8,128)(2,1)} %broadcast_in_dim.2), calls=%async_computation | async-start | bytes 1048576 | tf_op jit(solution)/shard_map/all_to_all | solution.py:317
  38.4 55.3 %copy-start.1 = (bf16[8,64,512]{2,1,0:T(8,128)(2,1)}, bf16[8,64,512]{2,1,0:T(8,128)(2,1)S(1)}, u32[]{:S(2)}) copy-start(bf16[8,64,512]{2,1,0:T(8,128)(2,1)S(1)} %all-to-all-done.refs_0_) | copy-start | bytes 1572868
  38.4 24.2 %collective-permute-start.2 = (bf16[3,224,512]{2,1,0:T(8,128)(2,1)S(1)}, bf16[3,224,512]{2,1,0:T(8,128)(2,1)S(1)}, u32[]{:S(2)}, u32[]{:S(2)}) collective-permute-start(bf16[3,224,512]{2,1,0:T(8,128)(2,1)S(1)} %pad_maximum_fusion.1), channel_id=1, source_target_pairs={{0,128},{128,256},{256,384},{384,0},{1,129},{129,257},{257,385},{3... | collective-permute-start | bytes 2064392 | tf_op jit(solution)/shard_map/ppermute | solution.py:328
  41.5 21.1 %collective-permute-start.3 = (bf16[3,224,512]{2,1,0:T(8,128)(2,1)S(1)}, bf16[3,224,512]{2,1,0:T(8,128)(2,1)S(1)}, u32[]{:S(2)}, u32[]{:S(2)}) collective-permute-start(bf16[3,224,512]{2,1,0:T(8,128)(2,1)S(1)} %pad_maximum_fusion.1), channel_id=1, source_target_pairs={{0,384},{128,0},{256,128},{384,256},{1,385},{129,1},{257,129},{385... | collective-permute-start | bytes 2064392 | tf_op jit(solution)/shard_map/ppermute | solution.py:328
  44.9 17.1 %collective-permute-start = (bf16[8,64,512]{2,1,0:T(8,128)(2,1)S(1)}, bf16[8,64,512]{2,1,0:T(8,128)(2,1)S(1)}, u32[]{:S(2)}, u32[]{:S(2)}) collective-permute-start(bf16[8,64,512]{2,1,0:T(8,128)(2,1)S(1)} %all-to-all-done.refs_0_), channel_id=1, source_target_pairs={{0,1},{1,2},{2,3},{3,4},{4,5},{5,6},{6,7},{7,0},{8,9},{9,10},{10,1... | collective-permute-start | bytes 1572872 | tf_op jit(solution)/shard_map/ppermute | solution.py:328
  48.1 14.5 %collective-permute-start.1 = (bf16[8,64,512]{2,1,0:T(8,128)(2,1)S(1)}, bf16[8,64,512]{2,1,0:T(8,128)(2,1)S(1)}, u32[]{:S(2)}, u32[]{:S(2)}) collective-permute-start(bf16[8,64,512]{2,1,0:T(8,128)(2,1)S(1)} %all-to-all-done.refs_0_), channel_id=1, source_target_pairs={{0,7},{1,0},{2,1},{3,2},{4,3},{5,4},{6,5},{7,6},{8,15},{9,8},{10,9... | collective-permute-start | bytes 1572872 | tf_op jit(solution)/shard_map/ppermute | solution.py:328
  62.0 31.7 %copy-start.2 = (bf16[8,64,512]{2,1,0:T(8,128)(2,1)}, bf16[8,64,512]{2,1,0:T(8,128)(2,1)S(1)}, u32[]{:S(2)}) copy-start(bf16[8,64,512]{2,1,0:T(8,128)(2,1)S(1)} %collective-permute-done.refs_1_) | copy-start | bytes 1572868
  62.6 31.1 %copy-start.3 = (bf16[8,64,512]{2,1,0:T(8,128)(2,1)}, bf16[8,64,512]{2,1,0:T(8,128)(2,1)S(1)}, u32[]{:S(2)}) copy-start(bf16[8,64,512]{2,1,0:T(8,128)(2,1)S(1)} %collective-permute-done.1.refs_7_) | copy-start | bytes 1572868
  62.6 31.1 %collective-permute-start.6 = (bf16[3,224,512]{2,1,0:T(8,128)(2,1)S(1)}, bf16[3,224,512]{2,1,0:T(8,128)(2,1)S(1)}, u32[]{:S(2)}, u32[]{:S(2)}) collective-permute-start(bf16[3,224,512]{2,1,0:T(8,128)(2,1)S(1)} %collective-permute-done.2), channel_id=1, source_target_pairs={{0,128},{128,256},{256,384},{384,0},{1,129},{129,257},{257,385},{3... | collective-permute-start | bytes 2064392 | tf_op jit(solution)/shard_map/ppermute | solution.py:328
  65.2 19.2 %collective-permute-start.4 = (bf16[8,64,512]{2,1,0:T(8,128)(2,1)S(1)}, bf16[8,64,512]{2,1,0:T(8,128)(2,1)S(1)}, u32[]{:S(2)}, u32[]{:S(2)}) collective-permute-start(bf16[8,64,512]{2,1,0:T(8,128)(2,1)S(1)} %collective-permute-done.refs_1_), channel_id=1, source_target_pairs={{0,1},{1,2},{2,3},{3,4},{4,5},{5,6},{6,7},{7,0},{8,9},{9,10},{10,1... | collective-permute-start | bytes 1572872 | tf_op jit(solution)/shard_map/ppermute | solution.py:328
  68.3 25.4 %collective-permute-start.5 = (bf16[8,64,512]{2,1,0:T(8,128)(2,1)S(1)}, bf16[8,64,512]{2,1,0:T(8,128)(2,1)S(1)}, u32[]{:S(2)}, u32[]{:S(2)}) collective-permute-start(bf16[8,64,512]{2,1,0:T(8,128)(2,1)S(1)} %collective-permute-done.1.refs_7_), channel_id=1, source_target_pairs={{0,7},{1,0},{2,1},{3,2},{4,3},{5,4},{6,5},{7,6},{8,15},{9,8},{10,9... | collective-permute-start | bytes 1572872 | tf_op jit(solution)/shard_map/ppermute | solution.py:328
  84.4 14.7 %copy-start.4 = (bf16[8,64,512]{2,1,0:T(8,128)(2,1)}, bf16[8,64,512]{2,1,0:T(8,128)(2,1)S(1)}, u32[]{:S(2)}) copy-start(bf16[8,64,512]{2,1,0:T(8,128)(2,1)S(1)} %collective-permute-done.4.refs_2_) | copy-start | bytes 1572868
  93.7 9.1 %copy-start.5 = (bf16[8,64,512]{2,1,0:T(8,128)(2,1)}, bf16[8,64,512]{2,1,0:T(8,128)(2,1)S(1)}, u32[]{:S(2)}) copy-start(bf16[8,64,512]{2,1,0:T(8,128)(2,1)S(1)} %collective-permute-done.5.refs_6_) | copy-start | bytes 1572868
  93.7 28.9 %copy-start.9 = (f32[4096]{0:T(1024)S(1)}, f32[4096]{0:T(1024)}, u32[]{:S(2)}) copy-start(f32[4096]{0:T(1024)} %param.7) | copy-start | bytes 49156
  94.2 40.5 %copy-start = (bf16[4,3,224,512]{3,2,1,0:T(8,128)(2,1)}, bf16[4,3,224,512]{3,2,1,0:T(8,128)(2,1)S(1)}, u32[]{:S(2)}) copy-start(bf16[4,3,224,512]{3,2,1,0:T(8,128)(2,1)S(1)} %pad_maximum_fusion.refs_8_.mine) | copy-start | bytes 8257540
  94.2 40.5 %collective-permute-start.7 = (bf16[4,3,224,512]{3,2,1,0:T(8,128)(2,1)S(1)}, bf16[4,3,224,512]{3,2,1,0:T(8,128)(2,1)}, u32[]{:S(2)}, u32[]{:S(2)}) collective-permute-start(bf16[4,3,224,512]{3,2,1,0:T(8,128)(2,1)S(1)} %pad_maximum_fusion.refs_8_.mine), channel_id=1, source_target_pairs={{0,64},{64,0},{1,65},{65,1},{2,66},{66,2},{3,67},{67,3},{4,68},{68... | collective-permute-start | bytes 8257544 | tf_op jit(solution)/shard_map/ppermute | solution.py:328
  99.2 18.0 %collective-permute-start.8 = (bf16[8,64,512]{2,1,0:T(8,128)(2,1)S(1)}, bf16[8,64,512]{2,1,0:T(8,128)(2,1)S(1)}, u32[]{:S(2)}, u32[]{:S(2)}) collective-permute-start(bf16[8,64,512]{2,1,0:T(8,128)(2,1)S(1)} %collective-permute-done.4.refs_2_), channel_id=1, source_target_pairs={{0,1},{1,2},{2,3},{3,4},{4,5},{5,6},{6,7},{7,0},{8,9},{9,10},{10,1... | collective-permute-start | bytes 1572872 | tf_op jit(solution)/shard_map/ppermute | solution.py:328
  102.8 15.5 %collective-permute-start.9 = (bf16[8,64,512]{2,1,0:T(8,128)(2,1)S(1)}, bf16[8,64,512]{2,1,0:T(8,128)(2,1)S(1)}, u32[]{:S(2)}, u32[]{:S(2)}) collective-permute-start(bf16[8,64,512]{2,1,0:T(8,128)(2,1)S(1)} %collective-permute-done.5.refs_6_), channel_id=1, source_target_pairs={{0,7},{1,0},{2,1},{3,2},{4,3},{5,4},{6,5},{7,6},{8,15},{9,8},{10,9... | collective-permute-start | bytes 1572872 | tf_op jit(solution)/shard_map/ppermute | solution.py:328
  117.2 17.5 %copy-start.6 = (bf16[8,64,512]{2,1,0:T(8,128)(2,1)}, bf16[8,64,512]{2,1,0:T(8,128)(2,1)S(1)}, u32[]{:S(2)}) copy-start(bf16[8,64,512]{2,1,0:T(8,128)(2,1)S(1)} %collective-permute-done.8.refs_3_) | copy-start | bytes 1572868
  119.1 15.5 %collective-permute-start.10 = (bf16[8,64,512]{2,1,0:T(8,128)(2,1)S(1)}, bf16[8,64,512]{2,1,0:T(8,128)(2,1)}, u32[]{:S(2)}, u32[]{:S(2)}) collective-permute-start(bf16[8,64,512]{2,1,0:T(8,128)(2,1)S(1)} %collective-permute-done.8.refs_3_), channel_id=1, source_target_pairs={{0,1},{1,2},{2,3},{3,4},{4,5},{5,6},{6,7},{7,0},{8,9},{9,10},{10,1... | collective-permute-start | bytes 1572872 | tf_op jit(solution)/shard_map/ppermute | solution.py:328
  153.2 15.3 %all-to-all-start.1 = ((f32[8,8,128]{2,1,0:T(8,128)}), f32[8,8,128]{2,1,0:T(8,128)S(1)}, u32[]{:S(2)}, u32[]{:S(2)}) async-start(f32[8,8,128]{2,1,0:T(8,128)} %get-tuple-element.38), calls=%async_computation.1 | async-start | bytes 65536 | tf_op jit(solution)/shard_map/all_to_all | solution.py:323
  158.7 73.3 %reduce-scatter.2.cloned.1.call-start = ((), (), s32[]{:S(2)}) async-start(), calls=%async_computation.8 | async-start | bytes 2064384 | tf_op jit(solution)/shard_map/reduce_scatter | solution.py:358
  216.8 14.5 %all-to-all-start.5 = ((f32[8,8,128]{2,1,0:T(8,128)}), f32[8,8,128]{2,1,0:T(8,128)S(1)}, u32[]{:S(2)}, u32[]{:S(2)}) async-start(f32[8,8,128]{2,1,0:T(8,128)} %gain_scale.1), calls=%async_computation.6 | async-start | bytes 65536 | tf_op jit(solution)/shard_map/all_to_all | solution.py:323
  (2 other events, 1.4 us)
Sparse Core Ops, SparseCore 0:
  11.1 96.5 all-gather.1
  188.5 35.3 reduce-scatter.1

commit v8 on v4

v8 whole, which is shorter than its diff:
```python
import math

import jax
import jax.numpy as jnp
from jax import lax
from jax.experimental import pallas as pl
from jax.experimental.pallas import tpu as pltpu
from jax.sharding import Mesh
from jax.sharding import PartitionSpec as P

FEATURES = 4096
FF = 14336
SEQ = 64
SEQS = 64
NX, NC, NZ, NY = 4, 2, 8, 8
LOCAL = 8
TOK = LOCAL * SEQ
UNITS = FF // (NZ * NY)
SHARE = FEATURES // (NX * NC)
COLS = FEATURES // (NZ * NY)
F32 = jnp.float32
BF16 = jnp.bfloat16

SMEM = pl.BlockSpec(memory_space=pltpu.SMEM)
VMEM = pl.BlockSpec(memory_space=pltpu.VMEM)


def params(mib):
    return pltpu.CompilerParams(vmem_limit_bytes=mib * 1024 * 1024)


def cost(macs, nbytes):
    return pl.CostEstimate(flops=2 * macs, bytes_accessed=nbytes, transcendentals=0)


TN = (((0,), (0,)), ((), ()))
NT = (((1,), (1,)), ((), ()))
HALF = TOK // 2
ANY = pl.BlockSpec(memory_space=pl.ANY)


def whole(shape):
    return pl.BlockSpec(shape, lambda i: (0,) * len(shape))


def lead(shape):
    return pl.BlockSpec(shape, lambda i: (i,) + (0,) * (len(shape) - 1))


def cotangent_kernel(idx, *refs):
    pieces, (weight, dy, gram, back, held, down, sems, down_sem, out_sem) = refs[:NY], refs[NY:]
    y = idx[1]

    def incoming(j):
        return pltpu.make_async_copy(pieces[j], held.at[:, lax.rem(y - j + NY, NY)], sems.at[j])

    fetch = pltpu.make_async_copy(weight.at[:, 2], down, down_sem)
    for j in range(NY):
        incoming(j).start()
    fetch.start()
    for j in range(NY):
        incoming(j).wait()
    keep = pltpu.make_async_copy(held, dy, out_sem)
    keep.start()
    for h in range(2):

        def step(z, acc):
            block = held[z, :, :, h * HALF : (h + 1) * HALF].reshape(SHARE, HALF)
            return acc + lax.dot_general(block, block, TN, preferred_element_type=F32)

        gram[h] = lax.fori_loop(0, NZ, step, jnp.zeros((HALF, HALF), F32))
    fetch.wait()
    back[...] = jnp.zeros_like(back)

    def share(d, carry):
        back[...] += jnp.dot(down[d], held[d].reshape(SHARE, TOK), preferred_element_type=F32)
        return carry

    lax.fori_loop(0, NX * NC, share, 0)
    keep.wait()


def cotangent_call(idx, pieces, weight):
    return pl.pallas_call(
        cotangent_kernel,
        out_shape=(
            jax.ShapeDtypeStruct((NZ, NY, COLS, TOK), BF16),
            jax.ShapeDtypeStruct((2, HALF, HALF), F32),
            jax.ShapeDtypeStruct((UNITS, TOK), F32),
        ),
        in_specs=[SMEM] + [ANY] * (NY + 1),
        out_specs=(ANY, VMEM, VMEM),
        scratch_shapes=[
            pltpu.VMEM((NZ, NY, COLS, TOK), BF16),
            pltpu.VMEM((NX * NC, UNITS, SHARE), BF16),
            pltpu.SemaphoreType.DMA((NY,)),
            pltpu.SemaphoreType.DMA,
            pltpu.SemaphoreType.DMA,
        ],
        compiler_params=params(60),
        cost_estimate=cost((UNITS + HALF) * TOK * FEATURES, 11 << 20),
        name="cotangent",
    )(idx, *pieces, weight)


def hidden_kernel(idx, *refs):
    pieces, (weight, gain, dy_gram, back, xs, hidden, inverse, down_sq, grads) = refs[:NZ], refs[NZ : NZ + 9]
    x, held, acc, sems, weight_sems, out_sems = refs[NZ + 9 :]
    z, y = idx[0], idx[1]

    def place(j):
        return lax.rem(z - j + NZ, NZ)

    def fetch(j):
        d = place(j)
        return pltpu.make_async_copy(weight.at[d, :2], held.at[d], weight_sems.at[j])

    def keep(j):
        d = place(j)
        return pltpu.make_async_copy(x.at[d], xs.at[d], out_sems.at[j])

    for j in range(NZ):
        for i in range(NY):
            slot = lax.rem(y - i + NY, NY)
            pltpu.make_async_copy(pieces[j].at[i], x.at[place(j), slot], sems.at[j]).start()
        fetch(j).start()
    acc[...] = jnp.zeros_like(acc)

    def share(j, total):
        d = place(j)
        pltpu.make_async_copy(pieces[0], x.at[d], sems.at[j]).wait()
        fetch(j).wait()
        keep(j).start()
        row = gain[pl.ds(d, 1), :]
        block = x[d].reshape(SHARE, TOK)
        for k in range(2):
            scaled = (held[d, k].astype(F32) * row).astype(BF16)
            acc[k] += jnp.dot(scaled, block, preferred_element_type=F32)
        for i in range(NY):
            wide = x[d, i].astype(F32)
            total += jnp.sum((wide * wide).reshape(COLS // 8, 8, TOK), axis=0)
        return total

    total = lax.fori_loop(0, NZ, share, jnp.zeros((8, TOK), F32))
    mean = jnp.sum(total, axis=0, keepdims=True) * (1.0 / FEATURES)
    inverse[...] = lax.rsqrt(mean + 1e-05)

    def rows(i, carry):
        r = pl.ds(pl.multiple_of(i * 32, 32), 32)
        inv = inverse[...]
        g = acc[0, r, :] * inv
        u = acc[1, r, :] * inv
        b = back[r, :]
        sigma = jax.nn.sigmoid(g)
        swish = g * sigma
        hidden[r, :] = (swish * u).astype(BF16)
        grads[0, r, :] = (b * u * sigma * (1.0 + g * (1.0 - sigma))).astype(BF16)
        grads[1, r, :] = (b * swish).astype(BF16)
        return carry

    lax.fori_loop(0, UNITS // 32, rows, 0)
    for h in range(2):
        own = hidden[:, h * HALF : (h + 1) * HALF]
        pairs = lax.dot_general(own, own, TN, preferred_element_type=F32) * dy_gram[h]
        for s in range(HALF // SEQ):
            part = pairs[s * SEQ : (s + 1) * SEQ, s * SEQ : (s + 1) * SEQ]
            value = jnp.sum(jnp.sum(part, axis=0, keepdims=True), axis=1, keepdims=True)
            i = h * (HALF // SEQ) + s
            down_sq[:, i : i + 1, :] = jnp.broadcast_to(value.reshape(1, 1, 1), (NY, 1, 128))

    def drain(j, carry):
        keep(j).wait()
        return carry

    lax.fori_loop(0, NZ, drain, 0)


def hidden_call(idx, pieces, weight, gain, dy_gram, back):
    return pl.pallas_call(
        hidden_kernel,
        out_shape=(
            jax.ShapeDtypeStruct((NZ, NY, COLS, TOK), BF16),
            jax.ShapeDtypeStruct((UNITS, TOK), BF16),
            jax.ShapeDtypeStruct((1, TOK), F32),
            jax.ShapeDtypeStruct((NY, LOCAL, 128), F32),
            jax.ShapeDtypeStruct((2, UNITS, TOK), BF16),
        ),
        in_specs=[SMEM] + [ANY] * (NZ + 1) + [VMEM] * 3,
        out_specs=(ANY,) + (VMEM,) * 4,
        scratch_shapes=[
            pltpu.VMEM((NZ, NY, COLS, TOK), BF16),
            pltpu.VMEM((NX * NC, 2, UNITS, SHARE), BF16),
            pltpu.VMEM((2, UNITS, TOK), F32),
            pltpu.SemaphoreType.DMA((NZ,)),
            pltpu.SemaphoreType.DMA((NZ,)),
            pltpu.SemaphoreType.DMA((NZ,)),
        ],
        compiler_params=params(60),
        cost_estimate=cost(2 * UNITS * TOK * FEATURES, 14 << 20),
        name="hidden",
    )(idx, *pieces, weight, gain, dy_gram, back)


def gain_kernel(grads, inverse, xs, weight, out):
    token = lax.broadcasted_iota(jnp.int32, (TOK, 128), 0)
    column = lax.broadcasted_iota(jnp.int32, (TOK, 128), 1)
    select = jnp.where(token // SEQ == column, 1.0, 0.0).astype(BF16)
    parts, wide = 2, SHARE // 2
    for d in range(2):
        for h in range(parts):
            f = slice(h * wide, (h + 1) * wide)
            normed = lax.dot_general(weight[d, 0, :, f], grads[0], TN, preferred_element_type=F32)
            normed += lax.dot_general(weight[d, 1, :, f], grads[1], TN, preferred_element_type=F32)
            group = wide // COLS
            block = xs[d, h * group : (h + 1) * group].reshape(wide, TOK)
            product = block.astype(F32) * inverse[...] * normed
            high = product.astype(BF16)
            low = (product - high.astype(F32)).astype(BF16)
            total = jnp.dot(high, select, preferred_element_type=F32)
            total += jnp.dot(low, select, preferred_element_type=F32)
            flat = total.T[:LOCAL]
            for k in range(wide // 128):
                tile = h * (wide // 128) + k
                out[d, tile * LOCAL : (tile + 1) * LOCAL, :] = flat[:, k * 128 : (k + 1) * 128]


def gain_call(grads, inverse, xs, weight):
    return pl.pallas_call(
        gain_kernel,
        grid=(NZ // 2,),
        out_shape=jax.ShapeDtypeStruct((NZ, SHARE // 128 * LOCAL, 128), F32),
        in_specs=[
            whole((2, UNITS, TOK)),
            whole((1, TOK)),
            lead((2, NY, COLS, TOK)),
            lead((2, 2, UNITS, SHARE)),
        ],
        out_specs=lead((2, SHARE // 128 * LOCAL, 128)),
        compiler_params=params(60),
        cost_estimate=cost(3 * UNITS * TOK * FEATURES, 9 << 20),
        name="gain_term",
    )(grads, inverse, xs, weight)


def join_kernel(part, gain_part, out):
    total = jnp.sum(part[...], axis=0, keepdims=True)
    out[:, :LOCAL, :] = jnp.broadcast_to(total, (NZ, LOCAL, 128))
    out[:, LOCAL:, :] = gain_part[...]


def join_call(part, gain_part):
    rows = LOCAL + gain_part.shape[1]
    return pl.pallas_call(join_kernel, out_shape=jax.ShapeDtypeStruct((NZ, rows, 128), F32), name="join_parts")(
        part, gain_part
    )


def gain_sq_kernel(part, total, square):
    gain = jnp.sum(part[...], axis=0)
    total[...] = gain
    rows = jnp.sum((gain * gain).reshape(SHARE // 128, LOCAL, 128), axis=0)
    value = jnp.sum(rows, axis=1, keepdims=True)
    square[...] = jnp.broadcast_to(value[None], square.shape)


def gain_scale_kernel(idx, part, total, out):
    square = jnp.sum(part[...], axis=0)
    bound = 0.5 * math.sqrt(SEQ * FEATURES)
    scale = jnp.minimum(1.0, bound / (jnp.sqrt(square) + 1e-06)) / SEQS
    rows = total[pl.ds(pl.multiple_of(idx[1] // 2 * LOCAL, LOCAL), LOCAL), :]
    value = jnp.sum(scale * rows, axis=0, keepdims=True)
    out[...] = jnp.broadcast_to(value[None], out.shape)


def grad_kernel(part, hidden, dy, out, added, scaled):
    @pl.when(pl.program_id(0) == 0)
    def _():
        bound = 0.6 * math.sqrt(SEQ * FF * FEATURES)
        total = jnp.sum(part[:, :LOCAL, :], axis=0)
        scale = jnp.minimum(1.0, bound / (jnp.sqrt(total) + 1e-06)) / SEQS
        first = lax.broadcasted_iota(jnp.int32, (1, 128), 1) < SEQ
        row = jnp.concatenate(
            [jnp.where(first, scale[2 * k : 2 * k + 1], scale[2 * k + 1 : 2 * k + 2]) for k in range(LOCAL // 2)],
            axis=1,
        )
        scaled[...] = (hidden[...].astype(F32) * row).astype(BF16)
        gain = jnp.sum(part[:, LOCAL:, :], axis=0, keepdims=True)
        added[...] = jnp.broadcast_to(gain, added.shape)

    for d in range(2):
        block = dy[d].reshape(SHARE, TOK)
        out[d] = lax.dot_general(scaled[...], block, NT, preferred_element_type=F32).astype(BF16)


def grad_call(part, hidden, dy):
    gain_shape = (NY, part.shape[1] - LOCAL, 128)
    return pl.pallas_call(
        grad_kernel,
        grid=(NZ // 2,),
        out_shape=(
            jax.ShapeDtypeStruct((NX * NC, UNITS, SHARE), BF16),
            jax.ShapeDtypeStruct(gain_shape, F32),
        ),
        in_specs=[whole(part.shape), whole((UNITS, TOK)), lead((2, NY, COLS, TOK))],
        out_specs=(lead((2, UNITS, SHARE)), whole(gain_shape)),
        scratch_shapes=[pltpu.VMEM((UNITS, TOK), BF16)],
        compiler_params=params(60),
        cost_estimate=cost(UNITS * TOK * FEATURES, 6 << 20),
        name="grad_down",
    )(part, hidden, dy)


def spread(block, axis, count):
    return lax.all_to_all(
        jnp.broadcast_to(block[None], (count,) + block.shape), axis, split_axis=0, concat_axis=0, tiled=True
    )


def exchange(blocks, axis):
    return lax.all_to_all(blocks, axis, split_axis=0, concat_axis=0, tiled=True)


def ring(block, axis, size):
    turn = lambda part, k: lax.ppermute(part, axis, [(i, (i + k) % size) for i in range(size)])
    up, down = [block], [block]
    for step in range(size // 2):
        up.append(turn(up[-1], 1))
        if step < size // 2 - 1:
            down.append(turn(down[-1], -1))
    return up + down[:0:-1]


def body(tokens, gain, cotangent, gate_weight, up_weight, down_weight):
    idx = jnp.stack([lax.axis_index("z"), lax.axis_index("y")]).astype(jnp.int32)
    dp = ("x", "core")
    weight = lax.all_gather(jnp.stack([gate_weight.T, up_weight.T, down_weight]), dp, axis=0)
    dy_pieces = ring(spread(cotangent.T, "z", NZ), "y", NY)
    pieces = ring(jnp.stack(ring(tokens.T, "y", NY)), "z", NZ)

    dy, dy_gram, back = cotangent_call(idx, dy_pieces, weight)
    xs, hidden, inverse, sq_part, grads = hidden_call(
        idx, pieces, weight, gain.reshape(NX * NC, SHARE), dy_gram, back
    )
    part = exchange(sq_part, "y")
    grads, sq_part = lax.optimization_barrier((grads, sq_part))
    gain_part = gain_call(grads, inverse, xs, weight)
    part = exchange(join_call(part, gain_part), "z")
    terms, added = grad_call(part, hidden, dy)
    grad_down = lax.psum_scatter(terms, dp, scatter_dimension=0).astype(F32)

    gain_z, gain_sq = pl.pallas_call(
        gain_sq_kernel,
        out_shape=(
            jax.ShapeDtypeStruct((SHARE // 128 * LOCAL, 128), F32),
            jax.ShapeDtypeStruct((NZ, LOCAL, 128), F32),
        ),
        name="gain_sq",
    )(exchange(added, "y"))
    gain_local = pl.pallas_call(
        gain_scale_kernel,
        out_shape=jax.ShapeDtypeStruct((NX * NC, 8, 128), F32),
        in_specs=[SMEM, VMEM, VMEM],
        name="gain_scale",
    )(idx, exchange(gain_sq, "z"), gain_z)
    gain_all = jnp.sum(exchange(gain_local, dp)[:, 0], axis=0)
    grad_gain = jnp.where(idx[1] % 2 == 0, gain_all[:COLS], gain_all[COLS:])
    return (grad_down, grad_gain)


def solution(mesh):
    split = Mesh(mesh.devices.reshape(NX, NC, NZ, NY), ("x", "core", "z", "y"))
    dp, tensor = ("x", "core"), ("z", "y")
    in_specs = (P(dp, tensor), P(), P(dp, tensor), P(dp, tensor), P(dp, tensor), P(tensor, dp))
    out_specs = (P(tensor, dp), P(tensor))
    return jax.shard_map(body, mesh=split, in_specs=in_specs, out_specs=out_specs, check_vma=False)
```

time: 250 us -> 216 us (0.86)
  waiting for transfers between devices: 51.2 us -> 14.8 us
  local copies, waits for them, and re-layouts: 26.1 us -> 3.83 us
  starting transfers between devices: 80.5 us -> 99.7 us
  other arithmetic: 2.45 us -> 5.03 us
    all_to_all x3 -> x1, waiting for transfers between devices: 31.5 us -> 0.01 us  [spread(): lax.all_to_all(jnp.broadcast_to(block[None], (count,) + block.shape), axi...]
    ppermute x15 -> x21, starting transfers between devices: 43.9 us -> 66.5 us  [ring(): lax.ppermute(part, axis, [(i, (i + k) % size) for i in range(size)])]
    unnamed x50 -> x29, local copies, waits for them, and re-layouts: 22.5 us -> 1.54 us
    all_to_all x3 -> x1, starting transfers between devices: 21.8 us -> 10 us  [spread(): lax.all_to_all(jnp.broadcast_to(block[None], (count,) + block.shape), axi...]
    all_to_all x2, starting transfers between devices: 14.7 us -> 23.1 us  [exchange(): return lax.all_to_all(blocks, axis, split_axis=0, concat_axis=0, tiled=True)]
    pallas_call x1, Pallas kernels: 7.48 us -> 11.3 us  [cotangent_call(): pl.pallas_call(cotangent_kernel, out_shape=(jax.ShapeDtypeStruct((NZ, NY,...]
    ppermute x15 -> x21, waiting for transfers between devices: 13.6 us -> 10 us  [ring(): lax.ppermute(part, axis, [(i, (i + k) % size) for i in range(size)])]
    another operation x1 -> x2, other arithmetic: 0.08 us -> 2.67 us  [the longest x1 2.1 us: body(): jnp.stack([gate_weight.T, up_weight.T, down_weight])]
  transfers between devices with their start and end apart: 23 -> 26, of which waited for: 7 -> 6; matrix products, arithmetic and copies ran while one was open for 2% -> 2% of each run, Pallas kernels for 9% -> 11%
where the time goes in v8:
time: 216 us; the launch traced here: 215 us
  starting transfers between devices  99.7 us (46%)
  Pallas kernels  38.7 us (18%)
  blocking collectives  38.2 us (18%)
  waiting for transfers between devices  14.8 us (7%)
  between operations  14.5 us (7%)
  other arithmetic  5.03 us (2%)
  local copies, waits for them, and re-layouts  3.83 us (2%)
    ppermute x21, starting transfers between devices, ring(): lax.ppermute(part, axis, [(i, (i + k) % size) for i in range(size)])  66.5 us
    all_to_all x3, blocking collectives, exchange(): return lax.all_to_all(blocks, axis, split_axis=0, concat_axis=0, tiled=True)  38.2 us
    all_to_all x2, starting transfers between devices, exchange(): return lax.all_to_all(blocks, axis, split_axis=0, concat_axis=0, tiled=True)  23.1 us
    pallas_call x1, Pallas kernels, cotangent_call(): pl.pallas_call(cotangent_kernel, out_shape=(jax.ShapeDtypeStruct((NZ, NY,...  11.3 us
    all_to_all x1, starting transfers between devices, spread(): lax.all_to_all(jnp.broadcast_to(block[None], (count,) + block.shape), axi...  10 us
    ppermute x21, waiting for transfers between devices, ring(): lax.ppermute(part, axis, [(i, (i + k) % size) for i in range(size)])  10 us
    pallas_call x1, Pallas kernels, gain_call(): pl.pallas_call(gain_kernel, grid=(NZ // 2,), out_shape=jax.ShapeDtypeStru...  9.03 us
    pallas_call x1, Pallas kernels, hidden_call(): pl.pallas_call(hidden_kernel, out_shape=(jax.ShapeDtypeStruct((NZ, NY, CO...  8.61 us
  transfers between devices with their start and end apart: 26, of which 6 were waited for; matrix products, arithmetic and copies ran while one was open for 2% of the time, Pallas kernels for 11%

profile of v8, /device:TPU:1, one launch (start us, length us, event | category | flops | bytes accessed | tf_op | source)
XLA Modules:
  0.0 214.8 jit_solution(10510153365958703226)
XLA Ops:
  9.3 4.0 %collective-permute-start = (bf16[64,512]{1,0:T(8,128)(2,1)}, bf16[64,512]{1,0:T(8,128)(2,1)S(1)}, u32[]{:S(2)}, u32[]{:S(2)}) collective-permute-start(bf16[64,512]{1,0:T(8,128)(2,1)} %bitcast.39), channel_id=1, source_target_pairs={{0,1},{1,2},{2,3},{3,4},{4,5},{5,6},{6,7},{7,0},{8,9},{9,10},{10,1... | collective-permute-start | bytes 196616 | tf_op jit(solution)/shard_map/ppermute | solution.py:324
  13.4 3.8 %collective-permute-start.4 = (bf16[64,512]{1,0:T(8,128)(2,1)}, bf16[64,512]{1,0:T(8,128)(2,1)S(1)}, u32[]{:S(2)}, u32[]{:S(2)}) collective-permute-start(bf16[64,512]{1,0:T(8,128)(2,1)} %bitcast.40), channel_id=1, source_target_pairs={{0,7},{1,0},{2,1},{3,2},{4,3},{5,4},{6,5},{7,6},{8,15},{9,8},{10,9... | collective-permute-start | bytes 196616 | tf_op jit(solution)/shard_map/ppermute | solution.py:324
  18.9 10.0 %all-to-all-start = ((bf16[8,64,512]{2,1,0:T(8,128)(2,1)}), bf16[8,64,512]{2,1,0:T(8,128)(2,1)S(1)}, u32[]{:S(2)}, u32[]{:S(2)}) async-start(bf16[8,64,512]{2,1,0:T(8,128)(2,1)} %broadcast_in_dim.2), calls=%async_computation | async-start | bytes 1048576 | tf_op jit(solution)/shard_map/all_to_all | solution.py:314
  31.7 4.6 %collective-permute-start.5 = (bf16[64,512]{1,0:T(8,128)(2,1)S(1)}, bf16[64,512]{1,0:T(8,128)(2,1)S(1)}, u32[]{:S(2)}, u32[]{:S(2)}) collective-permute-start(bf16[64,512]{1,0:T(8,128)(2,1)S(1)} %collective-permute-done.4), channel_id=1, source_target_pairs={{0,7},{1,0},{2,1},{3,2},{4,3},{5,4},{6,5},{7,6},{8,15},{9,8},{10,9... | collective-permute-start | bytes 196616 | tf_op jit(solution)/shard_map/ppermute | solution.py:324
  38.3 4.6 %collective-permute-start.6 = (bf16[64,512]{1,0:T(8,128)(2,1)S(1)}, bf16[64,512]{1,0:T(8,128)(2,1)S(1)}, u32[]{:S(2)}, u32[]{:S(2)}) collective-permute-start(bf16[64,512]{1,0:T(8,128)(2,1)S(1)} %collective-permute-done.5), channel_id=1, source_target_pairs={{0,7},{1,0},{2,1},{3,2},{4,3},{5,4},{6,5},{7,6},{8,15},{9,8},{10,9... | collective-permute-start | bytes 196616 | tf_op jit(solution)/shard_map/ppermute | solution.py:324
  44.9 4.7 %collective-permute-done.3 = bf16[64,512]{1,0:T(8,128)(2,1)S(1)} collective-permute-done((bf16[64,512]{1,0:T(8,128)(2,1)S(1)}, bf16[64,512]{1,0:T(8,128)(2,1)S(1)}, u32[]{:S(2)}, u32[]{:S(2)}) %collective-permute-start.3) | collective-permute-done | bytes 65568 | tf_op jit(solution)/shard_map/ppermute | solution.py:324
  51.6 3.4 %collective-permute-start.7 = (bf16[8,64,512]{2,1,0:T(8,128)(2,1)S(1)}, bf16[8,64,512]{2,1,0:T(8,128)(2,1)S(1)}, u32[]{:S(2)}, u32[]{:S(2)}) collective-permute-start(bf16[8,64,512]{2,1,0:T(8,128)(2,1)S(1)} %bitcast_dynamic-update-slice_fusion.1.refs_0_), channel_id=1, source_target_pairs={{0,8},{8,16},{16,24},{24,32},{32,40},{40,48},{48,56},{56,0},{1,9},... | collective-permute-start | bytes 1572872 | tf_op jit(solution)/shard_map/ppermute | solution.py:324
  55.0 4.6 %collective-permute-start.18 = (bf16[8,64,512]{2,1,0:T(8,128)(2,1)S(1)}, bf16[8,64,512]{2,1,0:T(8,128)(2,1)S(1)}, u32[]{:S(2)}, u32[]{:S(2)}) collective-permute-start(bf16[8,64,512]{2,1,0:T(8,128)(2,1)S(1)} %all-to-all-done.refs_0_), channel_id=1, source_target_pairs={{0,7},{1,0},{2,1},{3,2},{4,3},{5,4},{6,5},{7,6},{8,15},{9,8},{10,9... | collective-permute-start | bytes 1572872 | tf_op jit(solution)/shard_map/ppermute | solution.py:324
  59.6 3.1 %collective-permute-done.14.refs_1_ = bf16[8,64,512]{2,1,0:T(8,128)(2,1)S(1)} collective-permute-done((bf16[8,64,512]{2,1,0:T(8,128)(2,1)S(1)}, bf16[8,64,512]{2,1,0:T(8,128)(2,1)S(1)}, u32[]{:S(2)}, u32[]{:S(2)}) %collective-permute-start.14) | collective-permute-done | bytes 524320 | tf_op jit(solution)/shard_map/ppermute | solution.py:324
  64.6 4.1 %collective-permute-start.11 = (bf16[8,64,512]{2,1,0:T(8,128)(2,1)S(1)}, bf16[8,64,512]{2,1,0:T(8,128)(2,1)S(1)}, u32[]{:S(2)}, u32[]{:S(2)}) collective-permute-start(bf16[8,64,512]{2,1,0:T(8,128)(2,1)S(1)} %bitcast_dynamic-update-slice_fusion.1.refs_0_), channel_id=1, source_target_pairs={{0,56},{8,0},{16,8},{24,16},{32,24},{40,32},{48,40},{56,48},{1,57}... | collective-permute-start | bytes 1572872 | tf_op jit(solution)/shard_map/ppermute | solution.py:324
  70.7 4.6 %collective-permute-start.19 = (bf16[8,64,512]{2,1,0:T(8,128)(2,1)S(1)}, bf16[8,64,512]{2,1,0:T(8,128)(2,1)S(1)}, u32[]{:S(2)}, u32[]{:S(2)}) collective-permute-start(bf16[8,64,512]{2,1,0:T(8,128)(2,1)S(1)} %collective-permute-done.18.refs_7_), channel_id=1, source_target_pairs={{0,7},{1,0},{2,1},{3,2},{4,3},{5,4},{6,5},{7,6},{8,15},{9,8},{10,9... | collective-permute-start | bytes 1572872 | tf_op jit(solution)/shard_map/ppermute | solution.py:324
  77.3 4.6 %collective-permute-start.12 = (bf16[8,64,512]{2,1,0:T(8,128)(2,1)S(1)}, bf16[8,64,512]{2,1,0:T(8,128)(2,1)}, u32[]{:S(2)}, u32[]{:S(2)}) collective-permute-start(bf16[8,64,512]{2,1,0:T(8,128)(2,1)S(1)} %collective-permute-done.11.refs_7_), channel_id=1, source_target_pairs={{0,56},{8,0},{16,8},{24,16},{32,24},{40,32},{48,40},{56,48},{1,57}... | collective-permute-start | bytes 1572872 | tf_op jit(solution)/shard_map/ppermute | solution.py:324
  83.8 4.6 %collective-permute-start.20 = (bf16[8,64,512]{2,1,0:T(8,128)(2,1)S(1)}, bf16[8,64,512]{2,1,0:T(8,128)(2,1)}, u32[]{:S(2)}, u32[]{:S(2)}) collective-permute-start(bf16[8,64,512]{2,1,0:T(8,128)(2,1)S(1)} %collective-permute-done.19.refs_6_), channel_id=1, source_target_pairs={{0,7},{1,0},{2,1},{3,2},{4,3},{5,4},{6,5},{7,6},{8,15},{9,8},{10,9... | collective-permute-start | bytes 1572872 | tf_op jit(solution)/shard_map/ppermute | solution.py:324
  90.4 4.6 %collective-permute-start.13 = (bf16[8,64,512]{2,1,0:T(8,128)(2,1)}, bf16[8,64,512]{2,1,0:T(8,128)(2,1)}, u32[]{:S(2)}, u32[]{:S(2)}) collective-permute-start(bf16[8,64,512]{2,1,0:T(8,128)(2,1)} %collective-permute-done.12.refs_6_), channel_id=1, source_target_pairs={{0,56},{8,0},{16,8},{24,16},{32,24},{40,32},{48,40},{56,48},{1,57}... | collective-permute-start | bytes 1572872 | tf_op jit(solution)/shard_map/ppermute | solution.py:324
  100.1 11.3 %cotangent.1 = (bf16[8,8,64,512]{3,2,1,0:T(8,128)(2,1)}, f32[2,256,256]{2,1,0:T(8,128)}, f32[224,512]{1,0:T(8,128)}) custom-call(s32[2]{0:T(128)} %pad_add_fusion.idx, bf16[8,64,512]{2,1,0:T(8,128)(2,1)} %copy-done, bf16[8,64,512]{2,1,0:T(8,128)(2,1)} %copy-done.2, bf16[8,64,512]{2,1,0:T(8,128)(2,1)} %copy-done.4, ...), custom_call_target="tpu_custom_call" | custom-call | flops 2013265920 | bytes 11534336 | tf_op jit(solution)/shard_map/cotangent/pallas_call | solution.py:84
  111.4 8.6 %hidden.1 = (bf16[8,8,64,512]{3,2,1,0:T(8,128)(2,1)}, bf16[224,512]{1,0:T(8,128)(2,1)}, f32[1,512]{1,0:T(1,128)}, f32[8,8,128]{2,1,0:T(8,128)}, bf16[2,224,512]{2,1,0:T(8,128)(2,1)}) custom-call(s32[2]{0:T(128)} %pad_add_fusion.idx, bf16[8,64,512]{2,1,0:T(8,128)(2,1)} %copy-done.1, bf16[8,64,512]{2,1,0:T(8,128)(2,1)} %copy-done.6, ...), custom_call_target="tpu_custom_call" | custom-call | flops 1879048192 | bytes 14680064 | tf_op jit(solution)/shard_map/hidden/pallas_call | solution.py:179
  120.0 6.2 %all-to-all-start.1 = ((f32[8,8,128]{2,1,0:T(8,128)}), f32[8,8,128]{2,1,0:T(8,128)S(1)}, u32[]{:S(2)}, u32[]{:S(2)}) async-start(f32[8,8,128]{2,1,0:T(8,128)} %get-tuple-element.17), calls=%async_computation.1 | async-start | bytes 65536 | tf_op jit(solution)/shard_map/all_to_all | solution.py:320
  126.2 9.0 %gain_term.1.gain_part = f32[8,32,128]{2,1,0:T(8,128)} custom-call(bf16[2,224,512]{2,1,0:T(8,128)(2,1)} %get-tuple-element.19.grads, f32[1,512]{1,0:T(1,128)} %get-tuple-element.20.inverse, bf16[8,8,64,512]{3,2,1,0:T(8,128)(2,1)} %get-tuple-element.21.xs, bf16[8,3,224,512]{3,2,1,0:T(8,128)(2,1)} %bitcast.34), custom_call_target="tpu_custom_call" | custom-call | flops 2818572288 | bytes 9437184 | tf_op jit(solution)/shard_map/gain_term/pallas_call | solution.py:228
  137.5 12.8 %all_to_all.30.part = f32[8,40,128]{2,1,0:T(8,128)} all-to-all(f32[8,40,128]{2,1,0:T(8,128)} %join_parts.1), channel_id=1, replica_groups=mesh['x'=4,'core'=2,'z'=8,'y'=8] {'z'}, dimensions={0} | all-to-all | bytes 327680 | tf_op jit(solution)/shard_map/all_to_all | solution.py:320
  150.3 5.2 %grad_down.1 = (bf16[8,224,512]{2,1,0:T(8,128)(2,1)}, f32[8,32,128]{2,1,0:T(8,128)}) custom-call(f32[8,40,128]{2,1,0:T(8,128)} %all_to_all.30.part, bf16[224,512]{1,0:T(8,128)(2,1)} %get-tuple-element.22.hidden, bf16[8,8,64,512]{3,2,1,0:T(8,128)(2,1)} %get-tuple-element.23.dy), custom_call_target="tpu_custom_call" | custom-call | flops 939524096 | bytes 6291456 | tf_op jit(solution)/shard_map/grad_down/pallas_call | solution.py:297
  155.5 14.6 %all_to_all.31.part = f32[8,32,128]{2,1,0:T(8,128)} all-to-all(f32[8,32,128]{2,1,0:T(8,128)} %get-tuple-element.25), channel_id=1, replica_groups=mesh['x'=4,'core'=2,'z'=8,'y'=8] {'y'}, dimensions={0} | all-to-all | bytes 262144 | tf_op jit(solution)/shard_map/all_to_all | solution.py:320
  171.8 10.8 %all_to_all.32.part = f32[8,8,128]{2,1,0:T(8,128)} all-to-all(f32[8,8,128]{2,1,0:T(8,128)} %get-tuple-element.26), channel_id=1, replica_groups=mesh['x'=4,'core'=2,'z'=8,'y'=8] {'z'}, dimensions={0} | all-to-all | bytes 65536 | tf_op jit(solution)/shard_map/all_to_all | solution.py:320
  184.0 16.9 %all-to-all-start.5 = ((f32[8,8,128]{2,1,0:T(8,128)}), f32[8,8,128]{2,1,0:T(8,128)S(1)}, u32[]{:S(2)}, u32[]{:S(2)}) async-start(f32[8,8,128]{2,1,0:T(8,128)} %gain_scale.1), calls=%async_computation.6 | async-start | bytes 65536 | tf_op jit(solution)/shard_map/all_to_all | solution.py:320
  200.9 4.7 %all-to-all-done.5 = f32[8,8,128]{2,1,0:T(8,128)S(1)} async-done(((f32[8,8,128]{2,1,0:T(8,128)}), f32[8,8,128]{2,1,0:T(8,128)S(1)}, u32[]{:S(2)}, u32[]{:S(2)}) %all-to-all-start.5) | async-done | bytes 32800 | tf_op jit(solution)/shard_map/all_to_all | solution.py:320
  (77 shorter events, 35.0 us)
Async XLA Ops:
  7.2 92.9 %all-gather.3.cloned.1.call-start = ((), (), s32[]{:S(2)}) async-start(), calls=%async_computation.8 | async-start | bytes 6193152 | tf_op jit(solution)/shard_map/all_gather | solution.py:336
  9.3 20.4 %collective-permute-start = (bf16[64,512]{1,0:T(8,128)(2,1)}, bf16[64,512]{1,0:T(8,128)(2,1)S(1)}, u32[]{:S(2)}, u32[]{:S(2)}) collective-permute-start(bf16[64,512]{1,0:T(8,128)(2,1)} %bitcast.39), channel_id=1, source_target_pairs={{0,1},{1,2},{2,3},{3,4},{4,5},{5,6},{6,7},{7,0},{8,9},{9,10},{10,1... | collective-permute-start | bytes 196616 | tf_op jit(solution)/shard_map/ppermute | solution.py:324
  13.4 18.3 %collective-permute-start.4 = (bf16[64,512]{1,0:T(8,128)(2,1)}, bf16[64,512]{1,0:T(8,128)(2,1)S(1)}, u32[]{:S(2)}, u32[]{:S(2)}) collective-permute-start(bf16[64,512]{1,0:T(8,128)(2,1)} %bitcast.40), channel_id=1, source_target_pairs={{0,7},{1,0},{2,1},{3,2},{4,3},{5,4},{6,5},{7,6},{8,15},{9,8},{10,9... | collective-permute-start | bytes 196616 | tf_op jit(solution)/shard_map/ppermute | solution.py:324
  18.9 30.8 %all-to-all-start = ((bf16[8,64,512]{2,1,0:T(8,128)(2,1)}), bf16[8,64,512]{2,1,0:T(8,128)(2,1)S(1)}, u32[]{:S(2)}, u32[]{:S(2)}) async-start(bf16[8,64,512]{2,1,0:T(8,128)(2,1)} %broadcast_in_dim.2), calls=%async_computation | async-start | bytes 1048576 | tf_op jit(solution)/shard_map/all_to_all | solution.py:314
  29.8 6.6 %collective-permute-start.1 = (bf16[64,512]{1,0:T(8,128)(2,1)S(1)}, bf16[64,512]{1,0:T(8,128)(2,1)S(1)}, u32[]{:S(2)}, u32[]{:S(2)}) collective-permute-start(bf16[64,512]{1,0:T(8,128)(2,1)S(1)} %collective-permute-done), channel_id=1, source_target_pairs={{0,1},{1,2},{2,3},{3,4},{4,5},{5,6},{6,7},{7,0},{8,9},{9,10},{10,1... | collective-permute-start | bytes 196616 | tf_op jit(solution)/shard_map/ppermute | solution.py:324
  38.3 11.3 %collective-permute-start.6 = (bf16[64,512]{1,0:T(8,128)(2,1)S(1)}, bf16[64,512]{1,0:T(8,128)(2,1)S(1)}, u32[]{:S(2)}, u32[]{:S(2)}) collective-permute-start(bf16[64,512]{1,0:T(8,128)(2,1)S(1)} %collective-permute-done.5), channel_id=1, source_target_pairs={{0,7},{1,0},{2,1},{3,2},{4,3},{5,4},{6,5},{7,6},{8,15},{9,8},{10,9... | collective-permute-start | bytes 196616 | tf_op jit(solution)/shard_map/ppermute | solution.py:324
  43.0 6.6 %collective-permute-start.3 = (bf16[64,512]{1,0:T(8,128)(2,1)S(1)}, bf16[64,512]{1,0:T(8,128)(2,1)S(1)}, u32[]{:S(2)}, u32[]{:S(2)}) collective-permute-start(bf16[64,512]{1,0:T(8,128)(2,1)S(1)} %collective-permute-done.2), channel_id=1, source_target_pairs={{0,1},{1,2},{2,3},{3,4},{4,5},{5,6},{6,7},{7,0},{8,9},{9,10},{10,1... | collective-permute-start | bytes 196616 | tf_op jit(solution)/shard_map/ppermute | solution.py:324
  49.7 13.0 %collective-permute-start.14 = (bf16[8,64,512]{2,1,0:T(8,128)(2,1)S(1)}, bf16[8,64,512]{2,1,0:T(8,128)(2,1)S(1)}, u32[]{:S(2)}, u32[]{:S(2)}) collective-permute-start(bf16[8,64,512]{2,1,0:T(8,128)(2,1)S(1)} %all-to-all-done.refs_0_), channel_id=1, source_target_pairs={{0,1},{1,2},{2,3},{3,4},{4,5},{5,6},{6,7},{7,0},{8,9},{9,10},{10,1... | collective-permute-start | bytes 1572872 | tf_op jit(solution)/shard_map/ppermute | solution.py:324
  51.6 17.1 %collective-permute-start.7 = (bf16[8,64,512]{2,1,0:T(8,128)(2,1)S(1)}, bf16[8,64,512]{2,1,0:T(8,128)(2,1)S(1)}, u32[]{:S(2)}, u32[]{:S(2)}) collective-permute-start(bf16[8,64,512]{2,1,0:T(8,128)(2,1)S(1)} %bitcast_dynamic-update-slice_fusion.1.refs_0_), channel_id=1, source_target_pairs={{0,8},{8,16},{16,24},{24,32},{32,40},{40,48},{48,56},{56,0},{1,9},... | collective-permute-start | bytes 1572872 | tf_op jit(solution)/shard_map/ppermute | solution.py:324
  55.0 15.7 %collective-permute-start.18 = (bf16[8,64,512]{2,1,0:T(8,128)(2,1)S(1)}, bf16[8,64,512]{2,1,0:T(8,128)(2,1)S(1)}, u32[]{:S(2)}, u32[]{:S(2)}) collective-permute-start(bf16[8,64,512]{2,1,0:T(8,128)(2,1)S(1)} %all-to-all-done.refs_0_), channel_id=1, source_target_pairs={{0,7},{1,0},{2,1},{3,2},{4,3},{5,4},{6,5},{7,6},{8,15},{9,8},{10,9... | collective-permute-start | bytes 1572872 | tf_op jit(solution)/shard_map/ppermute | solution.py:324
  62.7 12.6 %collective-permute-start.15 = (bf16[8,64,512]{2,1,0:T(8,128)(2,1)S(1)}, bf16[8,64,512]{2,1,0:T(8,128)(2,1)S(1)}, u32[]{:S(2)}, u32[]{:S(2)}) collective-permute-start(bf16[8,64,512]{2,1,0:T(8,128)(2,1)S(1)} %collective-permute-done.14.refs_1_), channel_id=1, source_target_pairs={{0,1},{1,2},{2,3},{3,4},{4,5},{5,6},{6,7},{7,0},{8,9},{9,10},{10,1... | collective-permute-start | bytes 1572872 | tf_op jit(solution)/shard_map/ppermute | solution.py:324
  64.6 12.6 %collective-permute-start.11 = (bf16[8,64,512]{2,1,0:T(8,128)(2,1)S(1)}, bf16[8,64,512]{2,1,0:T(8,128)(2,1)S(1)}, u32[]{:S(2)}, u32[]{:S(2)}) collective-permute-start(bf16[8,64,512]{2,1,0:T(8,128)(2,1)S(1)} %bitcast_dynamic-update-slice_fusion.1.refs_0_), channel_id=1, source_target_pairs={{0,56},{8,0},{16,8},{24,16},{32,24},{40,32},{48,40},{56,48},{1,57}... | collective-permute-start | bytes 1572872 | tf_op jit(solution)/shard_map/ppermute | solution.py:324
  68.8 13.1 %collective-permute-start.8 = (bf16[8,64,512]{2,1,0:T(8,128)(2,1)S(1)}, bf16[8,64,512]{2,1,0:T(8,128)(2,1)S(1)}, u32[]{:S(2)}, u32[]{:S(2)}) collective-permute-start(bf16[8,64,512]{2,1,0:T(8,128)(2,1)S(1)} %collective-permute-done.7.refs_1_), channel_id=1, source_target_pairs={{0,8},{8,16},{16,24},{24,32},{32,40},{40,48},{48,56},{56,0},{1,9},... | collective-permute-start | bytes 1572872 | tf_op jit(solution)/shard_map/ppermute | solution.py:324
  70.7 13.1 %collective-permute-start.19 = (bf16[8,64,512]{2,1,0:T(8,128)(2,1)S(1)}, bf16[8,64,512]{2,1,0:T(8,128)(2,1)S(1)}, u32[]{:S(2)}, u32[]{:S(2)}) collective-permute-start(bf16[8,64,512]{2,1,0:T(8,128)(2,1)S(1)} %collective-permute-done.18.refs_7_), channel_id=1, source_target_pairs={{0,7},{1,0},{2,1},{3,2},{4,3},{5,4},{6,5},{7,6},{8,15},{9,8},{10,9... | collective-permute-start | bytes 1572872 | tf_op jit(solution)/shard_map/ppermute | solution.py:324
  75.3 13.1 %collective-permute-start.16 = (bf16[8,64,512]{2,1,0:T(8,128)(2,1)S(1)}, bf16[8,64,512]{2,1,0:T(8,128)(2,1)}, u32[]{:S(2)}, u32[]{:S(2)}) collective-permute-start(bf16[8,64,512]{2,1,0:T(8,128)(2,1)S(1)} %collective-permute-done.15.refs_2_), channel_id=1, source_target_pairs={{0,1},{1,2},{2,3},{3,4},{4,5},{5,6},{6,7},{7,0},{8,9},{9,10},{10,1... | collective-permute-start | bytes 1572872 | tf_op jit(solution)/shard_map/ppermute | solution.py:324
  77.3 13.1 %collective-permute-start.12 = (bf16[8,64,512]{2,1,0:T(8,128)(2,1)S(1)}, bf16[8,64,512]{2,1,0:T(8,128)(2,1)}, u32[]{:S(2)}, u32[]{:S(2)}) collective-permute-start(bf16[8,64,512]{2,1,0:T(8,128)(2,1)S(1)} %collective-permute-done.11.refs_7_), channel_id=1, source_target_pairs={{0,56},{8,0},{16,8},{24,16},{32,24},{40,32},{48,40},{56,48},{1,57}... | collective-permute-start | bytes 1572872 | tf_op jit(solution)/shard_map/ppermute | solution.py:324
  81.9 13.1 %collective-permute-start.9 = (bf16[8,64,512]{2,1,0:T(8,128)(2,1)S(1)}, bf16[8,64,512]{2,1,0:T(8,128)(2,1)}, u32[]{:S(2)}, u32[]{:S(2)}) collective-permute-start(bf16[8,64,512]{2,1,0:T(8,128)(2,1)S(1)} %collective-permute-done.8.refs_2_), channel_id=1, source_target_pairs={{0,8},{8,16},{16,24},{24,32},{32,40},{40,48},{48,56},{56,0},{1,9},... | collective-permute-start | bytes 1572872 | tf_op jit(solution)/shard_map/ppermute | solution.py:324
  83.8 14.3 %collective-permute-start.20 = (bf16[8,64,512]{2,1,0:T(8,128)(2,1)S(1)}, bf16[8,64,512]{2,1,0:T(8,128)(2,1)}, u32[]{:S(2)}, u32[]{:S(2)}) collective-permute-start(bf16[8,64,512]{2,1,0:T(8,128)(2,1)S(1)} %collective-permute-done.19.refs_6_), channel_id=1, source_target_pairs={{0,7},{1,0},{2,1},{3,2},{4,3},{5,4},{6,5},{7,6},{8,15},{9,8},{10,9... | collective-permute-start | bytes 1572872 | tf_op jit(solution)/shard_map/ppermute | solution.py:324
  88.4 11.6 %collective-permute-start.17 = (bf16[8,64,512]{2,1,0:T(8,128)(2,1)}, bf16[8,64,512]{2,1,0:T(8,128)(2,1)}, u32[]{:S(2)}, u32[]{:S(2)}) collective-permute-start(bf16[8,64,512]{2,1,0:T(8,128)(2,1)} %collective-permute-done.16.refs_3_), channel_id=1, source_target_pairs={{0,1},{1,2},{2,3},{3,4},{4,5},{5,6},{6,7},{7,0},{8,9},{9,10},{10,1... | collective-permute-start | bytes 1572872 | tf_op jit(solution)/shard_map/ppermute | solution.py:324
  90.4 21.0 %collective-permute-start.13 = (bf16[8,64,512]{2,1,0:T(8,128)(2,1)}, bf16[8,64,512]{2,1,0:T(8,128)(2,1)}, u32[]{:S(2)}, u32[]{:S(2)}) collective-permute-start(bf16[8,64,512]{2,1,0:T(8,128)(2,1)} %collective-permute-done.12.refs_6_), channel_id=1, source_target_pairs={{0,56},{8,0},{16,8},{24,16},{32,24},{40,32},{48,40},{56,48},{1,57}... | collective-permute-start | bytes 1572872 | tf_op jit(solution)/shard_map/ppermute | solution.py:324
  95.0 16.4 %collective-permute-start.10 = (bf16[8,64,512]{2,1,0:T(8,128)(2,1)}, bf16[8,64,512]{2,1,0:T(8,128)(2,1)}, u32[]{:S(2)}, u32[]{:S(2)}) collective-permute-start(bf16[8,64,512]{2,1,0:T(8,128)(2,1)} %collective-permute-done.9.refs_3_), channel_id=1, source_target_pairs={{0,8},{8,16},{16,24},{24,32},{32,40},{40,48},{48,56},{56,0},{1,9},... | collective-permute-start | bytes 1572872 | tf_op jit(solution)/shard_map/ppermute | solution.py:324
  120.0 15.3 %all-to-all-start.1 = ((f32[8,8,128]{2,1,0:T(8,128)}), f32[8,8,128]{2,1,0:T(8,128)S(1)}, u32[]{:S(2)}, u32[]{:S(2)}) async-start(f32[8,8,128]{2,1,0:T(8,128)} %get-tuple-element.17), calls=%async_computation.1 | async-start | bytes 65536 | tf_op jit(solution)/shard_map/all_to_all | solution.py:320
  126.2 80.0 %reduce-scatter.2.cloned.1.call-start = ((), (), s32[]{:S(2)}) async-start(), calls=%async_computation.7 | async-start | bytes 2064384 | tf_op jit(solution)/shard_map/reduce_scatter | solution.py:349
  184.0 21.6 %all-to-all-start.5 = ((f32[8,8,128]{2,1,0:T(8,128)}), f32[8,8,128]{2,1,0:T(8,128)S(1)}, u32[]{:S(2)}, u32[]{:S(2)}) async-start(f32[8,8,128]{2,1,0:T(8,128)} %gain_scale.1), calls=%async_computation.6 | async-start | bytes 65536 | tf_op jit(solution)/shard_map/all_to_all | solution.py:320
  (13 other events, 362.8 us)
Sparse Core Ops, SparseCore 0:
  10.1 48.8 all-gather.2
  155.6 42.3 reduce-scatter.1

commit v9 on v8

--- a/solution.py
+++ b/solution.py
@@ -250,26 +250,37 @@
 
 def join_call(part, gain_part):
     rows = LOCAL + gain_part.shape[1]
-    return pl.pallas_call(join_kernel, out_shape=jax.ShapeDtypeStruct((NZ, rows, 128), F32), name="join_parts")(
-        part, gain_part
-    )
-
-
-def gain_sq_kernel(part, total, square):
-    gain = jnp.sum(part[...], axis=0)
-    total[...] = gain
-    rows = jnp.sum((gain * gain).reshape(SHARE // 128, LOCAL, 128), axis=0)
-    value = jnp.sum(rows, axis=1, keepdims=True)
-    square[...] = jnp.broadcast_to(value[None], square.shape)
-
-
-def gain_scale_kernel(idx, part, total, out):
-    square = jnp.sum(part[...], axis=0)
+    return pl.pallas_call(
+        join_kernel,
+        out_shape=jax.ShapeDtypeStruct((NZ, rows, 128), F32),
+        in_specs=[VMEM, VMEM],
+        out_specs=VMEM,
+        compiler_params=params(60),
+        name="join_parts",
+    )(part, gain_part)
+
+
+def gain_sq_kernel(idx, part, out):
+    y = idx[1]
+    gain = jnp.sum(part[...], axis=0).reshape(SHARE // 128, LOCAL, 128)
+    rows = jnp.sum(gain * gain, axis=0)
+    value = jnp.broadcast_to(jnp.sum(rows, axis=1, keepdims=True), (LOCAL, COLS))
+    mine = jnp.zeros((LOCAL, COLS), F32)
+    for k in range(NY):
+        lanes = gain[k // 2, :, k % 2 * COLS : (k % 2 + 1) * COLS]
+        mine = jnp.where(y == k, lanes, mine)
+    out[...] = jnp.broadcast_to(jnp.concatenate([mine, value], axis=1)[None], out.shape)
+
+
+def gain_scale_kernel(idx, part, out):
     bound = 0.5 * math.sqrt(SEQ * FEATURES)
-    scale = jnp.minimum(1.0, bound / (jnp.sqrt(square) + 1e-06)) / SEQS
-    rows = total[pl.ds(pl.multiple_of(idx[1] // 2 * LOCAL, LOCAL), LOCAL), :]
-    value = jnp.sum(scale * rows, axis=0, keepdims=True)
-    out[...] = jnp.broadcast_to(value[None], out.shape)
+    total = jnp.zeros((1, COLS), F32)
+    for g in range(NX * NC):
+        group = part[g * NZ : (g + 1) * NZ]
+        square = jnp.sum(group, axis=0)[:, COLS:]
+        scale = jnp.minimum(1.0, bound / (jnp.sqrt(square) + 1e-06)) / SEQS
+        total += jnp.sum(scale * part[g * NZ + idx[0]][:, :COLS], axis=0, keepdims=True)
+    out[...] = total
 
 
 def grad_kernel(part, hidden, dy, out, added, scaled):
@@ -348,22 +359,23 @@
     terms, added = grad_call(part, hidden, dy)
     grad_down = lax.psum_scatter(terms, dp, scatter_dimension=0).astype(F32)
 
-    gain_z, gain_sq = pl.pallas_call(
+    everyone = ("x", "core", "z")
+    message = pl.pallas_call(
         gain_sq_kernel,
-        out_shape=(
-            jax.ShapeDtypeStruct((SHARE // 128 * LOCAL, 128), F32),
-            jax.ShapeDtypeStruct((NZ, LOCAL, 128), F32),
-        ),
+        out_shape=jax.ShapeDtypeStruct((NX * NC * NZ, LOCAL, 128), F32),
+        in_specs=[SMEM, VMEM],
+        out_specs=VMEM,
+        compiler_params=params(60),
         name="gain_sq",
-    )(exchange(added, "y"))
-    gain_local = pl.pallas_call(
+    )(idx, exchange(added, "y"))
+    grad_gain = pl.pallas_call(
         gain_scale_kernel,
-        out_shape=jax.ShapeDtypeStruct((NX * NC, 8, 128), F32),
-        in_specs=[SMEM, VMEM, VMEM],
-        name="gain_scale",
-    )(idx, exchange(gain_sq, "z"), gain_z)
-    gain_all = jnp.sum(exchange(gain_local, dp)[:, 0], axis=0)
-    grad_gain = jnp.where(idx[1] % 2 == 0, gain_all[:COLS], gain_all[COLS:])
+        out_shape=jax.ShapeDtypeStruct((1, COLS), F32),
+        in_specs=[SMEM, VMEM],
+        out_specs=VMEM,
+        compiler_params=params(60),
+        name="grad_gain",
+    )(idx, exchange(message, everyone)).reshape(COLS)
     return (grad_down, grad_gain)
 
 

time: 216 us -> 213 us (0.986)
  blocking collectives: 38.2 us -> 56.1 us
  starting transfers between devices: 99.7 us -> 82.8 us
  waiting for transfers between devices: 14.8 us -> 10 us
    all_to_all x3, blocking collectives: 38.2 us -> 56.1 us  [exchange(): return lax.all_to_all(blocks, axis, split_axis=0, concat_axis=0, tiled=True)]
    all_to_all x2 -> x1, starting transfers between devices: 23.1 us -> 6.18 us  [exchange(): return lax.all_to_all(blocks, axis, split_axis=0, concat_axis=0, tiled=True)]
    all_to_all x2 -> x1, waiting for transfers between devices: 4.72 us -> 0.01 us  [exchange(): return lax.all_to_all(blocks, axis, split_axis=0, concat_axis=0, tiled=True)]
  transfers between devices with their start and end apart: 26 -> 25, of which waited for: 6 -> 5; matrix products, arithmetic and copies ran while one was open for 2% -> 2% of each run, Pallas kernels for 11% -> 11%
where the time goes in v9:
time: 213 us; the launch traced here: 211 us
  starting transfers between devices  82.8 us (39%)
  blocking collectives  56.1 us (26%)
  Pallas kernels  39.5 us (19%)
  between operations  14.5 us (7%)
  waiting for transfers between devices  10 us (5%)
  other arithmetic  4.43 us (2%)
  local copies, waits for them, and re-layouts  3.83 us (2%)
    ppermute x21, starting transfers between devices, ring(): lax.ppermute(part, axis, [(i, (i + k) % size) for i in range(size)])  66.5 us
    all_to_all x3, blocking collectives, exchange(): return lax.all_to_all(blocks, axis, split_axis=0, concat_axis=0, tiled=True)  56.1 us
    pallas_call x1, Pallas kernels, cotangent_call(): pl.pallas_call(cotangent_kernel, out_shape=(jax.ShapeDtypeStruct((NZ, NY,...  11.3 us
    all_to_all x1, starting transfers between devices, spread(): lax.all_to_all(jnp.broadcast_to(block[None], (count,) + block.shape), axi...  10 us
    ppermute x21, waiting for transfers between devices, ring(): lax.ppermute(part, axis, [(i, (i + k) % size) for i in range(size)])  10 us
    pallas_call x1, Pallas kernels, gain_call(): pl.pallas_call(gain_kernel, grid=(NZ // 2,), out_shape=jax.ShapeDtypeStru...  9.03 us
    pallas_call x1, Pallas kernels, hidden_call(): pl.pallas_call(hidden_kernel, out_shape=(jax.ShapeDtypeStruct((NZ, NY, CO...  8.61 us
    all_to_all x1, starting transfers between devices, exchange(): return lax.all_to_all(blocks, axis, split_axis=0, concat_axis=0, tiled=True)  6.18 us
  transfers between devices with their start and end apart: 25, of which 5 were waited for; matrix products, arithmetic and copies ran while one was open for 2% of the time, Pallas kernels for 11%

profile of v9, /device:TPU:1, one launch (start us, length us, event | category | flops | bytes accessed | tf_op | source)
XLA Modules:
  0.0 211.2 jit_solution(11011865282487215474)
XLA Ops:
  7.2 2.1 pad_maximum_fusion
  9.3 4.0 %collective-permute-start = (bf16[64,512]{1,0:T(8,128)(2,1)}, bf16[64,512]{1,0:T(8,128)(2,1)S(1)}, u32[]{:S(2)}, u32[]{:S(2)}) collective-permute-start(bf16[64,512]{1,0:T(8,128)(2,1)} %bitcast.40), channel_id=1, source_target_pairs={{0,1},{1,2},{2,3},{3,4},{4,5},{5,6},{6,7},{7,0},{8,9},{9,10},{10,1... | collective-permute-start | bytes 196616 | tf_op jit(solution)/shard_map/ppermute | solution.py:335
  13.4 3.8 %collective-permute-start.4 = (bf16[64,512]{1,0:T(8,128)(2,1)}, bf16[64,512]{1,0:T(8,128)(2,1)S(1)}, u32[]{:S(2)}, u32[]{:S(2)}) collective-permute-start(bf16[64,512]{1,0:T(8,128)(2,1)} %bitcast.41), channel_id=1, source_target_pairs={{0,7},{1,0},{2,1},{3,2},{4,3},{5,4},{6,5},{7,6},{8,15},{9,8},{10,9... | collective-permute-start | bytes 196616 | tf_op jit(solution)/shard_map/ppermute | solution.py:335
  18.9 10.0 %all-to-all-start = ((bf16[8,64,512]{2,1,0:T(8,128)(2,1)}), bf16[8,64,512]{2,1,0:T(8,128)(2,1)S(1)}, u32[]{:S(2)}, u32[]{:S(2)}) async-start(bf16[8,64,512]{2,1,0:T(8,128)(2,1)} %broadcast_in_dim.2), calls=%async_computation | async-start | bytes 1048576 | tf_op jit(solution)/shard_map/all_to_all | solution.py:325
  31.7 4.6 %collective-permute-start.5 = (bf16[64,512]{1,0:T(8,128)(2,1)S(1)}, bf16[64,512]{1,0:T(8,128)(2,1)S(1)}, u32[]{:S(2)}, u32[]{:S(2)}) collective-permute-start(bf16[64,512]{1,0:T(8,128)(2,1)S(1)} %collective-permute-done.4), channel_id=1, source_target_pairs={{0,7},{1,0},{2,1},{3,2},{4,3},{5,4},{6,5},{7,6},{8,15},{9,8},{10,9... | collective-permute-start | bytes 196616 | tf_op jit(solution)/shard_map/ppermute | solution.py:335
  38.3 4.6 %collective-permute-start.6 = (bf16[64,512]{1,0:T(8,128)(2,1)S(1)}, bf16[64,512]{1,0:T(8,128)(2,1)S(1)}, u32[]{:S(2)}, u32[]{:S(2)}) collective-permute-start(bf16[64,512]{1,0:T(8,128)(2,1)S(1)} %collective-permute-done.5), channel_id=1, source_target_pairs={{0,7},{1,0},{2,1},{3,2},{4,3},{5,4},{6,5},{7,6},{8,15},{9,8},{10,9... | collective-permute-start | bytes 196616 | tf_op jit(solution)/shard_map/ppermute | solution.py:335
  44.9 4.7 %collective-permute-done.3 = bf16[64,512]{1,0:T(8,128)(2,1)S(1)} collective-permute-done((bf16[64,512]{1,0:T(8,128)(2,1)S(1)}, bf16[64,512]{1,0:T(8,128)(2,1)S(1)}, u32[]{:S(2)}, u32[]{:S(2)}) %collective-permute-start.3) | collective-permute-done | bytes 65568 | tf_op jit(solution)/shard_map/ppermute | solution.py:335
  51.6 3.4 %collective-permute-start.7 = (bf16[8,64,512]{2,1,0:T(8,128)(2,1)S(1)}, bf16[8,64,512]{2,1,0:T(8,128)(2,1)S(1)}, u32[]{:S(2)}, u32[]{:S(2)}) collective-permute-start(bf16[8,64,512]{2,1,0:T(8,128)(2,1)S(1)} %bitcast_dynamic-update-slice_fusion.1.refs_0_), channel_id=1, source_target_pairs={{0,8},{8,16},{16,24},{24,32},{32,40},{40,48},{48,56},{56,0},{1,9},... | collective-permute-start | bytes 1572872 | tf_op jit(solution)/shard_map/ppermute | solution.py:335
  55.0 4.6 %collective-permute-start.18 = (bf16[8,64,512]{2,1,0:T(8,128)(2,1)S(1)}, bf16[8,64,512]{2,1,0:T(8,128)(2,1)S(1)}, u32[]{:S(2)}, u32[]{:S(2)}) collective-permute-start(bf16[8,64,512]{2,1,0:T(8,128)(2,1)S(1)} %all-to-all-done.refs_0_), channel_id=1, source_target_pairs={{0,7},{1,0},{2,1},{3,2},{4,3},{5,4},{6,5},{7,6},{8,15},{9,8},{10,9... | collective-permute-start | bytes 1572872 | tf_op jit(solution)/shard_map/ppermute | solution.py:335
  59.6 3.1 %collective-permute-done.14.refs_1_ = bf16[8,64,512]{2,1,0:T(8,128)(2,1)S(1)} collective-permute-done((bf16[8,64,512]{2,1,0:T(8,128)(2,1)S(1)}, bf16[8,64,512]{2,1,0:T(8,128)(2,1)S(1)}, u32[]{:S(2)}, u32[]{:S(2)}) %collective-permute-start.14) | collective-permute-done | bytes 524320 | tf_op jit(solution)/shard_map/ppermute | solution.py:335
  64.6 4.1 %collective-permute-start.11 = (bf16[8,64,512]{2,1,0:T(8,128)(2,1)S(1)}, bf16[8,64,512]{2,1,0:T(8,128)(2,1)S(1)}, u32[]{:S(2)}, u32[]{:S(2)}) collective-permute-start(bf16[8,64,512]{2,1,0:T(8,128)(2,1)S(1)} %bitcast_dynamic-update-slice_fusion.1.refs_0_), channel_id=1, source_target_pairs={{0,56},{8,0},{16,8},{24,16},{32,24},{40,32},{48,40},{56,48},{1,57}... | collective-permute-start | bytes 1572872 | tf_op jit(solution)/shard_map/ppermute | solution.py:335
  70.7 4.6 %collective-permute-start.19 = (bf16[8,64,512]{2,1,0:T(8,128)(2,1)S(1)}, bf16[8,64,512]{2,1,0:T(8,128)(2,1)S(1)}, u32[]{:S(2)}, u32[]{:S(2)}) collective-permute-start(bf16[8,64,512]{2,1,0:T(8,128)(2,1)S(1)} %collective-permute-done.18.refs_7_), channel_id=1, source_target_pairs={{0,7},{1,0},{2,1},{3,2},{4,3},{5,4},{6,5},{7,6},{8,15},{9,8},{10,9... | collective-permute-start | bytes 1572872 | tf_op jit(solution)/shard_map/ppermute | solution.py:335
  77.3 4.6 %collective-permute-start.12 = (bf16[8,64,512]{2,1,0:T(8,128)(2,1)S(1)}, bf16[8,64,512]{2,1,0:T(8,128)(2,1)}, u32[]{:S(2)}, u32[]{:S(2)}) collective-permute-start(bf16[8,64,512]{2,1,0:T(8,128)(2,1)S(1)} %collective-permute-done.11.refs_7_), channel_id=1, source_target_pairs={{0,56},{8,0},{16,8},{24,16},{32,24},{40,32},{48,40},{56,48},{1,57}... | collective-permute-start | bytes 1572872 | tf_op jit(solution)/shard_map/ppermute | solution.py:335
  83.8 4.6 %collective-permute-start.20 = (bf16[8,64,512]{2,1,0:T(8,128)(2,1)S(1)}, bf16[8,64,512]{2,1,0:T(8,128)(2,1)}, u32[]{:S(2)}, u32[]{:S(2)}) collective-permute-start(bf16[8,64,512]{2,1,0:T(8,128)(2,1)S(1)} %collective-permute-done.19.refs_6_), channel_id=1, source_target_pairs={{0,7},{1,0},{2,1},{3,2},{4,3},{5,4},{6,5},{7,6},{8,15},{9,8},{10,9... | collective-permute-start | bytes 1572872 | tf_op jit(solution)/shard_map/ppermute | solution.py:335
  90.4 4.6 %collective-permute-start.13 = (bf16[8,64,512]{2,1,0:T(8,128)(2,1)}, bf16[8,64,512]{2,1,0:T(8,128)(2,1)}, u32[]{:S(2)}, u32[]{:S(2)}) collective-permute-start(bf16[8,64,512]{2,1,0:T(8,128)(2,1)} %collective-permute-done.12.refs_6_), channel_id=1, source_target_pairs={{0,56},{8,0},{16,8},{24,16},{32,24},{40,32},{48,40},{56,48},{1,57}... | collective-permute-start | bytes 1572872 | tf_op jit(solution)/shard_map/ppermute | solution.py:335
  100.1 11.3 %cotangent.1 = (bf16[8,8,64,512]{3,2,1,0:T(8,128)(2,1)}, f32[2,256,256]{2,1,0:T(8,128)}, f32[224,512]{1,0:T(8,128)}) custom-call(s32[2]{0:T(128)} %pad_add_fusion.idx, bf16[8,64,512]{2,1,0:T(8,128)(2,1)} %copy-done, bf16[8,64,512]{2,1,0:T(8,128)(2,1)} %copy-done.2, bf16[8,64,512]{2,1,0:T(8,128)(2,1)} %copy-done.4, ...), custom_call_target="tpu_custom_call" | custom-call | flops 2013265920 | bytes 11534336 | tf_op jit(solution)/shard_map/cotangent/pallas_call | solution.py:84
  111.4 8.6 %hidden.1 = (bf16[8,8,64,512]{3,2,1,0:T(8,128)(2,1)}, bf16[224,512]{1,0:T(8,128)(2,1)}, f32[1,512]{1,0:T(1,128)}, f32[8,8,128]{2,1,0:T(8,128)}, bf16[2,224,512]{2,1,0:T(8,128)(2,1)}) custom-call(s32[2]{0:T(128)} %pad_add_fusion.idx, bf16[8,64,512]{2,1,0:T(8,128)(2,1)} %copy-done.1, bf16[8,64,512]{2,1,0:T(8,128)(2,1)} %copy-done.6, ...), custom_call_target="tpu_custom_call" | custom-call | flops 1879048192 | bytes 14680064 | tf_op jit(solution)/shard_map/hidden/pallas_call | solution.py:179
  120.0 6.2 %all-to-all-start.1 = ((f32[8,8,128]{2,1,0:T(8,128)}), f32[8,8,128]{2,1,0:T(8,128)S(1)}, u32[]{:S(2)}, u32[]{:S(2)}) async-start(f32[8,8,128]{2,1,0:T(8,128)} %get-tuple-element.15), calls=%async_computation.1 | async-start | bytes 65536 | tf_op jit(solution)/shard_map/all_to_all | solution.py:331
  126.2 9.0 %gain_term.1.gain_part = f32[8,32,128]{2,1,0:T(8,128)} custom-call(bf16[2,224,512]{2,1,0:T(8,128)(2,1)} %get-tuple-element.17.grads, f32[1,512]{1,0:T(1,128)} %get-tuple-element.18.inverse, bf16[8,8,64,512]{3,2,1,0:T(8,128)(2,1)} %get-tuple-element.19.xs, bf16[8,3,224,512]{3,2,1,0:T(8,128)(2,1)} %bitcast.35), custom_call_target="tpu_custom_call" | custom-call | flops 2818572288 | bytes 9437184 | tf_op jit(solution)/shard_map/gain_term/pallas_call | solution.py:228
  137.5 12.8 %all_to_all.25.part = f32[8,40,128]{2,1,0:T(8,128)} all-to-all(f32[8,40,128]{2,1,0:T(8,128)} %join_parts.1), channel_id=1, replica_groups=mesh['x'=4,'core'=2,'z'=8,'y'=8] {'z'}, dimensions={0} | all-to-all | bytes 327680 | tf_op jit(solution)/shard_map/all_to_all | solution.py:331
  150.3 5.2 %grad_down.1 = (bf16[8,224,512]{2,1,0:T(8,128)(2,1)}, f32[8,32,128]{2,1,0:T(8,128)}) custom-call(f32[8,40,128]{2,1,0:T(8,128)} %all_to_all.25.part, bf16[224,512]{1,0:T(8,128)(2,1)} %get-tuple-element.20.hidden, bf16[8,8,64,512]{3,2,1,0:T(8,128)(2,1)} %get-tuple-element.21.dy), custom_call_target="tpu_custom_call" | custom-call | flops 939524096 | bytes 6291456 | tf_op jit(solution)/shard_map/grad_down/pallas_call | solution.py:308
  155.5 14.6 %all_to_all.26.part = f32[8,32,128]{2,1,0:T(8,128)} all-to-all(f32[8,32,128]{2,1,0:T(8,128)} %get-tuple-element.23), channel_id=1, replica_groups=mesh['x'=4,'core'=2,'z'=8,'y'=8] {'y'}, dimensions={0} | all-to-all | bytes 262144 | tf_op jit(solution)/shard_map/all_to_all | solution.py:331
  170.1 2.2 %gain_sq.1 = f32[64,8,128]{2,1,0:T(8,128)} custom-call(s32[2]{0:T(128)} %pad_add_fusion.idx, f32[8,32,128]{2,1,0:T(8,128)} %all_to_all.26.part), custom_call_target="tpu_custom_call" | custom-call | tf_op jit(solution)/shard_map/gain_sq/pallas_call | solution.py:363
  172.3 28.7 %all_to_all.27.part = f32[64,8,128]{2,1,0:T(8,128)} all-to-all(f32[64,8,128]{2,1,0:T(8,128)} %gain_sq.1), channel_id=1, replica_groups=mesh['x'=4,'core'=2,'z'=8,'y'=8] {'x','core','z'}, dimensions={0} | all-to-all | bytes 524288 | tf_op jit(solution)/shard_map/all_to_all | solution.py:331
  (73 shorter events, 30.9 us)
Async XLA Ops:
  7.2 92.9 %all-gather.3.cloned.1.call-start = ((), (), s32[]{:S(2)}) async-start(), calls=%async_computation.7 | async-start | bytes 6193152 | tf_op jit(solution)/shard_map/all_gather | solution.py:347
  9.3 20.4 %collective-permute-start = (bf16[64,512]{1,0:T(8,128)(2,1)}, bf16[64,512]{1,0:T(8,128)(2,1)S(1)}, u32[]{:S(2)}, u32[]{:S(2)}) collective-permute-start(bf16[64,512]{1,0:T(8,128)(2,1)} %bitcast.40), channel_id=1, source_target_pairs={{0,1},{1,2},{2,3},{3,4},{4,5},{5,6},{6,7},{7,0},{8,9},{9,10},{10,1... | collective-permute-start | bytes 196616 | tf_op jit(solution)/shard_map/ppermute | solution.py:335
  13.4 18.3 %collective-permute-start.4 = (bf16[64,512]{1,0:T(8,128)(2,1)}, bf16[64,512]{1,0:T(8,128)(2,1)S(1)}, u32[]{:S(2)}, u32[]{:S(2)}) collective-permute-start(bf16[64,512]{1,0:T(8,128)(2,1)} %bitcast.41), channel_id=1, source_target_pairs={{0,7},{1,0},{2,1},{3,2},{4,3},{5,4},{6,5},{7,6},{8,15},{9,8},{10,9... | collective-permute-start | bytes 196616 | tf_op jit(solution)/shard_map/ppermute | solution.py:335
  18.9 30.8 %all-to-all-start = ((bf16[8,64,512]{2,1,0:T(8,128)(2,1)}), bf16[8,64,512]{2,1,0:T(8,128)(2,1)S(1)}, u32[]{:S(2)}, u32[]{:S(2)}) async-start(bf16[8,64,512]{2,1,0:T(8,128)(2,1)} %broadcast_in_dim.2), calls=%async_computation | async-start | bytes 1048576 | tf_op jit(solution)/shard_map/all_to_all | solution.py:325
  29.8 6.6 %collective-permute-start.1 = (bf16[64,512]{1,0:T(8,128)(2,1)S(1)}, bf16[64,512]{1,0:T(8,128)(2,1)S(1)}, u32[]{:S(2)}, u32[]{:S(2)}) collective-permute-start(bf16[64,512]{1,0:T(8,128)(2,1)S(1)} %collective-permute-done), channel_id=1, source_target_pairs={{0,1},{1,2},{2,3},{3,4},{4,5},{5,6},{6,7},{7,0},{8,9},{9,10},{10,1... | collective-permute-start | bytes 196616 | tf_op jit(solution)/shard_map/ppermute | solution.py:335
  36.4 6.6 %collective-permute-start.2 = (bf16[64,512]{1,0:T(8,128)(2,1)S(1)}, bf16[64,512]{1,0:T(8,128)(2,1)S(1)}, u32[]{:S(2)}, u32[]{:S(2)}) collective-permute-start(bf16[64,512]{1,0:T(8,128)(2,1)S(1)} %collective-permute-done.1), channel_id=1, source_target_pairs={{0,1},{1,2},{2,3},{3,4},{4,5},{5,6},{6,7},{7,0},{8,9},{9,10},{10,1... | collective-permute-start | bytes 196616 | tf_op jit(solution)/shard_map/ppermute | solution.py:335
  38.3 11.3 %collective-permute-start.6 = (bf16[64,512]{1,0:T(8,128)(2,1)S(1)}, bf16[64,512]{1,0:T(8,128)(2,1)S(1)}, u32[]{:S(2)}, u32[]{:S(2)}) collective-permute-start(bf16[64,512]{1,0:T(8,128)(2,1)S(1)} %collective-permute-done.5), channel_id=1, source_target_pairs={{0,7},{1,0},{2,1},{3,2},{4,3},{5,4},{6,5},{7,6},{8,15},{9,8},{10,9... | collective-permute-start | bytes 196616 | tf_op jit(solution)/shard_map/ppermute | solution.py:335
  43.0 6.6 %collective-permute-start.3 = (bf16[64,512]{1,0:T(8,128)(2,1)S(1)}, bf16[64,512]{1,0:T(8,128)(2,1)S(1)}, u32[]{:S(2)}, u32[]{:S(2)}) collective-permute-start(bf16[64,512]{1,0:T(8,128)(2,1)S(1)} %collective-permute-done.2), channel_id=1, source_target_pairs={{0,1},{1,2},{2,3},{3,4},{4,5},{5,6},{6,7},{7,0},{8,9},{9,10},{10,1... | collective-permute-start | bytes 196616 | tf_op jit(solution)/shard_map/ppermute | solution.py:335
  49.7 13.0 %collective-permute-start.14 = (bf16[8,64,512]{2,1,0:T(8,128)(2,1)S(1)}, bf16[8,64,512]{2,1,0:T(8,128)(2,1)S(1)}, u32[]{:S(2)}, u32[]{:S(2)}) collective-permute-start(bf16[8,64,512]{2,1,0:T(8,128)(2,1)S(1)} %all-to-all-done.refs_0_), channel_id=1, source_target_pairs={{0,1},{1,2},{2,3},{3,4},{4,5},{5,6},{6,7},{7,0},{8,9},{9,10},{10,1... | collective-permute-start | bytes 1572872 | tf_op jit(solution)/shard_map/ppermute | solution.py:335
  51.6 17.1 %collective-permute-start.7 = (bf16[8,64,512]{2,1,0:T(8,128)(2,1)S(1)}, bf16[8,64,512]{2,1,0:T(8,128)(2,1)S(1)}, u32[]{:S(2)}, u32[]{:S(2)}) collective-permute-start(bf16[8,64,512]{2,1,0:T(8,128)(2,1)S(1)} %bitcast_dynamic-update-slice_fusion.1.refs_0_), channel_id=1, source_target_pairs={{0,8},{8,16},{16,24},{24,32},{32,40},{40,48},{48,56},{56,0},{1,9},... | collective-permute-start | bytes 1572872 | tf_op jit(solution)/shard_map/ppermute | solution.py:335
  55.0 15.7 %collective-permute-start.18 = (bf16[8,64,512]{2,1,0:T(8,128)(2,1)S(1)}, bf16[8,64,512]{2,1,0:T(8,128)(2,1)S(1)}, u32[]{:S(2)}, u32[]{:S(2)}) collective-permute-start(bf16[8,64,512]{2,1,0:T(8,128)(2,1)S(1)} %all-to-all-done.refs_0_), channel_id=1, source_target_pairs={{0,7},{1,0},{2,1},{3,2},{4,3},{5,4},{6,5},{7,6},{8,15},{9,8},{10,9... | collective-permute-start | bytes 1572872 | tf_op jit(solution)/shard_map/ppermute | solution.py:335
  62.7 12.6 %collective-permute-start.15 = (bf16[8,64,512]{2,1,0:T(8,128)(2,1)S(1)}, bf16[8,64,512]{2,1,0:T(8,128)(2,1)S(1)}, u32[]{:S(2)}, u32[]{:S(2)}) collective-permute-start(bf16[8,64,512]{2,1,0:T(8,128)(2,1)S(1)} %collective-permute-done.14.refs_1_), channel_id=1, source_target_pairs={{0,1},{1,2},{2,3},{3,4},{4,5},{5,6},{6,7},{7,0},{8,9},{9,10},{10,1... | collective-permute-start | bytes 1572872 | tf_op jit(solution)/shard_map/ppermute | solution.py:335
  64.6 12.6 %collective-permute-start.11 = (bf16[8,64,512]{2,1,0:T(8,128)(2,1)S(1)}, bf16[8,64,512]{2,1,0:T(8,128)(2,1)S(1)}, u32[]{:S(2)}, u32[]{:S(2)}) collective-permute-start(bf16[8,64,512]{2,1,0:T(8,128)(2,1)S(1)} %bitcast_dynamic-update-slice_fusion.1.refs_0_), channel_id=1, source_target_pairs={{0,56},{8,0},{16,8},{24,16},{32,24},{40,32},{48,40},{56,48},{1,57}... | collective-permute-start | bytes 1572872 | tf_op jit(solution)/shard_map/ppermute | solution.py:335
  68.8 13.1 %collective-permute-start.8 = (bf16[8,64,512]{2,1,0:T(8,128)(2,1)S(1)}, bf16[8,64,512]{2,1,0:T(8,128)(2,1)S(1)}, u32[]{:S(2)}, u32[]{:S(2)}) collective-permute-start(bf16[8,64,512]{2,1,0:T(8,128)(2,1)S(1)} %collective-permute-done.7.refs_1_), channel_id=1, source_target_pairs={{0,8},{8,16},{16,24},{24,32},{32,40},{40,48},{48,56},{56,0},{1,9},... | collective-permute-start | bytes 1572872 | tf_op jit(solution)/shard_map/ppermute | solution.py:335
  70.7 13.1 %collective-permute-start.19 = (bf16[8,64,512]{2,1,0:T(8,128)(2,1)S(1)}, bf16[8,64,512]{2,1,0:T(8,128)(2,1)S(1)}, u32[]{:S(2)}, u32[]{:S(2)}) collective-permute-start(bf16[8,64,512]{2,1,0:T(8,128)(2,1)S(1)} %collective-permute-done.18.refs_7_), channel_id=1, source_target_pairs={{0,7},{1,0},{2,1},{3,2},{4,3},{5,4},{6,5},{7,6},{8,15},{9,8},{10,9... | collective-permute-start | bytes 1572872 | tf_op jit(solution)/shard_map/ppermute | solution.py:335
  75.3 13.1 %collective-permute-start.16 = (bf16[8,64,512]{2,1,0:T(8,128)(2,1)S(1)}, bf16[8,64,512]{2,1,0:T(8,128)(2,1)}, u32[]{:S(2)}, u32[]{:S(2)}) collective-permute-start(bf16[8,64,512]{2,1,0:T(8,128)(2,1)S(1)} %collective-permute-done.15.refs_2_), channel_id=1, source_target_pairs={{0,1},{1,2},{2,3},{3,4},{4,5},{5,6},{6,7},{7,0},{8,9},{9,10},{10,1... | collective-permute-start | bytes 1572872 | tf_op jit(solution)/shard_map/ppermute | solution.py:335
  77.3 13.1 %collective-permute-start.12 = (bf16[8,64,512]{2,1,0:T(8,128)(2,1)S(1)}, bf16[8,64,512]{2,1,0:T(8,128)(2,1)}, u32[]{:S(2)}, u32[]{:S(2)}) collective-permute-start(bf16[8,64,512]{2,1,0:T(8,128)(2,1)S(1)} %collective-permute-done.11.refs_7_), channel_id=1, source_target_pairs={{0,56},{8,0},{16,8},{24,16},{32,24},{40,32},{48,40},{56,48},{1,57}... | collective-permute-start | bytes 1572872 | tf_op jit(solution)/shard_map/ppermute | solution.py:335
  81.9 13.1 %collective-permute-start.9 = (bf16[8,64,512]{2,1,0:T(8,128)(2,1)S(1)}, bf16[8,64,512]{2,1,0:T(8,128)(2,1)}, u32[]{:S(2)}, u32[]{:S(2)}) collective-permute-start(bf16[8,64,512]{2,1,0:T(8,128)(2,1)S(1)} %collective-permute-done.8.refs_2_), channel_id=1, source_target_pairs={{0,8},{8,16},{16,24},{24,32},{32,40},{40,48},{48,56},{56,0},{1,9},... | collective-permute-start | bytes 1572872 | tf_op jit(solution)/shard_map/ppermute | solution.py:335
  83.8 14.3 %collective-permute-start.20 = (bf16[8,64,512]{2,1,0:T(8,128)(2,1)S(1)}, bf16[8,64,512]{2,1,0:T(8,128)(2,1)}, u32[]{:S(2)}, u32[]{:S(2)}) collective-permute-start(bf16[8,64,512]{2,1,0:T(8,128)(2,1)S(1)} %collective-permute-done.19.refs_6_), channel_id=1, source_target_pairs={{0,7},{1,0},{2,1},{3,2},{4,3},{5,4},{6,5},{7,6},{8,15},{9,8},{10,9... | collective-permute-start | bytes 1572872 | tf_op jit(solution)/shard_map/ppermute | solution.py:335
  88.4 11.6 %collective-permute-start.17 = (bf16[8,64,512]{2,1,0:T(8,128)(2,1)}, bf16[8,64,512]{2,1,0:T(8,128)(2,1)}, u32[]{:S(2)}, u32[]{:S(2)}) collective-permute-start(bf16[8,64,512]{2,1,0:T(8,128)(2,1)} %collective-permute-done.16.refs_3_), channel_id=1, source_target_pairs={{0,1},{1,2},{2,3},{3,4},{4,5},{5,6},{6,7},{7,0},{8,9},{9,10},{10,1... | collective-permute-start | bytes 1572872 | tf_op jit(solution)/shard_map/ppermute | solution.py:335
  90.4 21.0 %collective-permute-start.13 = (bf16[8,64,512]{2,1,0:T(8,128)(2,1)}, bf16[8,64,512]{2,1,0:T(8,128)(2,1)}, u32[]{:S(2)}, u32[]{:S(2)}) collective-permute-start(bf16[8,64,512]{2,1,0:T(8,128)(2,1)} %collective-permute-done.12.refs_6_), channel_id=1, source_target_pairs={{0,56},{8,0},{16,8},{24,16},{32,24},{40,32},{48,40},{56,48},{1,57}... | collective-permute-start | bytes 1572872 | tf_op jit(solution)/shard_map/ppermute | solution.py:335
  95.0 16.4 %collective-permute-start.10 = (bf16[8,64,512]{2,1,0:T(8,128)(2,1)}, bf16[8,64,512]{2,1,0:T(8,128)(2,1)}, u32[]{:S(2)}, u32[]{:S(2)}) collective-permute-start(bf16[8,64,512]{2,1,0:T(8,128)(2,1)} %collective-permute-done.9.refs_3_), channel_id=1, source_target_pairs={{0,8},{8,16},{16,24},{24,32},{32,40},{40,48},{48,56},{56,0},{1,9},... | collective-permute-start | bytes 1572872 | tf_op jit(solution)/shard_map/ppermute | solution.py:335
  120.0 15.3 %all-to-all-start.1 = ((f32[8,8,128]{2,1,0:T(8,128)}), f32[8,8,128]{2,1,0:T(8,128)S(1)}, u32[]{:S(2)}, u32[]{:S(2)}) async-start(f32[8,8,128]{2,1,0:T(8,128)} %get-tuple-element.15), calls=%async_computation.1 | async-start | bytes 65536 | tf_op jit(solution)/shard_map/all_to_all | solution.py:331
  126.2 76.4 %reduce-scatter.2.cloned.1.call-start = ((), (), s32[]{:S(2)}) async-start(), calls=%async_computation.6 | async-start | bytes 2064384 | tf_op jit(solution)/shard_map/reduce_scatter | solution.py:360
  (12 other events, 356.2 us)
Sparse Core Ops, SparseCore 0:
  10.1 48.8 all-gather.2
  155.6 43.0 reduce-scatter.1

commit v10 on v8

--- a/solution.py
+++ b/solution.py
@@ -166,7 +166,7 @@
             part = pairs[s * SEQ : (s + 1) * SEQ, s * SEQ : (s + 1) * SEQ]
             value = jnp.sum(jnp.sum(part, axis=0, keepdims=True), axis=1, keepdims=True)
             i = h * (HALF // SEQ) + s
-            down_sq[:, i : i + 1, :] = jnp.broadcast_to(value.reshape(1, 1, 1), (NY, 1, 128))
+            down_sq[i : i + 1, :] = jnp.broadcast_to(value, (1, 128))
 
     def drain(j, carry):
         keep(j).wait()
@@ -182,7 +182,7 @@
             jax.ShapeDtypeStruct((NZ, NY, COLS, TOK), BF16),
             jax.ShapeDtypeStruct((UNITS, TOK), BF16),
             jax.ShapeDtypeStruct((1, TOK), F32),
-            jax.ShapeDtypeStruct((NY, LOCAL, 128), F32),
+            jax.ShapeDtypeStruct((LOCAL, 128), F32),
             jax.ShapeDtypeStruct((2, UNITS, TOK), BF16),
         ),
         in_specs=[SMEM] + [ANY] * (NZ + 1) + [VMEM] * 3,
@@ -201,7 +201,7 @@
     )(idx, *pieces, weight, gain, dy_gram, back)
 
 
-def gain_kernel(grads, inverse, xs, weight, out):
+def gain_kernel(grads, inverse, xs, weight, down_sq, out):
     token = lax.broadcasted_iota(jnp.int32, (TOK, 128), 0)
     column = lax.broadcasted_iota(jnp.int32, (TOK, 128), 1)
     select = jnp.where(token // SEQ == column, 1.0, 0.0).astype(BF16)
@@ -219,64 +219,48 @@
             total = jnp.dot(high, select, preferred_element_type=F32)
             total += jnp.dot(low, select, preferred_element_type=F32)
             flat = total.T[:LOCAL]
-            for k in range(wide // 128):
-                tile = h * (wide // 128) + k
-                out[d, tile * LOCAL : (tile + 1) * LOCAL, :] = flat[:, k * 128 : (k + 1) * 128]
-
-
-def gain_call(grads, inverse, xs, weight):
+            for k in range(group):
+                lanes = flat[:, k * COLS : (k + 1) * COLS]
+                out[d * NY + h * group + k] = jnp.concatenate([lanes, down_sq[:, :COLS]], axis=1)
+
+
+def gain_call(grads, inverse, xs, weight, down_sq):
     return pl.pallas_call(
         gain_kernel,
         grid=(NZ // 2,),
-        out_shape=jax.ShapeDtypeStruct((NZ, SHARE // 128 * LOCAL, 128), F32),
+        out_shape=jax.ShapeDtypeStruct((NZ * NY, LOCAL, 128), F32),
         in_specs=[
             whole((2, UNITS, TOK)),
             whole((1, TOK)),
             lead((2, NY, COLS, TOK)),
             lead((2, 2, UNITS, SHARE)),
+            whole((LOCAL, 128)),
         ],
-        out_specs=lead((2, SHARE // 128 * LOCAL, 128)),
+        out_specs=lead((2 * NY, LOCAL, 128)),
         compiler_params=params(60),
         cost_estimate=cost(3 * UNITS * TOK * FEATURES, 9 << 20),
         name="gain_term",
-    )(grads, inverse, xs, weight)
-
-
-def join_kernel(part, gain_part, out):
-    total = jnp.sum(part[...], axis=0, keepdims=True)
-    out[:, :LOCAL, :] = jnp.broadcast_to(total, (NZ, LOCAL, 128))
-    out[:, LOCAL:, :] = gain_part[...]
-
-
-def join_call(part, gain_part):
-    rows = LOCAL + gain_part.shape[1]
-    return pl.pallas_call(join_kernel, out_shape=jax.ShapeDtypeStruct((NZ, rows, 128), F32), name="join_parts")(
-        part, gain_part
-    )
-
-
-def gain_sq_kernel(part, total, square):
-    gain = jnp.sum(part[...], axis=0)
-    total[...] = gain
-    rows = jnp.sum((gain * gain).reshape(SHARE // 128, LOCAL, 128), axis=0)
-    value = jnp.sum(rows, axis=1, keepdims=True)
-    square[...] = jnp.broadcast_to(value[None], square.shape)
-
-
-def gain_scale_kernel(idx, part, total, out):
+    )(grads, inverse, xs, weight, down_sq)
+
+
+def gain_scale_kernel(part, gain, out):
     square = jnp.sum(part[...], axis=0)
     bound = 0.5 * math.sqrt(SEQ * FEATURES)
     scale = jnp.minimum(1.0, bound / (jnp.sqrt(square) + 1e-06)) / SEQS
-    rows = total[pl.ds(pl.multiple_of(idx[1] // 2 * LOCAL, LOCAL), LOCAL), :]
-    value = jnp.sum(scale * rows, axis=0, keepdims=True)
+    value = jnp.sum(scale * gain[...], axis=0, keepdims=True)
     out[...] = jnp.broadcast_to(value[None], out.shape)
 
 
-def grad_kernel(part, hidden, dy, out, added, scaled):
+def grad_kernel(part, hidden, dy, out, gain, square, scaled):
     @pl.when(pl.program_id(0) == 0)
     def _():
         bound = 0.6 * math.sqrt(SEQ * FF * FEATURES)
-        total = jnp.sum(part[:, :LOCAL, :], axis=0)
+        sums = jnp.sum(part[...], axis=0)
+        gain[...] = sums
+        own = sums[:, :COLS]
+        squares = jnp.sum(own * own, axis=1, keepdims=True)
+        square[...] = jnp.broadcast_to(squares[None], square.shape)
+        total = jnp.broadcast_to(sums[:, COLS : COLS + 1], (LOCAL, 128))
         scale = jnp.minimum(1.0, bound / (jnp.sqrt(total) + 1e-06)) / SEQS
         first = lax.broadcasted_iota(jnp.int32, (1, 128), 1) < SEQ
         row = jnp.concatenate(
@@ -284,8 +268,6 @@
             axis=1,
         )
         scaled[...] = (hidden[...].astype(F32) * row).astype(BF16)
-        gain = jnp.sum(part[:, LOCAL:, :], axis=0, keepdims=True)
-        added[...] = jnp.broadcast_to(gain, added.shape)
 
     for d in range(2):
         block = dy[d].reshape(SHARE, TOK)
@@ -293,16 +275,16 @@
 
 
 def grad_call(part, hidden, dy):
-    gain_shape = (NY, part.shape[1] - LOCAL, 128)
     return pl.pallas_call(
         grad_kernel,
         grid=(NZ // 2,),
         out_shape=(
             jax.ShapeDtypeStruct((NX * NC, UNITS, SHARE), BF16),
-            jax.ShapeDtypeStruct(gain_shape, F32),
+            jax.ShapeDtypeStruct((LOCAL, 128), F32),
+            jax.ShapeDtypeStruct(part.shape, F32),
         ),
         in_specs=[whole(part.shape), whole((UNITS, TOK)), lead((2, NY, COLS, TOK))],
-        out_specs=(lead((2, UNITS, SHARE)), whole(gain_shape)),
+        out_specs=(lead((2, UNITS, SHARE)), whole((LOCAL, 128)), whole(part.shape)),
         scratch_shapes=[pltpu.VMEM((UNITS, TOK), BF16)],
         compiler_params=params(60),
         cost_estimate=cost(UNITS * TOK * FEATURES, 6 << 20),
@@ -341,29 +323,19 @@
     xs, hidden, inverse, sq_part, grads = hidden_call(
         idx, pieces, weight, gain.reshape(NX * NC, SHARE), dy_gram, back
     )
-    part = exchange(sq_part, "y")
-    grads, sq_part = lax.optimization_barrier((grads, sq_part))
-    gain_part = gain_call(grads, inverse, xs, weight)
-    part = exchange(join_call(part, gain_part), "z")
-    terms, added = grad_call(part, hidden, dy)
+    tensor = ("z", "y")
+    part = exchange(gain_call(grads, inverse, xs, weight, sq_part), tensor)
+    terms, gain_mine, square = grad_call(part, hidden, dy)
     grad_down = lax.psum_scatter(terms, dp, scatter_dimension=0).astype(F32)
-
-    gain_z, gain_sq = pl.pallas_call(
-        gain_sq_kernel,
-        out_shape=(
-            jax.ShapeDtypeStruct((SHARE // 128 * LOCAL, 128), F32),
-            jax.ShapeDtypeStruct((NZ, LOCAL, 128), F32),
-        ),
-        name="gain_sq",
-    )(exchange(added, "y"))
     gain_local = pl.pallas_call(
         gain_scale_kernel,
         out_shape=jax.ShapeDtypeStruct((NX * NC, 8, 128), F32),
-        in_specs=[SMEM, VMEM, VMEM],
+        in_specs=[VMEM, VMEM],
+        out_specs=VMEM,
+        compiler_params=params(60),
         name="gain_scale",
-    )(idx, exchange(gain_sq, "z"), gain_z)
-    gain_all = jnp.sum(exchange(gain_local, dp)[:, 0], axis=0)
-    grad_gain = jnp.where(idx[1] % 2 == 0, gain_all[:COLS], gain_all[COLS:])
+    )(exchange(square, tensor), gain_mine)
+    grad_gain = jnp.sum(exchange(gain_local, dp)[:, 0, :COLS], axis=0)
     return (grad_down, grad_gain)
 
 

time: 216 us -> 207 us (0.958)
  starting transfers between devices: 99.7 us -> 76.6 us
  blocking collectives: 38.2 us -> 60 us
  waiting for transfers between devices: 14.8 us -> 10 us
  Pallas kernels: 38.7 us -> 36.3 us
    all_to_all x2 -> x0, starting transfers between devices: 23.1 us -> none  [exchange(): return lax.all_to_all(blocks, axis, split_axis=0, concat_axis=0, tiled=True)]
    all_to_all x3, blocking collectives: 38.2 us -> 60 us  [exchange(): return lax.all_to_all(blocks, axis, split_axis=0, concat_axis=0, tiled=True)]
    all_to_all x2 -> x0, waiting for transfers between devices: 4.72 us -> none  [exchange(): return lax.all_to_all(blocks, axis, split_axis=0, concat_axis=0, tiled=True)]
    pallas_call x2 -> x0, Pallas kernels: 3.21 us -> none  [the longest x1 1.61 us: body(): pl.pallas_call(gain_sq_kernel, out_shape=(jax.ShapeDtypeStruct((SHARE //...]
  transfers between devices with their start and end apart: 26 -> 24, of which waited for: 6 -> 5; matrix products, arithmetic and copies ran while one was open for 2% -> 2% of each run, Pallas kernels for 11% -> 6%
where the time goes in v10:
time: 207 us; the launch traced here: 206 us
  starting transfers between devices  76.6 us (37%)
  blocking collectives  60 us (29%)
  Pallas kernels  36.3 us (18%)
  between operations  14.5 us (7%)
  waiting for transfers between devices  10 us (5%)
  other arithmetic  4.98 us (2%)
  local copies, waits for them, and re-layouts  3.24 us (2%)
    ppermute x21, starting transfers between devices, ring(): lax.ppermute(part, axis, [(i, (i + k) % size) for i in range(size)])  66.5 us
    all_to_all x3, blocking collectives, exchange(): return lax.all_to_all(blocks, axis, split_axis=0, concat_axis=0, tiled=True)  60 us
    pallas_call x1, Pallas kernels, cotangent_call(): pl.pallas_call(cotangent_kernel, out_shape=(jax.ShapeDtypeStruct((NZ, NY,...  11.2 us
    all_to_all x1, starting transfers between devices, spread(): lax.all_to_all(jnp.broadcast_to(block[None], (count,) + block.shape), axi...  10 us
    ppermute x21, waiting for transfers between devices, ring(): lax.ppermute(part, axis, [(i, (i + k) % size) for i in range(size)])  9.97 us
    pallas_call x1, Pallas kernels, gain_call(): pl.pallas_call(gain_kernel, grid=(NZ // 2,), out_shape=jax.ShapeDtypeStru...  9.29 us
    pallas_call x1, Pallas kernels, hidden_call(): pl.pallas_call(hidden_kernel, out_shape=(jax.ShapeDtypeStruct((NZ, NY, CO...  8.65 us
    pallas_call x1, Pallas kernels, grad_call(): pl.pallas_call(grad_kernel, grid=(NZ // 2,), out_shape=(jax.ShapeDtypeStr...  5.41 us
  transfers between devices with their start and end apart: 24, of which 5 were waited for; matrix products, arithmetic and copies ran while one was open for 2% of the time, Pallas kernels for 6%

profile of v10, /device:TPU:1, one launch (start us, length us, event | category | flops | bytes accessed | tf_op | source)
XLA Modules:
  0.0 205.6 jit_solution(884594271015112331)
XLA Ops:
  7.2 2.1 %pad_maximum_fusion = bf16[3,224,512]{2,1,0:T(8,128)(2,1)} fusion(bf16[1,224,512]{2,1,0:T(8,128)(2,1)} %bitcast.35, bf16[1,224,512]{2,1,0:T(8,128)(2,1)} %bitcast.36, bf16[1,224,512]{2,1,0:T(8,128)(2,1)} %bitcast.37), kind=kLoop, calls=%fused_computation | loop fusion | flops 688128 | bytes 1376256 | tf_op jit(solution)/shard_map/stack | solution.py:318
  9.3 4.0 %collective-permute-start = (bf16[64,512]{1,0:T(8,128)(2,1)}, bf16[64,512]{1,0:T(8,128)(2,1)S(1)}, u32[]{:S(2)}, u32[]{:S(2)}) collective-permute-start(bf16[64,512]{1,0:T(8,128)(2,1)} %bitcast.39), channel_id=1, source_target_pairs={{0,1},{1,2},{2,3},{3,4},{4,5},{5,6},{6,7},{7,0},{8,9},{9,10},{10,1... | collective-permute-start | bytes 196616 | tf_op jit(solution)/shard_map/ppermute | solution.py:306
  13.4 3.8 %collective-permute-start.4 = (bf16[64,512]{1,0:T(8,128)(2,1)}, bf16[64,512]{1,0:T(8,128)(2,1)S(1)}, u32[]{:S(2)}, u32[]{:S(2)}) collective-permute-start(bf16[64,512]{1,0:T(8,128)(2,1)} %bitcast.40), channel_id=1, source_target_pairs={{0,7},{1,0},{2,1},{3,2},{4,3},{5,4},{6,5},{7,6},{8,15},{9,8},{10,9... | collective-permute-start | bytes 196616 | tf_op jit(solution)/shard_map/ppermute | solution.py:306
  18.9 10.0 %all-to-all-start = ((bf16[8,64,512]{2,1,0:T(8,128)(2,1)}), bf16[8,64,512]{2,1,0:T(8,128)(2,1)S(1)}, u32[]{:S(2)}, u32[]{:S(2)}) async-start(bf16[8,64,512]{2,1,0:T(8,128)(2,1)} %broadcast_in_dim.2), calls=%async_computation | async-start | bytes 1048576 | tf_op jit(solution)/shard_map/all_to_all | solution.py:296
  31.8 4.6 %collective-permute-start.5 = (bf16[64,512]{1,0:T(8,128)(2,1)S(1)}, bf16[64,512]{1,0:T(8,128)(2,1)S(1)}, u32[]{:S(2)}, u32[]{:S(2)}) collective-permute-start(bf16[64,512]{1,0:T(8,128)(2,1)S(1)} %collective-permute-done.4), channel_id=1, source_target_pairs={{0,7},{1,0},{2,1},{3,2},{4,3},{5,4},{6,5},{7,6},{8,15},{9,8},{10,9... | collective-permute-start | bytes 196616 | tf_op jit(solution)/shard_map/ppermute | solution.py:306
  38.4 4.6 %collective-permute-start.6 = (bf16[64,512]{1,0:T(8,128)(2,1)S(1)}, bf16[64,512]{1,0:T(8,128)(2,1)S(1)}, u32[]{:S(2)}, u32[]{:S(2)}) collective-permute-start(bf16[64,512]{1,0:T(8,128)(2,1)S(1)} %collective-permute-done.5), channel_id=1, source_target_pairs={{0,7},{1,0},{2,1},{3,2},{4,3},{5,4},{6,5},{7,6},{8,15},{9,8},{10,9... | collective-permute-start | bytes 196616 | tf_op jit(solution)/shard_map/ppermute | solution.py:306
  45.0 4.7 %collective-permute-done.3 = bf16[64,512]{1,0:T(8,128)(2,1)S(1)} collective-permute-done((bf16[64,512]{1,0:T(8,128)(2,1)S(1)}, bf16[64,512]{1,0:T(8,128)(2,1)S(1)}, u32[]{:S(2)}, u32[]{:S(2)}) %collective-permute-start.3) | collective-permute-done | bytes 65568 | tf_op jit(solution)/shard_map/ppermute | solution.py:306
  51.7 3.4 %collective-permute-start.7 = (bf16[8,64,512]{2,1,0:T(8,128)(2,1)S(1)}, bf16[8,64,512]{2,1,0:T(8,128)(2,1)S(1)}, u32[]{:S(2)}, u32[]{:S(2)}) collective-permute-start(bf16[8,64,512]{2,1,0:T(8,128)(2,1)S(1)} %bitcast_dynamic-update-slice_fusion.1.refs_0_), channel_id=1, source_target_pairs={{0,8},{8,16},{16,24},{24,32},{32,40},{40,48},{48,56},{56,0},{1,9},... | collective-permute-start | bytes 1572872 | tf_op jit(solution)/shard_map/ppermute | solution.py:306
  55.1 4.6 %collective-permute-start.18 = (bf16[8,64,512]{2,1,0:T(8,128)(2,1)S(1)}, bf16[8,64,512]{2,1,0:T(8,128)(2,1)S(1)}, u32[]{:S(2)}, u32[]{:S(2)}) collective-permute-start(bf16[8,64,512]{2,1,0:T(8,128)(2,1)S(1)} %all-to-all-done.refs_0_), channel_id=1, source_target_pairs={{0,7},{1,0},{2,1},{3,2},{4,3},{5,4},{6,5},{7,6},{8,15},{9,8},{10,9... | collective-permute-start | bytes 1572872 | tf_op jit(solution)/shard_map/ppermute | solution.py:306
  59.6 3.1 %collective-permute-done.14.refs_1_ = bf16[8,64,512]{2,1,0:T(8,128)(2,1)S(1)} collective-permute-done((bf16[8,64,512]{2,1,0:T(8,128)(2,1)S(1)}, bf16[8,64,512]{2,1,0:T(8,128)(2,1)S(1)}, u32[]{:S(2)}, u32[]{:S(2)}) %collective-permute-start.14) | collective-permute-done | bytes 524320 | tf_op jit(solution)/shard_map/ppermute | solution.py:306
  64.7 4.1 %collective-permute-start.11 = (bf16[8,64,512]{2,1,0:T(8,128)(2,1)S(1)}, bf16[8,64,512]{2,1,0:T(8,128)(2,1)S(1)}, u32[]{:S(2)}, u32[]{:S(2)}) collective-permute-start(bf16[8,64,512]{2,1,0:T(8,128)(2,1)S(1)} %bitcast_dynamic-update-slice_fusion.1.refs_0_), channel_id=1, source_target_pairs={{0,56},{8,0},{16,8},{24,16},{32,24},{40,32},{48,40},{56,48},{1,57}... | collective-permute-start | bytes 1572872 | tf_op jit(solution)/shard_map/ppermute | solution.py:306
  70.8 4.6 %collective-permute-start.19 = (bf16[8,64,512]{2,1,0:T(8,128)(2,1)S(1)}, bf16[8,64,512]{2,1,0:T(8,128)(2,1)S(1)}, u32[]{:S(2)}, u32[]{:S(2)}) collective-permute-start(bf16[8,64,512]{2,1,0:T(8,128)(2,1)S(1)} %collective-permute-done.18.refs_7_), channel_id=1, source_target_pairs={{0,7},{1,0},{2,1},{3,2},{4,3},{5,4},{6,5},{7,6},{8,15},{9,8},{10,9... | collective-permute-start | bytes 1572872 | tf_op jit(solution)/shard_map/ppermute | solution.py:306
  75.4 1.9 collective-permute-start.16
  77.3 4.6 %collective-permute-start.12 = (bf16[8,64,512]{2,1,0:T(8,128)(2,1)S(1)}, bf16[8,64,512]{2,1,0:T(8,128)(2,1)}, u32[]{:S(2)}, u32[]{:S(2)}) collective-permute-start(bf16[8,64,512]{2,1,0:T(8,128)(2,1)S(1)} %collective-permute-done.11.refs_7_), channel_id=1, source_target_pairs={{0,56},{8,0},{16,8},{24,16},{32,24},{40,32},{48,40},{56,48},{1,57}... | collective-permute-start | bytes 1572872 | tf_op jit(solution)/shard_map/ppermute | solution.py:306
  83.9 4.6 %collective-permute-start.20 = (bf16[8,64,512]{2,1,0:T(8,128)(2,1)S(1)}, bf16[8,64,512]{2,1,0:T(8,128)(2,1)}, u32[]{:S(2)}, u32[]{:S(2)}) collective-permute-start(bf16[8,64,512]{2,1,0:T(8,128)(2,1)S(1)} %collective-permute-done.19.refs_6_), channel_id=1, source_target_pairs={{0,7},{1,0},{2,1},{3,2},{4,3},{5,4},{6,5},{7,6},{8,15},{9,8},{10,9... | collective-permute-start | bytes 1572872 | tf_op jit(solution)/shard_map/ppermute | solution.py:306
  90.4 4.6 %collective-permute-start.13 = (bf16[8,64,512]{2,1,0:T(8,128)(2,1)}, bf16[8,64,512]{2,1,0:T(8,128)(2,1)}, u32[]{:S(2)}, u32[]{:S(2)}) collective-permute-start(bf16[8,64,512]{2,1,0:T(8,128)(2,1)} %collective-permute-done.12.refs_6_), channel_id=1, source_target_pairs={{0,56},{8,0},{16,8},{24,16},{32,24},{40,32},{48,40},{56,48},{1,57}... | collective-permute-start | bytes 1572872 | tf_op jit(solution)/shard_map/ppermute | solution.py:306
  98.2 1.9 collective-permute-done.17.refs_4_
  100.1 11.2 %cotangent.1 = (bf16[8,8,64,512]{3,2,1,0:T(8,128)(2,1)}, f32[2,256,256]{2,1,0:T(8,128)}, f32[224,512]{1,0:T(8,128)}) custom-call(s32[2]{0:T(128)} %pad_add_fusion.idx, bf16[8,64,512]{2,1,0:T(8,128)(2,1)} %copy-done, bf16[8,64,512]{2,1,0:T(8,128)(2,1)} %copy-done.2, bf16[8,64,512]{2,1,0:T(8,128)(2,1)} %copy-done.4, ...), custom_call_target="tpu_custom_call" | custom-call | flops 2013265920 | bytes 11534336 | tf_op jit(solution)/shard_map/cotangent/pallas_call | solution.py:84
  111.4 8.7 %hidden.1 = (bf16[8,8,64,512]{3,2,1,0:T(8,128)(2,1)}, bf16[224,512]{1,0:T(8,128)(2,1)}, f32[1,512]{1,0:T(1,128)}, f32[8,128]{1,0:T(8,128)}, bf16[2,224,512]{2,1,0:T(8,128)(2,1)}) custom-call(s32[2]{0:T(128)} %pad_add_fusion.idx, bf16[8,64,512]{2,1,0:T(8,128)(2,1)} %copy-done.1, bf16[8,64,512]{2,1,0:T(8,128)(2,1)} %copy-done.6, ...), custom_call_target="tpu_custom_call" | custom-call | flops 1879048192 | bytes 14680064 | tf_op jit(solution)/shard_map/hidden/pallas_call | solution.py:179
  120.1 9.3 %gain_term.1 = f32[64,8,128]{2,1,0:T(8,128)} custom-call(bf16[2,224,512]{2,1,0:T(8,128)(2,1)} %get-tuple-element.15.grads, f32[1,512]{1,0:T(1,128)} %get-tuple-element.16.inverse, bf16[8,8,64,512]{3,2,1,0:T(8,128)(2,1)} %get-tuple-element.17.xs, bf16[8,3,224,512]{3,2,1,0:T(8,128)(2,1)} %bitcast.34, f32[8,128]{1,0:T(8,128)} %get-tuple-element.18.down_sq), custom_call_target="tpu_custom_call" | custom-call | flops 2818572288 | bytes 9437184 | tf_op jit(solution)/shard_map/gain_term/pallas_call | solution.py:228
  129.4 22.6 %all_to_all.20.part = f32[64,8,128]{2,1,0:T(8,128)} all-to-all(f32[64,8,128]{2,1,0:T(8,128)} %gain_term.1), channel_id=1, replica_groups=mesh['x'=4,'core'=2,'z'=8,'y'=8] {'z','y'}, dimensions={0} | all-to-all | bytes 524288 | tf_op jit(solution)/shard_map/all_to_all | solution.py:302
  152.0 5.4 %grad_down.1 = (bf16[8,224,512]{2,1,0:T(8,128)(2,1)}, f32[8,128]{1,0:T(8,128)}, f32[64,8,128]{2,1,0:T(8,128)}) custom-call(f32[64,8,128]{2,1,0:T(8,128)} %all_to_all.20.part, bf16[224,512]{1,0:T(8,128)(2,1)} %get-tuple-element.19.hidden, bf16[8,8,64,512]{3,2,1,0:T(8,128)(2,1)} %get-tuple-element.20.dy), custom_call_target="tpu_custom_call" | custom-call | flops 939524096 | bytes 6291456 | tf_op jit(solution)/shard_map/grad_down/pallas_call | solution.py:278
  157.4 17.8 %all_to_all.21.part = f32[64,8,128]{2,1,0:T(8,128)} all-to-all(f32[64,8,128]{2,1,0:T(8,128)} %get-tuple-element.22), channel_id=1, replica_groups=mesh['x'=4,'core'=2,'z'=8,'y'=8] {'z','y'}, dimensions={0} | all-to-all | bytes 524288 | tf_op jit(solution)/shard_map/all_to_all | solution.py:302
  176.9 19.6 %all_to_all.22 = f32[8,8,128]{2,1,0:T(8,128)S(1)} all-to-all(f32[8,8,128]{2,1,0:T(8,128)} %gain_scale.1), channel_id=1, replica_groups=mesh['x'=4,'core'=2,'z'=8,'y'=8] {'x','core'}, dimensions={0} | all-to-all | bytes 65536 | tf_op jit(solution)/shard_map/all_to_all | solution.py:302
  (68 shorter events, 25.3 us)
Async XLA Ops:
  7.2 92.9 %all-gather.3.cloned.1.call-start = ((), (), s32[]{:S(2)}) async-start(), calls=%async_computation.6 | async-start | bytes 6193152 | tf_op jit(solution)/shard_map/all_gather | solution.py:318
  9.3 20.5 %collective-permute-start = (bf16[64,512]{1,0:T(8,128)(2,1)}, bf16[64,512]{1,0:T(8,128)(2,1)S(1)}, u32[]{:S(2)}, u32[]{:S(2)}) collective-permute-start(bf16[64,512]{1,0:T(8,128)(2,1)} %bitcast.39), channel_id=1, source_target_pairs={{0,1},{1,2},{2,3},{3,4},{4,5},{5,6},{6,7},{7,0},{8,9},{9,10},{10,1... | collective-permute-start | bytes 196616 | tf_op jit(solution)/shard_map/ppermute | solution.py:306
  13.4 18.4 %collective-permute-start.4 = (bf16[64,512]{1,0:T(8,128)(2,1)}, bf16[64,512]{1,0:T(8,128)(2,1)S(1)}, u32[]{:S(2)}, u32[]{:S(2)}) collective-permute-start(bf16[64,512]{1,0:T(8,128)(2,1)} %bitcast.40), channel_id=1, source_target_pairs={{0,7},{1,0},{2,1},{3,2},{4,3},{5,4},{6,5},{7,6},{8,15},{9,8},{10,9... | collective-permute-start | bytes 196616 | tf_op jit(solution)/shard_map/ppermute | solution.py:306
  18.9 30.8 %all-to-all-start = ((bf16[8,64,512]{2,1,0:T(8,128)(2,1)}), bf16[8,64,512]{2,1,0:T(8,128)(2,1)S(1)}, u32[]{:S(2)}, u32[]{:S(2)}) async-start(bf16[8,64,512]{2,1,0:T(8,128)(2,1)} %broadcast_in_dim.2), calls=%async_computation | async-start | bytes 1048576 | tf_op jit(solution)/shard_map/all_to_all | solution.py:296
  29.0 168.1 %reduce-scatter.2.cloned.1.call-start = ((), (), s32[]{:S(2)}) async-start(), calls=%async_computation.5 | async-start | bytes 2064384 | tf_op jit(solution)/shard_map/reduce_scatter | solution.py:329
  29.9 6.6 %collective-permute-start.1 = (bf16[64,512]{1,0:T(8,128)(2,1)S(1)}, bf16[64,512]{1,0:T(8,128)(2,1)S(1)}, u32[]{:S(2)}, u32[]{:S(2)}) collective-permute-start(bf16[64,512]{1,0:T(8,128)(2,1)S(1)} %collective-permute-done), channel_id=1, source_target_pairs={{0,1},{1,2},{2,3},{3,4},{4,5},{5,6},{6,7},{7,0},{8,9},{9,10},{10,1... | collective-permute-start | bytes 196616 | tf_op jit(solution)/shard_map/ppermute | solution.py:306
  31.8 6.6 %collective-permute-start.5 = (bf16[64,512]{1,0:T(8,128)(2,1)S(1)}, bf16[64,512]{1,0:T(8,128)(2,1)S(1)}, u32[]{:S(2)}, u32[]{:S(2)}) collective-permute-start(bf16[64,512]{1,0:T(8,128)(2,1)S(1)} %collective-permute-done.4), channel_id=1, source_target_pairs={{0,7},{1,0},{2,1},{3,2},{4,3},{5,4},{6,5},{7,6},{8,15},{9,8},{10,9... | collective-permute-start | bytes 196616 | tf_op jit(solution)/shard_map/ppermute | solution.py:306
  36.5 6.6 %collective-permute-start.2 = (bf16[64,512]{1,0:T(8,128)(2,1)S(1)}, bf16[64,512]{1,0:T(8,128)(2,1)S(1)}, u32[]{:S(2)}, u32[]{:S(2)}) collective-permute-start(bf16[64,512]{1,0:T(8,128)(2,1)S(1)} %collective-permute-done.1), channel_id=1, source_target_pairs={{0,1},{1,2},{2,3},{3,4},{4,5},{5,6},{6,7},{7,0},{8,9},{9,10},{10,1... | collective-permute-start | bytes 196616 | tf_op jit(solution)/shard_map/ppermute | solution.py:306
  38.4 11.3 %collective-permute-start.6 = (bf16[64,512]{1,0:T(8,128)(2,1)S(1)}, bf16[64,512]{1,0:T(8,128)(2,1)S(1)}, u32[]{:S(2)}, u32[]{:S(2)}) collective-permute-start(bf16[64,512]{1,0:T(8,128)(2,1)S(1)} %collective-permute-done.5), channel_id=1, source_target_pairs={{0,7},{1,0},{2,1},{3,2},{4,3},{5,4},{6,5},{7,6},{8,15},{9,8},{10,9... | collective-permute-start | bytes 196616 | tf_op jit(solution)/shard_map/ppermute | solution.py:306
  43.1 6.6 %collective-permute-start.3 = (bf16[64,512]{1,0:T(8,128)(2,1)S(1)}, bf16[64,512]{1,0:T(8,128)(2,1)S(1)}, u32[]{:S(2)}, u32[]{:S(2)}) collective-permute-start(bf16[64,512]{1,0:T(8,128)(2,1)S(1)} %collective-permute-done.2), channel_id=1, source_target_pairs={{0,1},{1,2},{2,3},{3,4},{4,5},{5,6},{6,7},{7,0},{8,9},{9,10},{10,1... | collective-permute-start | bytes 196616 | tf_op jit(solution)/shard_map/ppermute | solution.py:306
  49.7 13.0 %collective-permute-start.14 = (bf16[8,64,512]{2,1,0:T(8,128)(2,1)S(1)}, bf16[8,64,512]{2,1,0:T(8,128)(2,1)S(1)}, u32[]{:S(2)}, u32[]{:S(2)}) collective-permute-start(bf16[8,64,512]{2,1,0:T(8,128)(2,1)S(1)} %all-to-all-done.refs_0_), channel_id=1, source_target_pairs={{0,1},{1,2},{2,3},{3,4},{4,5},{5,6},{6,7},{7,0},{8,9},{9,10},{10,1... | collective-permute-start | bytes 1572872 | tf_op jit(solution)/shard_map/ppermute | solution.py:306
  51.7 17.1 %collective-permute-start.7 = (bf16[8,64,512]{2,1,0:T(8,128)(2,1)S(1)}, bf16[8,64,512]{2,1,0:T(8,128)(2,1)S(1)}, u32[]{:S(2)}, u32[]{:S(2)}) collective-permute-start(bf16[8,64,512]{2,1,0:T(8,128)(2,1)S(1)} %bitcast_dynamic-update-slice_fusion.1.refs_0_), channel_id=1, source_target_pairs={{0,8},{8,16},{16,24},{24,32},{32,40},{40,48},{48,56},{56,0},{1,9},... | collective-permute-start | bytes 1572872 | tf_op jit(solution)/shard_map/ppermute | solution.py:306
  55.1 15.7 %collective-permute-start.18 = (bf16[8,64,512]{2,1,0:T(8,128)(2,1)S(1)}, bf16[8,64,512]{2,1,0:T(8,128)(2,1)S(1)}, u32[]{:S(2)}, u32[]{:S(2)}) collective-permute-start(bf16[8,64,512]{2,1,0:T(8,128)(2,1)S(1)} %all-to-all-done.refs_0_), channel_id=1, source_target_pairs={{0,7},{1,0},{2,1},{3,2},{4,3},{5,4},{6,5},{7,6},{8,15},{9,8},{10,9... | collective-permute-start | bytes 1572872 | tf_op jit(solution)/shard_map/ppermute | solution.py:306
  62.8 12.6 %collective-permute-start.15 = (bf16[8,64,512]{2,1,0:T(8,128)(2,1)S(1)}, bf16[8,64,512]{2,1,0:T(8,128)(2,1)S(1)}, u32[]{:S(2)}, u32[]{:S(2)}) collective-permute-start(bf16[8,64,512]{2,1,0:T(8,128)(2,1)S(1)} %collective-permute-done.14.refs_1_), channel_id=1, source_target_pairs={{0,1},{1,2},{2,3},{3,4},{4,5},{5,6},{6,7},{7,0},{8,9},{9,10},{10,1... | collective-permute-start | bytes 1572872 | tf_op jit(solution)/shard_map/ppermute | solution.py:306
  64.7 12.6 %collective-permute-start.11 = (bf16[8,64,512]{2,1,0:T(8,128)(2,1)S(1)}, bf16[8,64,512]{2,1,0:T(8,128)(2,1)S(1)}, u32[]{:S(2)}, u32[]{:S(2)}) collective-permute-start(bf16[8,64,512]{2,1,0:T(8,128)(2,1)S(1)} %bitcast_dynamic-update-slice_fusion.1.refs_0_), channel_id=1, source_target_pairs={{0,56},{8,0},{16,8},{24,16},{32,24},{40,32},{48,40},{56,48},{1,57}... | collective-permute-start | bytes 1572872 | tf_op jit(solution)/shard_map/ppermute | solution.py:306
  68.8 13.1 %collective-permute-start.8 = (bf16[8,64,512]{2,1,0:T(8,128)(2,1)S(1)}, bf16[8,64,512]{2,1,0:T(8,128)(2,1)S(1)}, u32[]{:S(2)}, u32[]{:S(2)}) collective-permute-start(bf16[8,64,512]{2,1,0:T(8,128)(2,1)S(1)} %collective-permute-done.7.refs_1_), channel_id=1, source_target_pairs={{0,8},{8,16},{16,24},{24,32},{32,40},{40,48},{48,56},{56,0},{1,9},... | collective-permute-start | bytes 1572872 | tf_op jit(solution)/shard_map/ppermute | solution.py:306
  70.8 13.1 %collective-permute-start.19 = (bf16[8,64,512]{2,1,0:T(8,128)(2,1)S(1)}, bf16[8,64,512]{2,1,0:T(8,128)(2,1)S(1)}, u32[]{:S(2)}, u32[]{:S(2)}) collective-permute-start(bf16[8,64,512]{2,1,0:T(8,128)(2,1)S(1)} %collective-permute-done.18.refs_7_), channel_id=1, source_target_pairs={{0,7},{1,0},{2,1},{3,2},{4,3},{5,4},{6,5},{7,6},{8,15},{9,8},{10,9... | collective-permute-start | bytes 1572872 | tf_op jit(solution)/shard_map/ppermute | solution.py:306
  75.4 13.1 %collective-permute-start.16 = (bf16[8,64,512]{2,1,0:T(8,128)(2,1)S(1)}, bf16[8,64,512]{2,1,0:T(8,128)(2,1)}, u32[]{:S(2)}, u32[]{:S(2)}) collective-permute-start(bf16[8,64,512]{2,1,0:T(8,128)(2,1)S(1)} %collective-permute-done.15.refs_2_), channel_id=1, source_target_pairs={{0,1},{1,2},{2,3},{3,4},{4,5},{5,6},{6,7},{7,0},{8,9},{9,10},{10,1... | collective-permute-start | bytes 1572872 | tf_op jit(solution)/shard_map/ppermute | solution.py:306
  77.3 13.1 %collective-permute-start.12 = (bf16[8,64,512]{2,1,0:T(8,128)(2,1)S(1)}, bf16[8,64,512]{2,1,0:T(8,128)(2,1)}, u32[]{:S(2)}, u32[]{:S(2)}) collective-permute-start(bf16[8,64,512]{2,1,0:T(8,128)(2,1)S(1)} %collective-permute-done.11.refs_7_), channel_id=1, source_target_pairs={{0,56},{8,0},{16,8},{24,16},{32,24},{40,32},{48,40},{56,48},{1,57}... | collective-permute-start | bytes 1572872 | tf_op jit(solution)/shard_map/ppermute | solution.py:306
  81.9 13.1 %collective-permute-start.9 = (bf16[8,64,512]{2,1,0:T(8,128)(2,1)S(1)}, bf16[8,64,512]{2,1,0:T(8,128)(2,1)}, u32[]{:S(2)}, u32[]{:S(2)}) collective-permute-start(bf16[8,64,512]{2,1,0:T(8,128)(2,1)S(1)} %collective-permute-done.8.refs_2_), channel_id=1, source_target_pairs={{0,8},{8,16},{16,24},{24,32},{32,40},{40,48},{48,56},{56,0},{1,9},... | collective-permute-start | bytes 1572872 | tf_op jit(solution)/shard_map/ppermute | solution.py:306
  83.9 14.3 %collective-permute-start.20 = (bf16[8,64,512]{2,1,0:T(8,128)(2,1)S(1)}, bf16[8,64,512]{2,1,0:T(8,128)(2,1)}, u32[]{:S(2)}, u32[]{:S(2)}) collective-permute-start(bf16[8,64,512]{2,1,0:T(8,128)(2,1)S(1)} %collective-permute-done.19.refs_6_), channel_id=1, source_target_pairs={{0,7},{1,0},{2,1},{3,2},{4,3},{5,4},{6,5},{7,6},{8,15},{9,8},{10,9... | collective-permute-start | bytes 1572872 | tf_op jit(solution)/shard_map/ppermute | solution.py:306
  88.5 11.6 %collective-permute-start.17 = (bf16[8,64,512]{2,1,0:T(8,128)(2,1)}, bf16[8,64,512]{2,1,0:T(8,128)(2,1)}, u32[]{:S(2)}, u32[]{:S(2)}) collective-permute-start(bf16[8,64,512]{2,1,0:T(8,128)(2,1)} %collective-permute-done.16.refs_3_), channel_id=1, source_target_pairs={{0,1},{1,2},{2,3},{3,4},{4,5},{5,6},{6,7},{7,0},{8,9},{9,10},{10,1... | collective-permute-start | bytes 1572872 | tf_op jit(solution)/shard_map/ppermute | solution.py:306
  90.4 21.0 %collective-permute-start.13 = (bf16[8,64,512]{2,1,0:T(8,128)(2,1)}, bf16[8,64,512]{2,1,0:T(8,128)(2,1)}, u32[]{:S(2)}, u32[]{:S(2)}) collective-permute-start(bf16[8,64,512]{2,1,0:T(8,128)(2,1)} %collective-permute-done.12.refs_6_), channel_id=1, source_target_pairs={{0,56},{8,0},{16,8},{24,16},{32,24},{40,32},{48,40},{56,48},{1,57}... | collective-permute-start | bytes 1572872 | tf_op jit(solution)/shard_map/ppermute | solution.py:306
  95.0 16.4 %collective-permute-start.10 = (bf16[8,64,512]{2,1,0:T(8,128)(2,1)}, bf16[8,64,512]{2,1,0:T(8,128)(2,1)}, u32[]{:S(2)}, u32[]{:S(2)}) collective-permute-start(bf16[8,64,512]{2,1,0:T(8,128)(2,1)} %collective-permute-done.9.refs_3_), channel_id=1, source_target_pairs={{0,8},{8,16},{16,24},{24,32},{32,40},{40,48},{48,56},{56,0},{1,9},... | collective-permute-start | bytes 1572872 | tf_op jit(solution)/shard_map/ppermute | solution.py:306
  (10 other events, 348.8 us)
Sparse Core Ops, SparseCore 0:
  10.1 48.8 all-gather.2
  157.5 37.6 reduce-scatter.1
